TPU v7x, 32 devices: a whole 2x2x4 slice. The times are simulated.
32 devices in a mesh: store: 8 (over z, x), trainer: 4 (over y, core).
Axes of the slice: x: 2, y: 2, z: 4, core: 2. Of those that a mesh axis runs over, the one named last changes fastest.
Arguments:
- features: float32 [1024, 768], P('store'), may hold values from -6 to 6
- self_rows: float32 [4096, 768], P(('store', 'trainer')), may hold values from -6 to 6
- edge_row: int32 [4, 8, 8, 12, 2], P('trainer', 'store'), may hold values from 0 to 128, as said below
- recv_target: int32 [4, 8, 8, 12], P('trainer', 'store'), may hold values from 0 to 128, as said below
- cotangent: bfloat16 [4096, 768], P(('store', 'trainer')), may hold values from -6 to 6
- w_self: bfloat16 [768, 768], replicated, may hold values from -0.21875 to 0.21875
- w_neigh: bfloat16 [768, 768], replicated, may hold values from -0.21875 to 0.21875
Outputs:
- hidden: bfloat16 [4096, 768], P(('store', 'trainer'))
- grad_self: float32 [768, 768], P('store')
- grad_neigh: float32 [768, 768], P('store')
Inputs may be any that keep to these rules, and one draw needn't show every extreme that they name: `edge_row`: A slot that no target uses holds no rows, and every used slot holds at least one row. `recv_target`: slots of an owner to one destination may name the same target more than once; a target may have no slot.
All inputs are finite; a program needn't handle non-finite values.
Results may differ from a plain program's by a relative error of at most 0.0059.
Values may be sent and summed in bfloat16 or wider, within the bound.
No kernel may reach another device: no remote copies, remote signals or barrier semaphores. Data moves between devices by JAX's collectives and lax.ppermute only.
A program may use at most 64 MiB of HBM per device.

v0:
```python
import jax
import jax.numpy as jnp
from jax import lax
from jax.sharding import PartitionSpec as P


def per_device(features, self_rows, edge_row, recv_target, cotangent, w_self, w_neigh):
    owned = features.shape[0]
    width = features.shape[1]
    out_width = w_self.shape[1]
    tgt_count = self_rows.shape[0]
    store_table = jnp.concatenate([features, jnp.zeros((1, width), jnp.float32)], axis=0)
    edge_ids = edge_row[0, 0]
    picked = jnp.take(store_table, edge_ids, axis=0)
    partial_value = jnp.sum(picked, axis=2).astype(jnp.bfloat16)
    counts = jnp.sum((edge_ids < owned).astype(jnp.float32), axis=2).astype(jnp.bfloat16)
    own_rows = self_rows.astype(jnp.bfloat16)
    self_term = jnp.dot(own_rows, w_self, preferred_element_type=jnp.float32)
    arrived, arrived_counts = (
        lax.all_to_all(partial_value, "store", split_axis=0, concat_axis=0, tiled=True),
        lax.all_to_all(counts, "store", split_axis=0, concat_axis=0, tiled=True),
    )
    slot_targets = recv_target[0, 0].reshape(-1)
    matches = slot_targets[None, :] == jnp.arange(tgt_count, dtype=jnp.int32)[:, None]
    onehot = matches.astype(jnp.bfloat16)
    summed = jnp.dot(onehot, arrived.reshape(-1, width), preferred_element_type=jnp.float32)
    slot_numbers = arrived_counts.reshape(-1).astype(jnp.float32)
    number = jnp.sum(jnp.where(matches, slot_numbers[None, :], jnp.float32(0.0)), axis=1)
    neighbor_mean = (summed / jnp.maximum(number, 1.0)[:, None]).astype(jnp.bfloat16)
    preact = self_term + jnp.dot(neighbor_mean, w_neigh, preferred_element_type=jnp.float32)
    sigmoid_val = jax.nn.sigmoid(preact)
    hidden = (preact * sigmoid_val).astype(jnp.bfloat16)
    grad_out = (
        cotangent.astype(jnp.float32) * (sigmoid_val * (1.0 + preact * (1.0 - sigmoid_val)))
    ).astype(jnp.bfloat16)
    stacked = jnp.stack([own_rows, neighbor_mean], axis=1)
    terms = jnp.einsum(
        "tcf,th->fch", stacked, grad_out, preferred_element_type=jnp.float32
    ).reshape(width, 2 * out_width)
    store_part = lax.psum_scatter(terms, "store", scatter_dimension=0, tiled=True)
    grad_shard = lax.psum(store_part, "trainer")
    return (hidden, grad_shard[:, :out_width], grad_shard[:, out_width:])


def solution(mesh):
    in_specs = (
        P("store", None),
        P(("store", "trainer"), None),
        P("trainer", "store", None, None, None),
        P("trainer", "store", None, None),
        P(("store", "trainer"), None),
        P(),
        P(),
    )
    out_specs = (P(("store", "trainer"), None), P("store", None), P("store", None))
    return jax.shard_map(
        per_device, mesh=mesh, in_specs=in_specs, out_specs=out_specs, check_vma=False
    )
```

profile of v0, /device:TPU:0, one launch (start us, length us, event | category | flops | bytes accessed | tf_op | source)
XLA Modules:
  0.0 186.3 jit_solution(5632729517474135640)
XLA Ops:
  7.2 0.0 copy-start
  7.2 0.8 fusion.9
  8.0 0.6 copy.24
  8.6 7.3 %all-to-all-start.1 = ((bf16[8,1,12]{2,1,0:T(2,128)(2,1)}), bf16[8,1,12]{2,1,0:T(2,128)(2,1)S(1)}, u32[]{:S(2)}, u32[]{:S(2)}) async-start(bf16[8,1,12]{2,1,0:T(2,128)(2,1)} %copy.24), calls=%async_computation.1 | async-start | bytes 8192 | tf_op jit(solution)/shard_map/all_to_all | solution.py:21
  15.8 0.7 compare_and_fusion
  16.6 0.7 compare_select_fusion
  17.3 0.2 copy.22
  17.4 0.1 copy.23
  17.6 0.1 reshape.74
  17.7 0.0 copy-start.1
  17.7 1.1 convert_bitcast_fusion
  18.8 1.7 fusion.6
  20.5 0.0 copy-done.1
  20.6 1.0 gather_fusion
  21.5 0.0 copy-start.3
  21.6 0.3 reshape.73
  21.9 1.5 select_reduce_fusion
  23.4 0.0 copy-done.3
  23.4 0.1 eq.15
  23.5 0.0 all-to-all-done.1
  23.5 6.0 %all-to-all-start = ((bf16[8,12,768]{2,1,0:T(8,128)(2,1)}), bf16[8,12,768]{2,1,0:T(8,128)(2,1)S(1)}, u32[]{:S(2)}, u32[]{:S(2)}) async-start(bf16[8,12,768]{2,1,0:T(8,128)(2,1)} %select_reduce_fusion), calls=%async_computation | async-start | bytes 393216 | tf_op jit(solution)/shard_map/all_to_all | solution.py:20
  29.5 0.0 reduce-scatter.2.cloned.1.call-start
  29.6 0.1 reshape.71
  29.7 0.1 select_reduce_fusion.1
  29.8 7.5 %all-to-all-done = bf16[8,12,768]{2,1,0:T(8,128)(2,1)S(1)} async-done(((bf16[8,12,768]{2,1,0:T(8,128)(2,1)}), bf16[8,12,768]{2,1,0:T(8,128)(2,1)S(1)}, u32[]{:S(2)}, u32[]{:S(2)}) %all-to-all-start) | async-done | bytes 147488 | tf_op jit(solution)/shard_map/all_to_all | solution.py:20
  37.3 0.3 fusion
  37.7 0.0 copy-done
  37.7 0.0 copy-start.2
  37.7 1.0 multiply_convert_fusion.1
  38.7 0.0 copy-done.2
  38.7 3.0 %fusion.1 = f32[768,2,768]{2,0,1:T(8,128)} fusion(bf16[128,1,768]{2,0,1:T(8,128)(2,1)S(1)} %bitcast.26, bf16[128,1,768]{2,0,1:T(8,128)(2,1)S(1)} %convert_bitcast_fusion, f32[128,768]{1,0:T(8,128)S(1)} %get-tuple-element.6, bf16[128,768]{1,0:T(8,128)(2,1)S(1)} %copy-done.2), kind=kOutput, calls=%fused_computation.5 | convolution fusion | flops 303759360 | bytes 5701632 | tf_op jit(solution)/shard_map/tcf,th->fch/dot_general | solution.py:37
  41.7 6.0 %copy.26 = f32[768,1536]{1,0:T(8,128)} copy(f32[768,1536]{0,1:T(8,128)} %bitcast.25) | data formatting | bytes 9437184 | tf_op jit(solution)/shard_map/reshape | solution.py:39
  47.8 0.0 reduce-scatter.2.cloned.1.call-update
  47.8 0.0 all-reduce.3.cloned.1.call-start
  47.8 94.1 %reduce-scatter.2.cloned.1.call-done = f32[96,1536]{1,0:T(8,128)} async-done(((f32[768,1536]{1,0:T(8,128)}), f32[96,1536]{1,0:T(8,128)}) %reduce-scatter.2.cloned.1.call-update) | async-done | bytes 589840 | tf_op jit(solution)/shard_map/reduce_scatter | solution.py:40
  142.0 0.0 all-reduce.3.cloned.1.call-update
  142.0 35.6 %all-reduce.3.cloned.1.call-done = f32[96,1536]{1,0:T(8,128)} async-done(((f32[96,1536]{1,0:T(8,128)}), f32[96,1536]{1,0:T(8,128)}) %all-reduce.3.cloned.1.call-update) | async-done | bytes 589840 | tf_op jit(solution)/shard_map/psum | solution.py:41
  177.6 1.9 %fusion.12 = (f32[96,768]{1,0:T(8,128)}, f32[96,768]{1,0:T(8,128)}) fusion(f32[96,1536]{1,0:T(8,128)} %all-reduce.3.cloned.1.call-done), kind=kLoop, calls=%fused_computation.30 | loop fusion | bytes 1179648 | tf_op jit(solution)/shard_map/slice | solution.py:42
  (5 shorter events, 0.1 us)
Async XLA Ops:
  7.2 30.5 %copy-start = (bf16[768,768]{1,0:T(8,128)(2,1)S(1)}, bf16[768,768]{1,0:T(8,128)(2,1)}, u32[]{:S(2)}) copy-start(bf16[768,768]{1,0:T(8,128)(2,1)} %param.13) | copy-start | bytes 3538948
  8.6 14.9 %all-to-all-start.1 = ((bf16[8,1,12]{2,1,0:T(2,128)(2,1)}), bf16[8,1,12]{2,1,0:T(2,128)(2,1)S(1)}, u32[]{:S(2)}, u32[]{:S(2)}) async-start(bf16[8,1,12]{2,1,0:T(2,128)(2,1)} %copy.24), calls=%async_computation.1 | async-start | bytes 8192 | tf_op jit(solution)/shard_map/all_to_all | solution.py:21
  17.7 2.8 %copy-start.1 = (f32[128,768]{1,0:T(8,128)S(1)}, f32[128,768]{1,0:T(8,128)}, u32[]{:S(2)}) copy-start(f32[128,768]{1,0:T(8,128)} %param.7) | copy-start | bytes 1179652
  21.5 1.9 %copy-start.3 = (s32[1,1,8,12]{3,2,1,0:T(8,128)S(1)}, s32[1,1,8,12]{3,2,1,0:T(8,128)}, u32[]{:S(2)}) copy-start(s32[1,1,8,12]{3,2,1,0:T(8,128)} %param.10) | copy-start | bytes 1156
  23.5 13.8 %all-to-all-start = ((bf16[8,12,768]{2,1,0:T(8,128)(2,1)}), bf16[8,12,768]{2,1,0:T(8,128)(2,1)S(1)}, u32[]{:S(2)}, u32[]{:S(2)}) async-start(bf16[8,12,768]{2,1,0:T(8,128)(2,1)} %select_reduce_fusion), calls=%async_computation | async-start | bytes 393216 | tf_op jit(solution)/shard_map/all_to_all | solution.py:20
  29.5 112.5 %reduce-scatter.2.cloned.1.call-start = ((), (), s32[]{:S(2)}) async-start(), calls=%async_computation.3 | async-start | bytes 5308416 | tf_op jit(solution)/shard_map/reduce_scatter | solution.py:40
  37.7 1.1 copy-start.2
  47.8 129.8 %all-reduce.3.cloned.1.call-start = ((), (), s32[]{:S(2)}) async-start(), calls=%async_computation.4 | async-start | bytes 1179648 | tf_op jit(solution)/shard_map/psum | solution.py:41
Sparse Core Ops, SparseCore 0:
  47.9 93.9 reduce-scatter.1
  144.3 33.2 all-reduce.2
where the time goes:
time: 187 us; the launch traced here: 186 us
  waiting for transfers between devices  137 us (73%)
  between operations  14.2 us (8%)
  starting transfers between devices  13.3 us (7%)
  local copies, waits for them, and re-layouts  10.5 us (6%)
  matrix products  6.1 us (3%)
  other arithmetic  4.95 us (3%)
    reduce_scatter x1, waiting for transfers between devices, per_device(): lax.psum_scatter(terms, 'store', scatter_dimension=0, tiled=True)  94.1 us
    psum x1, waiting for transfers between devices, per_device(): grad_shard = lax.psum(store_part, 'trainer')  35.6 us
    all_to_all x1, waiting for transfers between devices, per_device(): lax.all_to_all(partial_value, 'store', split_axis=0, concat_axis=0, tiled...  7.52 us
    all_to_all x1, starting transfers between devices, per_device(): lax.all_to_all(counts, 'store', split_axis=0, concat_axis=0, tiled=True)  7.25 us
    reshape x1, local copies, waits for them, and re-layouts, per_device(): terms = jnp.einsum('tcf,th->fch', stacked, grad_out, preferred_element_ty...  6.04 us
    all_to_all x1, starting transfers between devices, per_device(): lax.all_to_all(partial_value, 'store', split_axis=0, concat_axis=0, tiled...  6.01 us
  transfers between devices with their start and end apart: 4, of which 3 were waited for; matrix products, arithmetic and copies ran while one was open for 4% of the time, Pallas kernels for 0%

commit v1 on v0

v1 whole, which is shorter than its diff:
```python
import functools

import jax
import jax.numpy as jnp
from jax import lax
from jax.experimental import pallas as pl
from jax.experimental.pallas import tpu as pltpu
from jax.sharding import PartitionSpec as P

BF16, F32 = jnp.bfloat16, jnp.float32
SLOT_PAD = 16
VMEM = pl.BlockSpec(memory_space=pltpu.VMEM)
ANY = pl.BlockSpec(memory_space=pl.ANY)
HBM = pl.BlockSpec(memory_space=pltpu.HBM)
PARAMS = pltpu.CompilerParams(vmem_limit_bytes=16 * 1024 * 1024)


def dot(a, b):
    return jnp.dot(a, b, preferred_element_type=F32)


def call(body, outs, args, unread=(), hbm=(), scratch=(), flops=0):
    moved = sum(a.size * a.dtype.itemsize for a in tuple(args) + tuple(outs))
    return pl.pallas_call(
        body,
        out_shape=list(outs),
        in_specs=[VMEM] * len(args) + [ANY] * len(unread) + [HBM] * len(hbm),
        out_specs=[VMEM] * len(outs),
        scratch_shapes=list(scratch),
        compiler_params=PARAMS,
        cost_estimate=pl.CostEstimate(flops=flops, bytes_accessed=moved, transcendentals=0),
    )(*args, *unread, *hbm)


def shape(dims, kind):
    return jax.ShapeDtypeStruct(dims, kind)


def slot_sums(cap, ids, feat_copy, feat_ref, out_ref):
    owned, slots = feat_ref.shape[0], ids.shape[1]
    row = lax.broadcasted_iota(jnp.int32, (owned, slots), 0)
    weight = jnp.zeros((owned, slots), F32)
    count = jnp.zeros((1, slots), F32)
    for m in range(ids.shape[0]):
        weight += (row == ids[m:m + 1, :]).astype(F32)
        count += (ids[m:m + 1, :] < owned).astype(F32)
    pick = weight.T.astype(BF16)
    r = lax.broadcasted_iota(jnp.int32, (slots, slots), 0)
    c = lax.broadcasted_iota(jnp.int32, (slots, slots), 1)
    here = ((r & (SLOT_PAD - 1)) == cap) & ((c - (c & (SLOT_PAD - 1))) == (r - (r & (SLOT_PAD - 1))))
    spread = jnp.where(here, jnp.broadcast_to(count, (slots, slots)), 0.0).astype(BF16)
    c2 = lax.broadcasted_iota(jnp.int32, (slots, 128), 0)
    l2 = lax.broadcasted_iota(jnp.int32, (slots, 128), 1)
    fold = ((c2 & (SLOT_PAD - 1)) == l2).astype(BF16)
    counts = dot(spread, fold)
    feat_copy.wait()
    feat = feat_ref[...]
    high = feat.astype(BF16)
    low = (feat - high.astype(F32)).astype(BF16)
    sums = dot(pick, high) + dot(pick, low)
    out_ref[:, :128] = (sums[:, :128] + counts).astype(BF16)
    out_ref[:, 128:] = sums[:, 128:].astype(BF16)


def slot_sums_kernel(cap, feat_hbm, edge_hbm, out_ref, feat_ref, edge_ref, sems):
    copies = [pltpu.make_async_copy(edge_hbm, edge_ref, sems.at[0]),
              pltpu.make_async_copy(feat_hbm, feat_ref, sems.at[1])]
    for copy in copies:
        copy.start()
    owned = feat_ref.shape[0]
    ns, mult, _ = edge_ref.shape
    fill = jnp.full((mult, SLOT_PAD - cap), owned, jnp.int32)
    copies[0].wait()
    ids = jnp.concatenate([p for d in range(ns) for p in (edge_ref[d], fill)], axis=1)
    slot_sums(cap, ids, copies[1], feat_ref, out_ref)


def neighbor_mean(cap, rows, recv, targets):
    slots = rows.shape[0]
    target = lax.broadcasted_iota(jnp.int32, (targets, slots), 0)
    onehot = (target == recv).astype(BF16)
    r = lax.broadcasted_iota(jnp.int32, (slots, slots), 0)
    c = lax.broadcasted_iota(jnp.int32, (slots, slots), 1)
    from_count = (c == (r - (r & (SLOT_PAD - 1)) + cap)).astype(BF16)
    copied = dot(from_count, rows[:, :128])
    r2 = lax.broadcasted_iota(jnp.int32, (slots, 128), 0)
    l2 = lax.broadcasted_iota(jnp.int32, (slots, 128), 1)
    counts = jnp.where((r2 & (SLOT_PAD - 1)) == l2, copied, 0.0).astype(BF16)
    number = jnp.sum(dot(onehot, counts), axis=1, keepdims=True)
    return (dot(onehot, rows) / jnp.maximum(number, 1.0)).astype(BF16)


def forward(preact, cot):
    sig = jax.nn.sigmoid(preact)
    hidden = (preact * sig).astype(BF16)
    grad = (cot.astype(F32) * (sig * (1.0 + preact * (1.0 - sig)))).astype(BF16)
    return hidden, grad


class Plan:
    def __init__(self, mesh, width, out_width):
        self.ns, self.nt = mesh.shape["store"], mesh.shape["trainer"]
        self.gx = 2 if self.ns % 2 == 0 else 1
        self.nz = self.ns // self.gx
        self.gc = 2
        self.gy = max(self.nt // self.gc, 1)
        self.shard = width // self.ns
        self.rows = self.nz * self.shard
        self.cols = out_width // self.gy
        self.peers = [(dx, dy) for dx in range(self.gx) for dy in range(self.gy)]

    def fits(self):
        pow2 = all((n & (n - 1)) == 0 for n in (self.ns, self.nt))
        return (pow2 and self.ns <= 8 and self.gy * self.gc == self.nt and self.cols % 128 == 0
                and self.shard % 16 == 0 and len(self.peers) <= 4 and self.nz <= 4)

    def place(self):
        s, t = lax.axis_index("store"), lax.axis_index("trainer")
        return s // self.gx, s % self.gx, t // self.gc, t % self.gc

    def send(self, array, to):
        pairs = []
        for s in range(self.ns):
            for t in range(self.nt):
                z, x, y, c = to(s // self.gx, s % self.gx, t // self.gc, t % self.gc)
                pairs.append((s * self.nt + t, (z * self.gx + x) * self.nt + y * self.gc + c))
        return lax.ppermute(array, ("store", "trainer"), pairs)


def write_rows(plan, trans_ref, outs):
    x = plan.place()[1]
    for (dx, dy), out in zip(plan.peers, outs):
        for z in range(plan.nz):
            start = pl.multiple_of((z * plan.gx + (x ^ dx)) * plan.shard, 16)
            out[z * plan.shard:(z + 1) * plan.shard, :] = trans_ref[pl.ds(start, plan.shard), :]


def own_kernel(plan, self_ref, _, own_ref, *rest):
    outs, trans_ref = rest[:-1], rest[-1]
    own_ref[...] = self_ref[...].astype(BF16)
    trans_ref[...] = self_ref[...].T.astype(BF16)
    write_rows(plan, trans_ref, outs)


def mean_kernel(plan, cap, rows_ref, recv_ref, mean_ref, *rest):
    outs, trans_ref = rest[:-1], rest[-1]
    mean = neighbor_mean(cap, rows_ref[...], recv_ref[...], mean_ref.shape[0])
    mean_ref[...] = mean
    trans_ref[...] = mean.astype(F32).T.astype(BF16)
    write_rows(plan, trans_ref, outs)


def layer_kernel(plan, ordered, mean_ref, self_ref, cot_ref, w_ref, *rest):
    hidden_ref, *outs = rest[ordered:-1]
    grad_ref = rest[-1]
    targets = self_ref.shape[0]
    preact = self_ref[...] + dot(mean_ref[...], w_ref[...])
    hidden, grad = forward(preact, cot_ref[...])
    hidden_ref[...] = hidden
    for b in range(grad_ref.shape[0]):
        grad_ref[b] = grad[:, b * 128:(b + 1) * 128]
    y = plan.place()[2]
    each = plan.cols // 128
    for (dx, dy), out in zip(plan.peers, outs):
        for b in range(each):
            out[b * targets:(b + 1) * targets, :] = grad_ref[(y ^ dy) * each + b]


def terms_kernel(plan, *refs):
    n = len(plan.peers)
    own, mean, grad = refs[:n], refs[n:2 * n], refs[2 * n:3 * n]
    keep_ref, send_ref, total_ref = refs[3 * n:]
    rows, each, targets = plan.rows, plan.cols // 128, own[0].shape[1]
    left = jnp.concatenate(
        [jnp.concatenate([o[...], m[...]], axis=0) for o, m in zip(own, mean)], axis=1)
    right = jnp.concatenate(
        [jnp.concatenate([g[b * targets:(b + 1) * targets, :] for b in range(each)], axis=1)
         for g in grad], axis=0)
    total_ref[...] = dot(left, right)
    c = plan.place()[3]
    keep_ref[...] = total_ref[pl.ds(pl.multiple_of(c * rows, 16), rows), :]
    send_ref[...] = total_ref[pl.ds(pl.multiple_of((1 - c) * rows, 16), rows), :].astype(BF16)


def core_sum_kernel(plan, keep_ref, got_ref, *rest):
    outs, total_ref = rest[:-1], rest[-1]
    total_ref[...] = keep_ref[...] + got_ref[...].astype(F32)
    z = plan.place()[0]
    for k, out in enumerate(outs):
        start = pl.multiple_of((z ^ k) * plan.shard, 16)
        out[...] = total_ref[pl.ds(start, plan.shard), :].astype(out.dtype)


def store_sum_kernel(*refs):
    total = refs[0][...]
    for r in refs[1:-1]:
        total += r[...].astype(F32)
    refs[-1][...] = total.astype(BF16)


def assemble_kernel(plan, *refs):
    parts, (self_ref, neigh_ref, both_ref) = refs[:-3], refs[-3:]
    _, _, y, c = plan.place()
    for i, part in enumerate(parts):
        cols = pl.ds(pl.multiple_of((y ^ (i // plan.gc)) * plan.cols, 128), plan.cols)
        both_ref[c ^ (i % plan.gc), :, cols] = part[...].astype(F32)
    self_ref[...] = both_ref[0]
    neigh_ref[...] = both_ref[1]


def per_device(plan, features, self_rows, edge_row, recv_target, cotangent, w_self, w_neigh):
    owned, width = features.shape
    out_width = w_self.shape[1]
    targets = self_rows.shape[0]
    ns, cap, mult = edge_row.shape[2:]
    slots = ns * SLOT_PAD
    edges = edge_row[0, 0].transpose(0, 2, 1)
    pad = ((0, 0), (0, SLOT_PAD - cap))
    recv = jnp.pad(recv_target[0, 0], pad, constant_values=targets).reshape(1, slots)

    (sums,) = call(
        functools.partial(slot_sums_kernel, cap), [shape((slots, width), BF16)], (),
        hbm=[features, edges], flops=4 * slots * owned * width,
        scratch=[pltpu.VMEM(features.shape, F32), pltpu.VMEM(edges.shape, jnp.int32),
                 pltpu.SemaphoreType.DMA((2,))])
    arrived = lax.all_to_all(sums.reshape(ns, SLOT_PAD, width), "store",
                             split_axis=0, concat_axis=0, tiled=True).reshape(slots, width)
    if not plan.fits():
        own = self_rows.astype(BF16)
        mean = neighbor_mean(cap, arrived, recv, targets)
        preact = dot(own, w_self) + dot(mean, w_neigh)
        hidden, grad = forward(preact, cotangent)
        both = jnp.concatenate([own.T.reshape(ns, -1, targets), mean.T.reshape(ns, -1, targets)], axis=1)
        terms = dot(both.reshape(2 * width, targets), grad)
        part = lax.psum_scatter(terms, "store", scatter_dimension=0, tiled=True)
        total = lax.psum(part, "trainer")
        return hidden, total[:plan.shard], total[plan.shard:]

    n, rows, cols = len(plan.peers), plan.rows, plan.cols
    own, *own_rows = call(
        functools.partial(own_kernel, plan),
        [shape((targets, width), BF16)] + [shape((rows, targets), BF16)] * n, [self_rows], unread=[sums],
        scratch=[pltpu.VMEM((width, targets), BF16)])
    self_term = dot(own, w_self)

    def exchange(arrays):
        return [arrays[0]] + [
            plan.send(a, lambda z, x, y, c, dx=dx, dy=dy: (z, x ^ dx, y ^ dy, c))
            for (dx, dy), a in zip(plan.peers[1:], arrays[1:])]

    own_all = exchange(own_rows)
    mean, *mean_rows = call(
        functools.partial(mean_kernel, plan, cap),
        [shape((targets, width), BF16)] + [shape((rows, targets), BF16)] * n, [arrived, recv],
        scratch=[pltpu.VMEM((width, targets), BF16)], flops=2 * targets * width * slots)
    mean_all = exchange(mean_rows)
    hidden, *grads = call(
        functools.partial(layer_kernel, plan, n - 1),
        [shape((targets, out_width), BF16)] + [shape((cols // 128 * targets, 128), BF16)] * n,
        [mean, self_term, cotangent, w_neigh], unread=own_all[1:],
        scratch=[pltpu.VMEM((out_width // 128, targets, 128), BF16)],
        flops=2 * targets * width * out_width)
    keep, give = call(
        functools.partial(terms_kernel, plan),
        [shape((rows, cols), F32), shape((rows, cols), BF16)],
        own_all + mean_all + exchange(grads), scratch=[pltpu.VMEM((2 * rows, cols), F32)],
        flops=4 * rows * cols * targets * n)
    got = plan.send(give, lambda z, x, y, c: (z, x, y, 1 - c))
    block = (plan.shard, cols)
    mine, *others = call(
        functools.partial(core_sum_kernel, plan),
        [shape(block, F32)] + [shape(block, BF16)] * (plan.nz - 1), [keep, got],
        scratch=[pltpu.VMEM((rows, cols), F32)])
    got = [plan.send(others[k - 1], lambda z, x, y, c, k=k: (z ^ k, x, y, c))
           for k in sorted(range(1, plan.nz), key=lambda k: (k < 2, k))]
    (quarter,) = call(store_sum_kernel, [shape(block, BF16)], [mine] + got)
    column = [quarter] + [plan.send(quarter, lambda z, x, y, c, i=i: (z, x, y ^ i, c))
                          for i in range(1, plan.gy)]
    quarters = [q for part in column
                for q in (part, plan.send(part, lambda z, x, y, c: (z, x, y, 1 - c)))]
    grads = call(functools.partial(assemble_kernel, plan),
                 [shape((plan.shard, out_width), F32)] * 2, quarters,
                 scratch=[pltpu.VMEM((2, plan.shard, out_width), F32)])
    return hidden, grads[0], grads[1]


def solution(mesh):
    in_specs = (
        P("store", None),
        P(("store", "trainer"), None),
        P("trainer", "store", None, None, None),
        P("trainer", "store", None, None),
        P(("store", "trainer"), None),
        P(),
        P(),
    )
    out_specs = (P(("store", "trainer"), None), P("store", None), P("store", None))

    def run(features, self_rows, edge_row, recv_target, cotangent, w_self, w_neigh):
        plan = Plan(mesh, features.shape[1], w_self.shape[1])
        return jax.shard_map(
            functools.partial(per_device, plan), mesh=mesh, in_specs=in_specs,
            out_specs=out_specs, check_vma=False,
        )(features, self_rows, edge_row, recv_target, cotangent, w_self, w_neigh)

    return run
```

time: 187 us -> 51.5 us (0.28)
  waiting for transfers between devices: 137 us -> 20.5 us
  between operations: 14.2 us -> 0.75 us
  starting transfers between devices: 13.3 us -> 22.2 us
  local copies, waits for them, and re-layouts: 10.5 us -> 1.89 us
  matrix products: 6.1 us -> 0.32 us
  Pallas kernels: 0 us -> 5.56 us
  other arithmetic: 4.95 us -> 0 us
    reduce_scatter x1 -> x0, waiting for transfers between devices: 94.1 us -> none  [per_device(): lax.psum_scatter(terms, 'store', scatter_dimension=0, tiled=True)]
    psum x1 -> x0, waiting for transfers between devices: 35.6 us -> none  [per_device(): grad_shard = lax.psum(store_part, 'trainer')]
    ppermute x0 -> x16, waiting for transfers between devices: none -> 16.9 us  [send(): return lax.ppermute(array, ('store', 'trainer'), pairs)]
    ppermute x0 -> x16, starting transfers between devices: none -> 15 us  [send(): return lax.ppermute(array, ('store', 'trainer'), pairs)]
    all_to_all x2 -> x1, starting transfers between devices: 13.3 us -> 7.27 us  [per_device(): lax.all_to_all(sums.reshape(ns, SLOT_PAD, width), 'store', split_axis=0,...]
    reshape x2 -> x1, local copies, waits for them, and re-layouts: 6.07 us -> 0.08 us  [per_device(): jnp.pad(recv_target[0, 0], pad, constant_values=targets).reshape(1, slots)]
    dot_general x4 -> x1, matrix products: 6.1 us -> 0.32 us  [dot(): return jnp.dot(a, b, preferred_element_type=F32)]
    pallas_call x0 -> x8, Pallas kernels: none -> 5.56 us  [call(): pl.pallas_call(body, out_shape=list(outs), in_specs=[VMEM] * len(args) +...]
  transfers between devices with their start and end apart: 4 -> 17, of which waited for: 3 -> 10; matrix products, arithmetic and copies ran while one was open for 4% -> 1% of each run, Pallas kernels for 0% -> 5%
where the time goes in v1:
time: 51.5 us; the launch traced here: 51.2 us
  starting transfers between devices  22.2 us (43%)
  waiting for transfers between devices  20.5 us (40%)
  Pallas kernels  5.56 us (11%)
  local copies, waits for them, and re-layouts  1.89 us (4%)
  between operations  0.75 us (1%)
    ppermute x16, waiting for transfers between devices, send(): return lax.ppermute(array, ('store', 'trainer'), pairs)  16.9 us
    ppermute x16, starting transfers between devices, send(): return lax.ppermute(array, ('store', 'trainer'), pairs)  15 us
    all_to_all x1, starting transfers between devices, per_device(): lax.all_to_all(sums.reshape(ns, SLOT_PAD, width), 'store', split_axis=0,...  7.27 us
    pallas_call x8, Pallas kernels, call(): pl.pallas_call(body, out_shape=list(outs), in_specs=[VMEM] * len(args) +...  5.56 us
    all_to_all x1, waiting for transfers between devices, per_device(): lax.all_to_all(sums.reshape(ns, SLOT_PAD, width), 'store', split_axis=0,...  3.55 us
    unnamed x14, local copies, waits for them, and re-layouts  1.81 us
  transfers between devices with their start and end apart: 17, of which 10 were waited for; matrix products, arithmetic and copies ran while one was open for 1% of the time, Pallas kernels for 5%

profile of v1, /device:TPU:0, one launch (start us, length us, event | category | flops | bytes accessed | tf_op | source)
XLA Modules:
  0.0 51.2 jit_solution(2475077744330232665)
XLA Ops:
  0.6 0.0 copy-start
  0.6 0.0 copy-start.2
  0.7 1.1 %copy-done.2 = f32[128,768]{1,0:T(8,128)S(1)} copy-done((f32[128,768]{1,0:T(8,128)S(1)}, f32[128,768]{1,0:T(8,128)}, u32[]{:S(2)}) %copy-start.2) | copy-done | bytes 393240
  1.7 0.0 copy-start.5
  1.7 0.7 %copy-done.5 = s32[1,1,8,12,2]{3,4,2,1,0:T(2,128)S(1)} copy-done((s32[1,1,8,12,2]{3,4,2,1,0:T(2,128)S(1)}, s32[1,1,8,12,2]{3,4,2,1,0:T(2,128)}, u32[]{:S(2)}) %copy-start.5) | copy-done | bytes 792
  2.4 0.0 copy-start.3
  2.4 0.0 copy-start.6
  2.4 1.4 %shard_map.94._ = bf16[128,768]{1,0:T(8,128)(2,1)} custom-call(f32[128,768]{1,0:T(8,128)S(1)} %copy-done.2, s32[8,2,12]{2,1,0:T(2,128)S(1)} %bitcast.9), custom_call_target="tpu_custom_call" | custom-call | flops 50331648 | bytes 196608 | tf_op jit(solution)/shard_map/pallas_call | solution.py:24
  3.8 7.3 %all-to-all-start = ((bf16[8,16,768]{2,1,0:T(8,128)(2,1)}), bf16[8,16,768]{2,1,0:T(8,128)(2,1)S(1)}, u32[]{:S(2)}, u32[]{:S(2)}) async-start(bf16[8,16,768]{2,1,0:T(8,128)(2,1)} %bitcast.2), calls=%async_computation | async-start | bytes 393216 | tf_op jit(solution)/shard_map/all_to_all | solution.py:226
  11.1 0.0 copy-done.3
  11.1 0.0 copy-start.1
  11.1 0.0 copy-start.4
  11.1 0.9 %shard_map.96 = (bf16[128,768]{1,0:T(8,128)(2,1)S(1)}, bf16[384,128]{1,0:T(8,128)(2,1)S(1)}, bf16[384,128]{1,0:T(8,128)(2,1)}, bf16[384,128]{1,0:T(8,128)(2,1)}, bf16[384,128]{1,0:T(8,128)(2,1)S(1)}) custom-call(f32[128,768]{1,0:T(8,128)S(1)} %copy-done.3, bf16[128,768]{1,0:T(8,128)(2,1)} %shard_map.94._), custom_call_target="tpu_custom_call" | custom-call | bytes 983040 | tf_op jit(solution)/shard_map/pallas_call | solution.py:24
  12.0 1.5 %collective-permute-start = (bf16[384,128]{1,0:T(8,128)(2,1)}, bf16[384,128]{1,0:T(8,128)(2,1)S(1)}, u32[]{:S(2)}, u32[]{:S(2)}) collective-permute-start(bf16[384,128]{1,0:T(8,128)(2,1)} %get-tuple-element.28), channel_id=1, source_target_pairs={{0,2},{1,3},{2,0},{3,1},{4,6},{5,7},{6,4},{7,5},{8,10},{9,11},{10,... | collective-permute-start | bytes 294920 | tf_op jit(solution)/shard_map/ppermute | solution.py:127
  13.5 2.0 %collective-permute-start.1 = (bf16[384,128]{1,0:T(8,128)(2,1)}, bf16[384,128]{1,0:T(8,128)(2,1)S(1)}, u32[]{:S(2)}, u32[]{:S(2)}) collective-permute-start(bf16[384,128]{1,0:T(8,128)(2,1)} %get-tuple-element.29), channel_id=1, source_target_pairs={{0,4},{1,5},{2,6},{3,7},{4,0},{5,1},{6,2},{7,3},{8,12},{9,13},{10,... | collective-permute-start | bytes 294920 | tf_op jit(solution)/shard_map/ppermute | solution.py:127
  15.5 0.0 collective-permute-start.2
  15.5 0.0 copy-done.6
  15.5 0.1 reshape.17.recv_ref
  15.6 3.6 %all-to-all-done = bf16[8,16,768]{2,1,0:T(8,128)(2,1)S(1)} async-done(((bf16[8,16,768]{2,1,0:T(8,128)(2,1)}), bf16[8,16,768]{2,1,0:T(8,128)(2,1)S(1)}, u32[]{:S(2)}, u32[]{:S(2)}) %all-to-all-start) | async-done | bytes 196640 | tf_op jit(solution)/shard_map/all_to_all | solution.py:226
  19.1 0.6 %shard_map.95 = (bf16[128,768]{1,0:T(8,128)(2,1)S(1)}, bf16[384,128]{1,0:T(8,128)(2,1)S(1)}, bf16[384,128]{1,0:T(8,128)(2,1)S(1)}, bf16[384,128]{1,0:T(8,128)(2,1)S(1)}, bf16[384,128]{1,0:T(8,128)(2,1)S(1)}) custom-call(bf16[128,768]{1,0:T(8,128)(2,1)S(1)} %bitcast.8, s32[1,128]{1,0:T(1,128)S(1)} %reshape.17.recv_ref), custom_call_target="tpu_custom_call" | custom-call | flops 25165824 | bytes 786944 | tf_op jit(solution)/shard_map/pallas_call | solution.py:24
  19.7 1.6 %collective-permute-start.3 = (bf16[384,128]{1,0:T(8,128)(2,1)S(1)}, bf16[384,128]{1,0:T(8,128)(2,1)S(1)}, u32[]{:S(2)}, u32[]{:S(2)}) collective-permute-start(bf16[384,128]{1,0:T(8,128)(2,1)S(1)} %get-tuple-element.34), channel_id=1, source_target_pairs={{0,2},{1,3},{2,0},{3,1},{4,6},{5,7},{6,4},{7,5},{8,10},{9,11},{10,... | collective-permute-start | bytes 294920 | tf_op jit(solution)/shard_map/ppermute | solution.py:127
  21.3 0.0 copy-done
  21.3 0.3 fusion.self_ref
  21.6 1.0 %collective-permute-start.4 = (bf16[384,128]{1,0:T(8,128)(2,1)S(1)}, bf16[384,128]{1,0:T(8,128)(2,1)S(1)}, u32[]{:S(2)}, u32[]{:S(2)}) collective-permute-start(bf16[384,128]{1,0:T(8,128)(2,1)S(1)} %get-tuple-element.35), channel_id=1, source_target_pairs={{0,4},{1,5},{2,6},{3,7},{4,0},{5,1},{6,2},{7,3},{8,12},{9,13},{10,... | collective-permute-start | bytes 294920 | tf_op jit(solution)/shard_map/ppermute | solution.py:127
  22.6 0.0 collective-permute-done.rest_0_.refs_1_
  22.6 1.0 %collective-permute-start.5 = (bf16[384,128]{1,0:T(8,128)(2,1)S(1)}, bf16[384,128]{1,0:T(8,128)(2,1)S(1)}, u32[]{:S(2)}, u32[]{:S(2)}) collective-permute-start(bf16[384,128]{1,0:T(8,128)(2,1)S(1)} %get-tuple-element.36), channel_id=1, source_target_pairs={{0,6},{1,7},{2,4},{3,5},{4,2},{5,3},{6,0},{7,1},{8,14},{9,15},{10,... | collective-permute-start | bytes 294920 | tf_op jit(solution)/shard_map/ppermute | solution.py:127
  23.6 0.0 collective-permute-done.1.rest_1_.refs_2_
  23.6 0.0 collective-permute-done.2.rest_2_.refs_3_
  23.6 0.0 copy-done.1
  23.7 0.0 copy-done.4
  23.7 1.1 %shard_map.97 = (bf16[128,768]{1,0:T(8,128)(2,1)}, bf16[384,128]{1,0:T(8,128)(2,1)S(1)}, bf16[384,128]{1,0:T(8,128)(2,1)S(1)}, bf16[384,128]{1,0:T(8,128)(2,1)S(1)}, bf16[384,128]{1,0:T(8,128)(2,1)S(1)}) custom-call(bf16[128,768]{1,0:T(8,128)(2,1)S(1)} %get-tuple-element.26.mean_ref, f32[128,768]{1,0:T(8,128)S(1)} %fusion.self_ref, ...), custom_call_target="tpu_custom_call" | custom-call | flops 150994944 | bytes 2555904 | tf_op jit(solution)/shard_map/pallas_call | solution.py:24
  24.7 1.5 %collective-permute-start.6 = (bf16[384,128]{1,0:T(8,128)(2,1)S(1)}, bf16[384,128]{1,0:T(8,128)(2,1)S(1)}, u32[]{:S(2)}, u32[]{:S(2)}) collective-permute-start(bf16[384,128]{1,0:T(8,128)(2,1)S(1)} %get-tuple-element.38), channel_id=1, source_target_pairs={{0,2},{1,3},{2,0},{3,1},{4,6},{5,7},{6,4},{7,5},{8,10},{9,11},{10,... | collective-permute-start | bytes 294920 | tf_op jit(solution)/shard_map/ppermute | solution.py:127
  26.2 1.0 %collective-permute-start.7 = (bf16[384,128]{1,0:T(8,128)(2,1)S(1)}, bf16[384,128]{1,0:T(8,128)(2,1)S(1)}, u32[]{:S(2)}, u32[]{:S(2)}) collective-permute-start(bf16[384,128]{1,0:T(8,128)(2,1)S(1)} %get-tuple-element.39), channel_id=1, source_target_pairs={{0,4},{1,5},{2,6},{3,7},{4,0},{5,1},{6,2},{7,3},{8,12},{9,13},{10,... | collective-permute-start | bytes 294920 | tf_op jit(solution)/shard_map/ppermute | solution.py:127
  27.2 0.0 collective-permute-done.3.refs_5_
  27.2 1.0 %collective-permute-start.8 = (bf16[384,128]{1,0:T(8,128)(2,1)S(1)}, bf16[384,128]{1,0:T(8,128)(2,1)S(1)}, u32[]{:S(2)}, u32[]{:S(2)}) collective-permute-start(bf16[384,128]{1,0:T(8,128)(2,1)S(1)} %get-tuple-element.40), channel_id=1, source_target_pairs={{0,6},{1,7},{2,4},{3,5},{4,2},{5,3},{6,0},{7,1},{8,14},{9,15},{10,... | collective-permute-start | bytes 294920 | tf_op jit(solution)/shard_map/ppermute | solution.py:127
  28.2 0.0 collective-permute-done.4.refs_6_
  28.2 1.1 %collective-permute-done.5.refs_7_ = bf16[384,128]{1,0:T(8,128)(2,1)S(1)} collective-permute-done((bf16[384,128]{1,0:T(8,128)(2,1)S(1)}, bf16[384,128]{1,0:T(8,128)(2,1)S(1)}, u32[]{:S(2)}, u32[]{:S(2)}) %collective-permute-start.5) | collective-permute-done | bytes 98336 | tf_op jit(solution)/shard_map/ppermute | solution.py:127
  29.3 1.1 %collective-permute-done.6.refs_9_ = bf16[384,128]{1,0:T(8,128)(2,1)S(1)} collective-permute-done((bf16[384,128]{1,0:T(8,128)(2,1)S(1)}, bf16[384,128]{1,0:T(8,128)(2,1)S(1)}, u32[]{:S(2)}, u32[]{:S(2)}) %collective-permute-start.6) | collective-permute-done | bytes 98336 | tf_op jit(solution)/shard_map/ppermute | solution.py:127
  30.4 0.4 collective-permute-done.7.refs_10_
  30.9 1.9 %collective-permute-done.8.refs_11_ = bf16[384,128]{1,0:T(8,128)(2,1)S(1)} collective-permute-done((bf16[384,128]{1,0:T(8,128)(2,1)S(1)}, bf16[384,128]{1,0:T(8,128)(2,1)S(1)}, u32[]{:S(2)}, u32[]{:S(2)}) %collective-permute-start.8) | collective-permute-done | bytes 98336 | tf_op jit(solution)/shard_map/ppermute | solution.py:127
  32.7 0.7 %shard_map.98 = (f32[384,384]{1,0:T(8,128)S(1)}, bf16[384,384]{1,0:T(8,128)(2,1)S(1)}) custom-call(bf16[384,128]{1,0:T(8,128)(2,1)S(1)} %get-tuple-element.32.refs_0_, bf16[384,128]{1,0:T(8,128)(2,1)S(1)} %collective-permute-done.rest_0_.refs_1_, bf16[384,128]{1,0:T(8,128)(2,1)S(1)} %collective-permute-done.1.rest_1_.refs_2_, ...), custom_call_target="tpu_custom_call" | custom-call | flops 301989888 | bytes 2064384 | tf_op jit(solution)/shard_map/pallas_call | solution.py:24
  33.4 0.1 collective-permute-start.9
  33.5 1.6 %collective-permute-done.9.got_ref = bf16[384,384]{1,0:T(8,128)(2,1)S(1)} collective-permute-done((bf16[384,384]{1,0:T(8,128)(2,1)S(1)}, bf16[384,384]{1,0:T(8,128)(2,1)S(1)}, u32[]{:S(2)}, u32[]{:S(2)}) %collective-permute-start.9) | collective-permute-done | bytes 294944 | tf_op jit(solution)/shard_map/ppermute | solution.py:127
  35.1 0.1 shard_map.99
  35.2 0.1 collective-permute-start.10
  35.3 2.7 %collective-permute-start.11 = (bf16[96,384]{1,0:T(8,128)(2,1)S(1)}, bf16[96,384]{1,0:T(8,128)(2,1)S(1)}, u32[]{:S(2)}, u32[]{:S(2)}) collective-permute-start(bf16[96,384]{1,0:T(8,128)(2,1)S(1)} %get-tuple-element.45), channel_id=1, source_target_pairs={{0,24},{1,25},{2,26},{3,27},{4,28},{5,29},{6,30},{7,31},{8,16},{9,... | collective-permute-start | bytes 221192 | tf_op jit(solution)/shard_map/ppermute | solution.py:127
  37.9 0.8 %collective-permute-start.12 = (bf16[96,384]{1,0:T(8,128)(2,1)S(1)}, bf16[96,384]{1,0:T(8,128)(2,1)S(1)}, u32[]{:S(2)}, u32[]{:S(2)}) collective-permute-start(bf16[96,384]{1,0:T(8,128)(2,1)S(1)} %get-tuple-element.46), channel_id=1, source_target_pairs={{0,8},{1,9},{2,10},{3,11},{4,12},{5,13},{6,14},{7,15},{8,0},{9,1},... | collective-permute-start | bytes 221192 | tf_op jit(solution)/shard_map/ppermute | solution.py:127
  38.8 4.8 %collective-permute-done.10.refs_1_ = bf16[96,384]{1,0:T(8,128)(2,1)S(1)} collective-permute-done((bf16[96,384]{1,0:T(8,128)(2,1)S(1)}, bf16[96,384]{1,0:T(8,128)(2,1)S(1)}, u32[]{:S(2)}, u32[]{:S(2)}) %collective-permute-start.10) | collective-permute-done | bytes 73760 | tf_op jit(solution)/shard_map/ppermute | solution.py:127
  43.5 0.0 collective-permute-done.11.refs_2_
  43.5 1.1 %collective-permute-done.12.refs_3_ = bf16[96,384]{1,0:T(8,128)(2,1)S(1)} collective-permute-done((bf16[96,384]{1,0:T(8,128)(2,1)S(1)}, bf16[96,384]{1,0:T(8,128)(2,1)S(1)}, u32[]{:S(2)}, u32[]{:S(2)}) %collective-permute-start.12) | collective-permute-done | bytes 73760 | tf_op jit(solution)/shard_map/ppermute | solution.py:127
  44.7 0.7 %collective-permute-start.14 = (bf16[96,384]{1,0:T(8,128)(2,1)S(1)}, bf16[96,384]{1,0:T(8,128)(2,1)S(1)}, u32[]{:S(2)}, u32[]{:S(2)}) collective-permute-start(bf16[96,384]{1,0:T(8,128)(2,1)S(1)} %shard_map.100.refs_0_), channel_id=1, source_target_pairs={{0,2},{1,3},{2,0},{3,1},{4,6},{5,7},{6,4},{7,5},{8,10},{9,11},{10,... | collective-permute-start | bytes 221192 | tf_op jit(solution)/shard_map/ppermute | solution.py:127
  45.4 0.0 collective-permute-start.13
  45.4 3.7 %collective-permute-done.14.refs_2_ = bf16[96,384]{1,0:T(8,128)(2,1)S(1)} collective-permute-done((bf16[96,384]{1,0:T(8,128)(2,1)S(1)}, bf16[96,384]{1,0:T(8,128)(2,1)S(1)}, u32[]{:S(2)}, u32[]{:S(2)}) %collective-permute-start.14) | collective-permute-done | bytes 73760 | tf_op jit(solution)/shard_map/ppermute | solution.py:127
  49.1 0.0 collective-permute-start.15
  49.1 0.0 collective-permute-done.13.refs_1_
  49.1 1.3 %collective-permute-done.15.refs_3_ = bf16[96,384]{1,0:T(8,128)(2,1)S(1)} collective-permute-done((bf16[96,384]{1,0:T(8,128)(2,1)S(1)}, bf16[96,384]{1,0:T(8,128)(2,1)S(1)}, u32[]{:S(2)}, u32[]{:S(2)}) %collective-permute-start.15) | collective-permute-done | bytes 73760 | tf_op jit(solution)/shard_map/ppermute | solution.py:127
  50.3 0.9 %shard_map.101 = (f32[96,768]{1,0:T(8,128)}, f32[96,768]{1,0:T(8,128)}) custom-call(bf16[96,384]{1,0:T(8,128)(2,1)S(1)} %shard_map.100.refs_0_, bf16[96,384]{1,0:T(8,128)(2,1)S(1)} %collective-permute-done.13.refs_1_, bf16[96,384]{1,0:T(8,128)(2,1)S(1)} %collective-permute-done.14.refs_2_, bf16[96,384]{1,0:T(8,128)(2,1)S(1)} %collective-permute-done.15.refs_3_), custom_call_target="tpu_custom_call" | custom-call | bytes 884736 | tf_op jit(solution)/shard_map/pallas_call | solution.py:24
  (2 shorter events, 0.0 us)
Async XLA Ops:
  0.6 20.6 %copy-start = (bf16[768,768]{1,0:T(8,128)(2,1)S(1)}, bf16[768,768]{1,0:T(8,128)(2,1)}, u32[]{:S(2)}) copy-start(bf16[768,768]{1,0:T(8,128)(2,1)} %param.12) | copy-start | bytes 3538948
  0.6 1.1 %copy-start.2 = (f32[128,768]{1,0:T(8,128)S(1)}, f32[128,768]{1,0:T(8,128)}, u32[]{:S(2)}) copy-start(f32[128,768]{1,0:T(8,128)} %feat_hbm.1) | copy-start | bytes 1179652
  1.7 0.7 %copy-start.5 = (s32[1,1,8,12,2]{3,4,2,1,0:T(2,128)S(1)}, s32[1,1,8,12,2]{3,4,2,1,0:T(2,128)}, u32[]{:S(2)}) copy-start(s32[1,1,8,12,2]{3,4,2,1,0:T(2,128)} %param.9) | copy-start | bytes 2308
  2.4 8.6 %copy-start.3 = (f32[128,768]{1,0:T(8,128)S(1)}, f32[128,768]{1,0:T(8,128)}, u32[]{:S(2)}) copy-start(f32[128,768]{1,0:T(8,128)} %self_ref.1) | copy-start | bytes 1179652
  2.4 13.1 %copy-start.6 = (s32[1,1,8,12]{3,2,1,0:T(8,128)S(1)}, s32[1,1,8,12]{3,2,1,0:T(8,128)}, u32[]{:S(2)}) copy-start(s32[1,1,8,12]{3,2,1,0:T(8,128)} %param.10) | copy-start | bytes 1156
  3.8 15.3 %all-to-all-start = ((bf16[8,16,768]{2,1,0:T(8,128)(2,1)}), bf16[8,16,768]{2,1,0:T(8,128)(2,1)S(1)}, u32[]{:S(2)}, u32[]{:S(2)}) async-start(bf16[8,16,768]{2,1,0:T(8,128)(2,1)} %bitcast.2), calls=%async_computation | async-start | bytes 393216 | tf_op jit(solution)/shard_map/all_to_all | solution.py:226
  11.1 12.6 %copy-start.1 = (bf16[768,768]{1,0:T(8,128)(2,1)S(1)}, bf16[768,768]{1,0:T(8,128)(2,1)}, u32[]{:S(2)}) copy-start(bf16[768,768]{1,0:T(8,128)(2,1)} %w_ref.1) | copy-start | bytes 3538948
  11.1 12.6 %copy-start.4 = (bf16[128,768]{1,0:T(8,128)(2,1)S(1)}, bf16[128,768]{1,0:T(8,128)(2,1)}, u32[]{:S(2)}) copy-start(bf16[128,768]{1,0:T(8,128)(2,1)} %cot_ref.1) | copy-start | bytes 589828
  12.0 10.7 %collective-permute-start = (bf16[384,128]{1,0:T(8,128)(2,1)}, bf16[384,128]{1,0:T(8,128)(2,1)S(1)}, u32[]{:S(2)}, u32[]{:S(2)}) collective-permute-start(bf16[384,128]{1,0:T(8,128)(2,1)} %get-tuple-element.28), channel_id=1, source_target_pairs={{0,2},{1,3},{2,0},{3,1},{4,6},{5,7},{6,4},{7,5},{8,10},{9,11},{10,... | collective-permute-start | bytes 294920 | tf_op jit(solution)/shard_map/ppermute | solution.py:127
  13.5 10.2 %collective-permute-start.1 = (bf16[384,128]{1,0:T(8,128)(2,1)}, bf16[384,128]{1,0:T(8,128)(2,1)S(1)}, u32[]{:S(2)}, u32[]{:S(2)}) collective-permute-start(bf16[384,128]{1,0:T(8,128)(2,1)} %get-tuple-element.29), channel_id=1, source_target_pairs={{0,4},{1,5},{2,6},{3,7},{4,0},{5,1},{6,2},{7,3},{8,12},{9,13},{10,... | collective-permute-start | bytes 294920 | tf_op jit(solution)/shard_map/ppermute | solution.py:127
  15.5 8.2 %collective-permute-start.2 = (bf16[384,128]{1,0:T(8,128)(2,1)S(1)}, bf16[384,128]{1,0:T(8,128)(2,1)S(1)}, u32[]{:S(2)}, u32[]{:S(2)}) collective-permute-start(bf16[384,128]{1,0:T(8,128)(2,1)S(1)} %get-tuple-element.30), channel_id=1, source_target_pairs={{0,6},{1,7},{2,4},{3,5},{4,2},{5,3},{6,0},{7,1},{8,14},{9,15},{10,... | collective-permute-start | bytes 294920 | tf_op jit(solution)/shard_map/ppermute | solution.py:127
  19.7 7.5 %collective-permute-start.3 = (bf16[384,128]{1,0:T(8,128)(2,1)S(1)}, bf16[384,128]{1,0:T(8,128)(2,1)S(1)}, u32[]{:S(2)}, u32[]{:S(2)}) collective-permute-start(bf16[384,128]{1,0:T(8,128)(2,1)S(1)} %get-tuple-element.34), channel_id=1, source_target_pairs={{0,2},{1,3},{2,0},{3,1},{4,6},{5,7},{6,4},{7,5},{8,10},{9,11},{10,... | collective-permute-start | bytes 294920 | tf_op jit(solution)/shard_map/ppermute | solution.py:127
  21.6 6.6 %collective-permute-start.4 = (bf16[384,128]{1,0:T(8,128)(2,1)S(1)}, bf16[384,128]{1,0:T(8,128)(2,1)S(1)}, u32[]{:S(2)}, u32[]{:S(2)}) collective-permute-start(bf16[384,128]{1,0:T(8,128)(2,1)S(1)} %get-tuple-element.35), channel_id=1, source_target_pairs={{0,4},{1,5},{2,6},{3,7},{4,0},{5,1},{6,2},{7,3},{8,12},{9,13},{10,... | collective-permute-start | bytes 294920 | tf_op jit(solution)/shard_map/ppermute | solution.py:127
  22.6 6.7 %collective-permute-start.5 = (bf16[384,128]{1,0:T(8,128)(2,1)S(1)}, bf16[384,128]{1,0:T(8,128)(2,1)S(1)}, u32[]{:S(2)}, u32[]{:S(2)}) collective-permute-start(bf16[384,128]{1,0:T(8,128)(2,1)S(1)} %get-tuple-element.36), channel_id=1, source_target_pairs={{0,6},{1,7},{2,4},{3,5},{4,2},{5,3},{6,0},{7,1},{8,14},{9,15},{10,... | collective-permute-start | bytes 294920 | tf_op jit(solution)/shard_map/ppermute | solution.py:127
  24.7 5.7 %collective-permute-start.6 = (bf16[384,128]{1,0:T(8,128)(2,1)S(1)}, bf16[384,128]{1,0:T(8,128)(2,1)S(1)}, u32[]{:S(2)}, u32[]{:S(2)}) collective-permute-start(bf16[384,128]{1,0:T(8,128)(2,1)S(1)} %get-tuple-element.38), channel_id=1, source_target_pairs={{0,2},{1,3},{2,0},{3,1},{4,6},{5,7},{6,4},{7,5},{8,10},{9,11},{10,... | collective-permute-start | bytes 294920 | tf_op jit(solution)/shard_map/ppermute | solution.py:127
  26.2 4.6 %collective-permute-start.7 = (bf16[384,128]{1,0:T(8,128)(2,1)S(1)}, bf16[384,128]{1,0:T(8,128)(2,1)S(1)}, u32[]{:S(2)}, u32[]{:S(2)}) collective-permute-start(bf16[384,128]{1,0:T(8,128)(2,1)S(1)} %get-tuple-element.39), channel_id=1, source_target_pairs={{0,4},{1,5},{2,6},{3,7},{4,0},{5,1},{6,2},{7,3},{8,12},{9,13},{10,... | collective-permute-start | bytes 294920 | tf_op jit(solution)/shard_map/ppermute | solution.py:127
  27.2 5.5 %collective-permute-start.8 = (bf16[384,128]{1,0:T(8,128)(2,1)S(1)}, bf16[384,128]{1,0:T(8,128)(2,1)S(1)}, u32[]{:S(2)}, u32[]{:S(2)}) collective-permute-start(bf16[384,128]{1,0:T(8,128)(2,1)S(1)} %get-tuple-element.40), channel_id=1, source_target_pairs={{0,6},{1,7},{2,4},{3,5},{4,2},{5,3},{6,0},{7,1},{8,14},{9,15},{10,... | collective-permute-start | bytes 294920 | tf_op jit(solution)/shard_map/ppermute | solution.py:127
  33.4 1.6 %collective-permute-start.9 = (bf16[384,384]{1,0:T(8,128)(2,1)S(1)}, bf16[384,384]{1,0:T(8,128)(2,1)S(1)}, u32[]{:S(2)}, u32[]{:S(2)}) collective-permute-start(bf16[384,384]{1,0:T(8,128)(2,1)S(1)} %get-tuple-element.42), channel_id=1, source_target_pairs={{0,1},{1,0},{2,3},{3,2},{4,5},{5,4},{6,7},{7,6},{8,9},{9,8},{10,11... | collective-permute-start | bytes 884744 | tf_op jit(solution)/shard_map/ppermute | solution.py:127
  35.2 8.3 %collective-permute-start.10 = (bf16[96,384]{1,0:T(8,128)(2,1)S(1)}, bf16[96,384]{1,0:T(8,128)(2,1)S(1)}, u32[]{:S(2)}, u32[]{:S(2)}) collective-permute-start(bf16[96,384]{1,0:T(8,128)(2,1)S(1)} %get-tuple-element.44), channel_id=1, source_target_pairs={{0,16},{1,17},{2,18},{3,19},{4,20},{5,21},{6,22},{7,23},{8,24},{9,... | collective-permute-start | bytes 221192 | tf_op jit(solution)/shard_map/ppermute | solution.py:127
  35.3 8.2 %collective-permute-start.11 = (bf16[96,384]{1,0:T(8,128)(2,1)S(1)}, bf16[96,384]{1,0:T(8,128)(2,1)S(1)}, u32[]{:S(2)}, u32[]{:S(2)}) collective-permute-start(bf16[96,384]{1,0:T(8,128)(2,1)S(1)} %get-tuple-element.45), channel_id=1, source_target_pairs={{0,24},{1,25},{2,26},{3,27},{4,28},{5,29},{6,30},{7,31},{8,16},{9,... | collective-permute-start | bytes 221192 | tf_op jit(solution)/shard_map/ppermute | solution.py:127
  37.9 6.7 %collective-permute-start.12 = (bf16[96,384]{1,0:T(8,128)(2,1)S(1)}, bf16[96,384]{1,0:T(8,128)(2,1)S(1)}, u32[]{:S(2)}, u32[]{:S(2)}) collective-permute-start(bf16[96,384]{1,0:T(8,128)(2,1)S(1)} %get-tuple-element.46), channel_id=1, source_target_pairs={{0,8},{1,9},{2,10},{3,11},{4,12},{5,13},{6,14},{7,15},{8,0},{9,1},... | collective-permute-start | bytes 221192 | tf_op jit(solution)/shard_map/ppermute | solution.py:127
  44.7 4.4 %collective-permute-start.14 = (bf16[96,384]{1,0:T(8,128)(2,1)S(1)}, bf16[96,384]{1,0:T(8,128)(2,1)S(1)}, u32[]{:S(2)}, u32[]{:S(2)}) collective-permute-start(bf16[96,384]{1,0:T(8,128)(2,1)S(1)} %shard_map.100.refs_0_), channel_id=1, source_target_pairs={{0,2},{1,3},{2,0},{3,1},{4,6},{5,7},{6,4},{7,5},{8,10},{9,11},{10,... | collective-permute-start | bytes 221192 | tf_op jit(solution)/shard_map/ppermute | solution.py:127
  45.4 3.7 %collective-permute-start.13 = (bf16[96,384]{1,0:T(8,128)(2,1)S(1)}, bf16[96,384]{1,0:T(8,128)(2,1)S(1)}, u32[]{:S(2)}, u32[]{:S(2)}) collective-permute-start(bf16[96,384]{1,0:T(8,128)(2,1)S(1)} %shard_map.100.refs_0_), channel_id=1, source_target_pairs={{0,1},{1,0},{2,3},{3,2},{4,5},{5,4},{6,7},{7,6},{8,9},{9,8},{10,11... | collective-permute-start | bytes 221192 | tf_op jit(solution)/shard_map/ppermute | solution.py:127
  49.1 1.3 %collective-permute-start.15 = (bf16[96,384]{1,0:T(8,128)(2,1)S(1)}, bf16[96,384]{1,0:T(8,128)(2,1)S(1)}, u32[]{:S(2)}, u32[]{:S(2)}) collective-permute-start(bf16[96,384]{1,0:T(8,128)(2,1)S(1)} %collective-permute-done.14.refs_2_), channel_id=1, source_target_pairs={{0,1},{1,0},{2,3},{3,2},{4,5},{5,4},{6,7},{7,6},{8,9},{9,8},{10,11... | collective-permute-start | bytes 221192 | tf_op jit(solution)/shard_map/ppermute | solution.py:127

commit v2 on v1

--- a/solution.py
+++ b/solution.py
@@ -11,33 +11,35 @@
 SLOT_PAD = 16
 VMEM = pl.BlockSpec(memory_space=pltpu.VMEM)
 ANY = pl.BlockSpec(memory_space=pl.ANY)
-HBM = pl.BlockSpec(memory_space=pltpu.HBM)
-PARAMS = pltpu.CompilerParams(vmem_limit_bytes=16 * 1024 * 1024)
 
 
 def dot(a, b):
     return jnp.dot(a, b, preferred_element_type=F32)
 
 
-def call(body, outs, args, unread=(), hbm=(), scratch=(), flops=0):
-    moved = sum(a.size * a.dtype.itemsize for a in tuple(args) + tuple(outs))
+def call(body, outs, args, unread=(), scratch=(), flops=0):
+    moved = sum(a.size * a.dtype.itemsize for a in (*args, *outs))
     return pl.pallas_call(
         body,
         out_shape=list(outs),
-        in_specs=[VMEM] * len(args) + [ANY] * len(unread) + [HBM] * len(hbm),
+        in_specs=[VMEM] * len(args) + [ANY] * len(unread),
         out_specs=[VMEM] * len(outs),
         scratch_shapes=list(scratch),
-        compiler_params=PARAMS,
+        compiler_params=pltpu.CompilerParams(vmem_limit_bytes=16 * 1024 * 1024),
         cost_estimate=pl.CostEstimate(flops=flops, bytes_accessed=moved, transcendentals=0),
-    )(*args, *unread, *hbm)
+    )(*args, *unread)
 
 
 def shape(dims, kind):
     return jax.ShapeDtypeStruct(dims, kind)
 
 
-def slot_sums(cap, ids, feat_copy, feat_ref, out_ref):
-    owned, slots = feat_ref.shape[0], ids.shape[1]
+def slot_sums_kernel(order, feat_ref, edge_ref, _, out_ref):
+    owned = feat_ref.shape[0]
+    _, mult, cap = edge_ref.shape
+    slots = len(order) * SLOT_PAD
+    fill = jnp.full((mult, SLOT_PAD - cap), owned, jnp.int32)
+    ids = jnp.concatenate([p for d in order for p in (edge_ref[d], fill)], axis=1)
     row = lax.broadcasted_iota(jnp.int32, (owned, slots), 0)
     weight = jnp.zeros((owned, slots), F32)
     count = jnp.zeros((1, slots), F32)
@@ -53,26 +55,12 @@
     l2 = lax.broadcasted_iota(jnp.int32, (slots, 128), 1)
     fold = ((c2 & (SLOT_PAD - 1)) == l2).astype(BF16)
     counts = dot(spread, fold)
-    feat_copy.wait()
     feat = feat_ref[...]
     high = feat.astype(BF16)
     low = (feat - high.astype(F32)).astype(BF16)
     sums = dot(pick, high) + dot(pick, low)
     out_ref[:, :128] = (sums[:, :128] + counts).astype(BF16)
     out_ref[:, 128:] = sums[:, 128:].astype(BF16)
-
-
-def slot_sums_kernel(cap, feat_hbm, edge_hbm, out_ref, feat_ref, edge_ref, sems):
-    copies = [pltpu.make_async_copy(edge_hbm, edge_ref, sems.at[0]),
-              pltpu.make_async_copy(feat_hbm, feat_ref, sems.at[1])]
-    for copy in copies:
-        copy.start()
-    owned = feat_ref.shape[0]
-    ns, mult, _ = edge_ref.shape
-    fill = jnp.full((mult, SLOT_PAD - cap), owned, jnp.int32)
-    copies[0].wait()
-    ids = jnp.concatenate([p for d in range(ns) for p in (edge_ref[d], fill)], axis=1)
-    slot_sums(cap, ids, copies[1], feat_ref, out_ref)
 
 
 def neighbor_mean(cap, rows, recv, targets):
@@ -111,7 +99,7 @@
 
     def fits(self):
         pow2 = all((n & (n - 1)) == 0 for n in (self.ns, self.nt))
-        return (pow2 and self.ns <= 8 and self.gy * self.gc == self.nt and self.cols % 128 == 0
+        return (pow2 and self.ns <= 8 and self.gx == 2 and self.gy == 2 and self.gy * self.gc == self.nt and self.cols % 128 == 0
                 and self.shard % 16 == 0 and len(self.peers) <= 4 and self.nz <= 4)
 
     def place(self):
@@ -126,6 +114,12 @@
                 pairs.append((s * self.nt + t, (z * self.gx + x) * self.nt + y * self.gc + c))
         return lax.ppermute(array, ("store", "trainer"), pairs)
 
+    def store_order(self):
+        up = [(z, x) for z in reversed(range(self.nz)) for x in reversed(range(self.gx))]
+        down = [(z, x) for z in range(self.nz) for x in range(self.gx)]
+        turns = [at for pair in zip(up, down) for at in pair]
+        return [z * self.gx + x for z, x in turns[:self.ns]]
+
 
 def write_rows(plan, trans_ref, outs):
     x = plan.place()[1]
@@ -135,47 +129,48 @@
             out[z * plan.shard:(z + 1) * plan.shard, :] = trans_ref[pl.ds(start, plan.shard), :]
 
 
-def own_kernel(plan, self_ref, _, own_ref, *rest):
-    outs, trans_ref = rest[:-1], rest[-1]
+def own_kernel(plan, self_ref, own_ref, here_ref, there_ref, token_ref, trans_ref):
     own_ref[...] = self_ref[...].astype(BF16)
     trans_ref[...] = self_ref[...].T.astype(BF16)
-    write_rows(plan, trans_ref, outs)
-
-
-def mean_kernel(plan, cap, rows_ref, recv_ref, mean_ref, *rest):
-    outs, trans_ref = rest[:-1], rest[-1]
-    mean = neighbor_mean(cap, rows_ref[...], recv_ref[...], mean_ref.shape[0])
-    mean_ref[...] = mean
+    x = plan.place()[1]
+    for dx, out in enumerate((here_ref, there_ref)):
+        for z in range(plan.nz):
+            start = pl.multiple_of((z * plan.gx + (x ^ dx)) * plan.shard, 16)
+            out[z * plan.shard:(z + 1) * plan.shard, :] = trans_ref[pl.ds(start, plan.shard), :]
+    token_ref[...] = jnp.zeros_like(token_ref)
+
+
+def layer_kernel(plan, cap, order, ordered, rows_ref, recv_ref, self_ref, cot_ref, w_ref, *rest):
+    hidden_ref, *outs = rest[ordered:-2]
+    trans_ref, grad_ref = rest[-2:]
+    targets = self_ref.shape[0]
+    y = plan.place()[2]
+    rows = jnp.concatenate(
+        [rows_ref[p * SLOT_PAD:(p + 1) * SLOT_PAD, :] for p in (order.index(s) for s in range(plan.ns))], axis=0)
+    mean = neighbor_mean(cap, rows, recv_ref[...], targets)
+    preact = self_ref[...] + dot(mean, w_ref[...])
+    hidden, grad = forward(preact, cot_ref[...])
+    hidden_ref[...] = hidden
     trans_ref[...] = mean.astype(F32).T.astype(BF16)
     write_rows(plan, trans_ref, outs)
-
-
-def layer_kernel(plan, ordered, mean_ref, self_ref, cot_ref, w_ref, *rest):
-    hidden_ref, *outs = rest[ordered:-1]
-    grad_ref = rest[-1]
-    targets = self_ref.shape[0]
-    preact = self_ref[...] + dot(mean_ref[...], w_ref[...])
-    hidden, grad = forward(preact, cot_ref[...])
-    hidden_ref[...] = hidden
     for b in range(grad_ref.shape[0]):
         grad_ref[b] = grad[:, b * 128:(b + 1) * 128]
-    y = plan.place()[2]
     each = plan.cols // 128
     for (dx, dy), out in zip(plan.peers, outs):
         for b in range(each):
-            out[b * targets:(b + 1) * targets, :] = grad_ref[(y ^ dy) * each + b]
+            at = plan.rows + b * targets
+            out[at:at + targets, :] = grad_ref[(y ^ dy) * each + b]
 
 
 def terms_kernel(plan, *refs):
     n = len(plan.peers)
-    own, mean, grad = refs[:n], refs[n:2 * n], refs[2 * n:3 * n]
-    keep_ref, send_ref, total_ref = refs[3 * n:]
+    own, late, (keep_ref, send_ref, total_ref) = refs[:n], refs[n:2 * n], refs[2 * n:]
     rows, each, targets = plan.rows, plan.cols // 128, own[0].shape[1]
     left = jnp.concatenate(
-        [jnp.concatenate([o[...], m[...]], axis=0) for o, m in zip(own, mean)], axis=1)
+        [jnp.concatenate([o[...], l[:rows, :]], axis=0) for o, l in zip(own, late)], axis=1)
     right = jnp.concatenate(
-        [jnp.concatenate([g[b * targets:(b + 1) * targets, :] for b in range(each)], axis=1)
-         for g in grad], axis=0)
+        [jnp.concatenate([l[rows + b * targets:rows + (b + 1) * targets, :] for b in range(each)], axis=1)
+         for l in late], axis=0)
     total_ref[...] = dot(left, right)
     c = plan.place()[3]
     keep_ref[...] = total_ref[pl.ds(pl.multiple_of(c * rows, 16), rows), :]
@@ -218,14 +213,23 @@
     pad = ((0, 0), (0, SLOT_PAD - cap))
     recv = jnp.pad(recv_target[0, 0], pad, constant_values=targets).reshape(1, slots)
 
+    fits = plan.fits()
+    order = plan.store_order() if fits else list(range(ns))
+    rows, cols, n = plan.rows, plan.cols, len(plan.peers)
+    token = jnp.zeros((8, 128), F32)
+    if fits:
+        own, own_here, own_there, token = call(
+            functools.partial(own_kernel, plan),
+            [shape((targets, width), BF16)] + [shape((rows, targets), BF16)] * 2 + [shape((8, 128), F32)],
+            [self_rows], scratch=[pltpu.VMEM((width, targets), BF16)])
+        own_x = plan.send(own_there, lambda z, x, y, c: (z, 1 - x, y, c))
+        own_y = plan.send(own_here, lambda z, x, y, c: (z, x, 1 - y, c))
     (sums,) = call(
-        functools.partial(slot_sums_kernel, cap), [shape((slots, width), BF16)], (),
-        hbm=[features, edges], flops=4 * slots * owned * width,
-        scratch=[pltpu.VMEM(features.shape, F32), pltpu.VMEM(edges.shape, jnp.int32),
-                 pltpu.SemaphoreType.DMA((2,))])
-    arrived = lax.all_to_all(sums.reshape(ns, SLOT_PAD, width), "store",
-                             split_axis=0, concat_axis=0, tiled=True).reshape(slots, width)
-    if not plan.fits():
+        functools.partial(slot_sums_kernel, order), [shape((slots, width), BF16)],
+        [features, edges], unread=[token], flops=4 * slots * owned * width)
+    arrived = lax.all_to_all(sums.reshape(ns, SLOT_PAD, width), "store", split_axis=0, concat_axis=0,
+                             tiled=True, axis_index_groups=[order]).reshape(slots, width)
+    if not fits:
         own = self_rows.astype(BF16)
         mean = neighbor_mean(cap, arrived, recv, targets)
         preact = dot(own, w_self) + dot(mean, w_neigh)
@@ -236,34 +240,28 @@
         total = lax.psum(part, "trainer")
         return hidden, total[:plan.shard], total[plan.shard:]
 
-    n, rows, cols = len(plan.peers), plan.rows, plan.cols
-    own, *own_rows = call(
-        functools.partial(own_kernel, plan),
-        [shape((targets, width), BF16)] + [shape((rows, targets), BF16)] * n, [self_rows], unread=[sums],
-        scratch=[pltpu.VMEM((width, targets), BF16)])
+    own_xy = plan.send(own_x, lambda z, x, y, c: (z, x, 1 - y, c))
+    own_all = [own_here, own_y, own_x, own_xy]
     self_term = dot(own, w_self)
 
     def exchange(arrays):
-        return [arrays[0]] + [
-            plan.send(a, lambda z, x, y, c, dx=dx, dy=dy: (z, x ^ dx, y ^ dy, c))
-            for (dx, dy), a in zip(plan.peers[1:], arrays[1:])]
-
-    own_all = exchange(own_rows)
-    mean, *mean_rows = call(
-        functools.partial(mean_kernel, plan, cap),
-        [shape((targets, width), BF16)] + [shape((rows, targets), BF16)] * n, [arrived, recv],
-        scratch=[pltpu.VMEM((width, targets), BF16)], flops=2 * targets * width * slots)
-    mean_all = exchange(mean_rows)
-    hidden, *grads = call(
-        functools.partial(layer_kernel, plan, n - 1),
-        [shape((targets, out_width), BF16)] + [shape((cols // 128 * targets, 128), BF16)] * n,
-        [mean, self_term, cotangent, w_neigh], unread=own_all[1:],
-        scratch=[pltpu.VMEM((out_width // 128, targets, 128), BF16)],
-        flops=2 * targets * width * out_width)
+        out = {}
+        for i in reversed(range(1, n)):
+            dx, dy = plan.peers[i]
+            out[i] = plan.send(arrays[i], lambda z, x, y, c, dx=dx, dy=dy: (z, x ^ dx, y ^ dy, c))
+        return [arrays[0]] + [out[i] for i in range(1, n)]
+
+    late_rows = rows + cols // 128 * targets
+    hidden, *late = call(
+        functools.partial(layer_kernel, plan, cap, order, n - 1),
+        [shape((targets, out_width), BF16)] + [shape((late_rows, targets), BF16)] * n,
+        [arrived, recv, self_term, cotangent, w_neigh], unread=own_all[1:],
+        scratch=[pltpu.VMEM((width, targets), BF16), pltpu.VMEM((out_width // 128, targets, 128), BF16)],
+        flops=2 * targets * width * (out_width + slots))
     keep, give = call(
         functools.partial(terms_kernel, plan),
         [shape((rows, cols), F32), shape((rows, cols), BF16)],
-        own_all + mean_all + exchange(grads), scratch=[pltpu.VMEM((2 * rows, cols), F32)],
+        own_all + exchange(late), scratch=[pltpu.VMEM((2 * rows, cols), F32)],
         flops=4 * rows * cols * targets * n)
     got = plan.send(give, lambda z, x, y, c: (z, x, y, 1 - c))
     block = (plan.shard, cols)
@@ -271,8 +269,8 @@
         functools.partial(core_sum_kernel, plan),
         [shape(block, F32)] + [shape(block, BF16)] * (plan.nz - 1), [keep, got],
         scratch=[pltpu.VMEM((rows, cols), F32)])
-    got = [plan.send(others[k - 1], lambda z, x, y, c, k=k: (z ^ k, x, y, c))
-           for k in sorted(range(1, plan.nz), key=lambda k: (k < 2, k))]
+    far_first = sorted(range(1, plan.nz), key=lambda k: (k < 2, k))
+    got = [plan.send(others[k - 1], lambda z, x, y, c, k=k: (z ^ k, x, y, c)) for k in far_first]
     (quarter,) = call(store_sum_kernel, [shape(block, BF16)], [mine] + got)
     column = [quarter] + [plan.send(quarter, lambda z, x, y, c, i=i: (z, x, y ^ i, c))
                           for i in range(1, plan.gy)]

time: 51.5 us -> 53 us (1.029)
  starting transfers between devices: 22.2 us -> 20.1 us
  waiting for transfers between devices: 20.5 us -> 22.5 us
  local copies, waits for them, and re-layouts: 1.89 us -> 3.55 us
  Pallas kernels: 5.56 us -> 4.4 us
  matrix products: 0.32 us -> 1.25 us
    ppermute x16 -> x13, waiting for transfers between devices: 16.9 us -> 22.5 us  [send(): return lax.ppermute(array, ('store', 'trainer'), pairs)]
    all_to_all x1, waiting for transfers between devices: 3.55 us -> 0.01 us  [per_device(): lax.all_to_all(sums.reshape(ns, SLOT_PAD, width), 'store', split_axis=0,...]
    ppermute x16 -> x13, starting transfers between devices: 15 us -> 13.1 us  [send(): return lax.ppermute(array, ('store', 'trainer'), pairs)]
    unnamed x14 -> x16, local copies, waits for them, and re-layouts: 1.81 us -> 3.47 us
    pallas_call x8 -> x7, Pallas kernels: 5.56 us -> 4.4 us  [call(): pl.pallas_call(body, out_shape=list(outs), in_specs=[VMEM] * len(args) +...]
    dot_general x1, matrix products: 0.32 us -> 1.25 us  [dot(): return jnp.dot(a, b, preferred_element_type=F32)]
  transfers between devices with their start and end apart: 17 -> 14, of which waited for: 10 -> 10; matrix products, arithmetic and copies ran while one was open for 1% -> 3% of each run, Pallas kernels for 5% -> 2%
where the time goes in v2:
time: 53 us; the launch traced here: 52.6 us
  waiting for transfers between devices  22.5 us (42%)
  starting transfers between devices  20.1 us (38%)
  Pallas kernels  4.4 us (8%)
  local copies, waits for them, and re-layouts  3.55 us (7%)
  matrix products  1.25 us (2%)
  between operations  0.73 us (1%)
    ppermute x13, waiting for transfers between devices, send(): return lax.ppermute(array, ('store', 'trainer'), pairs)  22.5 us
    ppermute x13, starting transfers between devices, send(): return lax.ppermute(array, ('store', 'trainer'), pairs)  13.1 us
    all_to_all x1, starting transfers between devices, per_device(): lax.all_to_all(sums.reshape(ns, SLOT_PAD, width), 'store', split_axis=0,...  7.01 us
    pallas_call x7, Pallas kernels, call(): pl.pallas_call(body, out_shape=list(outs), in_specs=[VMEM] * len(args) +...  4.4 us
    unnamed x16, local copies, waits for them, and re-layouts  3.47 us
    dot_general x1, matrix products, dot(): return jnp.dot(a, b, preferred_element_type=F32)  1.25 us
  transfers between devices with their start and end apart: 14, of which 10 were waited for; matrix products, arithmetic and copies ran while one was open for 3% of the time, Pallas kernels for 2%

profile of v2, /device:TPU:0, one launch (start us, length us, event | category | flops | bytes accessed | tf_op | source)
XLA Modules:
  0.0 52.6 jit_solution(3075637256170914183)
XLA Ops:
  0.6 0.0 copy-start
  0.6 0.0 copy-start.2
  0.7 1.1 %copy-done.2 = f32[128,768]{1,0:T(8,128)S(1)} copy-done((f32[128,768]{1,0:T(8,128)S(1)}, f32[128,768]{1,0:T(8,128)}, u32[]{:S(2)}) %copy-start.2) | copy-done | bytes 393240
  1.7 0.2 shard_map.94
  1.9 0.0 copy-start.5
  1.9 0.7 %copy-done.5 = bf16[128,768]{1,0:T(8,128)(2,1)} copy-done((bf16[128,768]{1,0:T(8,128)(2,1)}, bf16[128,768]{1,0:T(8,128)(2,1)S(1)}, u32[]{:S(2)}) %copy-start.5) | copy-done | bytes 196632
  2.6 2.9 %collective-permute-start.1 = (bf16[384,128]{1,0:T(8,128)(2,1)S(1)}, bf16[384,128]{1,0:T(8,128)(2,1)S(1)}, u32[]{:S(2)}, u32[]{:S(2)}) collective-permute-start(bf16[384,128]{1,0:T(8,128)(2,1)S(1)} %get-tuple-element.23), channel_id=1, source_target_pairs={{0,4},{1,5},{2,6},{3,7},{4,0},{5,1},{6,2},{7,3},{8,12},{9,13},{10,... | collective-permute-start | bytes 294920 | tf_op jit(solution)/shard_map/ppermute | solution.py:115
  5.5 0.0 copy-start.3
  5.5 1.0 %copy-done.3 = f32[128,768]{1,0:T(8,128)S(1)} copy-done((f32[128,768]{1,0:T(8,128)S(1)}, f32[128,768]{1,0:T(8,128)}, u32[]{:S(2)}) %copy-start.3) | copy-done | bytes 393240
  6.5 0.0 copy-start.6
  6.5 0.7 %copy-done.6 = s32[1,1,8,12,2]{3,4,2,1,0:T(2,128)S(1)} copy-done((s32[1,1,8,12,2]{3,4,2,1,0:T(2,128)S(1)}, s32[1,1,8,12,2]{3,4,2,1,0:T(2,128)}, u32[]{:S(2)}) %copy-start.6) | copy-done | bytes 792
  7.2 1.1 %shard_map.95 = bf16[128,768]{1,0:T(8,128)(2,1)} custom-call(f32[128,768]{1,0:T(8,128)S(1)} %copy-done.3, s32[8,2,12]{2,1,0:T(2,128)S(1)} %bitcast.9, f32[8,128]{1,0:T(8,128)S(1)} %get-tuple-element.20._), custom_call_target="tpu_custom_call" | custom-call | flops 50331648 | bytes 590592 | tf_op jit(solution)/shard_map/pallas_call | solution.py:22
  8.3 0.0 copy-start.7
  8.3 0.0 copy-start.1
  8.3 0.0 copy-start.4
  8.3 7.0 %all-to-all-start = ((bf16[8,16,768]{2,1,0:T(8,128)(2,1)}), bf16[8,16,768]{2,1,0:T(8,128)(2,1)S(1)}, u32[]{:S(2)}, u32[]{:S(2)}) async-start(bf16[8,16,768]{2,1,0:T(8,128)(2,1)} %bitcast.2), calls=%async_computation | async-start | bytes 393216 | tf_op jit(solution)/shard_map/all_to_all | solution.py:230
  15.3 1.5 %collective-permute-start = (bf16[384,128]{1,0:T(8,128)(2,1)S(1)}, bf16[384,128]{1,0:T(8,128)(2,1)S(1)}, u32[]{:S(2)}, u32[]{:S(2)}) collective-permute-start(bf16[384,128]{1,0:T(8,128)(2,1)S(1)} %get-tuple-element.22.refs_0_), channel_id=1, source_target_pairs={{0,2},{1,3},{2,0},{3,1},{4,6},{5,7},{6,4},{7,5},{8,10},{9,11},{10,... | collective-permute-start | bytes 294920 | tf_op jit(solution)/shard_map/ppermute | solution.py:115
  16.8 0.0 collective-permute-done.1.rest_1_.refs_2_
  16.8 0.5 collective-permute-start.2
  17.3 0.0 copy-done
  17.3 1.2 %fusion.self_ref = f32[128,768]{1,0:T(8,128)S(1)} fusion(bf16[128,768]{1,0:T(8,128)(2,1)} %copy-done.5, bf16[768,768]{1,0:T(8,128)(2,1)S(1)} %copy-done), kind=kOutput, calls=%fused_computation | convolution fusion | flops 150994944 | bytes 1769472 | tf_op jit(solution)/shard_map/dot_general | solution.py:17
  18.6 0.0 copy-done.7
  18.6 0.1 reshape.17.recv_ref
  18.7 1.8 %collective-permute-done.rest_0_.refs_1_ = bf16[384,128]{1,0:T(8,128)(2,1)S(1)} collective-permute-done((bf16[384,128]{1,0:T(8,128)(2,1)S(1)}, bf16[384,128]{1,0:T(8,128)(2,1)S(1)}, u32[]{:S(2)}, u32[]{:S(2)}) %collective-permute-start) | collective-permute-done | bytes 98336 | tf_op jit(solution)/shard_map/ppermute | solution.py:115
  20.5 1.1 %collective-permute-done.2.rest_2_.refs_3_ = bf16[384,128]{1,0:T(8,128)(2,1)S(1)} collective-permute-done((bf16[384,128]{1,0:T(8,128)(2,1)S(1)}, bf16[384,128]{1,0:T(8,128)(2,1)S(1)}, u32[]{:S(2)}, u32[]{:S(2)}) %collective-permute-start.2) | collective-permute-done | bytes 98336 | tf_op jit(solution)/shard_map/ppermute | solution.py:115
  21.6 0.0 all-to-all-done
  21.6 0.0 copy-done.1
  21.6 0.0 copy-done.4
  21.6 1.4 %shard_map.96 = (bf16[128,768]{1,0:T(8,128)(2,1)}, bf16[768,128]{1,0:T(8,128)(2,1)S(1)}, bf16[768,128]{1,0:T(8,128)(2,1)S(1)}, bf16[768,128]{1,0:T(8,128)(2,1)S(1)}, bf16[768,128]{1,0:T(8,128)(2,1)S(1)}) custom-call(bf16[128,768]{1,0:T(8,128)(2,1)S(1)} %bitcast.8, s32[1,128]{1,0:T(1,128)S(1)} %reshape.17.recv_ref, f32[128,768]{1,0:T(8,128)S(1)} %fusion.self_ref, ...), custom_call_target="tpu_custom_call" | custom-call | flops 176160768 | bytes 2949632 | tf_op jit(solution)/shard_map/pallas_call | solution.py:22
  23.0 1.3 %collective-permute-start.3 = (bf16[768,128]{1,0:T(8,128)(2,1)S(1)}, bf16[768,128]{1,0:T(8,128)(2,1)S(1)}, u32[]{:S(2)}, u32[]{:S(2)}) collective-permute-start(bf16[768,128]{1,0:T(8,128)(2,1)S(1)} %get-tuple-element.26), channel_id=1, source_target_pairs={{0,2},{1,3},{2,0},{3,1},{4,6},{5,7},{6,4},{7,5},{8,10},{9,11},{10,... | collective-permute-start | bytes 589832 | tf_op jit(solution)/shard_map/ppermute | solution.py:115
  24.3 0.6 %collective-permute-start.4 = (bf16[768,128]{1,0:T(8,128)(2,1)S(1)}, bf16[768,128]{1,0:T(8,128)(2,1)S(1)}, u32[]{:S(2)}, u32[]{:S(2)}) collective-permute-start(bf16[768,128]{1,0:T(8,128)(2,1)S(1)} %get-tuple-element.27), channel_id=1, source_target_pairs={{0,4},{1,5},{2,6},{3,7},{4,0},{5,1},{6,2},{7,3},{8,12},{9,13},{10,... | collective-permute-start | bytes 589832 | tf_op jit(solution)/shard_map/ppermute | solution.py:115
  24.9 1.6 %collective-permute-start.5 = (bf16[768,128]{1,0:T(8,128)(2,1)S(1)}, bf16[768,128]{1,0:T(8,128)(2,1)S(1)}, u32[]{:S(2)}, u32[]{:S(2)}) collective-permute-start(bf16[768,128]{1,0:T(8,128)(2,1)S(1)} %get-tuple-element.28), channel_id=1, source_target_pairs={{0,6},{1,7},{2,4},{3,5},{4,2},{5,3},{6,0},{7,1},{8,14},{9,15},{10,... | collective-permute-start | bytes 589832 | tf_op jit(solution)/shard_map/ppermute | solution.py:115
  26.5 3.8 %collective-permute-done.3.refs_5_ = bf16[768,128]{1,0:T(8,128)(2,1)S(1)} collective-permute-done((bf16[768,128]{1,0:T(8,128)(2,1)S(1)}, bf16[768,128]{1,0:T(8,128)(2,1)S(1)}, u32[]{:S(2)}, u32[]{:S(2)}) %collective-permute-start.3) | collective-permute-done | bytes 196640 | tf_op jit(solution)/shard_map/ppermute | solution.py:115
  30.3 1.0 %collective-permute-done.4.refs_6_ = bf16[768,128]{1,0:T(8,128)(2,1)S(1)} collective-permute-done((bf16[768,128]{1,0:T(8,128)(2,1)S(1)}, bf16[768,128]{1,0:T(8,128)(2,1)S(1)}, u32[]{:S(2)}, u32[]{:S(2)}) %collective-permute-start.4) | collective-permute-done | bytes 196640 | tf_op jit(solution)/shard_map/ppermute | solution.py:115
  31.3 2.6 %collective-permute-done.5.refs_7_ = bf16[768,128]{1,0:T(8,128)(2,1)S(1)} collective-permute-done((bf16[768,128]{1,0:T(8,128)(2,1)S(1)}, bf16[768,128]{1,0:T(8,128)(2,1)S(1)}, u32[]{:S(2)}, u32[]{:S(2)}) %collective-permute-start.5) | collective-permute-done | bytes 196640 | tf_op jit(solution)/shard_map/ppermute | solution.py:115
  33.9 0.7 %shard_map.97 = (f32[384,384]{1,0:T(8,128)S(1)}, bf16[384,384]{1,0:T(8,128)(2,1)S(1)}) custom-call(bf16[384,128]{1,0:T(8,128)(2,1)S(1)} %get-tuple-element.22.refs_0_, bf16[384,128]{1,0:T(8,128)(2,1)S(1)} %collective-permute-done.rest_0_.refs_1_, bf16[384,128]{1,0:T(8,128)(2,1)S(1)} %collective-permute-done.1.rest_1_.refs_2_, ...), custom_call_target="tpu_custom_call" | custom-call | flops 301989888 | bytes 2064384 | tf_op jit(solution)/shard_map/pallas_call | solution.py:22
  34.6 0.1 collective-permute-start.6
  34.7 1.6 %collective-permute-done.6.got_ref = bf16[384,384]{1,0:T(8,128)(2,1)S(1)} collective-permute-done((bf16[384,384]{1,0:T(8,128)(2,1)S(1)}, bf16[384,384]{1,0:T(8,128)(2,1)S(1)}, u32[]{:S(2)}, u32[]{:S(2)}) %collective-permute-start.6) | collective-permute-done | bytes 294944 | tf_op jit(solution)/shard_map/ppermute | solution.py:115
  36.2 0.1 shard_map.98
  36.4 0.7 %collective-permute-start.7 = (bf16[96,384]{1,0:T(8,128)(2,1)S(1)}, bf16[96,384]{1,0:T(8,128)(2,1)S(1)}, u32[]{:S(2)}, u32[]{:S(2)}) collective-permute-start(bf16[96,384]{1,0:T(8,128)(2,1)S(1)} %get-tuple-element.32), channel_id=1, source_target_pairs={{0,16},{1,17},{2,18},{3,19},{4,20},{5,21},{6,22},{7,23},{8,24},{9,... | collective-permute-start | bytes 221192 | tf_op jit(solution)/shard_map/ppermute | solution.py:115
  37.0 2.3 %collective-permute-start.8 = (bf16[96,384]{1,0:T(8,128)(2,1)S(1)}, bf16[96,384]{1,0:T(8,128)(2,1)S(1)}, u32[]{:S(2)}, u32[]{:S(2)}) collective-permute-start(bf16[96,384]{1,0:T(8,128)(2,1)S(1)} %get-tuple-element.33), channel_id=1, source_target_pairs={{0,24},{1,25},{2,26},{3,27},{4,28},{5,29},{6,30},{7,31},{8,16},{9,... | collective-permute-start | bytes 221192 | tf_op jit(solution)/shard_map/ppermute | solution.py:115
  39.4 0.5 %collective-permute-start.9 = (bf16[96,384]{1,0:T(8,128)(2,1)S(1)}, bf16[96,384]{1,0:T(8,128)(2,1)S(1)}, u32[]{:S(2)}, u32[]{:S(2)}) collective-permute-start(bf16[96,384]{1,0:T(8,128)(2,1)S(1)} %get-tuple-element.34), channel_id=1, source_target_pairs={{0,8},{1,9},{2,10},{3,11},{4,12},{5,13},{6,14},{7,15},{8,0},{9,1},... | collective-permute-start | bytes 221192 | tf_op jit(solution)/shard_map/ppermute | solution.py:115
  39.9 5.0 %collective-permute-done.7.refs_1_ = bf16[96,384]{1,0:T(8,128)(2,1)S(1)} collective-permute-done((bf16[96,384]{1,0:T(8,128)(2,1)S(1)}, bf16[96,384]{1,0:T(8,128)(2,1)S(1)}, u32[]{:S(2)}, u32[]{:S(2)}) %collective-permute-start.7) | collective-permute-done | bytes 73760 | tf_op jit(solution)/shard_map/ppermute | solution.py:115
  44.9 0.0 collective-permute-done.8.refs_2_
  45.0 1.0 %collective-permute-done.9.refs_3_ = bf16[96,384]{1,0:T(8,128)(2,1)S(1)} collective-permute-done((bf16[96,384]{1,0:T(8,128)(2,1)S(1)}, bf16[96,384]{1,0:T(8,128)(2,1)S(1)}, u32[]{:S(2)}, u32[]{:S(2)}) %collective-permute-start.9) | collective-permute-done | bytes 73760 | tf_op jit(solution)/shard_map/ppermute | solution.py:115
  46.0 1.1 %collective-permute-start.11 = (bf16[96,384]{1,0:T(8,128)(2,1)S(1)}, bf16[96,384]{1,0:T(8,128)(2,1)S(1)}, u32[]{:S(2)}, u32[]{:S(2)}) collective-permute-start(bf16[96,384]{1,0:T(8,128)(2,1)S(1)} %shard_map.99.refs_0_), channel_id=1, source_target_pairs={{0,2},{1,3},{2,0},{3,1},{4,6},{5,7},{6,4},{7,5},{8,10},{9,11},{10,... | collective-permute-start | bytes 221192 | tf_op jit(solution)/shard_map/ppermute | solution.py:115
  47.1 0.0 collective-permute-start.10
  47.1 3.4 %collective-permute-done.11.refs_2_ = bf16[96,384]{1,0:T(8,128)(2,1)S(1)} collective-permute-done((bf16[96,384]{1,0:T(8,128)(2,1)S(1)}, bf16[96,384]{1,0:T(8,128)(2,1)S(1)}, u32[]{:S(2)}, u32[]{:S(2)}) %collective-permute-start.11) | collective-permute-done | bytes 73760 | tf_op jit(solution)/shard_map/ppermute | solution.py:115
  50.5 0.0 collective-permute-start.12
  50.5 0.0 collective-permute-done.10.refs_1_
  50.5 1.3 %collective-permute-done.12.refs_3_ = bf16[96,384]{1,0:T(8,128)(2,1)S(1)} collective-permute-done((bf16[96,384]{1,0:T(8,128)(2,1)S(1)}, bf16[96,384]{1,0:T(8,128)(2,1)S(1)}, u32[]{:S(2)}, u32[]{:S(2)}) %collective-permute-start.12) | collective-permute-done | bytes 73760 | tf_op jit(solution)/shard_map/ppermute | solution.py:115
  51.7 0.9 %shard_map.100 = (f32[96,768]{1,0:T(8,128)}, f32[96,768]{1,0:T(8,128)}) custom-call(bf16[96,384]{1,0:T(8,128)(2,1)S(1)} %shard_map.99.refs_0_, bf16[96,384]{1,0:T(8,128)(2,1)S(1)} %collective-permute-done.10.refs_1_, bf16[96,384]{1,0:T(8,128)(2,1)S(1)} %collective-permute-done.11.refs_2_, bf16[96,384]{1,0:T(8,128)(2,1)S(1)} %collective-permute-done.12.refs_3_), custom_call_target="tpu_custom_call" | custom-call | bytes 884736 | tf_op jit(solution)/shard_map/pallas_call | solution.py:22
  (2 shorter events, 0.0 us)
Async XLA Ops:
  0.6 16.7 %copy-start = (bf16[768,768]{1,0:T(8,128)(2,1)S(1)}, bf16[768,768]{1,0:T(8,128)(2,1)}, u32[]{:S(2)}) copy-start(bf16[768,768]{1,0:T(8,128)(2,1)} %param.12) | copy-start | bytes 3538948
  0.6 1.1 %copy-start.2 = (f32[128,768]{1,0:T(8,128)S(1)}, f32[128,768]{1,0:T(8,128)}, u32[]{:S(2)}) copy-start(f32[128,768]{1,0:T(8,128)} %self_ref.1) | copy-start | bytes 1179652
  1.9 0.7 %copy-start.5 = (bf16[128,768]{1,0:T(8,128)(2,1)}, bf16[128,768]{1,0:T(8,128)(2,1)S(1)}, u32[]{:S(2)}) copy-start(bf16[128,768]{1,0:T(8,128)(2,1)S(1)} %get-tuple-element.21) | copy-start | bytes 589828
  2.6 14.2 %collective-permute-start.1 = (bf16[384,128]{1,0:T(8,128)(2,1)S(1)}, bf16[384,128]{1,0:T(8,128)(2,1)S(1)}, u32[]{:S(2)}, u32[]{:S(2)}) collective-permute-start(bf16[384,128]{1,0:T(8,128)(2,1)S(1)} %get-tuple-element.23), channel_id=1, source_target_pairs={{0,4},{1,5},{2,6},{3,7},{4,0},{5,1},{6,2},{7,3},{8,12},{9,13},{10,... | collective-permute-start | bytes 294920 | tf_op jit(solution)/shard_map/ppermute | solution.py:115
  5.5 1.0 %copy-start.3 = (f32[128,768]{1,0:T(8,128)S(1)}, f32[128,768]{1,0:T(8,128)}, u32[]{:S(2)}) copy-start(f32[128,768]{1,0:T(8,128)} %feat_ref.1) | copy-start | bytes 1179652
  6.5 0.7 %copy-start.6 = (s32[1,1,8,12,2]{3,4,2,1,0:T(2,128)S(1)}, s32[1,1,8,12,2]{3,4,2,1,0:T(2,128)}, u32[]{:S(2)}) copy-start(s32[1,1,8,12,2]{3,4,2,1,0:T(2,128)} %param.9) | copy-start | bytes 2308
  8.3 10.3 %copy-start.7 = (s32[1,1,8,12]{3,2,1,0:T(8,128)S(1)}, s32[1,1,8,12]{3,2,1,0:T(8,128)}, u32[]{:S(2)}) copy-start(s32[1,1,8,12]{3,2,1,0:T(8,128)} %param.10) | copy-start | bytes 1156
  8.3 13.3 %copy-start.1 = (bf16[768,768]{1,0:T(8,128)(2,1)S(1)}, bf16[768,768]{1,0:T(8,128)(2,1)}, u32[]{:S(2)}) copy-start(bf16[768,768]{1,0:T(8,128)(2,1)} %w_ref.1) | copy-start | bytes 3538948
  8.3 13.3 %copy-start.4 = (bf16[128,768]{1,0:T(8,128)(2,1)S(1)}, bf16[128,768]{1,0:T(8,128)(2,1)}, u32[]{:S(2)}) copy-start(bf16[128,768]{1,0:T(8,128)(2,1)} %cot_ref.1) | copy-start | bytes 589828
  8.3 13.3 %all-to-all-start = ((bf16[8,16,768]{2,1,0:T(8,128)(2,1)}), bf16[8,16,768]{2,1,0:T(8,128)(2,1)S(1)}, u32[]{:S(2)}, u32[]{:S(2)}) async-start(bf16[8,16,768]{2,1,0:T(8,128)(2,1)} %bitcast.2), calls=%async_computation | async-start | bytes 393216 | tf_op jit(solution)/shard_map/all_to_all | solution.py:230
  15.3 5.2 %collective-permute-start = (bf16[384,128]{1,0:T(8,128)(2,1)S(1)}, bf16[384,128]{1,0:T(8,128)(2,1)S(1)}, u32[]{:S(2)}, u32[]{:S(2)}) collective-permute-start(bf16[384,128]{1,0:T(8,128)(2,1)S(1)} %get-tuple-element.22.refs_0_), channel_id=1, source_target_pairs={{0,2},{1,3},{2,0},{3,1},{4,6},{5,7},{6,4},{7,5},{8,10},{9,11},{10,... | collective-permute-start | bytes 294920 | tf_op jit(solution)/shard_map/ppermute | solution.py:115
  16.8 4.7 %collective-permute-start.2 = (bf16[384,128]{1,0:T(8,128)(2,1)S(1)}, bf16[384,128]{1,0:T(8,128)(2,1)S(1)}, u32[]{:S(2)}, u32[]{:S(2)}) collective-permute-start(bf16[384,128]{1,0:T(8,128)(2,1)S(1)} %collective-permute-done.1.rest_1_.refs_2_), channel_id=1, source_target_pairs={{0,2},{1,3},{2,0},{3,1},{4,6},{5,7},{6,4},{7,5},{8,10},{9,11},{10,... | collective-permute-start | bytes 294920 | tf_op jit(solution)/shard_map/ppermute | solution.py:115
  23.0 7.3 %collective-permute-start.3 = (bf16[768,128]{1,0:T(8,128)(2,1)S(1)}, bf16[768,128]{1,0:T(8,128)(2,1)S(1)}, u32[]{:S(2)}, u32[]{:S(2)}) collective-permute-start(bf16[768,128]{1,0:T(8,128)(2,1)S(1)} %get-tuple-element.26), channel_id=1, source_target_pairs={{0,2},{1,3},{2,0},{3,1},{4,6},{5,7},{6,4},{7,5},{8,10},{9,11},{10,... | collective-permute-start | bytes 589832 | tf_op jit(solution)/shard_map/ppermute | solution.py:115
  24.3 7.0 %collective-permute-start.4 = (bf16[768,128]{1,0:T(8,128)(2,1)S(1)}, bf16[768,128]{1,0:T(8,128)(2,1)S(1)}, u32[]{:S(2)}, u32[]{:S(2)}) collective-permute-start(bf16[768,128]{1,0:T(8,128)(2,1)S(1)} %get-tuple-element.27), channel_id=1, source_target_pairs={{0,4},{1,5},{2,6},{3,7},{4,0},{5,1},{6,2},{7,3},{8,12},{9,13},{10,... | collective-permute-start | bytes 589832 | tf_op jit(solution)/shard_map/ppermute | solution.py:115
  24.9 9.0 %collective-permute-start.5 = (bf16[768,128]{1,0:T(8,128)(2,1)S(1)}, bf16[768,128]{1,0:T(8,128)(2,1)S(1)}, u32[]{:S(2)}, u32[]{:S(2)}) collective-permute-start(bf16[768,128]{1,0:T(8,128)(2,1)S(1)} %get-tuple-element.28), channel_id=1, source_target_pairs={{0,6},{1,7},{2,4},{3,5},{4,2},{5,3},{6,0},{7,1},{8,14},{9,15},{10,... | collective-permute-start | bytes 589832 | tf_op jit(solution)/shard_map/ppermute | solution.py:115
  34.6 1.6 %collective-permute-start.6 = (bf16[384,384]{1,0:T(8,128)(2,1)S(1)}, bf16[384,384]{1,0:T(8,128)(2,1)S(1)}, u32[]{:S(2)}, u32[]{:S(2)}) collective-permute-start(bf16[384,384]{1,0:T(8,128)(2,1)S(1)} %get-tuple-element.30), channel_id=1, source_target_pairs={{0,1},{1,0},{2,3},{3,2},{4,5},{5,4},{6,7},{7,6},{8,9},{9,8},{10,11... | collective-permute-start | bytes 884744 | tf_op jit(solution)/shard_map/ppermute | solution.py:115
  36.4 8.6 %collective-permute-start.7 = (bf16[96,384]{1,0:T(8,128)(2,1)S(1)}, bf16[96,384]{1,0:T(8,128)(2,1)S(1)}, u32[]{:S(2)}, u32[]{:S(2)}) collective-permute-start(bf16[96,384]{1,0:T(8,128)(2,1)S(1)} %get-tuple-element.32), channel_id=1, source_target_pairs={{0,16},{1,17},{2,18},{3,19},{4,20},{5,21},{6,22},{7,23},{8,24},{9,... | collective-permute-start | bytes 221192 | tf_op jit(solution)/shard_map/ppermute | solution.py:115
  37.0 7.9 %collective-permute-start.8 = (bf16[96,384]{1,0:T(8,128)(2,1)S(1)}, bf16[96,384]{1,0:T(8,128)(2,1)S(1)}, u32[]{:S(2)}, u32[]{:S(2)}) collective-permute-start(bf16[96,384]{1,0:T(8,128)(2,1)S(1)} %get-tuple-element.33), channel_id=1, source_target_pairs={{0,24},{1,25},{2,26},{3,27},{4,28},{5,29},{6,30},{7,31},{8,16},{9,... | collective-permute-start | bytes 221192 | tf_op jit(solution)/shard_map/ppermute | solution.py:115
  39.4 6.6 %collective-permute-start.9 = (bf16[96,384]{1,0:T(8,128)(2,1)S(1)}, bf16[96,384]{1,0:T(8,128)(2,1)S(1)}, u32[]{:S(2)}, u32[]{:S(2)}) collective-permute-start(bf16[96,384]{1,0:T(8,128)(2,1)S(1)} %get-tuple-element.34), channel_id=1, source_target_pairs={{0,8},{1,9},{2,10},{3,11},{4,12},{5,13},{6,14},{7,15},{8,0},{9,1},... | collective-permute-start | bytes 221192 | tf_op jit(solution)/shard_map/ppermute | solution.py:115
  46.0 4.4 %collective-permute-start.11 = (bf16[96,384]{1,0:T(8,128)(2,1)S(1)}, bf16[96,384]{1,0:T(8,128)(2,1)S(1)}, u32[]{:S(2)}, u32[]{:S(2)}) collective-permute-start(bf16[96,384]{1,0:T(8,128)(2,1)S(1)} %shard_map.99.refs_0_), channel_id=1, source_target_pairs={{0,2},{1,3},{2,0},{3,1},{4,6},{5,7},{6,4},{7,5},{8,10},{9,11},{10,... | collective-permute-start | bytes 221192 | tf_op jit(solution)/shard_map/ppermute | solution.py:115
  47.1 3.4 %collective-permute-start.10 = (bf16[96,384]{1,0:T(8,128)(2,1)S(1)}, bf16[96,384]{1,0:T(8,128)(2,1)S(1)}, u32[]{:S(2)}, u32[]{:S(2)}) collective-permute-start(bf16[96,384]{1,0:T(8,128)(2,1)S(1)} %shard_map.99.refs_0_), channel_id=1, source_target_pairs={{0,1},{1,0},{2,3},{3,2},{4,5},{5,4},{6,7},{7,6},{8,9},{9,8},{10,11... | collective-permute-start | bytes 221192 | tf_op jit(solution)/shard_map/ppermute | solution.py:115
  50.5 1.3 %collective-permute-start.12 = (bf16[96,384]{1,0:T(8,128)(2,1)S(1)}, bf16[96,384]{1,0:T(8,128)(2,1)S(1)}, u32[]{:S(2)}, u32[]{:S(2)}) collective-permute-start(bf16[96,384]{1,0:T(8,128)(2,1)S(1)} %collective-permute-done.11.refs_2_), channel_id=1, source_target_pairs={{0,1},{1,0},{2,3},{3,2},{4,5},{5,4},{6,7},{7,6},{8,9},{9,8},{10,11... | collective-permute-start | bytes 221192 | tf_op jit(solution)/shard_map/ppermute | solution.py:115

commit v3 on v2

--- a/solution.py
+++ b/solution.py
@@ -11,33 +11,46 @@
 SLOT_PAD = 16
 VMEM = pl.BlockSpec(memory_space=pltpu.VMEM)
 ANY = pl.BlockSpec(memory_space=pl.ANY)
+HBM = pl.BlockSpec(memory_space=pltpu.HBM)
 
 
 def dot(a, b):
     return jnp.dot(a, b, preferred_element_type=F32)
 
 
-def call(body, outs, args, unread=(), scratch=(), flops=0):
+def call(body, outs, args, unread=(), hbm=(), scratch=(), flops=0, vmem=16):
     moved = sum(a.size * a.dtype.itemsize for a in (*args, *outs))
     return pl.pallas_call(
         body,
         out_shape=list(outs),
-        in_specs=[VMEM] * len(args) + [ANY] * len(unread),
+        in_specs=[VMEM] * len(args) + [ANY] * len(unread) + [HBM] * len(hbm),
         out_specs=[VMEM] * len(outs),
         scratch_shapes=list(scratch),
-        compiler_params=pltpu.CompilerParams(vmem_limit_bytes=16 * 1024 * 1024),
+        compiler_params=pltpu.CompilerParams(vmem_limit_bytes=vmem * 1024 * 1024),
         cost_estimate=pl.CostEstimate(flops=flops, bytes_accessed=moved, transcendentals=0),
-    )(*args, *unread)
+    )(*args, *unread, *hbm)
 
 
 def shape(dims, kind):
     return jax.ShapeDtypeStruct(dims, kind)
 
 
-def slot_sums_kernel(order, feat_ref, edge_ref, _, out_ref):
+def slot_sums_kernel(plan, order, feat_hbm, edge_hbm, *rest):
+    with_own = len(rest) > 4
+    if with_own:
+        self_hbm, out_ref, *own_refs, feat_ref, edge_ref, sems, self_ref, trans_ref = rest
+    else:
+        out_ref, feat_ref, edge_ref, sems = rest
+    copies = [pltpu.make_async_copy(edge_hbm, edge_ref, sems.at[0]),
+              pltpu.make_async_copy(feat_hbm, feat_ref, sems.at[1])]
+    if with_own:
+        copies.append(pltpu.make_async_copy(self_hbm, self_ref, sems.at[2]))
+    for copy in copies:
+        copy.start()
     owned = feat_ref.shape[0]
     _, mult, cap = edge_ref.shape
     slots = len(order) * SLOT_PAD
+    copies[0].wait()
     fill = jnp.full((mult, SLOT_PAD - cap), owned, jnp.int32)
     ids = jnp.concatenate([p for d in order for p in (edge_ref[d], fill)], axis=1)
     row = lax.broadcasted_iota(jnp.int32, (owned, slots), 0)
@@ -55,12 +68,16 @@
     l2 = lax.broadcasted_iota(jnp.int32, (slots, 128), 1)
     fold = ((c2 & (SLOT_PAD - 1)) == l2).astype(BF16)
     counts = dot(spread, fold)
+    copies[1].wait()
     feat = feat_ref[...]
     high = feat.astype(BF16)
     low = (feat - high.astype(F32)).astype(BF16)
     sums = dot(pick, high) + dot(pick, low)
     out_ref[:, :128] = (sums[:, :128] + counts).astype(BF16)
     out_ref[:, 128:] = sums[:, 128:].astype(BF16)
+    if with_own:
+        copies[2].wait()
+        write_own(plan, self_ref, *own_refs, trans_ref)
 
 
 def neighbor_mean(cap, rows, recv, targets):
@@ -121,60 +138,49 @@
         return [z * self.gx + x for z, x in turns[:self.ns]]
 
 
-def write_rows(plan, trans_ref, outs):
+def write_rows(plan, trans_ref, *outs):
     x = plan.place()[1]
-    for (dx, dy), out in zip(plan.peers, outs):
+    for dx, out in enumerate(outs):
         for z in range(plan.nz):
             start = pl.multiple_of((z * plan.gx + (x ^ dx)) * plan.shard, 16)
             out[z * plan.shard:(z + 1) * plan.shard, :] = trans_ref[pl.ds(start, plan.shard), :]
 
 
-def own_kernel(plan, self_ref, own_ref, here_ref, there_ref, token_ref, trans_ref):
+def write_own(plan, self_ref, own_ref, here_ref, there_ref, trans_ref):
     own_ref[...] = self_ref[...].astype(BF16)
     trans_ref[...] = self_ref[...].T.astype(BF16)
-    x = plan.place()[1]
-    for dx, out in enumerate((here_ref, there_ref)):
-        for z in range(plan.nz):
-            start = pl.multiple_of((z * plan.gx + (x ^ dx)) * plan.shard, 16)
-            out[z * plan.shard:(z + 1) * plan.shard, :] = trans_ref[pl.ds(start, plan.shard), :]
-    token_ref[...] = jnp.zeros_like(token_ref)
-
-
-def layer_kernel(plan, cap, order, ordered, rows_ref, recv_ref, self_ref, cot_ref, w_ref, *rest):
-    hidden_ref, *outs = rest[ordered:-2]
-    trans_ref, grad_ref = rest[-2:]
+    write_rows(plan, trans_ref, here_ref, there_ref)
+
+
+def layer_kernel(plan, cap, order, ordered, arrived_ref, recv_ref, self_ref, cot_ref, w_ref, *rest):
+    hidden_ref, mean_here, mean_there, grad_here, grad_there, trans_ref, grad_ref = rest[ordered:]
     targets = self_ref.shape[0]
-    y = plan.place()[2]
     rows = jnp.concatenate(
-        [rows_ref[p * SLOT_PAD:(p + 1) * SLOT_PAD, :] for p in (order.index(s) for s in range(plan.ns))], axis=0)
+        [arrived_ref[p * SLOT_PAD:(p + 1) * SLOT_PAD, :] for p in (order.index(s) for s in range(plan.ns))], axis=0)
     mean = neighbor_mean(cap, rows, recv_ref[...], targets)
+    trans_ref[...] = mean.astype(F32).T.astype(BF16)
+    write_rows(plan, trans_ref, mean_here, mean_there)
     preact = self_ref[...] + dot(mean, w_ref[...])
     hidden, grad = forward(preact, cot_ref[...])
     hidden_ref[...] = hidden
-    trans_ref[...] = mean.astype(F32).T.astype(BF16)
-    write_rows(plan, trans_ref, outs)
     for b in range(grad_ref.shape[0]):
         grad_ref[b] = grad[:, b * 128:(b + 1) * 128]
-    each = plan.cols // 128
-    for (dx, dy), out in zip(plan.peers, outs):
+    y, each = plan.place()[2], plan.cols // 128
+    for dy, out in enumerate((grad_here, grad_there)):
         for b in range(each):
-            at = plan.rows + b * targets
-            out[at:at + targets, :] = grad_ref[(y ^ dy) * each + b]
-
-
-def terms_kernel(plan, *refs):
+            out[b * targets:(b + 1) * targets, :] = grad_ref[(y ^ dy) * each + b]
+
+
+def terms_kernel(plan, keep, *refs):
     n = len(plan.peers)
-    own, late, (keep_ref, send_ref, total_ref) = refs[:n], refs[n:2 * n], refs[2 * n:]
-    rows, each, targets = plan.rows, plan.cols // 128, own[0].shape[1]
-    left = jnp.concatenate(
-        [jnp.concatenate([o[...], l[:rows, :]], axis=0) for o, l in zip(own, late)], axis=1)
+    own, mean, grad, out_ref = refs[:n], refs[n:2 * n], refs[2 * n:3 * n], refs[3 * n]
+    targets = own[0].shape[1]
+    use_own = plan.place()[3] == (0 if keep else 1)
+    left = jnp.concatenate([jnp.where(use_own, o[...], m[...]) for o, m in zip(own, mean)], axis=1)
     right = jnp.concatenate(
-        [jnp.concatenate([l[rows + b * targets:rows + (b + 1) * targets, :] for b in range(each)], axis=1)
-         for l in late], axis=0)
-    total_ref[...] = dot(left, right)
-    c = plan.place()[3]
-    keep_ref[...] = total_ref[pl.ds(pl.multiple_of(c * rows, 16), rows), :]
-    send_ref[...] = total_ref[pl.ds(pl.multiple_of((1 - c) * rows, 16), rows), :].astype(BF16)
+        [jnp.concatenate([g[b * targets:(b + 1) * targets, :] for b in range(plan.cols // 128)], axis=1)
+         for g in grad], axis=0)
+    out_ref[...] = dot(left, right).astype(out_ref.dtype)
 
 
 def core_sum_kernel(plan, keep_ref, got_ref, *rest):
@@ -216,17 +222,16 @@
     fits = plan.fits()
     order = plan.store_order() if fits else list(range(ns))
     rows, cols, n = plan.rows, plan.cols, len(plan.peers)
-    token = jnp.zeros((8, 128), F32)
+    scratch = [pltpu.VMEM(features.shape, F32), pltpu.VMEM(edges.shape, jnp.int32),
+               pltpu.SemaphoreType.DMA((3,))]
+    outs, more = [shape((slots, width), BF16)], []
     if fits:
-        own, own_here, own_there, token = call(
-            functools.partial(own_kernel, plan),
-            [shape((targets, width), BF16)] + [shape((rows, targets), BF16)] * 2 + [shape((8, 128), F32)],
-            [self_rows], scratch=[pltpu.VMEM((width, targets), BF16)])
-        own_x = plan.send(own_there, lambda z, x, y, c: (z, 1 - x, y, c))
-        own_y = plan.send(own_here, lambda z, x, y, c: (z, x, 1 - y, c))
-    (sums,) = call(
-        functools.partial(slot_sums_kernel, order), [shape((slots, width), BF16)],
-        [features, edges], unread=[token], flops=4 * slots * owned * width)
+        outs += [shape((targets, width), BF16)] + [shape((rows, targets), BF16)] * 2
+        more = [self_rows]
+        scratch += [pltpu.VMEM(self_rows.shape, F32), pltpu.VMEM((width, targets), BF16)]
+    sums, *owns = call(
+        functools.partial(slot_sums_kernel, plan, order), outs, (), hbm=[features, edges] + more,
+        flops=4 * slots * owned * width, vmem=60 if fits else 16, scratch=scratch)
     arrived = lax.all_to_all(sums.reshape(ns, SLOT_PAD, width), "store", split_axis=0, concat_axis=0,
                              tiled=True, axis_index_groups=[order]).reshape(slots, width)
     if not fits:
@@ -240,29 +245,32 @@
         total = lax.psum(part, "trainer")
         return hidden, total[:plan.shard], total[plan.shard:]
 
-    own_xy = plan.send(own_x, lambda z, x, y, c: (z, x, 1 - y, c))
-    own_all = [own_here, own_y, own_x, own_xy]
+    def to_x(array):
+        return plan.send(array, lambda z, x, y, c: (z, 1 - x, y, c))
+
+    def to_y(array):
+        return plan.send(array, lambda z, x, y, c: (z, x, 1 - y, c))
+
+    own, own_here, own_there = owns
+    own_x = to_x(own_there)
+    own_all = [own_here, to_y(own_here), own_x, to_y(own_x)]
     self_term = dot(own, w_self)
 
-    def exchange(arrays):
-        out = {}
-        for i in reversed(range(1, n)):
-            dx, dy = plan.peers[i]
-            out[i] = plan.send(arrays[i], lambda z, x, y, c, dx=dx, dy=dy: (z, x ^ dx, y ^ dy, c))
-        return [arrays[0]] + [out[i] for i in range(1, n)]
-
-    late_rows = rows + cols // 128 * targets
-    hidden, *late = call(
+    hidden, mean_here, mean_there, grad_here, grad_there = call(
         functools.partial(layer_kernel, plan, cap, order, n - 1),
-        [shape((targets, out_width), BF16)] + [shape((late_rows, targets), BF16)] * n,
+        [shape((targets, out_width), BF16)] + [shape((rows, targets), BF16)] * 2
+        + [shape((cols // 128 * targets, 128), BF16)] * 2,
         [arrived, recv, self_term, cotangent, w_neigh], unread=own_all[1:],
         scratch=[pltpu.VMEM((width, targets), BF16), pltpu.VMEM((out_width // 128, targets, 128), BF16)],
         flops=2 * targets * width * (out_width + slots))
-    keep, give = call(
-        functools.partial(terms_kernel, plan),
-        [shape((rows, cols), F32), shape((rows, cols), BF16)],
-        own_all + exchange(late), scratch=[pltpu.VMEM((2 * rows, cols), F32)],
-        flops=4 * rows * cols * targets * n)
+    mean_x, grad_y = to_x(mean_there), to_y(grad_there)
+    mean_all = [mean_here, to_y(mean_here), mean_x, to_y(mean_x)]
+    grad_all = [grad_here, grad_y, to_x(grad_here), to_x(grad_y)]
+    factors = own_all + mean_all + grad_all
+    (give,) = call(functools.partial(terms_kernel, plan, False), [shape((rows, cols), BF16)], factors,
+                   flops=2 * rows * cols * targets * n)
+    (keep,) = call(functools.partial(terms_kernel, plan, True), [shape((rows, cols), F32)], factors,
+                   flops=2 * rows * cols * targets * n)
     got = plan.send(give, lambda z, x, y, c: (z, x, y, 1 - c))
     block = (plan.shard, cols)
     mine, *others = call(

time: 53 us -> 50.5 us (0.953)
  local copies, waits for them, and re-layouts: 3.55 us -> 0.12 us
  starting transfers between devices: 20.1 us -> 22.8 us
  waiting for transfers between devices: 22.5 us -> 19.9 us
  Pallas kernels: 4.4 us -> 5.39 us
    unnamed x16 -> x10, local copies, waits for them, and re-layouts: 3.47 us -> 0.03 us
    ppermute x13 -> x16, starting transfers between devices: 13.1 us -> 16 us  [send(): return lax.ppermute(array, ('store', 'trainer'), pairs)]
    ppermute x13 -> x16, waiting for transfers between devices: 22.5 us -> 19.9 us  [send(): return lax.ppermute(array, ('store', 'trainer'), pairs)]
    pallas_call x7, Pallas kernels: 4.4 us -> 5.39 us  [call(): pl.pallas_call(body, out_shape=list(outs), in_specs=[VMEM] * len(args) +...]
  transfers between devices with their start and end apart: 14 -> 17, of which waited for: 10 -> 11; matrix products, arithmetic and copies ran while one was open for 3% -> 3% of each run, Pallas kernels for 2% -> 1%
where the time goes in v3:
time: 50.5 us; the launch traced here: 50.2 us
  starting transfers between devices  22.8 us (45%)
  waiting for transfers between devices  19.9 us (39%)
  Pallas kernels  5.39 us (11%)
  matrix products  1.25 us (2%)
  between operations  0.75 us (1%)
    ppermute x16, waiting for transfers between devices, send(): return lax.ppermute(array, ('store', 'trainer'), pairs)  19.9 us
    ppermute x16, starting transfers between devices, send(): return lax.ppermute(array, ('store', 'trainer'), pairs)  16 us
    all_to_all x1, starting transfers between devices, per_device(): lax.all_to_all(sums.reshape(ns, SLOT_PAD, width), 'store', split_axis=0,...  6.87 us
    pallas_call x7, Pallas kernels, call(): pl.pallas_call(body, out_shape=list(outs), in_specs=[VMEM] * len(args) +...  5.39 us
    dot_general x1, matrix products, dot(): return jnp.dot(a, b, preferred_element_type=F32)  1.25 us
  transfers between devices with their start and end apart: 17, of which 11 were waited for; matrix products, arithmetic and copies ran while one was open for 3% of the time, Pallas kernels for 1%

profile of v3, /device:TPU:0, one launch (start us, length us, event | category | flops | bytes accessed | tf_op | source)
XLA Modules:
  0.0 50.2 jit_solution(3539426431382146418)
XLA Ops:
  0.6 0.0 copy-start
  0.6 2.2 %shard_map.94 = (bf16[128,768]{1,0:T(8,128)(2,1)}, bf16[128,768]{1,0:T(8,128)(2,1)}, bf16[384,128]{1,0:T(8,128)(2,1)}, bf16[384,128]{1,0:T(8,128)(2,1)}) custom-call(f32[128,768]{1,0:T(8,128)} %feat_hbm.1, s32[8,2,12]{2,1,0:T(2,128)} %bitcast.10, f32[128,768]{1,0:T(8,128)} %rest_0_.1), custom_call_target="tpu_custom_call" | custom-call | flops 50331648 | bytes 589824 | tf_op jit(solution)/shard_map/pallas_call | solution.py:23
  2.9 0.0 copy-start.4
  2.9 0.0 copy-start.1
  2.9 0.0 copy-start.3
  2.9 3.0 %collective-permute-start.1 = (bf16[384,128]{1,0:T(8,128)(2,1)}, bf16[384,128]{1,0:T(8,128)(2,1)S(1)}, u32[]{:S(2)}, u32[]{:S(2)}) collective-permute-start(bf16[384,128]{1,0:T(8,128)(2,1)} %get-tuple-element.21), channel_id=1, source_target_pairs={{0,4},{1,5},{2,6},{3,7},{4,0},{5,1},{6,2},{7,3},{8,12},{9,13},{10,... | collective-permute-start | bytes 294920 | tf_op jit(solution)/shard_map/ppermute | solution.py:132
  5.9 6.9 %all-to-all-start = ((bf16[8,16,768]{2,1,0:T(8,128)(2,1)}), bf16[8,16,768]{2,1,0:T(8,128)(2,1)S(1)}, u32[]{:S(2)}, u32[]{:S(2)}) async-start(bf16[8,16,768]{2,1,0:T(8,128)(2,1)} %bitcast.9), calls=%async_computation | async-start | bytes 393216 | tf_op jit(solution)/shard_map/all_to_all | solution.py:235
  12.8 1.5 %collective-permute-start = (bf16[384,128]{1,0:T(8,128)(2,1)}, bf16[384,128]{1,0:T(8,128)(2,1)S(1)}, u32[]{:S(2)}, u32[]{:S(2)}) collective-permute-start(bf16[384,128]{1,0:T(8,128)(2,1)} %get-tuple-element.20.refs_0_), channel_id=1, source_target_pairs={{0,2},{1,3},{2,0},{3,1},{4,6},{5,7},{6,4},{7,5},{8,10},{9,11},{10,... | collective-permute-start | bytes 294920 | tf_op jit(solution)/shard_map/ppermute | solution.py:132
  14.3 0.0 collective-permute-done.1.rest_1_.refs_2_
  14.3 0.5 %collective-permute-start.2 = (bf16[384,128]{1,0:T(8,128)(2,1)S(1)}, bf16[384,128]{1,0:T(8,128)(2,1)S(1)}, u32[]{:S(2)}, u32[]{:S(2)}) collective-permute-start(bf16[384,128]{1,0:T(8,128)(2,1)S(1)} %collective-permute-done.1.rest_1_.refs_2_), channel_id=1, source_target_pairs={{0,2},{1,3},{2,0},{3,1},{4,6},{5,7},{6,4},{7,5},{8,10},{9,11},{10,... | collective-permute-start | bytes 294920 | tf_op jit(solution)/shard_map/ppermute | solution.py:132
  14.8 0.0 copy-done
  14.8 1.2 %fusion.self_ref = f32[128,768]{1,0:T(8,128)S(1)} fusion(bf16[128,768]{1,0:T(8,128)(2,1)} %get-tuple-element.19, bf16[768,768]{1,0:T(8,128)(2,1)S(1)} %copy-done), kind=kOutput, calls=%fused_computation | convolution fusion | flops 150994944 | bytes 1769472 | tf_op jit(solution)/shard_map/dot_general | solution.py:18
  16.1 0.0 copy-start.2
  16.1 0.0 copy-done.4
  16.1 0.1 reshape.17.recv_ref
  16.2 2.0 %collective-permute-done.rest_0_.refs_1_ = bf16[384,128]{1,0:T(8,128)(2,1)S(1)} collective-permute-done((bf16[384,128]{1,0:T(8,128)(2,1)}, bf16[384,128]{1,0:T(8,128)(2,1)S(1)}, u32[]{:S(2)}, u32[]{:S(2)}) %collective-permute-start) | collective-permute-done | bytes 98336 | tf_op jit(solution)/shard_map/ppermute | solution.py:132
  18.2 1.1 %collective-permute-done.2.rest_2_.refs_3_ = bf16[384,128]{1,0:T(8,128)(2,1)S(1)} collective-permute-done((bf16[384,128]{1,0:T(8,128)(2,1)S(1)}, bf16[384,128]{1,0:T(8,128)(2,1)S(1)}, u32[]{:S(2)}, u32[]{:S(2)}) %collective-permute-start.2) | collective-permute-done | bytes 98336 | tf_op jit(solution)/shard_map/ppermute | solution.py:132
  19.2 0.0 all-to-all-done
  19.2 0.0 copy-done.1
  19.2 0.0 copy-done.3
  19.2 1.4 %shard_map.95 = (bf16[128,768]{1,0:T(8,128)(2,1)}, bf16[384,128]{1,0:T(8,128)(2,1)S(1)}, bf16[384,128]{1,0:T(8,128)(2,1)S(1)}, bf16[384,128]{1,0:T(8,128)(2,1)S(1)}, bf16[384,128]{1,0:T(8,128)(2,1)S(1)}) custom-call(bf16[128,768]{1,0:T(8,128)(2,1)S(1)} %bitcast.8, s32[1,128]{1,0:T(1,128)S(1)} %reshape.17.recv_ref, f32[128,768]{1,0:T(8,128)S(1)} %fusion.self_ref, ...), custom_call_target="tpu_custom_call" | custom-call | flops 176160768 | bytes 2556416 | tf_op jit(solution)/shard_map/pallas_call | solution.py:23
  20.6 0.6 %collective-permute-start.4 = (bf16[384,128]{1,0:T(8,128)(2,1)S(1)}, bf16[384,128]{1,0:T(8,128)(2,1)S(1)}, u32[]{:S(2)}, u32[]{:S(2)}) collective-permute-start(bf16[384,128]{1,0:T(8,128)(2,1)S(1)} %get-tuple-element.24), channel_id=1, source_target_pairs={{0,4},{1,5},{2,6},{3,7},{4,0},{5,1},{6,2},{7,3},{8,12},{9,13},{10,... | collective-permute-start | bytes 294920 | tf_op jit(solution)/shard_map/ppermute | solution.py:132
  21.2 1.5 %collective-permute-start.6 = (bf16[384,128]{1,0:T(8,128)(2,1)S(1)}, bf16[384,128]{1,0:T(8,128)(2,1)S(1)}, u32[]{:S(2)}, u32[]{:S(2)}) collective-permute-start(bf16[384,128]{1,0:T(8,128)(2,1)S(1)} %get-tuple-element.26), channel_id=1, source_target_pairs={{0,2},{1,3},{2,0},{3,1},{4,6},{5,7},{6,4},{7,5},{8,10},{9,11},{10,... | collective-permute-start | bytes 294920 | tf_op jit(solution)/shard_map/ppermute | solution.py:132
  22.7 0.5 collective-permute-start.3
  23.2 1.5 %collective-permute-start.7 = (bf16[384,128]{1,0:T(8,128)(2,1)S(1)}, bf16[384,128]{1,0:T(8,128)(2,1)S(1)}, u32[]{:S(2)}, u32[]{:S(2)}) collective-permute-start(bf16[384,128]{1,0:T(8,128)(2,1)S(1)} %get-tuple-element.25.refs_8_), channel_id=1, source_target_pairs={{0,4},{1,5},{2,6},{3,7},{4,0},{5,1},{6,2},{7,3},{8,12},{9,13},{10,... | collective-permute-start | bytes 294920 | tf_op jit(solution)/shard_map/ppermute | solution.py:132
  24.7 1.1 %collective-permute-done.4.refs_6_ = bf16[384,128]{1,0:T(8,128)(2,1)S(1)} collective-permute-done((bf16[384,128]{1,0:T(8,128)(2,1)S(1)}, bf16[384,128]{1,0:T(8,128)(2,1)S(1)}, u32[]{:S(2)}, u32[]{:S(2)}) %collective-permute-start.4) | collective-permute-done | bytes 98336 | tf_op jit(solution)/shard_map/ppermute | solution.py:132
  25.8 1.6 %collective-permute-start.5 = (bf16[384,128]{1,0:T(8,128)(2,1)S(1)}, bf16[384,128]{1,0:T(8,128)(2,1)S(1)}, u32[]{:S(2)}, u32[]{:S(2)}) collective-permute-start(bf16[384,128]{1,0:T(8,128)(2,1)S(1)} %collective-permute-done.4.refs_6_), channel_id=1, source_target_pairs={{0,2},{1,3},{2,0},{3,1},{4,6},{5,7},{6,4},{7,5},{8,10},{9,11},{10,... | collective-permute-start | bytes 294920 | tf_op jit(solution)/shard_map/ppermute | solution.py:132
  27.4 0.0 collective-permute-done.6.refs_9_
  27.4 0.9 %collective-permute-start.8 = (bf16[384,128]{1,0:T(8,128)(2,1)S(1)}, bf16[384,128]{1,0:T(8,128)(2,1)S(1)}, u32[]{:S(2)}, u32[]{:S(2)}) collective-permute-start(bf16[384,128]{1,0:T(8,128)(2,1)S(1)} %collective-permute-done.6.refs_9_), channel_id=1, source_target_pairs={{0,4},{1,5},{2,6},{3,7},{4,0},{5,1},{6,2},{7,3},{8,12},{9,13},{10,... | collective-permute-start | bytes 294920 | tf_op jit(solution)/shard_map/ppermute | solution.py:132
  28.3 0.0 collective-permute-done.3.refs_5_
  28.3 0.3 collective-permute-done.7.refs_10_
  28.5 1.9 %collective-permute-done.5.refs_7_ = bf16[384,128]{1,0:T(8,128)(2,1)S(1)} collective-permute-done((bf16[384,128]{1,0:T(8,128)(2,1)S(1)}, bf16[384,128]{1,0:T(8,128)(2,1)S(1)}, u32[]{:S(2)}, u32[]{:S(2)}) %collective-permute-start.5) | collective-permute-done | bytes 98336 | tf_op jit(solution)/shard_map/ppermute | solution.py:132
  30.4 1.6 %collective-permute-done.8.refs_11_ = bf16[384,128]{1,0:T(8,128)(2,1)S(1)} collective-permute-done((bf16[384,128]{1,0:T(8,128)(2,1)S(1)}, bf16[384,128]{1,0:T(8,128)(2,1)S(1)}, u32[]{:S(2)}, u32[]{:S(2)}) %collective-permute-start.8) | collective-permute-done | bytes 98336 | tf_op jit(solution)/shard_map/ppermute | solution.py:132
  32.0 0.0 copy-done.2
  32.0 0.4 shard_map.97
  32.4 0.1 collective-permute-start.9
  32.5 0.4 shard_map.96.keep_ref
  32.8 1.2 %collective-permute-done.9.got_ref = bf16[384,384]{1,0:T(8,128)(2,1)S(1)} collective-permute-done((bf16[384,384]{1,0:T(8,128)(2,1)S(1)}, bf16[384,384]{1,0:T(8,128)(2,1)S(1)}, u32[]{:S(2)}, u32[]{:S(2)}) %collective-permute-start.9) | collective-permute-done | bytes 294944 | tf_op jit(solution)/shard_map/ppermute | solution.py:132
  34.0 0.1 shard_map.98
  34.1 0.4 collective-permute-start.10
  34.5 3.0 %collective-permute-start.11 = (bf16[96,384]{1,0:T(8,128)(2,1)S(1)}, bf16[96,384]{1,0:T(8,128)(2,1)S(1)}, u32[]{:S(2)}, u32[]{:S(2)}) collective-permute-start(bf16[96,384]{1,0:T(8,128)(2,1)S(1)} %get-tuple-element.29), channel_id=1, source_target_pairs={{0,24},{1,25},{2,26},{3,27},{4,28},{5,29},{6,30},{7,31},{8,16},{9,... | collective-permute-start | bytes 221192 | tf_op jit(solution)/shard_map/ppermute | solution.py:132
  37.6 0.1 collective-permute-start.12
  37.7 5.4 %collective-permute-done.10.refs_1_ = bf16[96,384]{1,0:T(8,128)(2,1)S(1)} collective-permute-done((bf16[96,384]{1,0:T(8,128)(2,1)S(1)}, bf16[96,384]{1,0:T(8,128)(2,1)S(1)}, u32[]{:S(2)}, u32[]{:S(2)}) %collective-permute-start.10) | collective-permute-done | bytes 73760 | tf_op jit(solution)/shard_map/ppermute | solution.py:132
  43.1 0.0 collective-permute-done.11.refs_2_
  43.1 0.5 %collective-permute-done.12.refs_3_ = bf16[96,384]{1,0:T(8,128)(2,1)S(1)} collective-permute-done((bf16[96,384]{1,0:T(8,128)(2,1)S(1)}, bf16[96,384]{1,0:T(8,128)(2,1)S(1)}, u32[]{:S(2)}, u32[]{:S(2)}) %collective-permute-start.12) | collective-permute-done | bytes 73760 | tf_op jit(solution)/shard_map/ppermute | solution.py:132
  43.7 0.8 %collective-permute-start.14 = (bf16[96,384]{1,0:T(8,128)(2,1)S(1)}, bf16[96,384]{1,0:T(8,128)(2,1)S(1)}, u32[]{:S(2)}, u32[]{:S(2)}) collective-permute-start(bf16[96,384]{1,0:T(8,128)(2,1)S(1)} %shard_map.99.refs_0_), channel_id=1, source_target_pairs={{0,2},{1,3},{2,0},{3,1},{4,6},{5,7},{6,4},{7,5},{8,10},{9,11},{10,... | collective-permute-start | bytes 221192 | tf_op jit(solution)/shard_map/ppermute | solution.py:132
  44.5 0.0 collective-permute-start.13
  44.5 3.6 %collective-permute-done.14.refs_2_ = bf16[96,384]{1,0:T(8,128)(2,1)S(1)} collective-permute-done((bf16[96,384]{1,0:T(8,128)(2,1)S(1)}, bf16[96,384]{1,0:T(8,128)(2,1)S(1)}, u32[]{:S(2)}, u32[]{:S(2)}) %collective-permute-start.14) | collective-permute-done | bytes 73760 | tf_op jit(solution)/shard_map/ppermute | solution.py:132
  48.1 0.0 collective-permute-start.15
  48.1 0.0 collective-permute-done.13.refs_1_
  48.1 1.3 %collective-permute-done.15.refs_3_ = bf16[96,384]{1,0:T(8,128)(2,1)S(1)} collective-permute-done((bf16[96,384]{1,0:T(8,128)(2,1)S(1)}, bf16[96,384]{1,0:T(8,128)(2,1)S(1)}, u32[]{:S(2)}, u32[]{:S(2)}) %collective-permute-start.15) | collective-permute-done | bytes 73760 | tf_op jit(solution)/shard_map/ppermute | solution.py:132
  49.4 0.9 %shard_map.100 = (f32[96,768]{1,0:T(8,128)}, f32[96,768]{1,0:T(8,128)}) custom-call(bf16[96,384]{1,0:T(8,128)(2,1)S(1)} %shard_map.99.refs_0_, bf16[96,384]{1,0:T(8,128)(2,1)S(1)} %collective-permute-done.13.refs_1_, bf16[96,384]{1,0:T(8,128)(2,1)S(1)} %collective-permute-done.14.refs_2_, bf16[96,384]{1,0:T(8,128)(2,1)S(1)} %collective-permute-done.15.refs_3_), custom_call_target="tpu_custom_call" | custom-call | bytes 884736 | tf_op jit(solution)/shard_map/pallas_call | solution.py:23
  (2 shorter events, 0.0 us)
Async XLA Ops:
  0.6 14.2 %copy-start = (bf16[768,768]{1,0:T(8,128)(2,1)S(1)}, bf16[768,768]{1,0:T(8,128)(2,1)}, u32[]{:S(2)}) copy-start(bf16[768,768]{1,0:T(8,128)(2,1)} %param.12) | copy-start | bytes 3538948
  2.9 13.2 %copy-start.4 = (s32[1,1,8,12]{3,2,1,0:T(8,128)S(1)}, s32[1,1,8,12]{3,2,1,0:T(8,128)}, u32[]{:S(2)}) copy-start(s32[1,1,8,12]{3,2,1,0:T(8,128)} %param.10) | copy-start | bytes 1156
  2.9 16.3 %copy-start.1 = (bf16[768,768]{1,0:T(8,128)(2,1)S(1)}, bf16[768,768]{1,0:T(8,128)(2,1)}, u32[]{:S(2)}) copy-start(bf16[768,768]{1,0:T(8,128)(2,1)} %w_ref.1) | copy-start | bytes 3538948
  2.9 16.3 %copy-start.3 = (bf16[128,768]{1,0:T(8,128)(2,1)S(1)}, bf16[128,768]{1,0:T(8,128)(2,1)}, u32[]{:S(2)}) copy-start(bf16[128,768]{1,0:T(8,128)(2,1)} %cot_ref.1) | copy-start | bytes 589828
  2.9 11.4 %collective-permute-start.1 = (bf16[384,128]{1,0:T(8,128)(2,1)}, bf16[384,128]{1,0:T(8,128)(2,1)S(1)}, u32[]{:S(2)}, u32[]{:S(2)}) collective-permute-start(bf16[384,128]{1,0:T(8,128)(2,1)} %get-tuple-element.21), channel_id=1, source_target_pairs={{0,4},{1,5},{2,6},{3,7},{4,0},{5,1},{6,2},{7,3},{8,12},{9,13},{10,... | collective-permute-start | bytes 294920 | tf_op jit(solution)/shard_map/ppermute | solution.py:132
  5.9 13.3 %all-to-all-start = ((bf16[8,16,768]{2,1,0:T(8,128)(2,1)}), bf16[8,16,768]{2,1,0:T(8,128)(2,1)S(1)}, u32[]{:S(2)}, u32[]{:S(2)}) async-start(bf16[8,16,768]{2,1,0:T(8,128)(2,1)} %bitcast.9), calls=%async_computation | async-start | bytes 393216 | tf_op jit(solution)/shard_map/all_to_all | solution.py:235
  12.8 5.4 %collective-permute-start = (bf16[384,128]{1,0:T(8,128)(2,1)}, bf16[384,128]{1,0:T(8,128)(2,1)S(1)}, u32[]{:S(2)}, u32[]{:S(2)}) collective-permute-start(bf16[384,128]{1,0:T(8,128)(2,1)} %get-tuple-element.20.refs_0_), channel_id=1, source_target_pairs={{0,2},{1,3},{2,0},{3,1},{4,6},{5,7},{6,4},{7,5},{8,10},{9,11},{10,... | collective-permute-start | bytes 294920 | tf_op jit(solution)/shard_map/ppermute | solution.py:132
  14.3 4.9 %collective-permute-start.2 = (bf16[384,128]{1,0:T(8,128)(2,1)S(1)}, bf16[384,128]{1,0:T(8,128)(2,1)S(1)}, u32[]{:S(2)}, u32[]{:S(2)}) collective-permute-start(bf16[384,128]{1,0:T(8,128)(2,1)S(1)} %collective-permute-done.1.rest_1_.refs_2_), channel_id=1, source_target_pairs={{0,2},{1,3},{2,0},{3,1},{4,6},{5,7},{6,4},{7,5},{8,10},{9,11},{10,... | collective-permute-start | bytes 294920 | tf_op jit(solution)/shard_map/ppermute | solution.py:132
  16.1 15.9 %copy-start.2 = (bf16[384,128]{1,0:T(8,128)(2,1)S(1)}, bf16[384,128]{1,0:T(8,128)(2,1)}, u32[]{:S(2)}) copy-start(bf16[384,128]{1,0:T(8,128)(2,1)} %get-tuple-element.20.refs_0_) | copy-start | bytes 294916
  20.6 5.2 %collective-permute-start.4 = (bf16[384,128]{1,0:T(8,128)(2,1)S(1)}, bf16[384,128]{1,0:T(8,128)(2,1)S(1)}, u32[]{:S(2)}, u32[]{:S(2)}) collective-permute-start(bf16[384,128]{1,0:T(8,128)(2,1)S(1)} %get-tuple-element.24), channel_id=1, source_target_pairs={{0,4},{1,5},{2,6},{3,7},{4,0},{5,1},{6,2},{7,3},{8,12},{9,13},{10,... | collective-permute-start | bytes 294920 | tf_op jit(solution)/shard_map/ppermute | solution.py:132
  21.2 6.2 %collective-permute-start.6 = (bf16[384,128]{1,0:T(8,128)(2,1)S(1)}, bf16[384,128]{1,0:T(8,128)(2,1)S(1)}, u32[]{:S(2)}, u32[]{:S(2)}) collective-permute-start(bf16[384,128]{1,0:T(8,128)(2,1)S(1)} %get-tuple-element.26), channel_id=1, source_target_pairs={{0,2},{1,3},{2,0},{3,1},{4,6},{5,7},{6,4},{7,5},{8,10},{9,11},{10,... | collective-permute-start | bytes 294920 | tf_op jit(solution)/shard_map/ppermute | solution.py:132
  22.7 5.5 %collective-permute-start.3 = (bf16[384,128]{1,0:T(8,128)(2,1)S(1)}, bf16[384,128]{1,0:T(8,128)(2,1)S(1)}, u32[]{:S(2)}, u32[]{:S(2)}) collective-permute-start(bf16[384,128]{1,0:T(8,128)(2,1)S(1)} %get-tuple-element.23.refs_4_), channel_id=1, source_target_pairs={{0,2},{1,3},{2,0},{3,1},{4,6},{5,7},{6,4},{7,5},{8,10},{9,11},{10,... | collective-permute-start | bytes 294920 | tf_op jit(solution)/shard_map/ppermute | solution.py:132
  23.2 5.3 %collective-permute-start.7 = (bf16[384,128]{1,0:T(8,128)(2,1)S(1)}, bf16[384,128]{1,0:T(8,128)(2,1)S(1)}, u32[]{:S(2)}, u32[]{:S(2)}) collective-permute-start(bf16[384,128]{1,0:T(8,128)(2,1)S(1)} %get-tuple-element.25.refs_8_), channel_id=1, source_target_pairs={{0,4},{1,5},{2,6},{3,7},{4,0},{5,1},{6,2},{7,3},{8,12},{9,13},{10,... | collective-permute-start | bytes 294920 | tf_op jit(solution)/shard_map/ppermute | solution.py:132
  25.8 4.6 %collective-permute-start.5 = (bf16[384,128]{1,0:T(8,128)(2,1)S(1)}, bf16[384,128]{1,0:T(8,128)(2,1)S(1)}, u32[]{:S(2)}, u32[]{:S(2)}) collective-permute-start(bf16[384,128]{1,0:T(8,128)(2,1)S(1)} %collective-permute-done.4.refs_6_), channel_id=1, source_target_pairs={{0,2},{1,3},{2,0},{3,1},{4,6},{5,7},{6,4},{7,5},{8,10},{9,11},{10,... | collective-permute-start | bytes 294920 | tf_op jit(solution)/shard_map/ppermute | solution.py:132
  27.4 4.6 %collective-permute-start.8 = (bf16[384,128]{1,0:T(8,128)(2,1)S(1)}, bf16[384,128]{1,0:T(8,128)(2,1)S(1)}, u32[]{:S(2)}, u32[]{:S(2)}) collective-permute-start(bf16[384,128]{1,0:T(8,128)(2,1)S(1)} %collective-permute-done.6.refs_9_), channel_id=1, source_target_pairs={{0,4},{1,5},{2,6},{3,7},{4,0},{5,1},{6,2},{7,3},{8,12},{9,13},{10,... | collective-permute-start | bytes 294920 | tf_op jit(solution)/shard_map/ppermute | solution.py:132
  32.4 1.6 %collective-permute-start.9 = (bf16[384,384]{1,0:T(8,128)(2,1)S(1)}, bf16[384,384]{1,0:T(8,128)(2,1)S(1)}, u32[]{:S(2)}, u32[]{:S(2)}) collective-permute-start(bf16[384,384]{1,0:T(8,128)(2,1)S(1)} %shard_map.97), channel_id=1, source_target_pairs={{0,1},{1,0},{2,3},{3,2},{4,5},{5,4},{6,7},{7,6},{8,9},{9,8},{10,11... | collective-permute-start | bytes 884744 | tf_op jit(solution)/shard_map/ppermute | solution.py:132
  34.1 9.0 %collective-permute-start.10 = (bf16[96,384]{1,0:T(8,128)(2,1)S(1)}, bf16[96,384]{1,0:T(8,128)(2,1)S(1)}, u32[]{:S(2)}, u32[]{:S(2)}) collective-permute-start(bf16[96,384]{1,0:T(8,128)(2,1)S(1)} %get-tuple-element.28), channel_id=1, source_target_pairs={{0,16},{1,17},{2,18},{3,19},{4,20},{5,21},{6,22},{7,23},{8,24},{9,... | collective-permute-start | bytes 221192 | tf_op jit(solution)/shard_map/ppermute | solution.py:132
  34.5 8.6 %collective-permute-start.11 = (bf16[96,384]{1,0:T(8,128)(2,1)S(1)}, bf16[96,384]{1,0:T(8,128)(2,1)S(1)}, u32[]{:S(2)}, u32[]{:S(2)}) collective-permute-start(bf16[96,384]{1,0:T(8,128)(2,1)S(1)} %get-tuple-element.29), channel_id=1, source_target_pairs={{0,24},{1,25},{2,26},{3,27},{4,28},{5,29},{6,30},{7,31},{8,16},{9,... | collective-permute-start | bytes 221192 | tf_op jit(solution)/shard_map/ppermute | solution.py:132
  37.6 6.1 %collective-permute-start.12 = (bf16[96,384]{1,0:T(8,128)(2,1)S(1)}, bf16[96,384]{1,0:T(8,128)(2,1)S(1)}, u32[]{:S(2)}, u32[]{:S(2)}) collective-permute-start(bf16[96,384]{1,0:T(8,128)(2,1)S(1)} %get-tuple-element.30), channel_id=1, source_target_pairs={{0,8},{1,9},{2,10},{3,11},{4,12},{5,13},{6,14},{7,15},{8,0},{9,1},... | collective-permute-start | bytes 221192 | tf_op jit(solution)/shard_map/ppermute | solution.py:132
  43.7 4.4 %collective-permute-start.14 = (bf16[96,384]{1,0:T(8,128)(2,1)S(1)}, bf16[96,384]{1,0:T(8,128)(2,1)S(1)}, u32[]{:S(2)}, u32[]{:S(2)}) collective-permute-start(bf16[96,384]{1,0:T(8,128)(2,1)S(1)} %shard_map.99.refs_0_), channel_id=1, source_target_pairs={{0,2},{1,3},{2,0},{3,1},{4,6},{5,7},{6,4},{7,5},{8,10},{9,11},{10,... | collective-permute-start | bytes 221192 | tf_op jit(solution)/shard_map/ppermute | solution.py:132
  44.5 3.6 %collective-permute-start.13 = (bf16[96,384]{1,0:T(8,128)(2,1)S(1)}, bf16[96,384]{1,0:T(8,128)(2,1)S(1)}, u32[]{:S(2)}, u32[]{:S(2)}) collective-permute-start(bf16[96,384]{1,0:T(8,128)(2,1)S(1)} %shard_map.99.refs_0_), channel_id=1, source_target_pairs={{0,1},{1,0},{2,3},{3,2},{4,5},{5,4},{6,7},{7,6},{8,9},{9,8},{10,11... | collective-permute-start | bytes 221192 | tf_op jit(solution)/shard_map/ppermute | solution.py:132
  48.1 1.3 %collective-permute-start.15 = (bf16[96,384]{1,0:T(8,128)(2,1)S(1)}, bf16[96,384]{1,0:T(8,128)(2,1)S(1)}, u32[]{:S(2)}, u32[]{:S(2)}) collective-permute-start(bf16[96,384]{1,0:T(8,128)(2,1)S(1)} %collective-permute-done.14.refs_2_), channel_id=1, source_target_pairs={{0,1},{1,0},{2,3},{3,2},{4,5},{5,4},{6,7},{7,6},{8,9},{9,8},{10,11... | collective-permute-start | bytes 221192 | tf_op jit(solution)/shard_map/ppermute | solution.py:132

commit v4 on v3

--- a/solution.py
+++ b/solution.py
@@ -152,21 +152,24 @@
     write_rows(plan, trans_ref, here_ref, there_ref)
 
 
-def layer_kernel(plan, cap, order, ordered, arrived_ref, recv_ref, self_ref, cot_ref, w_ref, *rest):
-    hidden_ref, mean_here, mean_there, grad_here, grad_there, trans_ref, grad_ref = rest[ordered:]
+def mean_kernel(plan, cap, order, rows_ref, recv_ref, _, mean_ref, here_ref, there_ref, trans_ref):
+    rows = jnp.concatenate(
+        [rows_ref[p * SLOT_PAD:(p + 1) * SLOT_PAD, :] for p in (order.index(s) for s in range(plan.ns))], axis=0)
+    mean = neighbor_mean(cap, rows, recv_ref[...], mean_ref.shape[0])
+    mean_ref[...] = mean
+    trans_ref[...] = mean.astype(F32).T.astype(BF16)
+    write_rows(plan, trans_ref, here_ref, there_ref)
+
+
+def layer_kernel(plan, mean_ref, self_ref, cot_ref, w_ref, hidden_ref, here_ref, there_ref, grad_ref):
     targets = self_ref.shape[0]
-    rows = jnp.concatenate(
-        [arrived_ref[p * SLOT_PAD:(p + 1) * SLOT_PAD, :] for p in (order.index(s) for s in range(plan.ns))], axis=0)
-    mean = neighbor_mean(cap, rows, recv_ref[...], targets)
-    trans_ref[...] = mean.astype(F32).T.astype(BF16)
-    write_rows(plan, trans_ref, mean_here, mean_there)
-    preact = self_ref[...] + dot(mean, w_ref[...])
+    preact = self_ref[...] + dot(mean_ref[...], w_ref[...])
     hidden, grad = forward(preact, cot_ref[...])
     hidden_ref[...] = hidden
     for b in range(grad_ref.shape[0]):
         grad_ref[b] = grad[:, b * 128:(b + 1) * 128]
     y, each = plan.place()[2], plan.cols // 128
-    for dy, out in enumerate((grad_here, grad_there)):
+    for dy, out in enumerate((here_ref, there_ref)):
         for b in range(each):
             out[b * targets:(b + 1) * targets, :] = grad_ref[(y ^ dy) * each + b]
 
@@ -251,20 +254,28 @@
     def to_y(array):
         return plan.send(array, lambda z, x, y, c: (z, x, 1 - y, c))
 
+    def to_diagonal(array):
+        return plan.send(array, lambda z, x, y, c: (z, 1 - x, 1 - y, c))
+
+    def held(array, *until):
+        return lax.optimization_barrier((array,) + until)[0]
+
     own, own_here, own_there = owns
-    own_x = to_x(own_there)
-    own_all = [own_here, to_y(own_here), own_x, to_y(own_x)]
+    own_all = [own_here, to_y(own_here), to_x(own_there), to_diagonal(own_there)]
     self_term = dot(own, w_self)
 
-    hidden, mean_here, mean_there, grad_here, grad_there = call(
-        functools.partial(layer_kernel, plan, cap, order, n - 1),
-        [shape((targets, out_width), BF16)] + [shape((rows, targets), BF16)] * 2
-        + [shape((cols // 128 * targets, 128), BF16)] * 2,
-        [arrived, recv, self_term, cotangent, w_neigh], unread=own_all[1:],
-        scratch=[pltpu.VMEM((width, targets), BF16), pltpu.VMEM((out_width // 128, targets, 128), BF16)],
-        flops=2 * targets * width * (out_width + slots))
+    mean, mean_here, mean_there = call(
+        functools.partial(mean_kernel, plan, cap, order),
+        [shape((targets, width), BF16)] + [shape((rows, targets), BF16)] * 2, [arrived, recv, self_term],
+        scratch=[pltpu.VMEM((width, targets), BF16)], flops=2 * targets * width * slots)
+    hidden, grad_here, grad_there = call(
+        functools.partial(layer_kernel, plan),
+        [shape((targets, out_width), BF16)] + [shape((cols // 128 * targets, 128), BF16)] * 2,
+        [mean, self_term, cotangent, w_neigh],
+        scratch=[pltpu.VMEM((out_width // 128, targets, 128), BF16)],
+        flops=2 * targets * width * out_width)
     mean_x, grad_y = to_x(mean_there), to_y(grad_there)
-    mean_all = [mean_here, to_y(mean_here), mean_x, to_y(mean_x)]
+    mean_all = [mean_here, to_y(mean_here), mean_x, to_y(held(mean_x, *own_all[1:]))]
     grad_all = [grad_here, grad_y, to_x(grad_here), to_x(grad_y)]
     factors = own_all + mean_all + grad_all
     (give,) = call(functools.partial(terms_kernel, plan, False), [shape((rows, cols), BF16)], factors,

time: 50.5 us -> 49.4 us (0.978)
  waiting for transfers between devices: 19.9 us -> 16.9 us
  starting transfers between devices: 22.8 us -> 24.4 us
    ppermute x16, waiting for transfers between devices: 19.9 us -> 16.9 us  [send(): return lax.ppermute(array, ('store', 'trainer'), pairs)]
    all_to_all x1, starting transfers between devices: 6.87 us -> 9.28 us  [per_device(): lax.all_to_all(sums.reshape(ns, SLOT_PAD, width), 'store', split_axis=0,...]
    ppermute x16, starting transfers between devices: 16 us -> 15.2 us  [send(): return lax.ppermute(array, ('store', 'trainer'), pairs)]
    pallas_call x7 -> x8, Pallas kernels: 5.39 us -> 5.57 us  [call(): pl.pallas_call(body, out_shape=list(outs), in_specs=[VMEM] * len(args) +...]
  transfers between devices with their start and end apart: 17 -> 17, of which waited for: 11 -> 9; matrix products, arithmetic and copies ran while one was open for 3% -> 3% of each run, Pallas kernels for 1% -> 4%
where the time goes in v4:
time: 49.4 us; the launch traced here: 49.1 us
  starting transfers between devices  24.4 us (49%)
  waiting for transfers between devices  16.9 us (34%)
  Pallas kernels  5.57 us (11%)
  matrix products  1.36 us (3%)
  between operations  0.75 us (2%)
    ppermute x16, waiting for transfers between devices, send(): return lax.ppermute(array, ('store', 'trainer'), pairs)  16.9 us
    ppermute x16, starting transfers between devices, send(): return lax.ppermute(array, ('store', 'trainer'), pairs)  15.2 us
    all_to_all x1, starting transfers between devices, per_device(): lax.all_to_all(sums.reshape(ns, SLOT_PAD, width), 'store', split_axis=0,...  9.28 us
    pallas_call x8, Pallas kernels, call(): pl.pallas_call(body, out_shape=list(outs), in_specs=[VMEM] * len(args) +...  5.57 us
    dot_general x1, matrix products, dot(): return jnp.dot(a, b, preferred_element_type=F32)  1.36 us
  transfers between devices with their start and end apart: 17, of which 9 were waited for; matrix products, arithmetic and copies ran while one was open for 3% of the time, Pallas kernels for 4%

profile of v4, /device:TPU:0, one launch (start us, length us, event | category | flops | bytes accessed | tf_op | source)
XLA Modules:
  0.0 49.1 jit_solution(2903828684150451922)
XLA Ops:
  0.6 0.0 copy-start
  0.6 0.0 copy-start.4
  0.7 2.2 %shard_map.94 = (bf16[128,768]{1,0:T(8,128)(2,1)}, bf16[128,768]{1,0:T(8,128)(2,1)}, bf16[384,128]{1,0:T(8,128)(2,1)}, bf16[384,128]{1,0:T(8,128)(2,1)}) custom-call(f32[128,768]{1,0:T(8,128)} %feat_hbm.1, s32[8,2,12]{2,1,0:T(2,128)} %bitcast.10, f32[128,768]{1,0:T(8,128)} %rest_0_.1), custom_call_target="tpu_custom_call" | custom-call | flops 50331648 | bytes 589824 | tf_op jit(solution)/shard_map/pallas_call | solution.py:23
  2.9 9.3 %all-to-all-start = ((bf16[8,16,768]{2,1,0:T(8,128)(2,1)}), bf16[8,16,768]{2,1,0:T(8,128)(2,1)S(1)}, u32[]{:S(2)}, u32[]{:S(2)}) async-start(bf16[8,16,768]{2,1,0:T(8,128)(2,1)} %bitcast.9), calls=%async_computation | async-start | bytes 393216 | tf_op jit(solution)/shard_map/all_to_all | solution.py:238
  12.2 1.5 %collective-permute-start.2 = (bf16[384,128]{1,0:T(8,128)(2,1)}, bf16[384,128]{1,0:T(8,128)(2,1)S(1)}, u32[]{:S(2)}, u32[]{:S(2)}) collective-permute-start(bf16[384,128]{1,0:T(8,128)(2,1)} %get-tuple-element.25), channel_id=1, source_target_pairs={{0,6},{1,7},{2,4},{3,5},{4,2},{5,3},{6,0},{7,1},{8,14},{9,15},{10,... | collective-permute-start | bytes 294920 | tf_op jit(solution)/shard_map/ppermute | solution.py:132
  13.7 1.4 %collective-permute-start.1 = (bf16[384,128]{1,0:T(8,128)(2,1)}, bf16[384,128]{1,0:T(8,128)(2,1)S(1)}, u32[]{:S(2)}, u32[]{:S(2)}) collective-permute-start(bf16[384,128]{1,0:T(8,128)(2,1)} %get-tuple-element.25), channel_id=1, source_target_pairs={{0,4},{1,5},{2,6},{3,7},{4,0},{5,1},{6,2},{7,3},{8,12},{9,13},{10,... | collective-permute-start | bytes 294920 | tf_op jit(solution)/shard_map/ppermute | solution.py:132
  15.2 0.5 %collective-permute-start = (bf16[384,128]{1,0:T(8,128)(2,1)}, bf16[384,128]{1,0:T(8,128)(2,1)S(1)}, u32[]{:S(2)}, u32[]{:S(2)}) collective-permute-start(bf16[384,128]{1,0:T(8,128)(2,1)} %get-tuple-element.24.refs_0_), channel_id=1, source_target_pairs={{0,2},{1,3},{2,0},{3,1},{4,6},{5,7},{6,4},{7,5},{8,10},{9,11},{10,... | collective-permute-start | bytes 294920 | tf_op jit(solution)/shard_map/ppermute | solution.py:132
  15.7 0.0 copy-done.4
  15.7 0.1 reshape.17.recv_ref
  15.7 0.0 copy-done
  15.8 0.0 copy-start.1
  15.8 0.0 copy-start.3
  15.8 1.4 %fusion._.self_ref = f32[128,768]{1,0:T(8,128)S(1)} fusion(bf16[128,768]{1,0:T(8,128)(2,1)} %get-tuple-element.21, bf16[768,768]{1,0:T(8,128)(2,1)S(1)} %copy-done), kind=kOutput, calls=%fused_computation | convolution fusion | flops 150994944 | bytes 1769472 | tf_op jit(solution)/shard_map/dot_general | solution.py:18
  17.1 0.0 all-to-all-done
  17.1 0.0 copy-start.2
  17.2 0.5 %shard_map.95 = (bf16[128,768]{1,0:T(8,128)(2,1)S(1)}, bf16[384,128]{1,0:T(8,128)(2,1)S(1)}, bf16[384,128]{1,0:T(8,128)(2,1)S(1)}) custom-call(bf16[128,768]{1,0:T(8,128)(2,1)S(1)} %bitcast.8, s32[1,128]{1,0:T(1,128)S(1)} %reshape.17.recv_ref, f32[128,768]{1,0:T(8,128)S(1)} %fusion._.self_ref), custom_call_target="tpu_custom_call" | custom-call | flops 25165824 | bytes 983552 | tf_op jit(solution)/shard_map/pallas_call | solution.py:23
  17.7 1.7 %collective-permute-start.4 = (bf16[384,128]{1,0:T(8,128)(2,1)S(1)}, bf16[384,128]{1,0:T(8,128)(2,1)S(1)}, u32[]{:S(2)}, u32[]{:S(2)}) collective-permute-start(bf16[384,128]{1,0:T(8,128)(2,1)S(1)} %get-tuple-element.27), channel_id=1, source_target_pairs={{0,4},{1,5},{2,6},{3,7},{4,0},{5,1},{6,2},{7,3},{8,12},{9,13},{10,... | collective-permute-start | bytes 294920 | tf_op jit(solution)/shard_map/ppermute | solution.py:132
  19.3 0.0 copy-done.1
  19.3 0.0 copy-done.3
  19.4 1.1 %shard_map.96 = (bf16[128,768]{1,0:T(8,128)(2,1)}, bf16[384,128]{1,0:T(8,128)(2,1)S(1)}, bf16[384,128]{1,0:T(8,128)(2,1)S(1)}) custom-call(bf16[128,768]{1,0:T(8,128)(2,1)S(1)} %get-tuple-element.22.mean_ref, f32[128,768]{1,0:T(8,128)S(1)} %fusion._.self_ref, bf16[128,768]{1,0:T(8,128)(2,1)S(1)} %copy-done.3, bf16[768,768]{1,0:T(8,128)(2,1)S(1)} %copy-done.1), custom_call_target="tpu_custom_call" | custom-call | flops 150994944 | bytes 2359296 | tf_op jit(solution)/shard_map/pallas_call | solution.py:23
  20.4 1.5 %collective-permute-start.6 = (bf16[384,128]{1,0:T(8,128)(2,1)S(1)}, bf16[384,128]{1,0:T(8,128)(2,1)S(1)}, u32[]{:S(2)}, u32[]{:S(2)}) collective-permute-start(bf16[384,128]{1,0:T(8,128)(2,1)S(1)} %get-tuple-element.30), channel_id=1, source_target_pairs={{0,2},{1,3},{2,0},{3,1},{4,6},{5,7},{6,4},{7,5},{8,10},{9,11},{10,... | collective-permute-start | bytes 294920 | tf_op jit(solution)/shard_map/ppermute | solution.py:132
  21.9 0.0 collective-permute-done.2.refs_3_
  21.9 0.4 collective-permute-start.7
  22.4 0.0 collective-permute-done.1.refs_2_
  22.4 0.5 %collective-permute-start.3 = (bf16[384,128]{1,0:T(8,128)(2,1)S(1)}, bf16[384,128]{1,0:T(8,128)(2,1)S(1)}, u32[]{:S(2)}, u32[]{:S(2)}) collective-permute-start(bf16[384,128]{1,0:T(8,128)(2,1)S(1)} %get-tuple-element.26.refs_4_), channel_id=1, source_target_pairs={{0,2},{1,3},{2,0},{3,1},{4,6},{5,7},{6,4},{7,5},{8,10},{9,11},{10,... | collective-permute-start | bytes 294920 | tf_op jit(solution)/shard_map/ppermute | solution.py:132
  22.9 0.0 collective-permute-done.refs_1_
  22.9 0.0 collective-permute-done.4.refs_6_
  22.9 2.6 %collective-permute-done.6.refs_9_ = bf16[384,128]{1,0:T(8,128)(2,1)S(1)} collective-permute-done((bf16[384,128]{1,0:T(8,128)(2,1)S(1)}, bf16[384,128]{1,0:T(8,128)(2,1)S(1)}, u32[]{:S(2)}, u32[]{:S(2)}) %collective-permute-start.6) | collective-permute-done | bytes 98336 | tf_op jit(solution)/shard_map/ppermute | solution.py:132
  25.4 0.5 %collective-permute-start.8 = (bf16[384,128]{1,0:T(8,128)(2,1)S(1)}, bf16[384,128]{1,0:T(8,128)(2,1)S(1)}, u32[]{:S(2)}, u32[]{:S(2)}) collective-permute-start(bf16[384,128]{1,0:T(8,128)(2,1)S(1)} %collective-permute-done.6.refs_9_), channel_id=1, source_target_pairs={{0,4},{1,5},{2,6},{3,7},{4,0},{5,1},{6,2},{7,3},{8,12},{9,13},{10,... | collective-permute-start | bytes 294920 | tf_op jit(solution)/shard_map/ppermute | solution.py:132
  25.9 1.7 %collective-permute-start.5 = (bf16[384,128]{1,0:T(8,128)(2,1)S(1)}, bf16[384,128]{1,0:T(8,128)(2,1)S(1)}, u32[]{:S(2)}, u32[]{:S(2)}) collective-permute-start(bf16[384,128]{1,0:T(8,128)(2,1)S(1)} %collective-permute-done.4.refs_6_), channel_id=1, source_target_pairs={{0,2},{1,3},{2,0},{3,1},{4,6},{5,7},{6,4},{7,5},{8,10},{9,11},{10,... | collective-permute-start | bytes 294920 | tf_op jit(solution)/shard_map/ppermute | solution.py:132
  27.6 0.0 collective-permute-done.7.refs_10_
  27.6 0.3 collective-permute-done.3.refs_5_
  27.9 2.1 %collective-permute-done.8.refs_11_ = bf16[384,128]{1,0:T(8,128)(2,1)S(1)} collective-permute-done((bf16[384,128]{1,0:T(8,128)(2,1)S(1)}, bf16[384,128]{1,0:T(8,128)(2,1)S(1)}, u32[]{:S(2)}, u32[]{:S(2)}) %collective-permute-start.8) | collective-permute-done | bytes 98336 | tf_op jit(solution)/shard_map/ppermute | solution.py:132
  30.1 0.5 %collective-permute-done.5.refs_7_ = bf16[384,128]{1,0:T(8,128)(2,1)S(1)} collective-permute-done((bf16[384,128]{1,0:T(8,128)(2,1)S(1)}, bf16[384,128]{1,0:T(8,128)(2,1)S(1)}, u32[]{:S(2)}, u32[]{:S(2)}) %collective-permute-start.5) | collective-permute-done | bytes 98336 | tf_op jit(solution)/shard_map/ppermute | solution.py:132
  30.6 0.0 copy-done.2
  30.6 0.4 shard_map.98
  30.9 0.1 collective-permute-start.9
  31.0 0.4 shard_map.97.keep_ref
  31.4 1.2 %collective-permute-done.9.got_ref = bf16[384,384]{1,0:T(8,128)(2,1)S(1)} collective-permute-done((bf16[384,384]{1,0:T(8,128)(2,1)S(1)}, bf16[384,384]{1,0:T(8,128)(2,1)S(1)}, u32[]{:S(2)}, u32[]{:S(2)}) %collective-permute-start.9) | collective-permute-done | bytes 294944 | tf_op jit(solution)/shard_map/ppermute | solution.py:132
  32.6 0.1 shard_map.99
  32.7 1.7 %collective-permute-start.10 = (bf16[96,384]{1,0:T(8,128)(2,1)S(1)}, bf16[96,384]{1,0:T(8,128)(2,1)S(1)}, u32[]{:S(2)}, u32[]{:S(2)}) collective-permute-start(bf16[96,384]{1,0:T(8,128)(2,1)S(1)} %get-tuple-element.32), channel_id=1, source_target_pairs={{0,16},{1,17},{2,18},{3,19},{4,20},{5,21},{6,22},{7,23},{8,24},{9,... | collective-permute-start | bytes 221192 | tf_op jit(solution)/shard_map/ppermute | solution.py:132
  34.4 1.6 %collective-permute-start.11 = (bf16[96,384]{1,0:T(8,128)(2,1)S(1)}, bf16[96,384]{1,0:T(8,128)(2,1)S(1)}, u32[]{:S(2)}, u32[]{:S(2)}) collective-permute-start(bf16[96,384]{1,0:T(8,128)(2,1)S(1)} %get-tuple-element.33), channel_id=1, source_target_pairs={{0,24},{1,25},{2,26},{3,27},{4,28},{5,29},{6,30},{7,31},{8,16},{9,... | collective-permute-start | bytes 221192 | tf_op jit(solution)/shard_map/ppermute | solution.py:132
  36.0 0.2 collective-permute-start.12
  36.2 5.3 %collective-permute-done.10.refs_1_ = bf16[96,384]{1,0:T(8,128)(2,1)S(1)} collective-permute-done((bf16[96,384]{1,0:T(8,128)(2,1)S(1)}, bf16[96,384]{1,0:T(8,128)(2,1)S(1)}, u32[]{:S(2)}, u32[]{:S(2)}) %collective-permute-start.10) | collective-permute-done | bytes 73760 | tf_op jit(solution)/shard_map/ppermute | solution.py:132
  41.6 0.0 collective-permute-done.11.refs_2_
  41.6 0.9 %collective-permute-done.12.refs_3_ = bf16[96,384]{1,0:T(8,128)(2,1)S(1)} collective-permute-done((bf16[96,384]{1,0:T(8,128)(2,1)S(1)}, bf16[96,384]{1,0:T(8,128)(2,1)S(1)}, u32[]{:S(2)}, u32[]{:S(2)}) %collective-permute-start.12) | collective-permute-done | bytes 73760 | tf_op jit(solution)/shard_map/ppermute | solution.py:132
  42.5 1.7 %collective-permute-start.14 = (bf16[96,384]{1,0:T(8,128)(2,1)S(1)}, bf16[96,384]{1,0:T(8,128)(2,1)S(1)}, u32[]{:S(2)}, u32[]{:S(2)}) collective-permute-start(bf16[96,384]{1,0:T(8,128)(2,1)S(1)} %shard_map.100.refs_0_), channel_id=1, source_target_pairs={{0,2},{1,3},{2,0},{3,1},{4,6},{5,7},{6,4},{7,5},{8,10},{9,11},{10,... | collective-permute-start | bytes 221192 | tf_op jit(solution)/shard_map/ppermute | solution.py:132
  44.3 0.0 collective-permute-start.13
  44.3 2.7 %collective-permute-done.14.refs_2_ = bf16[96,384]{1,0:T(8,128)(2,1)S(1)} collective-permute-done((bf16[96,384]{1,0:T(8,128)(2,1)S(1)}, bf16[96,384]{1,0:T(8,128)(2,1)S(1)}, u32[]{:S(2)}, u32[]{:S(2)}) %collective-permute-start.14) | collective-permute-done | bytes 73760 | tf_op jit(solution)/shard_map/ppermute | solution.py:132
  47.0 0.0 collective-permute-start.15
  47.0 0.0 collective-permute-done.13.refs_1_
  47.0 1.3 %collective-permute-done.15.refs_3_ = bf16[96,384]{1,0:T(8,128)(2,1)S(1)} collective-permute-done((bf16[96,384]{1,0:T(8,128)(2,1)S(1)}, bf16[96,384]{1,0:T(8,128)(2,1)S(1)}, u32[]{:S(2)}, u32[]{:S(2)}) %collective-permute-start.15) | collective-permute-done | bytes 73760 | tf_op jit(solution)/shard_map/ppermute | solution.py:132
  48.2 0.9 %shard_map.101 = (f32[96,768]{1,0:T(8,128)}, f32[96,768]{1,0:T(8,128)}) custom-call(bf16[96,384]{1,0:T(8,128)(2,1)S(1)} %shard_map.100.refs_0_, bf16[96,384]{1,0:T(8,128)(2,1)S(1)} %collective-permute-done.13.refs_1_, bf16[96,384]{1,0:T(8,128)(2,1)S(1)} %collective-permute-done.14.refs_2_, bf16[96,384]{1,0:T(8,128)(2,1)S(1)} %collective-permute-done.15.refs_3_), custom_call_target="tpu_custom_call" | custom-call | bytes 884736 | tf_op jit(solution)/shard_map/pallas_call | solution.py:23
  (2 shorter events, 0.0 us)
Async XLA Ops:
  0.6 15.1 %copy-start = (bf16[768,768]{1,0:T(8,128)(2,1)S(1)}, bf16[768,768]{1,0:T(8,128)(2,1)}, u32[]{:S(2)}) copy-start(bf16[768,768]{1,0:T(8,128)(2,1)} %param.12) | copy-start | bytes 3538948
  0.6 15.0 %copy-start.4 = (s32[1,1,8,12]{3,2,1,0:T(8,128)S(1)}, s32[1,1,8,12]{3,2,1,0:T(8,128)}, u32[]{:S(2)}) copy-start(s32[1,1,8,12]{3,2,1,0:T(8,128)} %param.10) | copy-start | bytes 1156
  2.9 14.2 %all-to-all-start = ((bf16[8,16,768]{2,1,0:T(8,128)(2,1)}), bf16[8,16,768]{2,1,0:T(8,128)(2,1)S(1)}, u32[]{:S(2)}, u32[]{:S(2)}) async-start(bf16[8,16,768]{2,1,0:T(8,128)(2,1)} %bitcast.9), calls=%async_computation | async-start | bytes 393216 | tf_op jit(solution)/shard_map/all_to_all | solution.py:238
  12.2 9.8 %collective-permute-start.2 = (bf16[384,128]{1,0:T(8,128)(2,1)}, bf16[384,128]{1,0:T(8,128)(2,1)S(1)}, u32[]{:S(2)}, u32[]{:S(2)}) collective-permute-start(bf16[384,128]{1,0:T(8,128)(2,1)} %get-tuple-element.25), channel_id=1, source_target_pairs={{0,6},{1,7},{2,4},{3,5},{4,2},{5,3},{6,0},{7,1},{8,14},{9,15},{10,... | collective-permute-start | bytes 294920 | tf_op jit(solution)/shard_map/ppermute | solution.py:132
  13.7 8.7 %collective-permute-start.1 = (bf16[384,128]{1,0:T(8,128)(2,1)}, bf16[384,128]{1,0:T(8,128)(2,1)S(1)}, u32[]{:S(2)}, u32[]{:S(2)}) collective-permute-start(bf16[384,128]{1,0:T(8,128)(2,1)} %get-tuple-element.25), channel_id=1, source_target_pairs={{0,4},{1,5},{2,6},{3,7},{4,0},{5,1},{6,2},{7,3},{8,12},{9,13},{10,... | collective-permute-start | bytes 294920 | tf_op jit(solution)/shard_map/ppermute | solution.py:132
  15.2 7.7 %collective-permute-start = (bf16[384,128]{1,0:T(8,128)(2,1)}, bf16[384,128]{1,0:T(8,128)(2,1)S(1)}, u32[]{:S(2)}, u32[]{:S(2)}) collective-permute-start(bf16[384,128]{1,0:T(8,128)(2,1)} %get-tuple-element.24.refs_0_), channel_id=1, source_target_pairs={{0,2},{1,3},{2,0},{3,1},{4,6},{5,7},{6,4},{7,5},{8,10},{9,11},{10,... | collective-permute-start | bytes 294920 | tf_op jit(solution)/shard_map/ppermute | solution.py:132
  15.8 3.6 %copy-start.1 = (bf16[768,768]{1,0:T(8,128)(2,1)S(1)}, bf16[768,768]{1,0:T(8,128)(2,1)}, u32[]{:S(2)}) copy-start(bf16[768,768]{1,0:T(8,128)(2,1)} %w_ref.1) | copy-start | bytes 3538948
  15.8 3.6 %copy-start.3 = (bf16[128,768]{1,0:T(8,128)(2,1)S(1)}, bf16[128,768]{1,0:T(8,128)(2,1)}, u32[]{:S(2)}) copy-start(bf16[128,768]{1,0:T(8,128)(2,1)} %cot_ref.1) | copy-start | bytes 589828
  17.1 13.4 %copy-start.2 = (bf16[384,128]{1,0:T(8,128)(2,1)S(1)}, bf16[384,128]{1,0:T(8,128)(2,1)}, u32[]{:S(2)}) copy-start(bf16[384,128]{1,0:T(8,128)(2,1)} %get-tuple-element.24.refs_0_) | copy-start | bytes 294916
  17.7 5.2 %collective-permute-start.4 = (bf16[384,128]{1,0:T(8,128)(2,1)S(1)}, bf16[384,128]{1,0:T(8,128)(2,1)S(1)}, u32[]{:S(2)}, u32[]{:S(2)}) collective-permute-start(bf16[384,128]{1,0:T(8,128)(2,1)S(1)} %get-tuple-element.27), channel_id=1, source_target_pairs={{0,4},{1,5},{2,6},{3,7},{4,0},{5,1},{6,2},{7,3},{8,12},{9,13},{10,... | collective-permute-start | bytes 294920 | tf_op jit(solution)/shard_map/ppermute | solution.py:132
  20.4 5.0 %collective-permute-start.6 = (bf16[384,128]{1,0:T(8,128)(2,1)S(1)}, bf16[384,128]{1,0:T(8,128)(2,1)S(1)}, u32[]{:S(2)}, u32[]{:S(2)}) collective-permute-start(bf16[384,128]{1,0:T(8,128)(2,1)S(1)} %get-tuple-element.30), channel_id=1, source_target_pairs={{0,2},{1,3},{2,0},{3,1},{4,6},{5,7},{6,4},{7,5},{8,10},{9,11},{10,... | collective-permute-start | bytes 294920 | tf_op jit(solution)/shard_map/ppermute | solution.py:132
  21.9 5.7 %collective-permute-start.7 = (bf16[384,128]{1,0:T(8,128)(2,1)S(1)}, bf16[384,128]{1,0:T(8,128)(2,1)S(1)}, u32[]{:S(2)}, u32[]{:S(2)}) collective-permute-start(bf16[384,128]{1,0:T(8,128)(2,1)S(1)} %get-tuple-element.29.refs_8_), channel_id=1, source_target_pairs={{0,4},{1,5},{2,6},{3,7},{4,0},{5,1},{6,2},{7,3},{8,12},{9,13},{10,... | collective-permute-start | bytes 294920 | tf_op jit(solution)/shard_map/ppermute | solution.py:132
  22.4 5.6 %collective-permute-start.3 = (bf16[384,128]{1,0:T(8,128)(2,1)S(1)}, bf16[384,128]{1,0:T(8,128)(2,1)S(1)}, u32[]{:S(2)}, u32[]{:S(2)}) collective-permute-start(bf16[384,128]{1,0:T(8,128)(2,1)S(1)} %get-tuple-element.26.refs_4_), channel_id=1, source_target_pairs={{0,2},{1,3},{2,0},{3,1},{4,6},{5,7},{6,4},{7,5},{8,10},{9,11},{10,... | collective-permute-start | bytes 294920 | tf_op jit(solution)/shard_map/ppermute | solution.py:132
  25.4 4.6 %collective-permute-start.8 = (bf16[384,128]{1,0:T(8,128)(2,1)S(1)}, bf16[384,128]{1,0:T(8,128)(2,1)S(1)}, u32[]{:S(2)}, u32[]{:S(2)}) collective-permute-start(bf16[384,128]{1,0:T(8,128)(2,1)S(1)} %collective-permute-done.6.refs_9_), channel_id=1, source_target_pairs={{0,4},{1,5},{2,6},{3,7},{4,0},{5,1},{6,2},{7,3},{8,12},{9,13},{10,... | collective-permute-start | bytes 294920 | tf_op jit(solution)/shard_map/ppermute | solution.py:132
  25.9 4.6 %collective-permute-start.5 = (bf16[384,128]{1,0:T(8,128)(2,1)S(1)}, bf16[384,128]{1,0:T(8,128)(2,1)S(1)}, u32[]{:S(2)}, u32[]{:S(2)}) collective-permute-start(bf16[384,128]{1,0:T(8,128)(2,1)S(1)} %collective-permute-done.4.refs_6_), channel_id=1, source_target_pairs={{0,2},{1,3},{2,0},{3,1},{4,6},{5,7},{6,4},{7,5},{8,10},{9,11},{10,... | collective-permute-start | bytes 294920 | tf_op jit(solution)/shard_map/ppermute | solution.py:132
  30.9 1.6 %collective-permute-start.9 = (bf16[384,384]{1,0:T(8,128)(2,1)S(1)}, bf16[384,384]{1,0:T(8,128)(2,1)S(1)}, u32[]{:S(2)}, u32[]{:S(2)}) collective-permute-start(bf16[384,384]{1,0:T(8,128)(2,1)S(1)} %shard_map.98), channel_id=1, source_target_pairs={{0,1},{1,0},{2,3},{3,2},{4,5},{5,4},{6,7},{7,6},{8,9},{9,8},{10,11... | collective-permute-start | bytes 884744 | tf_op jit(solution)/shard_map/ppermute | solution.py:132
  32.7 8.9 %collective-permute-start.10 = (bf16[96,384]{1,0:T(8,128)(2,1)S(1)}, bf16[96,384]{1,0:T(8,128)(2,1)S(1)}, u32[]{:S(2)}, u32[]{:S(2)}) collective-permute-start(bf16[96,384]{1,0:T(8,128)(2,1)S(1)} %get-tuple-element.32), channel_id=1, source_target_pairs={{0,16},{1,17},{2,18},{3,19},{4,20},{5,21},{6,22},{7,23},{8,24},{9,... | collective-permute-start | bytes 221192 | tf_op jit(solution)/shard_map/ppermute | solution.py:132
  34.4 7.2 %collective-permute-start.11 = (bf16[96,384]{1,0:T(8,128)(2,1)S(1)}, bf16[96,384]{1,0:T(8,128)(2,1)S(1)}, u32[]{:S(2)}, u32[]{:S(2)}) collective-permute-start(bf16[96,384]{1,0:T(8,128)(2,1)S(1)} %get-tuple-element.33), channel_id=1, source_target_pairs={{0,24},{1,25},{2,26},{3,27},{4,28},{5,29},{6,30},{7,31},{8,16},{9,... | collective-permute-start | bytes 221192 | tf_op jit(solution)/shard_map/ppermute | solution.py:132
  36.0 6.5 %collective-permute-start.12 = (bf16[96,384]{1,0:T(8,128)(2,1)S(1)}, bf16[96,384]{1,0:T(8,128)(2,1)S(1)}, u32[]{:S(2)}, u32[]{:S(2)}) collective-permute-start(bf16[96,384]{1,0:T(8,128)(2,1)S(1)} %get-tuple-element.34), channel_id=1, source_target_pairs={{0,8},{1,9},{2,10},{3,11},{4,12},{5,13},{6,14},{7,15},{8,0},{9,1},... | collective-permute-start | bytes 221192 | tf_op jit(solution)/shard_map/ppermute | solution.py:132
  42.5 4.4 %collective-permute-start.14 = (bf16[96,384]{1,0:T(8,128)(2,1)S(1)}, bf16[96,384]{1,0:T(8,128)(2,1)S(1)}, u32[]{:S(2)}, u32[]{:S(2)}) collective-permute-start(bf16[96,384]{1,0:T(8,128)(2,1)S(1)} %shard_map.100.refs_0_), channel_id=1, source_target_pairs={{0,2},{1,3},{2,0},{3,1},{4,6},{5,7},{6,4},{7,5},{8,10},{9,11},{10,... | collective-permute-start | bytes 221192 | tf_op jit(solution)/shard_map/ppermute | solution.py:132
  44.3 2.7 %collective-permute-start.13 = (bf16[96,384]{1,0:T(8,128)(2,1)S(1)}, bf16[96,384]{1,0:T(8,128)(2,1)S(1)}, u32[]{:S(2)}, u32[]{:S(2)}) collective-permute-start(bf16[96,384]{1,0:T(8,128)(2,1)S(1)} %shard_map.100.refs_0_), channel_id=1, source_target_pairs={{0,1},{1,0},{2,3},{3,2},{4,5},{5,4},{6,7},{7,6},{8,9},{9,8},{10,11... | collective-permute-start | bytes 221192 | tf_op jit(solution)/shard_map/ppermute | solution.py:132
  47.0 1.3 %collective-permute-start.15 = (bf16[96,384]{1,0:T(8,128)(2,1)S(1)}, bf16[96,384]{1,0:T(8,128)(2,1)S(1)}, u32[]{:S(2)}, u32[]{:S(2)}) collective-permute-start(bf16[96,384]{1,0:T(8,128)(2,1)S(1)} %collective-permute-done.14.refs_2_), channel_id=1, source_target_pairs={{0,1},{1,0},{2,3},{3,2},{4,5},{5,4},{6,7},{7,6},{8,9},{9,8},{10,11... | collective-permute-start | bytes 221192 | tf_op jit(solution)/shard_map/ppermute | solution.py:132

commit v5 on v4

--- a/solution.py
+++ b/solution.py
@@ -174,16 +174,24 @@
             out[b * targets:(b + 1) * targets, :] = grad_ref[(y ^ dy) * each + b]
 
 
-def terms_kernel(plan, keep, *refs):
+def left_kernel(plan, *refs):
     n = len(plan.peers)
-    own, mean, grad, out_ref = refs[:n], refs[n:2 * n], refs[2 * n:3 * n], refs[3 * n]
+    own, mean, (give_ref, keep_ref) = refs[:n], refs[n:2 * n], refs[2 * n:]
     targets = own[0].shape[1]
-    use_own = plan.place()[3] == (0 if keep else 1)
-    left = jnp.concatenate([jnp.where(use_own, o[...], m[...]) for o, m in zip(own, mean)], axis=1)
+    keep_own = plan.place()[3] == 0
+    for i, (o, m) in enumerate(zip(own, mean)):
+        at = slice(i * targets, (i + 1) * targets)
+        keep_ref[:, at] = jnp.where(keep_own, o[...], m[...])
+        give_ref[:, at] = jnp.where(keep_own, m[...], o[...])
+
+
+def terms_kernel(plan, left_ref, *refs):
+    grad, out_ref = refs[:-1], refs[-1]
+    targets = left_ref.shape[1] // len(grad)
     right = jnp.concatenate(
         [jnp.concatenate([g[b * targets:(b + 1) * targets, :] for b in range(plan.cols // 128)], axis=1)
          for g in grad], axis=0)
-    out_ref[...] = dot(left, right).astype(out_ref.dtype)
+    out_ref[...] = dot(left_ref[...], right).astype(out_ref.dtype)
 
 
 def core_sum_kernel(plan, keep_ref, got_ref, *rest):
@@ -277,10 +285,11 @@
     mean_x, grad_y = to_x(mean_there), to_y(grad_there)
     mean_all = [mean_here, to_y(mean_here), mean_x, to_y(held(mean_x, *own_all[1:]))]
     grad_all = [grad_here, grad_y, to_x(grad_here), to_x(grad_y)]
-    factors = own_all + mean_all + grad_all
-    (give,) = call(functools.partial(terms_kernel, plan, False), [shape((rows, cols), BF16)], factors,
+    give_left, keep_left = call(functools.partial(left_kernel, plan), [shape((rows, n * targets), BF16)] * 2,
+                                own_all + mean_all)
+    (give,) = call(functools.partial(terms_kernel, plan), [shape((rows, cols), BF16)], [give_left] + grad_all,
                    flops=2 * rows * cols * targets * n)
-    (keep,) = call(functools.partial(terms_kernel, plan, True), [shape((rows, cols), F32)], factors,
+    (keep,) = call(functools.partial(terms_kernel, plan), [shape((rows, cols), F32)], [keep_left] + grad_all,
                    flops=2 * rows * cols * targets * n)
     got = plan.send(give, lambda z, x, y, c: (z, x, y, 1 - c))
     block = (plan.shard, cols)

time: 49.4 us -> 49.4 us (level)
  waiting for transfers between devices: 16.9 us -> 16.1 us
  starting transfers between devices: 24.4 us -> 25 us
    ppermute x16, waiting for transfers between devices: 16.9 us -> 16.1 us  [send(): return lax.ppermute(array, ('store', 'trainer'), pairs)]
    ppermute x16, starting transfers between devices: 15.2 us -> 15.7 us  [send(): return lax.ppermute(array, ('store', 'trainer'), pairs)]
    pallas_call x8 -> x9, Pallas kernels: 5.57 us -> 5.73 us  [call(): pl.pallas_call(body, out_shape=list(outs), in_specs=[VMEM] * len(args) +...]
where the time goes in v5:
time: 49.4 us; the launch traced here: 49.1 us
  starting transfers between devices  25 us (51%)
  waiting for transfers between devices  16.1 us (33%)
  Pallas kernels  5.73 us (12%)
  matrix products  1.36 us (3%)
  between operations  0.76 us (2%)
    ppermute x16, waiting for transfers between devices, send(): return lax.ppermute(array, ('store', 'trainer'), pairs)  16.1 us
    ppermute x16, starting transfers between devices, send(): return lax.ppermute(array, ('store', 'trainer'), pairs)  15.7 us
    all_to_all x1, starting transfers between devices, per_device(): lax.all_to_all(sums.reshape(ns, SLOT_PAD, width), 'store', split_axis=0,...  9.28 us
    pallas_call x9, Pallas kernels, call(): pl.pallas_call(body, out_shape=list(outs), in_specs=[VMEM] * len(args) +...  5.73 us
    dot_general x1, matrix products, dot(): return jnp.dot(a, b, preferred_element_type=F32)  1.36 us
  transfers between devices with their start and end apart: 17, of which 9 were waited for; matrix products, arithmetic and copies ran while one was open for 3% of the time, Pallas kernels for 4%

profile of v5, /device:TPU:0, one launch (start us, length us, event | category | flops | bytes accessed | tf_op | source)
XLA Modules:
  0.0 49.1 jit_solution(11259601954448001356)
XLA Ops:
  0.6 0.0 copy-start
  0.6 0.0 copy-start.4
  0.7 2.2 %shard_map.94 = (bf16[128,768]{1,0:T(8,128)(2,1)}, bf16[128,768]{1,0:T(8,128)(2,1)}, bf16[384,128]{1,0:T(8,128)(2,1)}, bf16[384,128]{1,0:T(8,128)(2,1)}) custom-call(f32[128,768]{1,0:T(8,128)} %feat_hbm.1, s32[8,2,12]{2,1,0:T(2,128)} %bitcast.10, f32[128,768]{1,0:T(8,128)} %rest_0_.1), custom_call_target="tpu_custom_call" | custom-call | flops 50331648 | bytes 589824 | tf_op jit(solution)/shard_map/pallas_call | solution.py:23
  2.9 9.3 %all-to-all-start = ((bf16[8,16,768]{2,1,0:T(8,128)(2,1)}), bf16[8,16,768]{2,1,0:T(8,128)(2,1)S(1)}, u32[]{:S(2)}, u32[]{:S(2)}) async-start(bf16[8,16,768]{2,1,0:T(8,128)(2,1)} %bitcast.9), calls=%async_computation | async-start | bytes 393216 | tf_op jit(solution)/shard_map/all_to_all | solution.py:246
  12.2 0.6 %collective-permute-start.1 = (bf16[384,128]{1,0:T(8,128)(2,1)}, bf16[384,128]{1,0:T(8,128)(2,1)S(1)}, u32[]{:S(2)}, u32[]{:S(2)}) collective-permute-start(bf16[384,128]{1,0:T(8,128)(2,1)} %get-tuple-element.27), channel_id=1, source_target_pairs={{0,4},{1,5},{2,6},{3,7},{4,0},{5,1},{6,2},{7,3},{8,12},{9,13},{10,... | collective-permute-start | bytes 294920 | tf_op jit(solution)/shard_map/ppermute | solution.py:132
  12.8 2.4 %collective-permute-start.2 = (bf16[384,128]{1,0:T(8,128)(2,1)}, bf16[384,128]{1,0:T(8,128)(2,1)S(1)}, u32[]{:S(2)}, u32[]{:S(2)}) collective-permute-start(bf16[384,128]{1,0:T(8,128)(2,1)} %get-tuple-element.27), channel_id=1, source_target_pairs={{0,6},{1,7},{2,4},{3,5},{4,2},{5,3},{6,0},{7,1},{8,14},{9,15},{10,... | collective-permute-start | bytes 294920 | tf_op jit(solution)/shard_map/ppermute | solution.py:132
  15.2 0.5 %collective-permute-start = (bf16[384,128]{1,0:T(8,128)(2,1)}, bf16[384,128]{1,0:T(8,128)(2,1)S(1)}, u32[]{:S(2)}, u32[]{:S(2)}) collective-permute-start(bf16[384,128]{1,0:T(8,128)(2,1)} %get-tuple-element.26.refs_0_), channel_id=1, source_target_pairs={{0,2},{1,3},{2,0},{3,1},{4,6},{5,7},{6,4},{7,5},{8,10},{9,11},{10,... | collective-permute-start | bytes 294920 | tf_op jit(solution)/shard_map/ppermute | solution.py:132
  15.7 0.0 copy-done.4
  15.7 0.1 reshape.17.recv_ref
  15.8 0.0 copy-done
  15.8 0.0 copy-start.1
  15.8 0.0 copy-start.2
  15.8 1.4 %fusion._.self_ref = f32[128,768]{1,0:T(8,128)S(1)} fusion(bf16[128,768]{1,0:T(8,128)(2,1)} %get-tuple-element.23, bf16[768,768]{1,0:T(8,128)(2,1)S(1)} %copy-done), kind=kOutput, calls=%fused_computation | convolution fusion | flops 150994944 | bytes 1769472 | tf_op jit(solution)/shard_map/dot_general | solution.py:18
  17.2 0.0 all-to-all-done
  17.2 0.0 copy-start.3
  17.2 0.5 %shard_map.95 = (bf16[128,768]{1,0:T(8,128)(2,1)S(1)}, bf16[384,128]{1,0:T(8,128)(2,1)S(1)}, bf16[384,128]{1,0:T(8,128)(2,1)S(1)}) custom-call(bf16[128,768]{1,0:T(8,128)(2,1)S(1)} %bitcast.8, s32[1,128]{1,0:T(1,128)S(1)} %reshape.17.recv_ref, f32[128,768]{1,0:T(8,128)S(1)} %fusion._.self_ref), custom_call_target="tpu_custom_call" | custom-call | flops 25165824 | bytes 983552 | tf_op jit(solution)/shard_map/pallas_call | solution.py:23
  17.7 1.7 %collective-permute-start.4 = (bf16[384,128]{1,0:T(8,128)(2,1)S(1)}, bf16[384,128]{1,0:T(8,128)(2,1)S(1)}, u32[]{:S(2)}, u32[]{:S(2)}) collective-permute-start(bf16[384,128]{1,0:T(8,128)(2,1)S(1)} %get-tuple-element.29), channel_id=1, source_target_pairs={{0,4},{1,5},{2,6},{3,7},{4,0},{5,1},{6,2},{7,3},{8,12},{9,13},{10,... | collective-permute-start | bytes 294920 | tf_op jit(solution)/shard_map/ppermute | solution.py:132
  19.4 0.0 copy-done.1
  19.4 0.0 copy-done.2
  19.4 1.1 %shard_map.96 = (bf16[128,768]{1,0:T(8,128)(2,1)}, bf16[384,128]{1,0:T(8,128)(2,1)S(1)}, bf16[384,128]{1,0:T(8,128)(2,1)S(1)}) custom-call(bf16[128,768]{1,0:T(8,128)(2,1)S(1)} %get-tuple-element.24.mean_ref, f32[128,768]{1,0:T(8,128)S(1)} %fusion._.self_ref, bf16[128,768]{1,0:T(8,128)(2,1)S(1)} %copy-done.2, bf16[768,768]{1,0:T(8,128)(2,1)S(1)} %copy-done.1), custom_call_target="tpu_custom_call" | custom-call | flops 150994944 | bytes 2359296 | tf_op jit(solution)/shard_map/pallas_call | solution.py:23
  20.4 1.5 %collective-permute-start.6 = (bf16[384,128]{1,0:T(8,128)(2,1)S(1)}, bf16[384,128]{1,0:T(8,128)(2,1)S(1)}, u32[]{:S(2)}, u32[]{:S(2)}) collective-permute-start(bf16[384,128]{1,0:T(8,128)(2,1)S(1)} %get-tuple-element.33), channel_id=1, source_target_pairs={{0,2},{1,3},{2,0},{3,1},{4,6},{5,7},{6,4},{7,5},{8,10},{9,11},{10,... | collective-permute-start | bytes 294920 | tf_op jit(solution)/shard_map/ppermute | solution.py:132
  21.9 0.0 collective-permute-done.refs_1_
  21.9 0.5 %collective-permute-start.3 = (bf16[384,128]{1,0:T(8,128)(2,1)S(1)}, bf16[384,128]{1,0:T(8,128)(2,1)S(1)}, u32[]{:S(2)}, u32[]{:S(2)}) collective-permute-start(bf16[384,128]{1,0:T(8,128)(2,1)S(1)} %get-tuple-element.28.refs_4_), channel_id=1, source_target_pairs={{0,2},{1,3},{2,0},{3,1},{4,6},{5,7},{6,4},{7,5},{8,10},{9,11},{10,... | collective-permute-start | bytes 294920 | tf_op jit(solution)/shard_map/ppermute | solution.py:132
  22.5 0.0 collective-permute-done.1.refs_2_
  22.5 0.0 collective-permute-done.2.refs_3_
  22.5 0.0 collective-permute-done.4.refs_6_
  22.5 1.6 %collective-permute-start.5 = (bf16[384,128]{1,0:T(8,128)(2,1)S(1)}, bf16[384,128]{1,0:T(8,128)(2,1)S(1)}, u32[]{:S(2)}, u32[]{:S(2)}) collective-permute-start(bf16[384,128]{1,0:T(8,128)(2,1)S(1)} %collective-permute-done.4.refs_6_), channel_id=1, source_target_pairs={{0,2},{1,3},{2,0},{3,1},{4,6},{5,7},{6,4},{7,5},{8,10},{9,11},{10,... | collective-permute-start | bytes 294920 | tf_op jit(solution)/shard_map/ppermute | solution.py:132
  24.1 1.4 %collective-permute-start.7 = (bf16[384,128]{1,0:T(8,128)(2,1)S(1)}, bf16[384,128]{1,0:T(8,128)(2,1)S(1)}, u32[]{:S(2)}, u32[]{:S(2)}) collective-permute-start(bf16[384,128]{1,0:T(8,128)(2,1)S(1)} %get-tuple-element.32.refs_0_), channel_id=1, source_target_pairs={{0,4},{1,5},{2,6},{3,7},{4,0},{5,1},{6,2},{7,3},{8,12},{9,13},{10,... | collective-permute-start | bytes 294920 | tf_op jit(solution)/shard_map/ppermute | solution.py:132
  25.5 0.5 %collective-permute-done.6.refs_1_ = bf16[384,128]{1,0:T(8,128)(2,1)S(1)} collective-permute-done((bf16[384,128]{1,0:T(8,128)(2,1)S(1)}, bf16[384,128]{1,0:T(8,128)(2,1)S(1)}, u32[]{:S(2)}, u32[]{:S(2)}) %collective-permute-start.6) | collective-permute-done | bytes 98336 | tf_op jit(solution)/shard_map/ppermute | solution.py:132
  26.1 0.4 collective-permute-start.8
  26.4 1.1 %collective-permute-done.3.refs_5_ = bf16[384,128]{1,0:T(8,128)(2,1)S(1)} collective-permute-done((bf16[384,128]{1,0:T(8,128)(2,1)S(1)}, bf16[384,128]{1,0:T(8,128)(2,1)S(1)}, u32[]{:S(2)}, u32[]{:S(2)}) %collective-permute-start.3) | collective-permute-done | bytes 98336 | tf_op jit(solution)/shard_map/ppermute | solution.py:132
  27.5 1.1 %collective-permute-done.5.refs_7_ = bf16[384,128]{1,0:T(8,128)(2,1)S(1)} collective-permute-done((bf16[384,128]{1,0:T(8,128)(2,1)S(1)}, bf16[384,128]{1,0:T(8,128)(2,1)S(1)}, u32[]{:S(2)}, u32[]{:S(2)}) %collective-permute-start.5) | collective-permute-done | bytes 98336 | tf_op jit(solution)/shard_map/ppermute | solution.py:132
  28.5 0.0 copy-done.3
  28.5 0.2 shard_map.97
  28.7 0.0 collective-permute-done.7.refs_2_
  28.7 1.9 %collective-permute-done.8.refs_3_ = bf16[384,128]{1,0:T(8,128)(2,1)S(1)} collective-permute-done((bf16[384,128]{1,0:T(8,128)(2,1)S(1)}, bf16[384,128]{1,0:T(8,128)(2,1)S(1)}, u32[]{:S(2)}, u32[]{:S(2)}) %collective-permute-start.8) | collective-permute-done | bytes 98336 | tf_op jit(solution)/shard_map/ppermute | solution.py:132
  30.7 0.4 shard_map.99
  31.0 0.1 collective-permute-start.9
  31.1 0.4 shard_map.98.keep_ref
  31.5 1.2 %collective-permute-done.9.got_ref = bf16[384,384]{1,0:T(8,128)(2,1)S(1)} collective-permute-done((bf16[384,384]{1,0:T(8,128)(2,1)S(1)}, bf16[384,384]{1,0:T(8,128)(2,1)S(1)}, u32[]{:S(2)}, u32[]{:S(2)}) %collective-permute-start.9) | collective-permute-done | bytes 294944 | tf_op jit(solution)/shard_map/ppermute | solution.py:132
  32.7 0.1 shard_map.100
  32.8 0.9 %collective-permute-start.10 = (bf16[96,384]{1,0:T(8,128)(2,1)S(1)}, bf16[96,384]{1,0:T(8,128)(2,1)S(1)}, u32[]{:S(2)}, u32[]{:S(2)}) collective-permute-start(bf16[96,384]{1,0:T(8,128)(2,1)S(1)} %get-tuple-element.36), channel_id=1, source_target_pairs={{0,16},{1,17},{2,18},{3,19},{4,20},{5,21},{6,22},{7,23},{8,24},{9,... | collective-permute-start | bytes 221192 | tf_op jit(solution)/shard_map/ppermute | solution.py:132
  33.7 2.4 %collective-permute-start.11 = (bf16[96,384]{1,0:T(8,128)(2,1)S(1)}, bf16[96,384]{1,0:T(8,128)(2,1)S(1)}, u32[]{:S(2)}, u32[]{:S(2)}) collective-permute-start(bf16[96,384]{1,0:T(8,128)(2,1)S(1)} %get-tuple-element.37), channel_id=1, source_target_pairs={{0,24},{1,25},{2,26},{3,27},{4,28},{5,29},{6,30},{7,31},{8,16},{9,... | collective-permute-start | bytes 221192 | tf_op jit(solution)/shard_map/ppermute | solution.py:132
  36.0 0.3 collective-permute-start.12
  36.3 5.3 %collective-permute-done.10.refs_1_ = bf16[96,384]{1,0:T(8,128)(2,1)S(1)} collective-permute-done((bf16[96,384]{1,0:T(8,128)(2,1)S(1)}, bf16[96,384]{1,0:T(8,128)(2,1)S(1)}, u32[]{:S(2)}, u32[]{:S(2)}) %collective-permute-start.10) | collective-permute-done | bytes 73760 | tf_op jit(solution)/shard_map/ppermute | solution.py:132
  41.6 0.0 collective-permute-done.11.refs_2_
  41.6 0.9 %collective-permute-done.12.refs_3_ = bf16[96,384]{1,0:T(8,128)(2,1)S(1)} collective-permute-done((bf16[96,384]{1,0:T(8,128)(2,1)S(1)}, bf16[96,384]{1,0:T(8,128)(2,1)S(1)}, u32[]{:S(2)}, u32[]{:S(2)}) %collective-permute-start.12) | collective-permute-done | bytes 73760 | tf_op jit(solution)/shard_map/ppermute | solution.py:132
  42.5 1.5 %collective-permute-start.14 = (bf16[96,384]{1,0:T(8,128)(2,1)S(1)}, bf16[96,384]{1,0:T(8,128)(2,1)S(1)}, u32[]{:S(2)}, u32[]{:S(2)}) collective-permute-start(bf16[96,384]{1,0:T(8,128)(2,1)S(1)} %shard_map.101.refs_0_), channel_id=1, source_target_pairs={{0,2},{1,3},{2,0},{3,1},{4,6},{5,7},{6,4},{7,5},{8,10},{9,11},{10,... | collective-permute-start | bytes 221192 | tf_op jit(solution)/shard_map/ppermute | solution.py:132
  44.0 0.0 collective-permute-start.13
  44.0 2.9 %collective-permute-done.14.refs_2_ = bf16[96,384]{1,0:T(8,128)(2,1)S(1)} collective-permute-done((bf16[96,384]{1,0:T(8,128)(2,1)S(1)}, bf16[96,384]{1,0:T(8,128)(2,1)S(1)}, u32[]{:S(2)}, u32[]{:S(2)}) %collective-permute-start.14) | collective-permute-done | bytes 73760 | tf_op jit(solution)/shard_map/ppermute | solution.py:132
  46.9 0.0 collective-permute-start.15
  46.9 0.0 collective-permute-done.13.refs_1_
  47.0 1.3 %collective-permute-done.15.refs_3_ = bf16[96,384]{1,0:T(8,128)(2,1)S(1)} collective-permute-done((bf16[96,384]{1,0:T(8,128)(2,1)S(1)}, bf16[96,384]{1,0:T(8,128)(2,1)S(1)}, u32[]{:S(2)}, u32[]{:S(2)}) %collective-permute-start.15) | collective-permute-done | bytes 73760 | tf_op jit(solution)/shard_map/ppermute | solution.py:132
  48.2 0.9 %shard_map.102 = (f32[96,768]{1,0:T(8,128)}, f32[96,768]{1,0:T(8,128)}) custom-call(bf16[96,384]{1,0:T(8,128)(2,1)S(1)} %shard_map.101.refs_0_, bf16[96,384]{1,0:T(8,128)(2,1)S(1)} %collective-permute-done.13.refs_1_, bf16[96,384]{1,0:T(8,128)(2,1)S(1)} %collective-permute-done.14.refs_2_, bf16[96,384]{1,0:T(8,128)(2,1)S(1)} %collective-permute-done.15.refs_3_), custom_call_target="tpu_custom_call" | custom-call | bytes 884736 | tf_op jit(solution)/shard_map/pallas_call | solution.py:23
  (2 shorter events, 0.0 us)
Async XLA Ops:
  0.6 15.1 %copy-start = (bf16[768,768]{1,0:T(8,128)(2,1)S(1)}, bf16[768,768]{1,0:T(8,128)(2,1)}, u32[]{:S(2)}) copy-start(bf16[768,768]{1,0:T(8,128)(2,1)} %param.12) | copy-start | bytes 3538948
  0.6 15.0 %copy-start.4 = (s32[1,1,8,12]{3,2,1,0:T(8,128)S(1)}, s32[1,1,8,12]{3,2,1,0:T(8,128)}, u32[]{:S(2)}) copy-start(s32[1,1,8,12]{3,2,1,0:T(8,128)} %param.10) | copy-start | bytes 1156
  2.9 14.2 %all-to-all-start = ((bf16[8,16,768]{2,1,0:T(8,128)(2,1)}), bf16[8,16,768]{2,1,0:T(8,128)(2,1)S(1)}, u32[]{:S(2)}, u32[]{:S(2)}) async-start(bf16[8,16,768]{2,1,0:T(8,128)(2,1)} %bitcast.9), calls=%async_computation | async-start | bytes 393216 | tf_op jit(solution)/shard_map/all_to_all | solution.py:246
  12.2 10.3 %collective-permute-start.1 = (bf16[384,128]{1,0:T(8,128)(2,1)}, bf16[384,128]{1,0:T(8,128)(2,1)S(1)}, u32[]{:S(2)}, u32[]{:S(2)}) collective-permute-start(bf16[384,128]{1,0:T(8,128)(2,1)} %get-tuple-element.27), channel_id=1, source_target_pairs={{0,4},{1,5},{2,6},{3,7},{4,0},{5,1},{6,2},{7,3},{8,12},{9,13},{10,... | collective-permute-start | bytes 294920 | tf_op jit(solution)/shard_map/ppermute | solution.py:132
  12.8 9.7 %collective-permute-start.2 = (bf16[384,128]{1,0:T(8,128)(2,1)}, bf16[384,128]{1,0:T(8,128)(2,1)S(1)}, u32[]{:S(2)}, u32[]{:S(2)}) collective-permute-start(bf16[384,128]{1,0:T(8,128)(2,1)} %get-tuple-element.27), channel_id=1, source_target_pairs={{0,6},{1,7},{2,4},{3,5},{4,2},{5,3},{6,0},{7,1},{8,14},{9,15},{10,... | collective-permute-start | bytes 294920 | tf_op jit(solution)/shard_map/ppermute | solution.py:132
  15.2 6.8 %collective-permute-start = (bf16[384,128]{1,0:T(8,128)(2,1)}, bf16[384,128]{1,0:T(8,128)(2,1)S(1)}, u32[]{:S(2)}, u32[]{:S(2)}) collective-permute-start(bf16[384,128]{1,0:T(8,128)(2,1)} %get-tuple-element.26.refs_0_), channel_id=1, source_target_pairs={{0,2},{1,3},{2,0},{3,1},{4,6},{5,7},{6,4},{7,5},{8,10},{9,11},{10,... | collective-permute-start | bytes 294920 | tf_op jit(solution)/shard_map/ppermute | solution.py:132
  15.8 3.6 %copy-start.1 = (bf16[768,768]{1,0:T(8,128)(2,1)S(1)}, bf16[768,768]{1,0:T(8,128)(2,1)}, u32[]{:S(2)}) copy-start(bf16[768,768]{1,0:T(8,128)(2,1)} %w_ref.1) | copy-start | bytes 3538948
  15.8 3.6 %copy-start.2 = (bf16[128,768]{1,0:T(8,128)(2,1)S(1)}, bf16[128,768]{1,0:T(8,128)(2,1)}, u32[]{:S(2)}) copy-start(bf16[128,768]{1,0:T(8,128)(2,1)} %cot_ref.1) | copy-start | bytes 589828
  17.2 11.4 %copy-start.3 = (bf16[384,128]{1,0:T(8,128)(2,1)S(1)}, bf16[384,128]{1,0:T(8,128)(2,1)}, u32[]{:S(2)}) copy-start(bf16[384,128]{1,0:T(8,128)(2,1)} %get-tuple-element.26.refs_0_) | copy-start | bytes 294916
  17.7 4.8 %collective-permute-start.4 = (bf16[384,128]{1,0:T(8,128)(2,1)S(1)}, bf16[384,128]{1,0:T(8,128)(2,1)S(1)}, u32[]{:S(2)}, u32[]{:S(2)}) collective-permute-start(bf16[384,128]{1,0:T(8,128)(2,1)S(1)} %get-tuple-element.29), channel_id=1, source_target_pairs={{0,4},{1,5},{2,6},{3,7},{4,0},{5,1},{6,2},{7,3},{8,12},{9,13},{10,... | collective-permute-start | bytes 294920 | tf_op jit(solution)/shard_map/ppermute | solution.py:132
  20.4 5.6 %collective-permute-start.6 = (bf16[384,128]{1,0:T(8,128)(2,1)S(1)}, bf16[384,128]{1,0:T(8,128)(2,1)S(1)}, u32[]{:S(2)}, u32[]{:S(2)}) collective-permute-start(bf16[384,128]{1,0:T(8,128)(2,1)S(1)} %get-tuple-element.33), channel_id=1, source_target_pairs={{0,2},{1,3},{2,0},{3,1},{4,6},{5,7},{6,4},{7,5},{8,10},{9,11},{10,... | collective-permute-start | bytes 294920 | tf_op jit(solution)/shard_map/ppermute | solution.py:132
  21.9 5.5 %collective-permute-start.3 = (bf16[384,128]{1,0:T(8,128)(2,1)S(1)}, bf16[384,128]{1,0:T(8,128)(2,1)S(1)}, u32[]{:S(2)}, u32[]{:S(2)}) collective-permute-start(bf16[384,128]{1,0:T(8,128)(2,1)S(1)} %get-tuple-element.28.refs_4_), channel_id=1, source_target_pairs={{0,2},{1,3},{2,0},{3,1},{4,6},{5,7},{6,4},{7,5},{8,10},{9,11},{10,... | collective-permute-start | bytes 294920 | tf_op jit(solution)/shard_map/ppermute | solution.py:132
  22.5 6.1 %collective-permute-start.5 = (bf16[384,128]{1,0:T(8,128)(2,1)S(1)}, bf16[384,128]{1,0:T(8,128)(2,1)S(1)}, u32[]{:S(2)}, u32[]{:S(2)}) collective-permute-start(bf16[384,128]{1,0:T(8,128)(2,1)S(1)} %collective-permute-done.4.refs_6_), channel_id=1, source_target_pairs={{0,2},{1,3},{2,0},{3,1},{4,6},{5,7},{6,4},{7,5},{8,10},{9,11},{10,... | collective-permute-start | bytes 294920 | tf_op jit(solution)/shard_map/ppermute | solution.py:132
  24.1 4.7 %collective-permute-start.7 = (bf16[384,128]{1,0:T(8,128)(2,1)S(1)}, bf16[384,128]{1,0:T(8,128)(2,1)S(1)}, u32[]{:S(2)}, u32[]{:S(2)}) collective-permute-start(bf16[384,128]{1,0:T(8,128)(2,1)S(1)} %get-tuple-element.32.refs_0_), channel_id=1, source_target_pairs={{0,4},{1,5},{2,6},{3,7},{4,0},{5,1},{6,2},{7,3},{8,12},{9,13},{10,... | collective-permute-start | bytes 294920 | tf_op jit(solution)/shard_map/ppermute | solution.py:132
  26.1 4.6 %collective-permute-start.8 = (bf16[384,128]{1,0:T(8,128)(2,1)S(1)}, bf16[384,128]{1,0:T(8,128)(2,1)S(1)}, u32[]{:S(2)}, u32[]{:S(2)}) collective-permute-start(bf16[384,128]{1,0:T(8,128)(2,1)S(1)} %collective-permute-done.6.refs_1_), channel_id=1, source_target_pairs={{0,4},{1,5},{2,6},{3,7},{4,0},{5,1},{6,2},{7,3},{8,12},{9,13},{10,... | collective-permute-start | bytes 294920 | tf_op jit(solution)/shard_map/ppermute | solution.py:132
  31.0 1.6 %collective-permute-start.9 = (bf16[384,384]{1,0:T(8,128)(2,1)S(1)}, bf16[384,384]{1,0:T(8,128)(2,1)S(1)}, u32[]{:S(2)}, u32[]{:S(2)}) collective-permute-start(bf16[384,384]{1,0:T(8,128)(2,1)S(1)} %shard_map.99), channel_id=1, source_target_pairs={{0,1},{1,0},{2,3},{3,2},{4,5},{5,4},{6,7},{7,6},{8,9},{9,8},{10,11... | collective-permute-start | bytes 884744 | tf_op jit(solution)/shard_map/ppermute | solution.py:132
  32.8 8.8 %collective-permute-start.10 = (bf16[96,384]{1,0:T(8,128)(2,1)S(1)}, bf16[96,384]{1,0:T(8,128)(2,1)S(1)}, u32[]{:S(2)}, u32[]{:S(2)}) collective-permute-start(bf16[96,384]{1,0:T(8,128)(2,1)S(1)} %get-tuple-element.36), channel_id=1, source_target_pairs={{0,16},{1,17},{2,18},{3,19},{4,20},{5,21},{6,22},{7,23},{8,24},{9,... | collective-permute-start | bytes 221192 | tf_op jit(solution)/shard_map/ppermute | solution.py:132
  33.7 7.9 %collective-permute-start.11 = (bf16[96,384]{1,0:T(8,128)(2,1)S(1)}, bf16[96,384]{1,0:T(8,128)(2,1)S(1)}, u32[]{:S(2)}, u32[]{:S(2)}) collective-permute-start(bf16[96,384]{1,0:T(8,128)(2,1)S(1)} %get-tuple-element.37), channel_id=1, source_target_pairs={{0,24},{1,25},{2,26},{3,27},{4,28},{5,29},{6,30},{7,31},{8,16},{9,... | collective-permute-start | bytes 221192 | tf_op jit(solution)/shard_map/ppermute | solution.py:132
  36.0 6.5 %collective-permute-start.12 = (bf16[96,384]{1,0:T(8,128)(2,1)S(1)}, bf16[96,384]{1,0:T(8,128)(2,1)S(1)}, u32[]{:S(2)}, u32[]{:S(2)}) collective-permute-start(bf16[96,384]{1,0:T(8,128)(2,1)S(1)} %get-tuple-element.38), channel_id=1, source_target_pairs={{0,8},{1,9},{2,10},{3,11},{4,12},{5,13},{6,14},{7,15},{8,0},{9,1},... | collective-permute-start | bytes 221192 | tf_op jit(solution)/shard_map/ppermute | solution.py:132
  42.5 4.4 %collective-permute-start.14 = (bf16[96,384]{1,0:T(8,128)(2,1)S(1)}, bf16[96,384]{1,0:T(8,128)(2,1)S(1)}, u32[]{:S(2)}, u32[]{:S(2)}) collective-permute-start(bf16[96,384]{1,0:T(8,128)(2,1)S(1)} %shard_map.101.refs_0_), channel_id=1, source_target_pairs={{0,2},{1,3},{2,0},{3,1},{4,6},{5,7},{6,4},{7,5},{8,10},{9,11},{10,... | collective-permute-start | bytes 221192 | tf_op jit(solution)/shard_map/ppermute | solution.py:132
  44.0 2.9 %collective-permute-start.13 = (bf16[96,384]{1,0:T(8,128)(2,1)S(1)}, bf16[96,384]{1,0:T(8,128)(2,1)S(1)}, u32[]{:S(2)}, u32[]{:S(2)}) collective-permute-start(bf16[96,384]{1,0:T(8,128)(2,1)S(1)} %shard_map.101.refs_0_), channel_id=1, source_target_pairs={{0,1},{1,0},{2,3},{3,2},{4,5},{5,4},{6,7},{7,6},{8,9},{9,8},{10,11... | collective-permute-start | bytes 221192 | tf_op jit(solution)/shard_map/ppermute | solution.py:132
  46.9 1.3 %collective-permute-start.15 = (bf16[96,384]{1,0:T(8,128)(2,1)S(1)}, bf16[96,384]{1,0:T(8,128)(2,1)S(1)}, u32[]{:S(2)}, u32[]{:S(2)}) collective-permute-start(bf16[96,384]{1,0:T(8,128)(2,1)S(1)} %collective-permute-done.14.refs_2_), channel_id=1, source_target_pairs={{0,1},{1,0},{2,3},{3,2},{4,5},{5,4},{6,7},{7,6},{8,9},{9,8},{10,11... | collective-permute-start | bytes 221192 | tf_op jit(solution)/shard_map/ppermute | solution.py:132

commit v6 on v5

--- a/solution.py
+++ b/solution.py
@@ -33,6 +33,38 @@
 
 def shape(dims, kind):
     return jax.ShapeDtypeStruct(dims, kind)
+
+
+def pack_rows(cap, width):
+    return cap * (width // 128) + 8
+
+
+def pack(sums, counts, cap):
+    blocks = sums.shape[1] // 128
+    out = []
+    for d in range(sums.shape[0] // SLOT_PAD):
+        at = d * SLOT_PAD
+        part = [sums[at:at + SLOT_PAD, j * 128:(j + 1) * 128] for j in range(blocks)]
+        out += [p[:8] for p in part]
+        out += [jnp.concatenate([part[j][8:cap], part[j + 1][8:cap]], axis=0) for j in range(0, blocks, 2)]
+        out.append(counts[at + 8:at + SLOT_PAD])
+    return jnp.concatenate(out, axis=0).astype(BF16)
+
+
+def unpack(packed, order, cap, blocks):
+    size = packed.shape[0] // len(order)
+    rows = []
+    for s in range(len(order)):
+        at = order.index(s) * size
+        part = packed[at:at + size, :].astype(F32)
+        tail, counts = part[blocks * 8:size - 8], part[size - 8:]
+        columns = []
+        for j in range(blocks):
+            low = tail[j // 2 * 8 + j % 2 * 4:j // 2 * 8 + j % 2 * 4 + 4]
+            rest = counts[4:] if j == 0 else jnp.zeros((4, 128), F32)
+            columns.append(jnp.concatenate([part[j * 8:j * 8 + 8], low, rest], axis=0))
+        rows.append(jnp.concatenate(columns, axis=1))
+    return jnp.concatenate(rows, axis=0).astype(BF16)
 
 
 def slot_sums_kernel(plan, order, feat_hbm, edge_hbm, *rest):
@@ -73,8 +105,7 @@
     high = feat.astype(BF16)
     low = (feat - high.astype(F32)).astype(BF16)
     sums = dot(pick, high) + dot(pick, low)
-    out_ref[:, :128] = (sums[:, :128] + counts).astype(BF16)
-    out_ref[:, 128:] = sums[:, 128:].astype(BF16)
+    out_ref[...] = pack(sums, counts, cap)
     if with_own:
         copies[2].wait()
         write_own(plan, self_ref, *own_refs, trans_ref)
@@ -117,11 +148,17 @@
     def fits(self):
         pow2 = all((n & (n - 1)) == 0 for n in (self.ns, self.nt))
         return (pow2 and self.ns <= 8 and self.gx == 2 and self.gy == 2 and self.gy * self.gc == self.nt and self.cols % 128 == 0
-                and self.shard % 16 == 0 and len(self.peers) <= 4 and self.nz <= 4)
+                and self.shard % 16 == 0 and len(self.peers) <= 4 and self.nz == 4)
 
     def place(self):
         s, t = lax.axis_index("store"), lax.axis_index("trainer")
         return s // self.gx, s % self.gx, t // self.gc, t % self.gc
+
+    def far(self):
+        return list(range(2, self.nz))
+
+    def near(self):
+        return list(range(min(2, self.nz)))[::-1]
 
     def send(self, array, to):
         pairs = []
@@ -153,9 +190,11 @@
 
 
 def mean_kernel(plan, cap, order, rows_ref, recv_ref, _, mean_ref, here_ref, there_ref, trans_ref):
-    rows = jnp.concatenate(
-        [rows_ref[p * SLOT_PAD:(p + 1) * SLOT_PAD, :] for p in (order.index(s) for s in range(plan.ns))], axis=0)
-    mean = neighbor_mean(cap, rows, recv_ref[...], mean_ref.shape[0])
+    rows = unpack(rows_ref[...], order, cap, mean_ref.shape[1] // 128)
+    targets = mean_ref.shape[0]
+    fill = jnp.full((1, SLOT_PAD - cap), targets, jnp.int32)
+    recv = jnp.concatenate([p for s in range(plan.ns) for p in (recv_ref[s:s + 1, :], fill)], axis=1)
+    mean = neighbor_mean(cap, rows, recv, targets)
     mean_ref[...] = mean
     trans_ref[...] = mean.astype(F32).T.astype(BF16)
     write_rows(plan, trans_ref, here_ref, there_ref)
@@ -165,7 +204,7 @@
     targets = self_ref.shape[0]
     preact = self_ref[...] + dot(mean_ref[...], w_ref[...])
     hidden, grad = forward(preact, cot_ref[...])
-    hidden_ref[...] = hidden
+    hidden_ref[...] = hidden.astype(F32)
     for b in range(grad_ref.shape[0]):
         grad_ref[b] = grad[:, b * 128:(b + 1) * 128]
     y, each = plan.place()[2], plan.cols // 128
@@ -176,31 +215,33 @@
 
 def left_kernel(plan, *refs):
     n = len(plan.peers)
-    own, mean, (give_ref, keep_ref) = refs[:n], refs[n:2 * n], refs[2 * n:]
+    own, mean, outs = refs[n - 1::-1], refs[n:2 * n], refs[2 * n:]
     targets = own[0].shape[1]
-    keep_own = plan.place()[3] == 0
+    z, _, _, c = plan.place()
+    keep_own = c == 0
     for i, (o, m) in enumerate(zip(own, mean)):
         at = slice(i * targets, (i + 1) * targets)
-        keep_ref[:, at] = jnp.where(keep_own, o[...], m[...])
-        give_ref[:, at] = jnp.where(keep_own, m[...], o[...])
-
-
-def terms_kernel(plan, left_ref, *refs):
+        for j, shards in enumerate((plan.far(), plan.near())):
+            for r, k in enumerate(shards):
+                rows = pl.ds(pl.multiple_of((z ^ k) * plan.shard, 16), plan.shard)
+                to = slice(r * plan.shard, (r + 1) * plan.shard)
+                outs[j][to, at] = jnp.where(keep_own, m[rows, :], o[rows, :])
+                outs[2 + j][to, at] = jnp.where(keep_own, o[rows, :], m[rows, :])
+
+
+def terms_kernel(left_ref, *refs):
     grad, out_ref = refs[:-1], refs[-1]
     targets = left_ref.shape[1] // len(grad)
     right = jnp.concatenate(
-        [jnp.concatenate([g[b * targets:(b + 1) * targets, :] for b in range(plan.cols // 128)], axis=1)
+        [jnp.concatenate([g[b * targets:(b + 1) * targets, :] for b in range(grad[0].shape[0] // targets)], axis=1)
          for g in grad], axis=0)
     out_ref[...] = dot(left_ref[...], right).astype(out_ref.dtype)
 
 
-def core_sum_kernel(plan, keep_ref, got_ref, *rest):
-    outs, total_ref = rest[:-1], rest[-1]
-    total_ref[...] = keep_ref[...] + got_ref[...].astype(F32)
-    z = plan.place()[0]
-    for k, out in enumerate(outs):
-        start = pl.multiple_of((z ^ k) * plan.shard, 16)
-        out[...] = total_ref[pl.ds(start, plan.shard), :].astype(out.dtype)
+def core_sum_kernel(plan, keep_ref, got_ref, *outs):
+    for r, out in enumerate(outs):
+        at = slice(r * plan.shard, (r + 1) * plan.shard)
+        out[...] = (keep_ref[at, :] + got_ref[at, :].astype(F32)).astype(out.dtype)
 
 
 def store_sum_kernel(*refs):
@@ -227,15 +268,13 @@
     ns, cap, mult = edge_row.shape[2:]
     slots = ns * SLOT_PAD
     edges = edge_row[0, 0].transpose(0, 2, 1)
-    pad = ((0, 0), (0, SLOT_PAD - cap))
-    recv = jnp.pad(recv_target[0, 0], pad, constant_values=targets).reshape(1, slots)
-
     fits = plan.fits()
     order = plan.store_order() if fits else list(range(ns))
     rows, cols, n = plan.rows, plan.cols, len(plan.peers)
     scratch = [pltpu.VMEM(features.shape, F32), pltpu.VMEM(edges.shape, jnp.int32),
                pltpu.SemaphoreType.DMA((3,))]
-    outs, more = [shape((slots, width), BF16)], []
+    packed = pack_rows(cap, width)
+    outs, more = [shape((ns * packed, 128), BF16)], []
     if fits:
         outs += [shape((targets, width), BF16)] + [shape((rows, targets), BF16)] * 2
         more = [self_rows]
@@ -243,11 +282,12 @@
     sums, *owns = call(
         functools.partial(slot_sums_kernel, plan, order), outs, (), hbm=[features, edges] + more,
         flops=4 * slots * owned * width, vmem=60 if fits else 16, scratch=scratch)
-    arrived = lax.all_to_all(sums.reshape(ns, SLOT_PAD, width), "store", split_axis=0, concat_axis=0,
-                             tiled=True, axis_index_groups=[order]).reshape(slots, width)
+    arrived = lax.all_to_all(sums.reshape(ns, packed, 128), "store", split_axis=0, concat_axis=0,
+                             tiled=True, axis_index_groups=[order]).reshape(ns * packed, 128)
     if not fits:
         own = self_rows.astype(BF16)
-        mean = neighbor_mean(cap, arrived, recv, targets)
+        recv = jnp.pad(recv_target[0, 0], ((0, 0), (0, SLOT_PAD - cap)), constant_values=targets).reshape(1, slots)
+        mean = neighbor_mean(cap, unpack(arrived, order, cap, width // 128), recv, targets)
         preact = dot(own, w_self) + dot(mean, w_neigh)
         hidden, grad = forward(preact, cotangent)
         both = jnp.concatenate([own.T.reshape(ns, -1, targets), mean.T.reshape(ns, -1, targets)], axis=1)
@@ -274,31 +314,43 @@
 
     mean, mean_here, mean_there = call(
         functools.partial(mean_kernel, plan, cap, order),
-        [shape((targets, width), BF16)] + [shape((rows, targets), BF16)] * 2, [arrived, recv, self_term],
+        [shape((targets, width), BF16)] + [shape((rows, targets), BF16)] * 2, [arrived, recv_target[0, 0], self_term],
         scratch=[pltpu.VMEM((width, targets), BF16)], flops=2 * targets * width * slots)
     hidden, grad_here, grad_there = call(
         functools.partial(layer_kernel, plan),
-        [shape((targets, out_width), BF16)] + [shape((cols // 128 * targets, 128), BF16)] * 2,
+        [shape((targets, out_width), F32)] + [shape((cols // 128 * targets, 128), BF16)] * 2,
         [mean, self_term, cotangent, w_neigh],
         scratch=[pltpu.VMEM((out_width // 128, targets, 128), BF16)],
         flops=2 * targets * width * out_width)
     mean_x, grad_y = to_x(mean_there), to_y(grad_there)
+    grad_x = to_x(grad_here)
     mean_all = [mean_here, to_y(mean_here), mean_x, to_y(held(mean_x, *own_all[1:]))]
-    grad_all = [grad_here, grad_y, to_x(grad_here), to_x(grad_y)]
-    give_left, keep_left = call(functools.partial(left_kernel, plan), [shape((rows, n * targets), BF16)] * 2,
-                                own_all + mean_all)
-    (give,) = call(functools.partial(terms_kernel, plan), [shape((rows, cols), BF16)], [give_left] + grad_all,
-                   flops=2 * rows * cols * targets * n)
-    (keep,) = call(functools.partial(terms_kernel, plan), [shape((rows, cols), F32)], [keep_left] + grad_all,
-                   flops=2 * rows * cols * targets * n)
-    got = plan.send(give, lambda z, x, y, c: (z, x, y, 1 - c))
+    grad_all = [grad_here, grad_y, grad_x, to_x(held(grad_y, mean_x, *own_all[1:]))]
+    def to_core(array):
+        return plan.send(array, lambda z, x, y, c: (z, x, y, 1 - c))
+
+    def to_z(array, k):
+        return plan.send(array, lambda z, x, y, c: (z ^ k, x, y, c))
+
+    def terms(left, kind):
+        return call(terms_kernel, [shape((left.shape[0], cols), kind)], [left] + grad_all,
+                    flops=2 * left.shape[0] * cols * targets * n)[0]
+
     block = (plan.shard, cols)
-    mine, *others = call(
-        functools.partial(core_sum_kernel, plan),
-        [shape(block, F32)] + [shape(block, BF16)] * (plan.nz - 1), [keep, got],
-        scratch=[pltpu.VMEM((rows, cols), F32)])
-    far_first = sorted(range(1, plan.nz), key=lambda k: (k < 2, k))
-    got = [plan.send(others[k - 1], lambda z, x, y, c, k=k: (z ^ k, x, y, c)) for k in far_first]
+    halves = [plan.far(), plan.near()]
+    lefts = call(functools.partial(left_kernel, plan),
+                 [shape((len(half) * plan.shard, n * targets), BF16) for half in halves * 2],
+                 own_all[::-1] + mean_all)
+    got, mine = [], None
+    for half, give_left, keep_left in zip(halves, lefts[:2], lefts[2:]):
+        came = to_core(terms(give_left, BF16))
+        sums = call(functools.partial(core_sum_kernel, plan),
+                    [shape(block, BF16 if k else F32) for k in half], [terms(keep_left, F32), came])
+        for k, part in zip(half, sums):
+            if k:
+                got.append(to_z(part, k))
+            else:
+                mine = part
     (quarter,) = call(store_sum_kernel, [shape(block, BF16)], [mine] + got)
     column = [quarter] + [plan.send(quarter, lambda z, x, y, c, i=i: (z, x, y ^ i, c))
                           for i in range(1, plan.gy)]
@@ -307,7 +359,7 @@
     grads = call(functools.partial(assemble_kernel, plan),
                  [shape((plan.shard, out_width), F32)] * 2, quarters,
                  scratch=[pltpu.VMEM((2, plan.shard, out_width), F32)])
-    return hidden, grads[0], grads[1]
+    return hidden.astype(BF16), grads[0], grads[1]
 
 
 def solution(mesh):

time: 49.4 us -> 47.5 us (0.962)
  waiting for transfers between devices: 16.1 us -> 13.6 us
  other arithmetic: 0 us -> 0.7 us
  starting transfers between devices: 25 us -> 25.6 us
    ppermute x16 -> x17, waiting for transfers between devices: 16.1 us -> 13.6 us  [send(): return lax.ppermute(array, ('store', 'trainer'), pairs)]
    convert_element_type x0 -> x1, other arithmetic: none -> 0.7 us  [per_device(): return (hidden.astype(BF16), grads[0], grads[1])]
    ppermute x16 -> x17, starting transfers between devices: 15.7 us -> 16.3 us  [send(): return lax.ppermute(array, ('store', 'trainer'), pairs)]
    pallas_call x9 -> x12, Pallas kernels: 5.73 us -> 5.3 us  [call(): pl.pallas_call(body, out_shape=list(outs), in_specs=[VMEM] * len(args) +...]
  transfers between devices with their start and end apart: 17 -> 18, of which waited for: 9 -> 9; matrix products, arithmetic and copies ran while one was open for 3% -> 4% of each run, Pallas kernels for 4% -> 4%
where the time goes in v6:
time: 47.5 us; the launch traced here: 47.2 us
  starting transfers between devices  25.6 us (54%)
  waiting for transfers between devices  13.6 us (29%)
  Pallas kernels  5.3 us (11%)
  matrix products  1.25 us (3%)
  between operations  0.78 us (2%)
  other arithmetic  0.7 us (1%)
    ppermute x17, starting transfers between devices, send(): return lax.ppermute(array, ('store', 'trainer'), pairs)  16.3 us
    ppermute x17, waiting for transfers between devices, send(): return lax.ppermute(array, ('store', 'trainer'), pairs)  13.6 us
    all_to_all x1, starting transfers between devices, per_device(): lax.all_to_all(sums.reshape(ns, packed, 128), 'store', split_axis=0, conc...  9.27 us
    pallas_call x12, Pallas kernels, call(): pl.pallas_call(body, out_shape=list(outs), in_specs=[VMEM] * len(args) +...  5.3 us
    dot_general x1, matrix products, dot(): return jnp.dot(a, b, preferred_element_type=F32)  1.25 us
  transfers between devices with their start and end apart: 18, of which 9 were waited for; matrix products, arithmetic and copies ran while one was open for 4% of the time, Pallas kernels for 4%

profile of v6, /device:TPU:0, one launch (start us, length us, event | category | flops | bytes accessed | tf_op | source)
XLA Modules:
  0.0 47.2 jit_solution(5336060342736750589)
XLA Ops:
  0.6 0.0 copy-start
  0.6 2.2 %shard_map.94 = (bf16[640,128]{1,0:T(8,128)(2,1)}, bf16[128,768]{1,0:T(8,128)(2,1)}, bf16[384,128]{1,0:T(8,128)(2,1)}, bf16[384,128]{1,0:T(8,128)(2,1)}) custom-call(f32[128,768]{1,0:T(8,128)} %feat_hbm.1, s32[8,2,12]{2,1,0:T(2,128)} %bitcast.11, f32[128,768]{1,0:T(8,128)} %rest_0_.1), custom_call_target="tpu_custom_call" | custom-call | flops 50331648 | bytes 557056 | tf_op jit(solution)/shard_map/pallas_call | solution.py:23
  2.9 0.0 copy-start.4
  2.9 9.3 %all-to-all-start = ((bf16[8,80,128]{2,1,0:T(8,128)(2,1)}), bf16[8,80,128]{2,1,0:T(8,128)(2,1)S(1)}, u32[]{:S(2)}, u32[]{:S(2)}) async-start(bf16[8,80,128]{2,1,0:T(8,128)(2,1)} %bitcast.10), calls=%async_computation | async-start | bytes 327680 | tf_op jit(solution)/shard_map/all_to_all | solution.py:285
  12.2 0.0 copy-start.1
  12.2 0.0 copy-start.2
  12.2 1.5 %collective-permute-start = (bf16[384,128]{1,0:T(8,128)(2,1)}, bf16[384,128]{1,0:T(8,128)(2,1)S(1)}, u32[]{:S(2)}, u32[]{:S(2)}) collective-permute-start(bf16[384,128]{1,0:T(8,128)(2,1)} %get-tuple-element.29), channel_id=1, source_target_pairs={{0,6},{1,7},{2,4},{3,5},{4,2},{5,3},{6,0},{7,1},{8,14},{9,15},{10,... | collective-permute-start | bytes 294920 | tf_op jit(solution)/shard_map/ppermute | solution.py:169
  13.7 1.4 %collective-permute-start.1 = (bf16[384,128]{1,0:T(8,128)(2,1)}, bf16[384,128]{1,0:T(8,128)(2,1)S(1)}, u32[]{:S(2)}, u32[]{:S(2)}) collective-permute-start(bf16[384,128]{1,0:T(8,128)(2,1)} %get-tuple-element.29), channel_id=1, source_target_pairs={{0,4},{1,5},{2,6},{3,7},{4,0},{5,1},{6,2},{7,3},{8,12},{9,13},{10,... | collective-permute-start | bytes 294920 | tf_op jit(solution)/shard_map/ppermute | solution.py:169
  15.2 0.5 %collective-permute-start.2 = (bf16[384,128]{1,0:T(8,128)(2,1)}, bf16[384,128]{1,0:T(8,128)(2,1)S(1)}, u32[]{:S(2)}, u32[]{:S(2)}) collective-permute-start(bf16[384,128]{1,0:T(8,128)(2,1)} %get-tuple-element.30.refs_3_), channel_id=1, source_target_pairs={{0,2},{1,3},{2,0},{3,1},{4,6},{5,7},{6,4},{7,5},{8,10},{9,11},{10,... | collective-permute-start | bytes 294920 | tf_op jit(solution)/shard_map/ppermute | solution.py:169
  15.7 0.0 copy-done
  15.7 1.2 %fusion._.self_ref = f32[128,768]{1,0:T(8,128)S(1)} fusion(bf16[128,768]{1,0:T(8,128)(2,1)} %get-tuple-element.26, bf16[768,768]{1,0:T(8,128)(2,1)S(1)} %copy-done), kind=kOutput, calls=%fused_computation | convolution fusion | flops 150994944 | bytes 1769472 | tf_op jit(solution)/shard_map/dot_general | solution.py:18
  16.9 0.0 all-to-all-done
  16.9 0.0 copy-done.4
  17.0 0.0 copy-start.3
  17.0 0.5 %shard_map.95 = (bf16[128,768]{1,0:T(8,128)(2,1)S(1)}, bf16[384,128]{1,0:T(8,128)(2,1)S(1)}, bf16[384,128]{1,0:T(8,128)(2,1)S(1)}) custom-call(bf16[640,128]{1,0:T(8,128)(2,1)S(1)} %bitcast.8, s32[8,12]{1,0:T(8,128)S(1)} %bitcast.9, f32[128,768]{1,0:T(8,128)S(1)} %fusion._.self_ref), custom_call_target="tpu_custom_call" | custom-call | flops 25165824 | bytes 950656 | tf_op jit(solution)/shard_map/pallas_call | solution.py:23
  17.5 1.2 %collective-permute-start.4 = (bf16[384,128]{1,0:T(8,128)(2,1)S(1)}, bf16[384,128]{1,0:T(8,128)(2,1)S(1)}, u32[]{:S(2)}, u32[]{:S(2)}) collective-permute-start(bf16[384,128]{1,0:T(8,128)(2,1)S(1)} %get-tuple-element.32), channel_id=1, source_target_pairs={{0,4},{1,5},{2,6},{3,7},{4,0},{5,1},{6,2},{7,3},{8,12},{9,13},{10,... | collective-permute-start | bytes 294920 | tf_op jit(solution)/shard_map/ppermute | solution.py:169
  18.7 0.0 copy-done.1
  18.7 0.0 copy-done.2
  18.7 0.4 shard_map.96
  19.1 1.6 %collective-permute-start.6 = (bf16[384,128]{1,0:T(8,128)(2,1)S(1)}, bf16[384,128]{1,0:T(8,128)(2,1)S(1)}, u32[]{:S(2)}, u32[]{:S(2)}) collective-permute-start(bf16[384,128]{1,0:T(8,128)(2,1)S(1)} %get-tuple-element.36), channel_id=1, source_target_pairs={{0,2},{1,3},{2,0},{3,1},{4,6},{5,7},{6,4},{7,5},{8,10},{9,11},{10,... | collective-permute-start | bytes 294920 | tf_op jit(solution)/shard_map/ppermute | solution.py:169
  20.7 0.0 collective-permute-done.refs_0_
  20.7 0.5 %collective-permute-start.3 = (bf16[384,128]{1,0:T(8,128)(2,1)S(1)}, bf16[384,128]{1,0:T(8,128)(2,1)S(1)}, u32[]{:S(2)}, u32[]{:S(2)}) collective-permute-start(bf16[384,128]{1,0:T(8,128)(2,1)S(1)} %get-tuple-element.31.refs_4_), channel_id=1, source_target_pairs={{0,2},{1,3},{2,0},{3,1},{4,6},{5,7},{6,4},{7,5},{8,10},{9,11},{10,... | collective-permute-start | bytes 294920 | tf_op jit(solution)/shard_map/ppermute | solution.py:169
  21.2 0.0 collective-permute-done.1.refs_1_
  21.2 0.9 %collective-permute-start.7 = (bf16[384,128]{1,0:T(8,128)(2,1)S(1)}, bf16[384,128]{1,0:T(8,128)(2,1)S(1)}, u32[]{:S(2)}, u32[]{:S(2)}) collective-permute-start(bf16[384,128]{1,0:T(8,128)(2,1)S(1)} %get-tuple-element.35.refs_0_), channel_id=1, source_target_pairs={{0,4},{1,5},{2,6},{3,7},{4,0},{5,1},{6,2},{7,3},{8,12},{9,13},{10,... | collective-permute-start | bytes 294920 | tf_op jit(solution)/shard_map/ppermute | solution.py:169
  22.1 0.0 collective-permute-done.2.refs_2_
  22.1 0.2 collective-permute-done.4.refs_6_
  22.3 1.4 %collective-permute-start.5 = (bf16[384,128]{1,0:T(8,128)(2,1)S(1)}, bf16[384,128]{1,0:T(8,128)(2,1)S(1)}, u32[]{:S(2)}, u32[]{:S(2)}) collective-permute-start(bf16[384,128]{1,0:T(8,128)(2,1)S(1)} %collective-permute-done.4.refs_6_), channel_id=1, source_target_pairs={{0,2},{1,3},{2,0},{3,1},{4,6},{5,7},{6,4},{7,5},{8,10},{9,11},{10,... | collective-permute-start | bytes 294920 | tf_op jit(solution)/shard_map/ppermute | solution.py:169
  23.7 0.6 %collective-permute-done.6.refs_1_ = bf16[384,128]{1,0:T(8,128)(2,1)S(1)} collective-permute-done((bf16[384,128]{1,0:T(8,128)(2,1)S(1)}, bf16[384,128]{1,0:T(8,128)(2,1)S(1)}, u32[]{:S(2)}, u32[]{:S(2)}) %collective-permute-start.6) | collective-permute-done | bytes 98336 | tf_op jit(solution)/shard_map/ppermute | solution.py:169
  24.3 1.1 %collective-permute-start.8 = (bf16[384,128]{1,0:T(8,128)(2,1)S(1)}, bf16[384,128]{1,0:T(8,128)(2,1)S(1)}, u32[]{:S(2)}, u32[]{:S(2)}) collective-permute-start(bf16[384,128]{1,0:T(8,128)(2,1)S(1)} %collective-permute-done.6.refs_1_), channel_id=1, source_target_pairs={{0,4},{1,5},{2,6},{3,7},{4,0},{5,1},{6,2},{7,3},{8,12},{9,13},{10,... | collective-permute-start | bytes 294920 | tf_op jit(solution)/shard_map/ppermute | solution.py:169
  25.4 0.9 %collective-permute-done.3.refs_5_ = bf16[384,128]{1,0:T(8,128)(2,1)S(1)} collective-permute-done((bf16[384,128]{1,0:T(8,128)(2,1)S(1)}, bf16[384,128]{1,0:T(8,128)(2,1)S(1)}, u32[]{:S(2)}, u32[]{:S(2)}) %collective-permute-start.3) | collective-permute-done | bytes 98336 | tf_op jit(solution)/shard_map/ppermute | solution.py:169
  26.3 1.1 %collective-permute-done.5.refs_7_ = bf16[384,128]{1,0:T(8,128)(2,1)S(1)} collective-permute-done((bf16[384,128]{1,0:T(8,128)(2,1)S(1)}, bf16[384,128]{1,0:T(8,128)(2,1)S(1)}, u32[]{:S(2)}, u32[]{:S(2)}) %collective-permute-start.5) | collective-permute-done | bytes 98336 | tf_op jit(solution)/shard_map/ppermute | solution.py:169
  27.3 0.0 copy-done.3
  27.3 0.1 shard_map.97
  27.5 0.0 collective-permute-done.7.refs_2_
  27.5 1.4 %collective-permute-done.8.refs_3_ = bf16[384,128]{1,0:T(8,128)(2,1)S(1)} collective-permute-done((bf16[384,128]{1,0:T(8,128)(2,1)S(1)}, bf16[384,128]{1,0:T(8,128)(2,1)S(1)}, u32[]{:S(2)}, u32[]{:S(2)}) %collective-permute-start.8) | collective-permute-done | bytes 98336 | tf_op jit(solution)/shard_map/ppermute | solution.py:169
  28.9 0.3 shard_map.102
  29.2 0.1 collective-permute-start.10
  29.3 0.3 shard_map.99
  29.5 0.6 %collective-permute-start.9 = (bf16[192,384]{1,0:T(8,128)(2,1)S(1)}, bf16[192,384]{1,0:T(8,128)(2,1)S(1)}, u32[]{:S(2)}, u32[]{:S(2)}) collective-permute-start(bf16[192,384]{1,0:T(8,128)(2,1)S(1)} %shard_map.99), channel_id=1, source_target_pairs={{0,1},{1,0},{2,3},{3,2},{4,5},{5,4},{6,7},{7,6},{8,9},{9,8},{10,11... | collective-permute-start | bytes 442376 | tf_op jit(solution)/shard_map/ppermute | solution.py:169
  30.1 0.3 shard_map.98.keep_ref
  30.3 0.3 shard_map.101.keep_ref
  30.6 0.0 collective-permute-done.10.got_ref
  30.7 1.9 %collective-permute-start.11 = (bf16[96,384]{1,0:T(8,128)(2,1)S(1)}, bf16[96,384]{1,0:T(8,128)(2,1)S(1)}, u32[]{:S(2)}, u32[]{:S(2)}) collective-permute-start(bf16[96,384]{1,0:T(8,128)(2,1)S(1)} %get-tuple-element.42), channel_id=1, source_target_pairs={{0,16},{1,17},{2,18},{3,19},{4,20},{5,21},{6,22},{7,23},{8,24},{9,... | collective-permute-start | bytes 221192 | tf_op jit(solution)/shard_map/ppermute | solution.py:169
  32.5 1.9 %collective-permute-start.12 = (bf16[96,384]{1,0:T(8,128)(2,1)S(1)}, bf16[96,384]{1,0:T(8,128)(2,1)S(1)}, u32[]{:S(2)}, u32[]{:S(2)}) collective-permute-start(bf16[96,384]{1,0:T(8,128)(2,1)S(1)} %get-tuple-element.43), channel_id=1, source_target_pairs={{0,24},{1,25},{2,26},{3,27},{4,28},{5,29},{6,30},{7,31},{8,16},{9,... | collective-permute-start | bytes 221192 | tf_op jit(solution)/shard_map/ppermute | solution.py:169
  34.4 0.0 collective-permute-done.9.got_ref
  34.4 0.1 collective-permute-start.13
  34.5 5.3 %collective-permute-done.11.refs_1_ = bf16[96,384]{1,0:T(8,128)(2,1)S(1)} collective-permute-done((bf16[96,384]{1,0:T(8,128)(2,1)S(1)}, bf16[96,384]{1,0:T(8,128)(2,1)S(1)}, u32[]{:S(2)}, u32[]{:S(2)}) %collective-permute-start.11) | collective-permute-done | bytes 73760 | tf_op jit(solution)/shard_map/ppermute | solution.py:169
  39.8 0.0 collective-permute-done.12.refs_2_
  39.9 0.7 %collective-permute-done.13.refs_3_ = bf16[96,384]{1,0:T(8,128)(2,1)S(1)} collective-permute-done((bf16[96,384]{1,0:T(8,128)(2,1)S(1)}, bf16[96,384]{1,0:T(8,128)(2,1)S(1)}, u32[]{:S(2)}, u32[]{:S(2)}) %collective-permute-start.13) | collective-permute-done | bytes 73760 | tf_op jit(solution)/shard_map/ppermute | solution.py:169
  40.6 1.7 %collective-permute-start.15 = (bf16[96,384]{1,0:T(8,128)(2,1)S(1)}, bf16[96,384]{1,0:T(8,128)(2,1)S(1)}, u32[]{:S(2)}, u32[]{:S(2)}) collective-permute-start(bf16[96,384]{1,0:T(8,128)(2,1)S(1)} %shard_map.104.refs_0_), channel_id=1, source_target_pairs={{0,2},{1,3},{2,0},{3,1},{4,6},{5,7},{6,4},{7,5},{8,10},{9,11},{10,... | collective-permute-start | bytes 221192 | tf_op jit(solution)/shard_map/ppermute | solution.py:169
  42.3 0.0 collective-permute-start.14
  42.3 2.7 %collective-permute-done.15.refs_2_ = bf16[96,384]{1,0:T(8,128)(2,1)S(1)} collective-permute-done((bf16[96,384]{1,0:T(8,128)(2,1)S(1)}, bf16[96,384]{1,0:T(8,128)(2,1)S(1)}, u32[]{:S(2)}, u32[]{:S(2)}) %collective-permute-start.15) | collective-permute-done | bytes 73760 | tf_op jit(solution)/shard_map/ppermute | solution.py:169
  45.0 0.0 collective-permute-start.16
  45.1 0.7 %convert_element_type.3 = bf16[128,768]{1,0:T(8,128)(2,1)} convert(f32[128,768]{1,0:T(8,128)S(1)} %get-tuple-element.28) | non-fusion elementwise | flops 98304 | bytes 589824 | tf_op jit(solution)/shard_map/convert_element_type | solution.py:362
  45.8 0.0 collective-permute-done.14.refs_1_
  45.8 0.6 %collective-permute-done.16.refs_3_ = bf16[96,384]{1,0:T(8,128)(2,1)S(1)} collective-permute-done((bf16[96,384]{1,0:T(8,128)(2,1)S(1)}, bf16[96,384]{1,0:T(8,128)(2,1)S(1)}, u32[]{:S(2)}, u32[]{:S(2)}) %collective-permute-start.16) | collective-permute-done | bytes 73760 | tf_op jit(solution)/shard_map/ppermute | solution.py:169
  46.3 0.9 %shard_map.105 = (f32[96,768]{1,0:T(8,128)}, f32[96,768]{1,0:T(8,128)}) custom-call(bf16[96,384]{1,0:T(8,128)(2,1)S(1)} %shard_map.104.refs_0_, bf16[96,384]{1,0:T(8,128)(2,1)S(1)} %collective-permute-done.14.refs_1_, bf16[96,384]{1,0:T(8,128)(2,1)S(1)} %collective-permute-done.15.refs_2_, bf16[96,384]{1,0:T(8,128)(2,1)S(1)} %collective-permute-done.16.refs_3_), custom_call_target="tpu_custom_call" | custom-call | bytes 884736 | tf_op jit(solution)/shard_map/pallas_call | solution.py:23
  (3 shorter events, 0.1 us)
Async XLA Ops:
  0.6 15.0 %copy-start = (bf16[768,768]{1,0:T(8,128)(2,1)S(1)}, bf16[768,768]{1,0:T(8,128)(2,1)}, u32[]{:S(2)}) copy-start(bf16[768,768]{1,0:T(8,128)(2,1)} %param.12) | copy-start | bytes 3538948
  2.9 14.0 %copy-start.4 = (s32[1,1,8,12]{3,2,1,0:T(8,128)S(1)}, s32[1,1,8,12]{3,2,1,0:T(8,128)}, u32[]{:S(2)}) copy-start(s32[1,1,8,12]{3,2,1,0:T(8,128)} %param.10) | copy-start | bytes 1156
  2.9 14.0 %all-to-all-start = ((bf16[8,80,128]{2,1,0:T(8,128)(2,1)}), bf16[8,80,128]{2,1,0:T(8,128)(2,1)S(1)}, u32[]{:S(2)}, u32[]{:S(2)}) async-start(bf16[8,80,128]{2,1,0:T(8,128)(2,1)} %bitcast.10), calls=%async_computation | async-start | bytes 327680 | tf_op jit(solution)/shard_map/all_to_all | solution.py:285
  12.2 6.5 %copy-start.1 = (bf16[768,768]{1,0:T(8,128)(2,1)S(1)}, bf16[768,768]{1,0:T(8,128)(2,1)}, u32[]{:S(2)}) copy-start(bf16[768,768]{1,0:T(8,128)(2,1)} %w_ref.1) | copy-start | bytes 3538948
  12.2 6.5 %copy-start.2 = (bf16[128,768]{1,0:T(8,128)(2,1)S(1)}, bf16[128,768]{1,0:T(8,128)(2,1)}, u32[]{:S(2)}) copy-start(bf16[128,768]{1,0:T(8,128)(2,1)} %cot_ref.1) | copy-start | bytes 589828
  12.2 8.5 %collective-permute-start = (bf16[384,128]{1,0:T(8,128)(2,1)}, bf16[384,128]{1,0:T(8,128)(2,1)S(1)}, u32[]{:S(2)}, u32[]{:S(2)}) collective-permute-start(bf16[384,128]{1,0:T(8,128)(2,1)} %get-tuple-element.29), channel_id=1, source_target_pairs={{0,6},{1,7},{2,4},{3,5},{4,2},{5,3},{6,0},{7,1},{8,14},{9,15},{10,... | collective-permute-start | bytes 294920 | tf_op jit(solution)/shard_map/ppermute | solution.py:169
  13.7 7.5 %collective-permute-start.1 = (bf16[384,128]{1,0:T(8,128)(2,1)}, bf16[384,128]{1,0:T(8,128)(2,1)S(1)}, u32[]{:S(2)}, u32[]{:S(2)}) collective-permute-start(bf16[384,128]{1,0:T(8,128)(2,1)} %get-tuple-element.29), channel_id=1, source_target_pairs={{0,4},{1,5},{2,6},{3,7},{4,0},{5,1},{6,2},{7,3},{8,12},{9,13},{10,... | collective-permute-start | bytes 294920 | tf_op jit(solution)/shard_map/ppermute | solution.py:169
  15.2 6.9 %collective-permute-start.2 = (bf16[384,128]{1,0:T(8,128)(2,1)}, bf16[384,128]{1,0:T(8,128)(2,1)S(1)}, u32[]{:S(2)}, u32[]{:S(2)}) collective-permute-start(bf16[384,128]{1,0:T(8,128)(2,1)} %get-tuple-element.30.refs_3_), channel_id=1, source_target_pairs={{0,2},{1,3},{2,0},{3,1},{4,6},{5,7},{6,4},{7,5},{8,10},{9,11},{10,... | collective-permute-start | bytes 294920 | tf_op jit(solution)/shard_map/ppermute | solution.py:169
  17.0 10.4 %copy-start.3 = (bf16[384,128]{1,0:T(8,128)(2,1)S(1)}, bf16[384,128]{1,0:T(8,128)(2,1)}, u32[]{:S(2)}) copy-start(bf16[384,128]{1,0:T(8,128)(2,1)} %get-tuple-element.30.refs_3_) | copy-start | bytes 294916
  17.5 4.8 %collective-permute-start.4 = (bf16[384,128]{1,0:T(8,128)(2,1)S(1)}, bf16[384,128]{1,0:T(8,128)(2,1)S(1)}, u32[]{:S(2)}, u32[]{:S(2)}) collective-permute-start(bf16[384,128]{1,0:T(8,128)(2,1)S(1)} %get-tuple-element.32), channel_id=1, source_target_pairs={{0,4},{1,5},{2,6},{3,7},{4,0},{5,1},{6,2},{7,3},{8,12},{9,13},{10,... | collective-permute-start | bytes 294920 | tf_op jit(solution)/shard_map/ppermute | solution.py:169
  19.1 5.2 %collective-permute-start.6 = (bf16[384,128]{1,0:T(8,128)(2,1)S(1)}, bf16[384,128]{1,0:T(8,128)(2,1)S(1)}, u32[]{:S(2)}, u32[]{:S(2)}) collective-permute-start(bf16[384,128]{1,0:T(8,128)(2,1)S(1)} %get-tuple-element.36), channel_id=1, source_target_pairs={{0,2},{1,3},{2,0},{3,1},{4,6},{5,7},{6,4},{7,5},{8,10},{9,11},{10,... | collective-permute-start | bytes 294920 | tf_op jit(solution)/shard_map/ppermute | solution.py:169
  20.7 5.6 %collective-permute-start.3 = (bf16[384,128]{1,0:T(8,128)(2,1)S(1)}, bf16[384,128]{1,0:T(8,128)(2,1)S(1)}, u32[]{:S(2)}, u32[]{:S(2)}) collective-permute-start(bf16[384,128]{1,0:T(8,128)(2,1)S(1)} %get-tuple-element.31.refs_4_), channel_id=1, source_target_pairs={{0,2},{1,3},{2,0},{3,1},{4,6},{5,7},{6,4},{7,5},{8,10},{9,11},{10,... | collective-permute-start | bytes 294920 | tf_op jit(solution)/shard_map/ppermute | solution.py:169
  21.2 6.3 %collective-permute-start.7 = (bf16[384,128]{1,0:T(8,128)(2,1)S(1)}, bf16[384,128]{1,0:T(8,128)(2,1)S(1)}, u32[]{:S(2)}, u32[]{:S(2)}) collective-permute-start(bf16[384,128]{1,0:T(8,128)(2,1)S(1)} %get-tuple-element.35.refs_0_), channel_id=1, source_target_pairs={{0,4},{1,5},{2,6},{3,7},{4,0},{5,1},{6,2},{7,3},{8,12},{9,13},{10,... | collective-permute-start | bytes 294920 | tf_op jit(solution)/shard_map/ppermute | solution.py:169
  22.3 5.0 %collective-permute-start.5 = (bf16[384,128]{1,0:T(8,128)(2,1)S(1)}, bf16[384,128]{1,0:T(8,128)(2,1)S(1)}, u32[]{:S(2)}, u32[]{:S(2)}) collective-permute-start(bf16[384,128]{1,0:T(8,128)(2,1)S(1)} %collective-permute-done.4.refs_6_), channel_id=1, source_target_pairs={{0,2},{1,3},{2,0},{3,1},{4,6},{5,7},{6,4},{7,5},{8,10},{9,11},{10,... | collective-permute-start | bytes 294920 | tf_op jit(solution)/shard_map/ppermute | solution.py:169
  24.3 4.6 %collective-permute-start.8 = (bf16[384,128]{1,0:T(8,128)(2,1)S(1)}, bf16[384,128]{1,0:T(8,128)(2,1)S(1)}, u32[]{:S(2)}, u32[]{:S(2)}) collective-permute-start(bf16[384,128]{1,0:T(8,128)(2,1)S(1)} %collective-permute-done.6.refs_1_), channel_id=1, source_target_pairs={{0,4},{1,5},{2,6},{3,7},{4,0},{5,1},{6,2},{7,3},{8,12},{9,13},{10,... | collective-permute-start | bytes 294920 | tf_op jit(solution)/shard_map/ppermute | solution.py:169
  29.2 1.4 %collective-permute-start.10 = (bf16[192,384]{1,0:T(8,128)(2,1)S(1)}, bf16[192,384]{1,0:T(8,128)(2,1)S(1)}, u32[]{:S(2)}, u32[]{:S(2)}) collective-permute-start(bf16[192,384]{1,0:T(8,128)(2,1)S(1)} %shard_map.102), channel_id=1, source_target_pairs={{0,1},{1,0},{2,3},{3,2},{4,5},{5,4},{6,7},{7,6},{8,9},{9,8},{10,11... | collective-permute-start | bytes 442376 | tf_op jit(solution)/shard_map/ppermute | solution.py:169
  29.5 4.9 %collective-permute-start.9 = (bf16[192,384]{1,0:T(8,128)(2,1)S(1)}, bf16[192,384]{1,0:T(8,128)(2,1)S(1)}, u32[]{:S(2)}, u32[]{:S(2)}) collective-permute-start(bf16[192,384]{1,0:T(8,128)(2,1)S(1)} %shard_map.99), channel_id=1, source_target_pairs={{0,1},{1,0},{2,3},{3,2},{4,5},{5,4},{6,7},{7,6},{8,9},{9,8},{10,11... | collective-permute-start | bytes 442376 | tf_op jit(solution)/shard_map/ppermute | solution.py:169
  30.7 9.2 %collective-permute-start.11 = (bf16[96,384]{1,0:T(8,128)(2,1)S(1)}, bf16[96,384]{1,0:T(8,128)(2,1)S(1)}, u32[]{:S(2)}, u32[]{:S(2)}) collective-permute-start(bf16[96,384]{1,0:T(8,128)(2,1)S(1)} %get-tuple-element.42), channel_id=1, source_target_pairs={{0,16},{1,17},{2,18},{3,19},{4,20},{5,21},{6,22},{7,23},{8,24},{9,... | collective-permute-start | bytes 221192 | tf_op jit(solution)/shard_map/ppermute | solution.py:169
  32.5 7.3 %collective-permute-start.12 = (bf16[96,384]{1,0:T(8,128)(2,1)S(1)}, bf16[96,384]{1,0:T(8,128)(2,1)S(1)}, u32[]{:S(2)}, u32[]{:S(2)}) collective-permute-start(bf16[96,384]{1,0:T(8,128)(2,1)S(1)} %get-tuple-element.43), channel_id=1, source_target_pairs={{0,24},{1,25},{2,26},{3,27},{4,28},{5,29},{6,30},{7,31},{8,16},{9,... | collective-permute-start | bytes 221192 | tf_op jit(solution)/shard_map/ppermute | solution.py:169
  34.4 6.1 %collective-permute-start.13 = (bf16[96,384]{1,0:T(8,128)(2,1)S(1)}, bf16[96,384]{1,0:T(8,128)(2,1)S(1)}, u32[]{:S(2)}, u32[]{:S(2)}) collective-permute-start(bf16[96,384]{1,0:T(8,128)(2,1)S(1)} %get-tuple-element.44), channel_id=1, source_target_pairs={{0,8},{1,9},{2,10},{3,11},{4,12},{5,13},{6,14},{7,15},{8,0},{9,1},... | collective-permute-start | bytes 221192 | tf_op jit(solution)/shard_map/ppermute | solution.py:169
  40.6 4.4 %collective-permute-start.15 = (bf16[96,384]{1,0:T(8,128)(2,1)S(1)}, bf16[96,384]{1,0:T(8,128)(2,1)S(1)}, u32[]{:S(2)}, u32[]{:S(2)}) collective-permute-start(bf16[96,384]{1,0:T(8,128)(2,1)S(1)} %shard_map.104.refs_0_), channel_id=1, source_target_pairs={{0,2},{1,3},{2,0},{3,1},{4,6},{5,7},{6,4},{7,5},{8,10},{9,11},{10,... | collective-permute-start | bytes 221192 | tf_op jit(solution)/shard_map/ppermute | solution.py:169
  42.3 3.5 %collective-permute-start.14 = (bf16[96,384]{1,0:T(8,128)(2,1)S(1)}, bf16[96,384]{1,0:T(8,128)(2,1)S(1)}, u32[]{:S(2)}, u32[]{:S(2)}) collective-permute-start(bf16[96,384]{1,0:T(8,128)(2,1)S(1)} %shard_map.104.refs_0_), channel_id=1, source_target_pairs={{0,1},{1,0},{2,3},{3,2},{4,5},{5,4},{6,7},{7,6},{8,9},{9,8},{10,11... | collective-permute-start | bytes 221192 | tf_op jit(solution)/shard_map/ppermute | solution.py:169
  45.0 1.3 %collective-permute-start.16 = (bf16[96,384]{1,0:T(8,128)(2,1)S(1)}, bf16[96,384]{1,0:T(8,128)(2,1)S(1)}, u32[]{:S(2)}, u32[]{:S(2)}) collective-permute-start(bf16[96,384]{1,0:T(8,128)(2,1)S(1)} %collective-permute-done.15.refs_2_), channel_id=1, source_target_pairs={{0,1},{1,0},{2,3},{3,2},{4,5},{5,4},{6,7},{7,6},{8,9},{9,8},{10,11... | collective-permute-start | bytes 221192 | tf_op jit(solution)/shard_map/ppermute | solution.py:169

commit v7 on v6

--- a/solution.py
+++ b/solution.py
@@ -189,26 +189,22 @@
     write_rows(plan, trans_ref, here_ref, there_ref)
 
 
-def mean_kernel(plan, cap, order, rows_ref, recv_ref, _, mean_ref, here_ref, there_ref, trans_ref):
-    rows = unpack(rows_ref[...], order, cap, mean_ref.shape[1] // 128)
-    targets = mean_ref.shape[0]
+def layer_kernel(plan, cap, order, rows_ref, recv_ref, self_ref, cot_ref, w_ref, hidden_ref, mean_here, mean_there,
+                 grad_here, grad_there, trans_ref, grad_ref):
+    targets = self_ref.shape[0]
+    rows = unpack(rows_ref[...], order, cap, hidden_ref.shape[1] // 128)
     fill = jnp.full((1, SLOT_PAD - cap), targets, jnp.int32)
     recv = jnp.concatenate([p for s in range(plan.ns) for p in (recv_ref[s:s + 1, :], fill)], axis=1)
     mean = neighbor_mean(cap, rows, recv, targets)
-    mean_ref[...] = mean
+    preact = self_ref[...] + dot(mean, w_ref[...])
     trans_ref[...] = mean.astype(F32).T.astype(BF16)
-    write_rows(plan, trans_ref, here_ref, there_ref)
-
-
-def layer_kernel(plan, mean_ref, self_ref, cot_ref, w_ref, hidden_ref, here_ref, there_ref, grad_ref):
-    targets = self_ref.shape[0]
-    preact = self_ref[...] + dot(mean_ref[...], w_ref[...])
+    write_rows(plan, trans_ref, mean_here, mean_there)
     hidden, grad = forward(preact, cot_ref[...])
     hidden_ref[...] = hidden.astype(F32)
     for b in range(grad_ref.shape[0]):
         grad_ref[b] = grad[:, b * 128:(b + 1) * 128]
     y, each = plan.place()[2], plan.cols // 128
-    for dy, out in enumerate((here_ref, there_ref)):
+    for dy, out in enumerate((grad_here, grad_there)):
         for b in range(each):
             out[b * targets:(b + 1) * targets, :] = grad_ref[(y ^ dy) * each + b]
 
@@ -312,16 +308,13 @@
     own_all = [own_here, to_y(own_here), to_x(own_there), to_diagonal(own_there)]
     self_term = dot(own, w_self)
 
-    mean, mean_here, mean_there = call(
-        functools.partial(mean_kernel, plan, cap, order),
-        [shape((targets, width), BF16)] + [shape((rows, targets), BF16)] * 2, [arrived, recv_target[0, 0], self_term],
-        scratch=[pltpu.VMEM((width, targets), BF16)], flops=2 * targets * width * slots)
-    hidden, grad_here, grad_there = call(
-        functools.partial(layer_kernel, plan),
-        [shape((targets, out_width), F32)] + [shape((cols // 128 * targets, 128), BF16)] * 2,
-        [mean, self_term, cotangent, w_neigh],
-        scratch=[pltpu.VMEM((out_width // 128, targets, 128), BF16)],
-        flops=2 * targets * width * out_width)
+    hidden, mean_here, mean_there, grad_here, grad_there = call(
+        functools.partial(layer_kernel, plan, cap, order),
+        [shape((targets, out_width), F32)] + [shape((rows, targets), BF16)] * 2
+        + [shape((cols // 128 * targets, 128), BF16)] * 2,
+        [arrived, recv_target[0, 0], self_term, cotangent, w_neigh],
+        scratch=[pltpu.VMEM((width, targets), BF16), pltpu.VMEM((out_width // 128, targets, 128), BF16)],
+        flops=2 * targets * width * (out_width + slots))
     mean_x, grad_y = to_x(mean_there), to_y(grad_there)
     grad_x = to_x(grad_here)
     mean_all = [mean_here, to_y(mean_here), mean_x, to_y(held(mean_x, *own_all[1:]))]

time: 47.5 us -> 47.6 us (level)
  waiting for transfers between devices: 13.6 us -> 14.2 us
    ppermute x17, waiting for transfers between devices: 13.6 us -> 14.2 us  [send(): return lax.ppermute(array, ('store', 'trainer'), pairs)]
    pallas_call x12 -> x11, Pallas kernels: 5.3 us -> 5.12 us  [call(): pl.pallas_call(body, out_shape=list(outs), in_specs=[VMEM] * len(args) +...]
where the time goes in v7:
time: 47.6 us; the launch traced here: 47.3 us
  starting transfers between devices  25.2 us (53%)
  waiting for transfers between devices  14.2 us (30%)
  Pallas kernels  5.12 us (11%)
  matrix products  1.25 us (3%)
  between operations  0.8 us (2%)
  other arithmetic  0.7 us (1%)
    ppermute x17, starting transfers between devices, send(): return lax.ppermute(array, ('store', 'trainer'), pairs)  15.8 us
    ppermute x17, waiting for transfers between devices, send(): return lax.ppermute(array, ('store', 'trainer'), pairs)  14.2 us
    all_to_all x1, starting transfers between devices, per_device(): lax.all_to_all(sums.reshape(ns, packed, 128), 'store', split_axis=0, conc...  9.4 us
    pallas_call x11, Pallas kernels, call(): pl.pallas_call(body, out_shape=list(outs), in_specs=[VMEM] * len(args) +...  5.12 us
    dot_general x1, matrix products, dot(): return jnp.dot(a, b, preferred_element_type=F32)  1.25 us
  transfers between devices with their start and end apart: 18, of which 9 were waited for; matrix products, arithmetic and copies ran while one was open for 4% of the time, Pallas kernels for 4%

profile of v7, /device:TPU:0, one launch (start us, length us, event | category | flops | bytes accessed | tf_op | source)
XLA Modules:
  0.0 47.3 jit_solution(3936397495150430076)
XLA Ops:
  0.6 0.0 copy-start
  0.6 2.2 %shard_map.94 = (bf16[640,128]{1,0:T(8,128)(2,1)}, bf16[128,768]{1,0:T(8,128)(2,1)}, bf16[384,128]{1,0:T(8,128)(2,1)}, bf16[384,128]{1,0:T(8,128)(2,1)}) custom-call(f32[128,768]{1,0:T(8,128)} %feat_hbm.1, s32[8,2,12]{2,1,0:T(2,128)} %bitcast.11, f32[128,768]{1,0:T(8,128)} %rest_0_.1), custom_call_target="tpu_custom_call" | custom-call | flops 50331648 | bytes 557056 | tf_op jit(solution)/shard_map/pallas_call | solution.py:23
  2.9 0.0 copy-start.1
  2.9 0.0 copy-start.2
  2.9 0.0 copy-start.4
  2.9 9.4 %all-to-all-start = ((bf16[8,80,128]{2,1,0:T(8,128)(2,1)}), bf16[8,80,128]{2,1,0:T(8,128)(2,1)S(1)}, u32[]{:S(2)}, u32[]{:S(2)}) async-start(bf16[8,80,128]{2,1,0:T(8,128)(2,1)} %bitcast.10), calls=%async_computation | async-start | bytes 327680 | tf_op jit(solution)/shard_map/all_to_all | solution.py:281
  12.3 1.5 %collective-permute-start = (bf16[384,128]{1,0:T(8,128)(2,1)}, bf16[384,128]{1,0:T(8,128)(2,1)S(1)}, u32[]{:S(2)}, u32[]{:S(2)}) collective-permute-start(bf16[384,128]{1,0:T(8,128)(2,1)} %get-tuple-element.27), channel_id=1, source_target_pairs={{0,6},{1,7},{2,4},{3,5},{4,2},{5,3},{6,0},{7,1},{8,14},{9,15},{10,... | collective-permute-start | bytes 294920 | tf_op jit(solution)/shard_map/ppermute | solution.py:169
  13.8 1.4 %collective-permute-start.1 = (bf16[384,128]{1,0:T(8,128)(2,1)}, bf16[384,128]{1,0:T(8,128)(2,1)S(1)}, u32[]{:S(2)}, u32[]{:S(2)}) collective-permute-start(bf16[384,128]{1,0:T(8,128)(2,1)} %get-tuple-element.27), channel_id=1, source_target_pairs={{0,4},{1,5},{2,6},{3,7},{4,0},{5,1},{6,2},{7,3},{8,12},{9,13},{10,... | collective-permute-start | bytes 294920 | tf_op jit(solution)/shard_map/ppermute | solution.py:169
  15.3 0.5 %collective-permute-start.2 = (bf16[384,128]{1,0:T(8,128)(2,1)}, bf16[384,128]{1,0:T(8,128)(2,1)S(1)}, u32[]{:S(2)}, u32[]{:S(2)}) collective-permute-start(bf16[384,128]{1,0:T(8,128)(2,1)} %get-tuple-element.28.refs_3_), channel_id=1, source_target_pairs={{0,2},{1,3},{2,0},{3,1},{4,6},{5,7},{6,4},{7,5},{8,10},{9,11},{10,... | collective-permute-start | bytes 294920 | tf_op jit(solution)/shard_map/ppermute | solution.py:169
  15.8 0.0 copy-done
  15.8 1.2 %fusion.self_ref = f32[128,768]{1,0:T(8,128)S(1)} fusion(bf16[128,768]{1,0:T(8,128)(2,1)} %get-tuple-element.25, bf16[768,768]{1,0:T(8,128)(2,1)S(1)} %copy-done), kind=kOutput, calls=%fused_computation | convolution fusion | flops 150994944 | bytes 1769472 | tf_op jit(solution)/shard_map/dot_general | solution.py:18
  17.1 0.0 copy-start.3
  17.1 0.0 all-to-all-done
  17.1 0.0 copy-done.1
  17.1 0.0 copy-done.2
  17.1 0.0 copy-done.4
  17.1 0.7 %shard_map.95 = (f32[128,768]{1,0:T(8,128)S(1)}, bf16[384,128]{1,0:T(8,128)(2,1)S(1)}, bf16[384,128]{1,0:T(8,128)(2,1)S(1)}, bf16[384,128]{1,0:T(8,128)(2,1)S(1)}, bf16[384,128]{1,0:T(8,128)(2,1)S(1)}) custom-call(bf16[640,128]{1,0:T(8,128)(2,1)S(1)} %bitcast.8, s32[8,12]{1,0:T(8,128)S(1)} %bitcast.9, f32[128,768]{1,0:T(8,128)S(1)} %fusion.self_ref, ...), custom_call_target="tpu_custom_call" | custom-call | flops 176160768 | bytes 2720128 | tf_op jit(solution)/shard_map/pallas_call | solution.py:23
  17.9 1.2 %collective-permute-start.4 = (bf16[384,128]{1,0:T(8,128)(2,1)S(1)}, bf16[384,128]{1,0:T(8,128)(2,1)S(1)}, u32[]{:S(2)}, u32[]{:S(2)}) collective-permute-start(bf16[384,128]{1,0:T(8,128)(2,1)S(1)} %get-tuple-element.30), channel_id=1, source_target_pairs={{0,4},{1,5},{2,6},{3,7},{4,0},{5,1},{6,2},{7,3},{8,12},{9,13},{10,... | collective-permute-start | bytes 294920 | tf_op jit(solution)/shard_map/ppermute | solution.py:169
  19.1 1.5 %collective-permute-start.6 = (bf16[384,128]{1,0:T(8,128)(2,1)S(1)}, bf16[384,128]{1,0:T(8,128)(2,1)S(1)}, u32[]{:S(2)}, u32[]{:S(2)}) collective-permute-start(bf16[384,128]{1,0:T(8,128)(2,1)S(1)} %get-tuple-element.34), channel_id=1, source_target_pairs={{0,2},{1,3},{2,0},{3,1},{4,6},{5,7},{6,4},{7,5},{8,10},{9,11},{10,... | collective-permute-start | bytes 294920 | tf_op jit(solution)/shard_map/ppermute | solution.py:169
  20.6 0.0 collective-permute-done.refs_0_
  20.6 0.5 %collective-permute-start.3 = (bf16[384,128]{1,0:T(8,128)(2,1)S(1)}, bf16[384,128]{1,0:T(8,128)(2,1)S(1)}, u32[]{:S(2)}, u32[]{:S(2)}) collective-permute-start(bf16[384,128]{1,0:T(8,128)(2,1)S(1)} %get-tuple-element.29.refs_4_), channel_id=1, source_target_pairs={{0,2},{1,3},{2,0},{3,1},{4,6},{5,7},{6,4},{7,5},{8,10},{9,11},{10,... | collective-permute-start | bytes 294920 | tf_op jit(solution)/shard_map/ppermute | solution.py:169
  21.1 0.2 collective-permute-done.1.refs_1_
  21.3 0.7 %collective-permute-start.7 = (bf16[384,128]{1,0:T(8,128)(2,1)S(1)}, bf16[384,128]{1,0:T(8,128)(2,1)S(1)}, u32[]{:S(2)}, u32[]{:S(2)}) collective-permute-start(bf16[384,128]{1,0:T(8,128)(2,1)S(1)} %get-tuple-element.33.refs_0_), channel_id=1, source_target_pairs={{0,4},{1,5},{2,6},{3,7},{4,0},{5,1},{6,2},{7,3},{8,12},{9,13},{10,... | collective-permute-start | bytes 294920 | tf_op jit(solution)/shard_map/ppermute | solution.py:169
  22.0 0.0 collective-permute-done.2.refs_2_
  22.0 1.0 %collective-permute-done.4.refs_6_ = bf16[384,128]{1,0:T(8,128)(2,1)S(1)} collective-permute-done((bf16[384,128]{1,0:T(8,128)(2,1)S(1)}, bf16[384,128]{1,0:T(8,128)(2,1)S(1)}, u32[]{:S(2)}, u32[]{:S(2)}) %collective-permute-start.4) | collective-permute-done | bytes 98336 | tf_op jit(solution)/shard_map/ppermute | solution.py:169
  22.9 1.5 %collective-permute-start.5 = (bf16[384,128]{1,0:T(8,128)(2,1)S(1)}, bf16[384,128]{1,0:T(8,128)(2,1)S(1)}, u32[]{:S(2)}, u32[]{:S(2)}) collective-permute-start(bf16[384,128]{1,0:T(8,128)(2,1)S(1)} %collective-permute-done.4.refs_6_), channel_id=1, source_target_pairs={{0,2},{1,3},{2,0},{3,1},{4,6},{5,7},{6,4},{7,5},{8,10},{9,11},{10,... | collective-permute-start | bytes 294920 | tf_op jit(solution)/shard_map/ppermute | solution.py:169
  24.5 0.0 collective-permute-done.6.refs_1_
  24.5 1.5 %collective-permute-start.8 = (bf16[384,128]{1,0:T(8,128)(2,1)S(1)}, bf16[384,128]{1,0:T(8,128)(2,1)S(1)}, u32[]{:S(2)}, u32[]{:S(2)}) collective-permute-start(bf16[384,128]{1,0:T(8,128)(2,1)S(1)} %collective-permute-done.6.refs_1_), channel_id=1, source_target_pairs={{0,4},{1,5},{2,6},{3,7},{4,0},{5,1},{6,2},{7,3},{8,12},{9,13},{10,... | collective-permute-start | bytes 294920 | tf_op jit(solution)/shard_map/ppermute | solution.py:169
  25.9 0.2 collective-permute-done.3.refs_5_
  26.2 1.4 %collective-permute-done.5.refs_7_ = bf16[384,128]{1,0:T(8,128)(2,1)S(1)} collective-permute-done((bf16[384,128]{1,0:T(8,128)(2,1)S(1)}, bf16[384,128]{1,0:T(8,128)(2,1)S(1)}, u32[]{:S(2)}, u32[]{:S(2)}) %collective-permute-start.5) | collective-permute-done | bytes 98336 | tf_op jit(solution)/shard_map/ppermute | solution.py:169
  27.6 0.0 copy-done.3
  27.6 0.1 shard_map.96
  27.7 0.0 collective-permute-done.7.refs_2_
  27.7 1.4 %collective-permute-done.8.refs_3_ = bf16[384,128]{1,0:T(8,128)(2,1)S(1)} collective-permute-done((bf16[384,128]{1,0:T(8,128)(2,1)S(1)}, bf16[384,128]{1,0:T(8,128)(2,1)S(1)}, u32[]{:S(2)}, u32[]{:S(2)}) %collective-permute-start.8) | collective-permute-done | bytes 98336 | tf_op jit(solution)/shard_map/ppermute | solution.py:169
  29.1 0.3 shard_map.101
  29.4 0.1 collective-permute-start.10
  29.4 0.3 shard_map.98
  29.7 0.6 %collective-permute-start.9 = (bf16[192,384]{1,0:T(8,128)(2,1)S(1)}, bf16[192,384]{1,0:T(8,128)(2,1)S(1)}, u32[]{:S(2)}, u32[]{:S(2)}) collective-permute-start(bf16[192,384]{1,0:T(8,128)(2,1)S(1)} %shard_map.98), channel_id=1, source_target_pairs={{0,1},{1,0},{2,3},{3,2},{4,5},{5,4},{6,7},{7,6},{8,9},{9,8},{10,11... | collective-permute-start | bytes 442376 | tf_op jit(solution)/shard_map/ppermute | solution.py:169
  30.3 0.3 shard_map.97.keep_ref
  30.5 0.3 shard_map.100.keep_ref
  30.8 0.0 collective-permute-done.10.got_ref
  30.8 1.9 %collective-permute-start.11 = (bf16[96,384]{1,0:T(8,128)(2,1)S(1)}, bf16[96,384]{1,0:T(8,128)(2,1)S(1)}, u32[]{:S(2)}, u32[]{:S(2)}) collective-permute-start(bf16[96,384]{1,0:T(8,128)(2,1)S(1)} %get-tuple-element.40), channel_id=1, source_target_pairs={{0,16},{1,17},{2,18},{3,19},{4,20},{5,21},{6,22},{7,23},{8,24},{9,... | collective-permute-start | bytes 221192 | tf_op jit(solution)/shard_map/ppermute | solution.py:169
  32.7 1.6 %collective-permute-start.12 = (bf16[96,384]{1,0:T(8,128)(2,1)S(1)}, bf16[96,384]{1,0:T(8,128)(2,1)S(1)}, u32[]{:S(2)}, u32[]{:S(2)}) collective-permute-start(bf16[96,384]{1,0:T(8,128)(2,1)S(1)} %get-tuple-element.41), channel_id=1, source_target_pairs={{0,24},{1,25},{2,26},{3,27},{4,28},{5,29},{6,30},{7,31},{8,16},{9,... | collective-permute-start | bytes 221192 | tf_op jit(solution)/shard_map/ppermute | solution.py:169
  34.3 0.0 collective-permute-done.9.got_ref
  34.4 0.1 collective-permute-start.13
  34.5 5.4 %collective-permute-done.11.refs_1_ = bf16[96,384]{1,0:T(8,128)(2,1)S(1)} collective-permute-done((bf16[96,384]{1,0:T(8,128)(2,1)S(1)}, bf16[96,384]{1,0:T(8,128)(2,1)S(1)}, u32[]{:S(2)}, u32[]{:S(2)}) %collective-permute-start.11) | collective-permute-done | bytes 73760 | tf_op jit(solution)/shard_map/ppermute | solution.py:169
  39.9 0.0 collective-permute-done.12.refs_2_
  39.9 0.8 %collective-permute-done.13.refs_3_ = bf16[96,384]{1,0:T(8,128)(2,1)S(1)} collective-permute-done((bf16[96,384]{1,0:T(8,128)(2,1)S(1)}, bf16[96,384]{1,0:T(8,128)(2,1)S(1)}, u32[]{:S(2)}, u32[]{:S(2)}) %collective-permute-start.13) | collective-permute-done | bytes 73760 | tf_op jit(solution)/shard_map/ppermute | solution.py:169
  40.8 1.2 %collective-permute-start.15 = (bf16[96,384]{1,0:T(8,128)(2,1)S(1)}, bf16[96,384]{1,0:T(8,128)(2,1)S(1)}, u32[]{:S(2)}, u32[]{:S(2)}) collective-permute-start(bf16[96,384]{1,0:T(8,128)(2,1)S(1)} %shard_map.103.refs_0_), channel_id=1, source_target_pairs={{0,2},{1,3},{2,0},{3,1},{4,6},{5,7},{6,4},{7,5},{8,10},{9,11},{10,... | collective-permute-start | bytes 221192 | tf_op jit(solution)/shard_map/ppermute | solution.py:169
  42.0 0.0 collective-permute-start.14
  42.0 3.2 %collective-permute-done.15.refs_2_ = bf16[96,384]{1,0:T(8,128)(2,1)S(1)} collective-permute-done((bf16[96,384]{1,0:T(8,128)(2,1)S(1)}, bf16[96,384]{1,0:T(8,128)(2,1)S(1)}, u32[]{:S(2)}, u32[]{:S(2)}) %collective-permute-start.15) | collective-permute-done | bytes 73760 | tf_op jit(solution)/shard_map/ppermute | solution.py:169
  45.2 0.0 collective-permute-start.16
  45.2 0.7 %convert_element_type.3 = bf16[128,768]{1,0:T(8,128)(2,1)} convert(f32[128,768]{1,0:T(8,128)S(1)} %get-tuple-element.26) | non-fusion elementwise | flops 98304 | bytes 589824 | tf_op jit(solution)/shard_map/convert_element_type | solution.py:355
  45.9 0.0 collective-permute-done.14.refs_1_
  45.9 0.6 %collective-permute-done.16.refs_3_ = bf16[96,384]{1,0:T(8,128)(2,1)S(1)} collective-permute-done((bf16[96,384]{1,0:T(8,128)(2,1)S(1)}, bf16[96,384]{1,0:T(8,128)(2,1)S(1)}, u32[]{:S(2)}, u32[]{:S(2)}) %collective-permute-start.16) | collective-permute-done | bytes 73760 | tf_op jit(solution)/shard_map/ppermute | solution.py:169
  46.5 0.9 %shard_map.104 = (f32[96,768]{1,0:T(8,128)}, f32[96,768]{1,0:T(8,128)}) custom-call(bf16[96,384]{1,0:T(8,128)(2,1)S(1)} %shard_map.103.refs_0_, bf16[96,384]{1,0:T(8,128)(2,1)S(1)} %collective-permute-done.14.refs_1_, bf16[96,384]{1,0:T(8,128)(2,1)S(1)} %collective-permute-done.15.refs_2_, bf16[96,384]{1,0:T(8,128)(2,1)S(1)} %collective-permute-done.16.refs_3_), custom_call_target="tpu_custom_call" | custom-call | bytes 884736 | tf_op jit(solution)/shard_map/pallas_call | solution.py:23
  (3 shorter events, 0.1 us)
Async XLA Ops:
  0.6 15.2 %copy-start = (bf16[768,768]{1,0:T(8,128)(2,1)S(1)}, bf16[768,768]{1,0:T(8,128)(2,1)}, u32[]{:S(2)}) copy-start(bf16[768,768]{1,0:T(8,128)(2,1)} %param.12) | copy-start | bytes 3538948
  2.9 14.2 %copy-start.1 = (bf16[768,768]{1,0:T(8,128)(2,1)S(1)}, bf16[768,768]{1,0:T(8,128)(2,1)}, u32[]{:S(2)}) copy-start(bf16[768,768]{1,0:T(8,128)(2,1)} %w_ref.1) | copy-start | bytes 3538948
  2.9 14.2 %copy-start.2 = (bf16[128,768]{1,0:T(8,128)(2,1)S(1)}, bf16[128,768]{1,0:T(8,128)(2,1)}, u32[]{:S(2)}) copy-start(bf16[128,768]{1,0:T(8,128)(2,1)} %cot_ref.1) | copy-start | bytes 589828
  2.9 14.2 %copy-start.4 = (s32[1,1,8,12]{3,2,1,0:T(8,128)S(1)}, s32[1,1,8,12]{3,2,1,0:T(8,128)}, u32[]{:S(2)}) copy-start(s32[1,1,8,12]{3,2,1,0:T(8,128)} %param.10) | copy-start | bytes 1156
  2.9 14.2 %all-to-all-start = ((bf16[8,80,128]{2,1,0:T(8,128)(2,1)}), bf16[8,80,128]{2,1,0:T(8,128)(2,1)S(1)}, u32[]{:S(2)}, u32[]{:S(2)}) async-start(bf16[8,80,128]{2,1,0:T(8,128)(2,1)} %bitcast.10), calls=%async_computation | async-start | bytes 327680 | tf_op jit(solution)/shard_map/all_to_all | solution.py:281
  12.3 8.3 %collective-permute-start = (bf16[384,128]{1,0:T(8,128)(2,1)}, bf16[384,128]{1,0:T(8,128)(2,1)S(1)}, u32[]{:S(2)}, u32[]{:S(2)}) collective-permute-start(bf16[384,128]{1,0:T(8,128)(2,1)} %get-tuple-element.27), channel_id=1, source_target_pairs={{0,6},{1,7},{2,4},{3,5},{4,2},{5,3},{6,0},{7,1},{8,14},{9,15},{10,... | collective-permute-start | bytes 294920 | tf_op jit(solution)/shard_map/ppermute | solution.py:169
  13.8 7.5 %collective-permute-start.1 = (bf16[384,128]{1,0:T(8,128)(2,1)}, bf16[384,128]{1,0:T(8,128)(2,1)S(1)}, u32[]{:S(2)}, u32[]{:S(2)}) collective-permute-start(bf16[384,128]{1,0:T(8,128)(2,1)} %get-tuple-element.27), channel_id=1, source_target_pairs={{0,4},{1,5},{2,6},{3,7},{4,0},{5,1},{6,2},{7,3},{8,12},{9,13},{10,... | collective-permute-start | bytes 294920 | tf_op jit(solution)/shard_map/ppermute | solution.py:169
  15.3 6.7 %collective-permute-start.2 = (bf16[384,128]{1,0:T(8,128)(2,1)}, bf16[384,128]{1,0:T(8,128)(2,1)S(1)}, u32[]{:S(2)}, u32[]{:S(2)}) collective-permute-start(bf16[384,128]{1,0:T(8,128)(2,1)} %get-tuple-element.28.refs_3_), channel_id=1, source_target_pairs={{0,2},{1,3},{2,0},{3,1},{4,6},{5,7},{6,4},{7,5},{8,10},{9,11},{10,... | collective-permute-start | bytes 294920 | tf_op jit(solution)/shard_map/ppermute | solution.py:169
  17.1 10.5 %copy-start.3 = (bf16[384,128]{1,0:T(8,128)(2,1)S(1)}, bf16[384,128]{1,0:T(8,128)(2,1)}, u32[]{:S(2)}) copy-start(bf16[384,128]{1,0:T(8,128)(2,1)} %get-tuple-element.28.refs_3_) | copy-start | bytes 294916
  17.9 5.1 %collective-permute-start.4 = (bf16[384,128]{1,0:T(8,128)(2,1)S(1)}, bf16[384,128]{1,0:T(8,128)(2,1)S(1)}, u32[]{:S(2)}, u32[]{:S(2)}) collective-permute-start(bf16[384,128]{1,0:T(8,128)(2,1)S(1)} %get-tuple-element.30), channel_id=1, source_target_pairs={{0,4},{1,5},{2,6},{3,7},{4,0},{5,1},{6,2},{7,3},{8,12},{9,13},{10,... | collective-permute-start | bytes 294920 | tf_op jit(solution)/shard_map/ppermute | solution.py:169
  19.1 5.4 %collective-permute-start.6 = (bf16[384,128]{1,0:T(8,128)(2,1)S(1)}, bf16[384,128]{1,0:T(8,128)(2,1)S(1)}, u32[]{:S(2)}, u32[]{:S(2)}) collective-permute-start(bf16[384,128]{1,0:T(8,128)(2,1)S(1)} %get-tuple-element.34), channel_id=1, source_target_pairs={{0,2},{1,3},{2,0},{3,1},{4,6},{5,7},{6,4},{7,5},{8,10},{9,11},{10,... | collective-permute-start | bytes 294920 | tf_op jit(solution)/shard_map/ppermute | solution.py:169
  20.6 5.6 %collective-permute-start.3 = (bf16[384,128]{1,0:T(8,128)(2,1)S(1)}, bf16[384,128]{1,0:T(8,128)(2,1)S(1)}, u32[]{:S(2)}, u32[]{:S(2)}) collective-permute-start(bf16[384,128]{1,0:T(8,128)(2,1)S(1)} %get-tuple-element.29.refs_4_), channel_id=1, source_target_pairs={{0,2},{1,3},{2,0},{3,1},{4,6},{5,7},{6,4},{7,5},{8,10},{9,11},{10,... | collective-permute-start | bytes 294920 | tf_op jit(solution)/shard_map/ppermute | solution.py:169
  21.3 6.4 %collective-permute-start.7 = (bf16[384,128]{1,0:T(8,128)(2,1)S(1)}, bf16[384,128]{1,0:T(8,128)(2,1)S(1)}, u32[]{:S(2)}, u32[]{:S(2)}) collective-permute-start(bf16[384,128]{1,0:T(8,128)(2,1)S(1)} %get-tuple-element.33.refs_0_), channel_id=1, source_target_pairs={{0,4},{1,5},{2,6},{3,7},{4,0},{5,1},{6,2},{7,3},{8,12},{9,13},{10,... | collective-permute-start | bytes 294920 | tf_op jit(solution)/shard_map/ppermute | solution.py:169
  22.9 4.6 %collective-permute-start.5 = (bf16[384,128]{1,0:T(8,128)(2,1)S(1)}, bf16[384,128]{1,0:T(8,128)(2,1)S(1)}, u32[]{:S(2)}, u32[]{:S(2)}) collective-permute-start(bf16[384,128]{1,0:T(8,128)(2,1)S(1)} %collective-permute-done.4.refs_6_), channel_id=1, source_target_pairs={{0,2},{1,3},{2,0},{3,1},{4,6},{5,7},{6,4},{7,5},{8,10},{9,11},{10,... | collective-permute-start | bytes 294920 | tf_op jit(solution)/shard_map/ppermute | solution.py:169
  24.5 4.6 %collective-permute-start.8 = (bf16[384,128]{1,0:T(8,128)(2,1)S(1)}, bf16[384,128]{1,0:T(8,128)(2,1)S(1)}, u32[]{:S(2)}, u32[]{:S(2)}) collective-permute-start(bf16[384,128]{1,0:T(8,128)(2,1)S(1)} %collective-permute-done.6.refs_1_), channel_id=1, source_target_pairs={{0,4},{1,5},{2,6},{3,7},{4,0},{5,1},{6,2},{7,3},{8,12},{9,13},{10,... | collective-permute-start | bytes 294920 | tf_op jit(solution)/shard_map/ppermute | solution.py:169
  29.4 1.4 %collective-permute-start.10 = (bf16[192,384]{1,0:T(8,128)(2,1)S(1)}, bf16[192,384]{1,0:T(8,128)(2,1)S(1)}, u32[]{:S(2)}, u32[]{:S(2)}) collective-permute-start(bf16[192,384]{1,0:T(8,128)(2,1)S(1)} %shard_map.101), channel_id=1, source_target_pairs={{0,1},{1,0},{2,3},{3,2},{4,5},{5,4},{6,7},{7,6},{8,9},{9,8},{10,11... | collective-permute-start | bytes 442376 | tf_op jit(solution)/shard_map/ppermute | solution.py:169
  29.7 4.6 %collective-permute-start.9 = (bf16[192,384]{1,0:T(8,128)(2,1)S(1)}, bf16[192,384]{1,0:T(8,128)(2,1)S(1)}, u32[]{:S(2)}, u32[]{:S(2)}) collective-permute-start(bf16[192,384]{1,0:T(8,128)(2,1)S(1)} %shard_map.98), channel_id=1, source_target_pairs={{0,1},{1,0},{2,3},{3,2},{4,5},{5,4},{6,7},{7,6},{8,9},{9,8},{10,11... | collective-permute-start | bytes 442376 | tf_op jit(solution)/shard_map/ppermute | solution.py:169
  30.8 9.1 %collective-permute-start.11 = (bf16[96,384]{1,0:T(8,128)(2,1)S(1)}, bf16[96,384]{1,0:T(8,128)(2,1)S(1)}, u32[]{:S(2)}, u32[]{:S(2)}) collective-permute-start(bf16[96,384]{1,0:T(8,128)(2,1)S(1)} %get-tuple-element.40), channel_id=1, source_target_pairs={{0,16},{1,17},{2,18},{3,19},{4,20},{5,21},{6,22},{7,23},{8,24},{9,... | collective-permute-start | bytes 221192 | tf_op jit(solution)/shard_map/ppermute | solution.py:169
  32.7 7.2 %collective-permute-start.12 = (bf16[96,384]{1,0:T(8,128)(2,1)S(1)}, bf16[96,384]{1,0:T(8,128)(2,1)S(1)}, u32[]{:S(2)}, u32[]{:S(2)}) collective-permute-start(bf16[96,384]{1,0:T(8,128)(2,1)S(1)} %get-tuple-element.41), channel_id=1, source_target_pairs={{0,24},{1,25},{2,26},{3,27},{4,28},{5,29},{6,30},{7,31},{8,16},{9,... | collective-permute-start | bytes 221192 | tf_op jit(solution)/shard_map/ppermute | solution.py:169
  34.4 6.4 %collective-permute-start.13 = (bf16[96,384]{1,0:T(8,128)(2,1)S(1)}, bf16[96,384]{1,0:T(8,128)(2,1)S(1)}, u32[]{:S(2)}, u32[]{:S(2)}) collective-permute-start(bf16[96,384]{1,0:T(8,128)(2,1)S(1)} %get-tuple-element.42), channel_id=1, source_target_pairs={{0,8},{1,9},{2,10},{3,11},{4,12},{5,13},{6,14},{7,15},{8,0},{9,1},... | collective-permute-start | bytes 221192 | tf_op jit(solution)/shard_map/ppermute | solution.py:169
  40.8 4.4 %collective-permute-start.15 = (bf16[96,384]{1,0:T(8,128)(2,1)S(1)}, bf16[96,384]{1,0:T(8,128)(2,1)S(1)}, u32[]{:S(2)}, u32[]{:S(2)}) collective-permute-start(bf16[96,384]{1,0:T(8,128)(2,1)S(1)} %shard_map.103.refs_0_), channel_id=1, source_target_pairs={{0,2},{1,3},{2,0},{3,1},{4,6},{5,7},{6,4},{7,5},{8,10},{9,11},{10,... | collective-permute-start | bytes 221192 | tf_op jit(solution)/shard_map/ppermute | solution.py:169
  42.0 3.9 %collective-permute-start.14 = (bf16[96,384]{1,0:T(8,128)(2,1)S(1)}, bf16[96,384]{1,0:T(8,128)(2,1)S(1)}, u32[]{:S(2)}, u32[]{:S(2)}) collective-permute-start(bf16[96,384]{1,0:T(8,128)(2,1)S(1)} %shard_map.103.refs_0_), channel_id=1, source_target_pairs={{0,1},{1,0},{2,3},{3,2},{4,5},{5,4},{6,7},{7,6},{8,9},{9,8},{10,11... | collective-permute-start | bytes 221192 | tf_op jit(solution)/shard_map/ppermute | solution.py:169
  45.2 1.3 %collective-permute-start.16 = (bf16[96,384]{1,0:T(8,128)(2,1)S(1)}, bf16[96,384]{1,0:T(8,128)(2,1)S(1)}, u32[]{:S(2)}, u32[]{:S(2)}) collective-permute-start(bf16[96,384]{1,0:T(8,128)(2,1)S(1)} %collective-permute-done.15.refs_2_), channel_id=1, source_target_pairs={{0,1},{1,0},{2,3},{3,2},{4,5},{5,4},{6,7},{7,6},{8,9},{9,8},{10,11... | collective-permute-start | bytes 221192 | tf_op jit(solution)/shard_map/ppermute | solution.py:169

commit v8 on v7

--- a/solution.py
+++ b/solution.py
@@ -172,7 +172,7 @@
         up = [(z, x) for z in reversed(range(self.nz)) for x in reversed(range(self.gx))]
         down = [(z, x) for z in range(self.nz) for x in range(self.gx)]
         turns = [at for pair in zip(up, down) for at in pair]
-        return [z * self.gx + x for z, x in turns[:self.ns]]
+        return [z * self.gx + x for z, x in turns[:self.ns]][::-1]
 
 
 def write_rows(plan, trans_ref, *outs):

time: 47.6 us -> 46.6 us (0.979)
  starting transfers between devices: 25.2 us -> 23.5 us
  waiting for transfers between devices: 14.2 us -> 14.9 us
    all_to_all x1, starting transfers between devices: 9.4 us -> 7.95 us  [per_device(): lax.all_to_all(sums.reshape(ns, packed, 128), 'store', split_axis=0, conc...]
    all_to_all x1, waiting for transfers between devices: 0.01 us -> 0.49 us  [per_device(): lax.all_to_all(sums.reshape(ns, packed, 128), 'store', split_axis=0, conc...]
  transfers between devices with their start and end apart: 18 -> 18, of which waited for: 9 -> 8; matrix products, arithmetic and copies ran while one was open for 4% -> 4% of each run, Pallas kernels for 4% -> 4%
where the time goes in v8:
time: 46.6 us; the launch traced here: 46.3 us
  starting transfers between devices  23.5 us (50%)
  waiting for transfers between devices  14.9 us (32%)
  Pallas kernels  5.12 us (11%)
  matrix products  1.25 us (3%)
  between operations  0.78 us (2%)
  other arithmetic  0.7 us (2%)
    ppermute x17, starting transfers between devices, send(): return lax.ppermute(array, ('store', 'trainer'), pairs)  15.6 us
    ppermute x17, waiting for transfers between devices, send(): return lax.ppermute(array, ('store', 'trainer'), pairs)  14.4 us
    all_to_all x1, starting transfers between devices, per_device(): lax.all_to_all(sums.reshape(ns, packed, 128), 'store', split_axis=0, conc...  7.95 us
    pallas_call x11, Pallas kernels, call(): pl.pallas_call(body, out_shape=list(outs), in_specs=[VMEM] * len(args) +...  5.12 us
    dot_general x1, matrix products, dot(): return jnp.dot(a, b, preferred_element_type=F32)  1.25 us
  transfers between devices with their start and end apart: 18, of which 8 were waited for; matrix products, arithmetic and copies ran while one was open for 4% of the time, Pallas kernels for 4%

profile of v8, /device:TPU:0, one launch (start us, length us, event | category | flops | bytes accessed | tf_op | source)
XLA Modules:
  0.0 46.3 jit_solution(7744007166274093320)
XLA Ops:
  0.6 0.0 copy-start
  0.6 2.2 %shard_map.94 = (bf16[640,128]{1,0:T(8,128)(2,1)}, bf16[128,768]{1,0:T(8,128)(2,1)}, bf16[384,128]{1,0:T(8,128)(2,1)}, bf16[384,128]{1,0:T(8,128)(2,1)}) custom-call(f32[128,768]{1,0:T(8,128)} %feat_hbm.1, s32[8,2,12]{2,1,0:T(2,128)} %bitcast.11, f32[128,768]{1,0:T(8,128)} %rest_0_.1), custom_call_target="tpu_custom_call" | custom-call | flops 50331648 | bytes 557056 | tf_op jit(solution)/shard_map/pallas_call | solution.py:23
  2.9 0.0 copy-start.1
  2.9 0.0 copy-start.2
  2.9 0.0 copy-start.4
  2.9 8.0 %all-to-all-start = ((bf16[8,80,128]{2,1,0:T(8,128)(2,1)}), bf16[8,80,128]{2,1,0:T(8,128)(2,1)S(1)}, u32[]{:S(2)}, u32[]{:S(2)}) async-start(bf16[8,80,128]{2,1,0:T(8,128)(2,1)} %bitcast.10), calls=%async_computation | async-start | bytes 327680 | tf_op jit(solution)/shard_map/all_to_all | solution.py:281
  10.9 1.5 %collective-permute-start = (bf16[384,128]{1,0:T(8,128)(2,1)}, bf16[384,128]{1,0:T(8,128)(2,1)S(1)}, u32[]{:S(2)}, u32[]{:S(2)}) collective-permute-start(bf16[384,128]{1,0:T(8,128)(2,1)} %get-tuple-element.27), channel_id=1, source_target_pairs={{0,6},{1,7},{2,4},{3,5},{4,2},{5,3},{6,0},{7,1},{8,14},{9,15},{10,... | collective-permute-start | bytes 294920 | tf_op jit(solution)/shard_map/ppermute | solution.py:169
  12.4 1.5 %collective-permute-start.1 = (bf16[384,128]{1,0:T(8,128)(2,1)}, bf16[384,128]{1,0:T(8,128)(2,1)S(1)}, u32[]{:S(2)}, u32[]{:S(2)}) collective-permute-start(bf16[384,128]{1,0:T(8,128)(2,1)} %get-tuple-element.27), channel_id=1, source_target_pairs={{0,4},{1,5},{2,6},{3,7},{4,0},{5,1},{6,2},{7,3},{8,12},{9,13},{10,... | collective-permute-start | bytes 294920 | tf_op jit(solution)/shard_map/ppermute | solution.py:169
  13.9 0.5 %collective-permute-start.2 = (bf16[384,128]{1,0:T(8,128)(2,1)}, bf16[384,128]{1,0:T(8,128)(2,1)S(1)}, u32[]{:S(2)}, u32[]{:S(2)}) collective-permute-start(bf16[384,128]{1,0:T(8,128)(2,1)} %get-tuple-element.28.refs_3_), channel_id=1, source_target_pairs={{0,2},{1,3},{2,0},{3,1},{4,6},{5,7},{6,4},{7,5},{8,10},{9,11},{10,... | collective-permute-start | bytes 294920 | tf_op jit(solution)/shard_map/ppermute | solution.py:169
  14.4 0.0 copy-done
  14.4 1.2 %fusion.self_ref = f32[128,768]{1,0:T(8,128)S(1)} fusion(bf16[128,768]{1,0:T(8,128)(2,1)} %get-tuple-element.25, bf16[768,768]{1,0:T(8,128)(2,1)S(1)} %copy-done), kind=kOutput, calls=%fused_computation | convolution fusion | flops 150994944 | bytes 1769472 | tf_op jit(solution)/shard_map/dot_general | solution.py:18
  15.6 0.0 copy-start.3
  15.6 0.5 %all-to-all-done = bf16[8,80,128]{2,1,0:T(8,128)(2,1)S(1)} async-done(((bf16[8,80,128]{2,1,0:T(8,128)(2,1)}), bf16[8,80,128]{2,1,0:T(8,128)(2,1)S(1)}, u32[]{:S(2)}, u32[]{:S(2)}) %all-to-all-start) | async-done | bytes 163872 | tf_op jit(solution)/shard_map/all_to_all | solution.py:281
  16.1 0.0 copy-done.1
  16.1 0.0 copy-done.2
  16.1 0.0 copy-done.4
  16.1 0.7 %shard_map.95 = (f32[128,768]{1,0:T(8,128)S(1)}, bf16[384,128]{1,0:T(8,128)(2,1)S(1)}, bf16[384,128]{1,0:T(8,128)(2,1)S(1)}, bf16[384,128]{1,0:T(8,128)(2,1)S(1)}, bf16[384,128]{1,0:T(8,128)(2,1)S(1)}) custom-call(bf16[640,128]{1,0:T(8,128)(2,1)S(1)} %bitcast.8, s32[8,12]{1,0:T(8,128)S(1)} %bitcast.9, f32[128,768]{1,0:T(8,128)S(1)} %fusion.self_ref, ...), custom_call_target="tpu_custom_call" | custom-call | flops 176160768 | bytes 2720128 | tf_op jit(solution)/shard_map/pallas_call | solution.py:23
  16.9 0.8 %collective-permute-start.4 = (bf16[384,128]{1,0:T(8,128)(2,1)S(1)}, bf16[384,128]{1,0:T(8,128)(2,1)S(1)}, u32[]{:S(2)}, u32[]{:S(2)}) collective-permute-start(bf16[384,128]{1,0:T(8,128)(2,1)S(1)} %get-tuple-element.30), channel_id=1, source_target_pairs={{0,4},{1,5},{2,6},{3,7},{4,0},{5,1},{6,2},{7,3},{8,12},{9,13},{10,... | collective-permute-start | bytes 294920 | tf_op jit(solution)/shard_map/ppermute | solution.py:169
  17.7 1.5 %collective-permute-start.6 = (bf16[384,128]{1,0:T(8,128)(2,1)S(1)}, bf16[384,128]{1,0:T(8,128)(2,1)S(1)}, u32[]{:S(2)}, u32[]{:S(2)}) collective-permute-start(bf16[384,128]{1,0:T(8,128)(2,1)S(1)} %get-tuple-element.34), channel_id=1, source_target_pairs={{0,2},{1,3},{2,0},{3,1},{4,6},{5,7},{6,4},{7,5},{8,10},{9,11},{10,... | collective-permute-start | bytes 294920 | tf_op jit(solution)/shard_map/ppermute | solution.py:169
  19.2 0.0 collective-permute-done.refs_0_
  19.2 0.5 %collective-permute-start.3 = (bf16[384,128]{1,0:T(8,128)(2,1)S(1)}, bf16[384,128]{1,0:T(8,128)(2,1)S(1)}, u32[]{:S(2)}, u32[]{:S(2)}) collective-permute-start(bf16[384,128]{1,0:T(8,128)(2,1)S(1)} %get-tuple-element.29.refs_4_), channel_id=1, source_target_pairs={{0,2},{1,3},{2,0},{3,1},{4,6},{5,7},{6,4},{7,5},{8,10},{9,11},{10,... | collective-permute-start | bytes 294920 | tf_op jit(solution)/shard_map/ppermute | solution.py:169
  19.7 0.0 collective-permute-done.1.refs_1_
  19.7 1.3 %collective-permute-start.7 = (bf16[384,128]{1,0:T(8,128)(2,1)S(1)}, bf16[384,128]{1,0:T(8,128)(2,1)S(1)}, u32[]{:S(2)}, u32[]{:S(2)}) collective-permute-start(bf16[384,128]{1,0:T(8,128)(2,1)S(1)} %get-tuple-element.33.refs_0_), channel_id=1, source_target_pairs={{0,4},{1,5},{2,6},{3,7},{4,0},{5,1},{6,2},{7,3},{8,12},{9,13},{10,... | collective-permute-start | bytes 294920 | tf_op jit(solution)/shard_map/ppermute | solution.py:169
  21.0 0.0 collective-permute-done.2.refs_2_
  21.0 1.1 %collective-permute-done.4.refs_6_ = bf16[384,128]{1,0:T(8,128)(2,1)S(1)} collective-permute-done((bf16[384,128]{1,0:T(8,128)(2,1)S(1)}, bf16[384,128]{1,0:T(8,128)(2,1)S(1)}, u32[]{:S(2)}, u32[]{:S(2)}) %collective-permute-start.4) | collective-permute-done | bytes 98336 | tf_op jit(solution)/shard_map/ppermute | solution.py:169
  22.1 1.4 %collective-permute-start.5 = (bf16[384,128]{1,0:T(8,128)(2,1)S(1)}, bf16[384,128]{1,0:T(8,128)(2,1)S(1)}, u32[]{:S(2)}, u32[]{:S(2)}) collective-permute-start(bf16[384,128]{1,0:T(8,128)(2,1)S(1)} %collective-permute-done.4.refs_6_), channel_id=1, source_target_pairs={{0,2},{1,3},{2,0},{3,1},{4,6},{5,7},{6,4},{7,5},{8,10},{9,11},{10,... | collective-permute-start | bytes 294920 | tf_op jit(solution)/shard_map/ppermute | solution.py:169
  23.4 0.0 collective-permute-done.6.refs_1_
  23.4 1.2 %collective-permute-start.8 = (bf16[384,128]{1,0:T(8,128)(2,1)S(1)}, bf16[384,128]{1,0:T(8,128)(2,1)S(1)}, u32[]{:S(2)}, u32[]{:S(2)}) collective-permute-start(bf16[384,128]{1,0:T(8,128)(2,1)S(1)} %collective-permute-done.6.refs_1_), channel_id=1, source_target_pairs={{0,4},{1,5},{2,6},{3,7},{4,0},{5,1},{6,2},{7,3},{8,12},{9,13},{10,... | collective-permute-start | bytes 294920 | tf_op jit(solution)/shard_map/ppermute | solution.py:169
  24.7 0.0 collective-permute-done.3.refs_5_
  24.7 2.0 %collective-permute-done.5.refs_7_ = bf16[384,128]{1,0:T(8,128)(2,1)S(1)} collective-permute-done((bf16[384,128]{1,0:T(8,128)(2,1)S(1)}, bf16[384,128]{1,0:T(8,128)(2,1)S(1)}, u32[]{:S(2)}, u32[]{:S(2)}) %collective-permute-start.5) | collective-permute-done | bytes 98336 | tf_op jit(solution)/shard_map/ppermute | solution.py:169
  26.7 0.0 copy-done.3
  26.7 0.1 shard_map.96
  26.8 0.0 collective-permute-done.7.refs_2_
  26.8 1.2 %collective-permute-done.8.refs_3_ = bf16[384,128]{1,0:T(8,128)(2,1)S(1)} collective-permute-done((bf16[384,128]{1,0:T(8,128)(2,1)S(1)}, bf16[384,128]{1,0:T(8,128)(2,1)S(1)}, u32[]{:S(2)}, u32[]{:S(2)}) %collective-permute-start.8) | collective-permute-done | bytes 98336 | tf_op jit(solution)/shard_map/ppermute | solution.py:169
  28.1 0.3 shard_map.101
  28.3 0.1 collective-permute-start.10
  28.4 0.3 shard_map.98
  28.7 0.6 %collective-permute-start.9 = (bf16[192,384]{1,0:T(8,128)(2,1)S(1)}, bf16[192,384]{1,0:T(8,128)(2,1)S(1)}, u32[]{:S(2)}, u32[]{:S(2)}) collective-permute-start(bf16[192,384]{1,0:T(8,128)(2,1)S(1)} %shard_map.98), channel_id=1, source_target_pairs={{0,1},{1,0},{2,3},{3,2},{4,5},{5,4},{6,7},{7,6},{8,9},{9,8},{10,11... | collective-permute-start | bytes 442376 | tf_op jit(solution)/shard_map/ppermute | solution.py:169
  29.2 0.3 shard_map.97.keep_ref
  29.5 0.3 shard_map.100.keep_ref
  29.8 0.0 collective-permute-done.10.got_ref
  29.8 1.7 %collective-permute-start.11 = (bf16[96,384]{1,0:T(8,128)(2,1)S(1)}, bf16[96,384]{1,0:T(8,128)(2,1)S(1)}, u32[]{:S(2)}, u32[]{:S(2)}) collective-permute-start(bf16[96,384]{1,0:T(8,128)(2,1)S(1)} %get-tuple-element.40), channel_id=1, source_target_pairs={{0,16},{1,17},{2,18},{3,19},{4,20},{5,21},{6,22},{7,23},{8,24},{9,... | collective-permute-start | bytes 221192 | tf_op jit(solution)/shard_map/ppermute | solution.py:169
  31.6 1.6 %collective-permute-start.12 = (bf16[96,384]{1,0:T(8,128)(2,1)S(1)}, bf16[96,384]{1,0:T(8,128)(2,1)S(1)}, u32[]{:S(2)}, u32[]{:S(2)}) collective-permute-start(bf16[96,384]{1,0:T(8,128)(2,1)S(1)} %get-tuple-element.41), channel_id=1, source_target_pairs={{0,24},{1,25},{2,26},{3,27},{4,28},{5,29},{6,30},{7,31},{8,16},{9,... | collective-permute-start | bytes 221192 | tf_op jit(solution)/shard_map/ppermute | solution.py:169
  33.2 0.0 collective-permute-done.9.got_ref
  33.2 0.2 collective-permute-start.13
  33.5 5.3 %collective-permute-done.11.refs_1_ = bf16[96,384]{1,0:T(8,128)(2,1)S(1)} collective-permute-done((bf16[96,384]{1,0:T(8,128)(2,1)S(1)}, bf16[96,384]{1,0:T(8,128)(2,1)S(1)}, u32[]{:S(2)}, u32[]{:S(2)}) %collective-permute-start.11) | collective-permute-done | bytes 73760 | tf_op jit(solution)/shard_map/ppermute | solution.py:169
  38.7 0.0 collective-permute-done.12.refs_2_
  38.8 1.0 %collective-permute-done.13.refs_3_ = bf16[96,384]{1,0:T(8,128)(2,1)S(1)} collective-permute-done((bf16[96,384]{1,0:T(8,128)(2,1)S(1)}, bf16[96,384]{1,0:T(8,128)(2,1)S(1)}, u32[]{:S(2)}, u32[]{:S(2)}) %collective-permute-start.13) | collective-permute-done | bytes 73760 | tf_op jit(solution)/shard_map/ppermute | solution.py:169
  39.8 1.1 %collective-permute-start.15 = (bf16[96,384]{1,0:T(8,128)(2,1)S(1)}, bf16[96,384]{1,0:T(8,128)(2,1)S(1)}, u32[]{:S(2)}, u32[]{:S(2)}) collective-permute-start(bf16[96,384]{1,0:T(8,128)(2,1)S(1)} %shard_map.103.refs_0_), channel_id=1, source_target_pairs={{0,2},{1,3},{2,0},{3,1},{4,6},{5,7},{6,4},{7,5},{8,10},{9,11},{10,... | collective-permute-start | bytes 221192 | tf_op jit(solution)/shard_map/ppermute | solution.py:169
  40.9 0.0 collective-permute-start.14
  40.9 3.3 %collective-permute-done.15.refs_2_ = bf16[96,384]{1,0:T(8,128)(2,1)S(1)} collective-permute-done((bf16[96,384]{1,0:T(8,128)(2,1)S(1)}, bf16[96,384]{1,0:T(8,128)(2,1)S(1)}, u32[]{:S(2)}, u32[]{:S(2)}) %collective-permute-start.15) | collective-permute-done | bytes 73760 | tf_op jit(solution)/shard_map/ppermute | solution.py:169
  44.2 0.0 collective-permute-start.16
  44.2 0.7 %convert_element_type.3 = bf16[128,768]{1,0:T(8,128)(2,1)} convert(f32[128,768]{1,0:T(8,128)S(1)} %get-tuple-element.26) | non-fusion elementwise | flops 98304 | bytes 589824 | tf_op jit(solution)/shard_map/convert_element_type | solution.py:355
  44.9 0.0 collective-permute-done.14.refs_1_
  44.9 0.6 %collective-permute-done.16.refs_3_ = bf16[96,384]{1,0:T(8,128)(2,1)S(1)} collective-permute-done((bf16[96,384]{1,0:T(8,128)(2,1)S(1)}, bf16[96,384]{1,0:T(8,128)(2,1)S(1)}, u32[]{:S(2)}, u32[]{:S(2)}) %collective-permute-start.16) | collective-permute-done | bytes 73760 | tf_op jit(solution)/shard_map/ppermute | solution.py:169
  45.4 0.9 %shard_map.104 = (f32[96,768]{1,0:T(8,128)}, f32[96,768]{1,0:T(8,128)}) custom-call(bf16[96,384]{1,0:T(8,128)(2,1)S(1)} %shard_map.103.refs_0_, bf16[96,384]{1,0:T(8,128)(2,1)S(1)} %collective-permute-done.14.refs_1_, bf16[96,384]{1,0:T(8,128)(2,1)S(1)} %collective-permute-done.15.refs_2_, bf16[96,384]{1,0:T(8,128)(2,1)S(1)} %collective-permute-done.16.refs_3_), custom_call_target="tpu_custom_call" | custom-call | bytes 884736 | tf_op jit(solution)/shard_map/pallas_call | solution.py:23
  (3 shorter events, 0.1 us)
Async XLA Ops:
  0.6 13.7 %copy-start = (bf16[768,768]{1,0:T(8,128)(2,1)S(1)}, bf16[768,768]{1,0:T(8,128)(2,1)}, u32[]{:S(2)}) copy-start(bf16[768,768]{1,0:T(8,128)(2,1)} %param.12) | copy-start | bytes 3538948
  2.9 13.2 %copy-start.1 = (bf16[768,768]{1,0:T(8,128)(2,1)S(1)}, bf16[768,768]{1,0:T(8,128)(2,1)}, u32[]{:S(2)}) copy-start(bf16[768,768]{1,0:T(8,128)(2,1)} %w_ref.1) | copy-start | bytes 3538948
  2.9 13.2 %copy-start.2 = (bf16[128,768]{1,0:T(8,128)(2,1)S(1)}, bf16[128,768]{1,0:T(8,128)(2,1)}, u32[]{:S(2)}) copy-start(bf16[128,768]{1,0:T(8,128)(2,1)} %cot_ref.1) | copy-start | bytes 589828
  2.9 13.2 %copy-start.4 = (s32[1,1,8,12]{3,2,1,0:T(8,128)S(1)}, s32[1,1,8,12]{3,2,1,0:T(8,128)}, u32[]{:S(2)}) copy-start(s32[1,1,8,12]{3,2,1,0:T(8,128)} %param.10) | copy-start | bytes 1156
  2.9 13.2 %all-to-all-start = ((bf16[8,80,128]{2,1,0:T(8,128)(2,1)}), bf16[8,80,128]{2,1,0:T(8,128)(2,1)S(1)}, u32[]{:S(2)}, u32[]{:S(2)}) async-start(bf16[8,80,128]{2,1,0:T(8,128)(2,1)} %bitcast.10), calls=%async_computation | async-start | bytes 327680 | tf_op jit(solution)/shard_map/all_to_all | solution.py:281
  10.9 8.3 %collective-permute-start = (bf16[384,128]{1,0:T(8,128)(2,1)}, bf16[384,128]{1,0:T(8,128)(2,1)S(1)}, u32[]{:S(2)}, u32[]{:S(2)}) collective-permute-start(bf16[384,128]{1,0:T(8,128)(2,1)} %get-tuple-element.27), channel_id=1, source_target_pairs={{0,6},{1,7},{2,4},{3,5},{4,2},{5,3},{6,0},{7,1},{8,14},{9,15},{10,... | collective-permute-start | bytes 294920 | tf_op jit(solution)/shard_map/ppermute | solution.py:169
  12.4 7.3 %collective-permute-start.1 = (bf16[384,128]{1,0:T(8,128)(2,1)}, bf16[384,128]{1,0:T(8,128)(2,1)S(1)}, u32[]{:S(2)}, u32[]{:S(2)}) collective-permute-start(bf16[384,128]{1,0:T(8,128)(2,1)} %get-tuple-element.27), channel_id=1, source_target_pairs={{0,4},{1,5},{2,6},{3,7},{4,0},{5,1},{6,2},{7,3},{8,12},{9,13},{10,... | collective-permute-start | bytes 294920 | tf_op jit(solution)/shard_map/ppermute | solution.py:169
  13.9 7.2 %collective-permute-start.2 = (bf16[384,128]{1,0:T(8,128)(2,1)}, bf16[384,128]{1,0:T(8,128)(2,1)S(1)}, u32[]{:S(2)}, u32[]{:S(2)}) collective-permute-start(bf16[384,128]{1,0:T(8,128)(2,1)} %get-tuple-element.28.refs_3_), channel_id=1, source_target_pairs={{0,2},{1,3},{2,0},{3,1},{4,6},{5,7},{6,4},{7,5},{8,10},{9,11},{10,... | collective-permute-start | bytes 294920 | tf_op jit(solution)/shard_map/ppermute | solution.py:169
  15.6 11.1 %copy-start.3 = (bf16[384,128]{1,0:T(8,128)(2,1)S(1)}, bf16[384,128]{1,0:T(8,128)(2,1)}, u32[]{:S(2)}) copy-start(bf16[384,128]{1,0:T(8,128)(2,1)} %get-tuple-element.28.refs_3_) | copy-start | bytes 294916
  16.9 5.2 %collective-permute-start.4 = (bf16[384,128]{1,0:T(8,128)(2,1)S(1)}, bf16[384,128]{1,0:T(8,128)(2,1)S(1)}, u32[]{:S(2)}, u32[]{:S(2)}) collective-permute-start(bf16[384,128]{1,0:T(8,128)(2,1)S(1)} %get-tuple-element.30), channel_id=1, source_target_pairs={{0,4},{1,5},{2,6},{3,7},{4,0},{5,1},{6,2},{7,3},{8,12},{9,13},{10,... | collective-permute-start | bytes 294920 | tf_op jit(solution)/shard_map/ppermute | solution.py:169
  17.7 5.8 %collective-permute-start.6 = (bf16[384,128]{1,0:T(8,128)(2,1)S(1)}, bf16[384,128]{1,0:T(8,128)(2,1)S(1)}, u32[]{:S(2)}, u32[]{:S(2)}) collective-permute-start(bf16[384,128]{1,0:T(8,128)(2,1)S(1)} %get-tuple-element.34), channel_id=1, source_target_pairs={{0,2},{1,3},{2,0},{3,1},{4,6},{5,7},{6,4},{7,5},{8,10},{9,11},{10,... | collective-permute-start | bytes 294920 | tf_op jit(solution)/shard_map/ppermute | solution.py:169
  19.2 5.5 %collective-permute-start.3 = (bf16[384,128]{1,0:T(8,128)(2,1)S(1)}, bf16[384,128]{1,0:T(8,128)(2,1)S(1)}, u32[]{:S(2)}, u32[]{:S(2)}) collective-permute-start(bf16[384,128]{1,0:T(8,128)(2,1)S(1)} %get-tuple-element.29.refs_4_), channel_id=1, source_target_pairs={{0,2},{1,3},{2,0},{3,1},{4,6},{5,7},{6,4},{7,5},{8,10},{9,11},{10,... | collective-permute-start | bytes 294920 | tf_op jit(solution)/shard_map/ppermute | solution.py:169
  19.7 7.2 %collective-permute-start.7 = (bf16[384,128]{1,0:T(8,128)(2,1)S(1)}, bf16[384,128]{1,0:T(8,128)(2,1)S(1)}, u32[]{:S(2)}, u32[]{:S(2)}) collective-permute-start(bf16[384,128]{1,0:T(8,128)(2,1)S(1)} %get-tuple-element.33.refs_0_), channel_id=1, source_target_pairs={{0,4},{1,5},{2,6},{3,7},{4,0},{5,1},{6,2},{7,3},{8,12},{9,13},{10,... | collective-permute-start | bytes 294920 | tf_op jit(solution)/shard_map/ppermute | solution.py:169
  22.1 4.6 %collective-permute-start.5 = (bf16[384,128]{1,0:T(8,128)(2,1)S(1)}, bf16[384,128]{1,0:T(8,128)(2,1)S(1)}, u32[]{:S(2)}, u32[]{:S(2)}) collective-permute-start(bf16[384,128]{1,0:T(8,128)(2,1)S(1)} %collective-permute-done.4.refs_6_), channel_id=1, source_target_pairs={{0,2},{1,3},{2,0},{3,1},{4,6},{5,7},{6,4},{7,5},{8,10},{9,11},{10,... | collective-permute-start | bytes 294920 | tf_op jit(solution)/shard_map/ppermute | solution.py:169
  23.4 4.6 %collective-permute-start.8 = (bf16[384,128]{1,0:T(8,128)(2,1)S(1)}, bf16[384,128]{1,0:T(8,128)(2,1)S(1)}, u32[]{:S(2)}, u32[]{:S(2)}) collective-permute-start(bf16[384,128]{1,0:T(8,128)(2,1)S(1)} %collective-permute-done.6.refs_1_), channel_id=1, source_target_pairs={{0,4},{1,5},{2,6},{3,7},{4,0},{5,1},{6,2},{7,3},{8,12},{9,13},{10,... | collective-permute-start | bytes 294920 | tf_op jit(solution)/shard_map/ppermute | solution.py:169
  28.3 1.4 %collective-permute-start.10 = (bf16[192,384]{1,0:T(8,128)(2,1)S(1)}, bf16[192,384]{1,0:T(8,128)(2,1)S(1)}, u32[]{:S(2)}, u32[]{:S(2)}) collective-permute-start(bf16[192,384]{1,0:T(8,128)(2,1)S(1)} %shard_map.101), channel_id=1, source_target_pairs={{0,1},{1,0},{2,3},{3,2},{4,5},{5,4},{6,7},{7,6},{8,9},{9,8},{10,11... | collective-permute-start | bytes 442376 | tf_op jit(solution)/shard_map/ppermute | solution.py:169
  28.7 4.5 %collective-permute-start.9 = (bf16[192,384]{1,0:T(8,128)(2,1)S(1)}, bf16[192,384]{1,0:T(8,128)(2,1)S(1)}, u32[]{:S(2)}, u32[]{:S(2)}) collective-permute-start(bf16[192,384]{1,0:T(8,128)(2,1)S(1)} %shard_map.98), channel_id=1, source_target_pairs={{0,1},{1,0},{2,3},{3,2},{4,5},{5,4},{6,7},{7,6},{8,9},{9,8},{10,11... | collective-permute-start | bytes 442376 | tf_op jit(solution)/shard_map/ppermute | solution.py:169
  29.8 8.9 %collective-permute-start.11 = (bf16[96,384]{1,0:T(8,128)(2,1)S(1)}, bf16[96,384]{1,0:T(8,128)(2,1)S(1)}, u32[]{:S(2)}, u32[]{:S(2)}) collective-permute-start(bf16[96,384]{1,0:T(8,128)(2,1)S(1)} %get-tuple-element.40), channel_id=1, source_target_pairs={{0,16},{1,17},{2,18},{3,19},{4,20},{5,21},{6,22},{7,23},{8,24},{9,... | collective-permute-start | bytes 221192 | tf_op jit(solution)/shard_map/ppermute | solution.py:169
  31.6 7.2 %collective-permute-start.12 = (bf16[96,384]{1,0:T(8,128)(2,1)S(1)}, bf16[96,384]{1,0:T(8,128)(2,1)S(1)}, u32[]{:S(2)}, u32[]{:S(2)}) collective-permute-start(bf16[96,384]{1,0:T(8,128)(2,1)S(1)} %get-tuple-element.41), channel_id=1, source_target_pairs={{0,24},{1,25},{2,26},{3,27},{4,28},{5,29},{6,30},{7,31},{8,16},{9,... | collective-permute-start | bytes 221192 | tf_op jit(solution)/shard_map/ppermute | solution.py:169
  33.2 6.5 %collective-permute-start.13 = (bf16[96,384]{1,0:T(8,128)(2,1)S(1)}, bf16[96,384]{1,0:T(8,128)(2,1)S(1)}, u32[]{:S(2)}, u32[]{:S(2)}) collective-permute-start(bf16[96,384]{1,0:T(8,128)(2,1)S(1)} %get-tuple-element.42), channel_id=1, source_target_pairs={{0,8},{1,9},{2,10},{3,11},{4,12},{5,13},{6,14},{7,15},{8,0},{9,1},... | collective-permute-start | bytes 221192 | tf_op jit(solution)/shard_map/ppermute | solution.py:169
  39.8 4.4 %collective-permute-start.15 = (bf16[96,384]{1,0:T(8,128)(2,1)S(1)}, bf16[96,384]{1,0:T(8,128)(2,1)S(1)}, u32[]{:S(2)}, u32[]{:S(2)}) collective-permute-start(bf16[96,384]{1,0:T(8,128)(2,1)S(1)} %shard_map.103.refs_0_), channel_id=1, source_target_pairs={{0,2},{1,3},{2,0},{3,1},{4,6},{5,7},{6,4},{7,5},{8,10},{9,11},{10,... | collective-permute-start | bytes 221192 | tf_op jit(solution)/shard_map/ppermute | solution.py:169
  40.9 4.0 %collective-permute-start.14 = (bf16[96,384]{1,0:T(8,128)(2,1)S(1)}, bf16[96,384]{1,0:T(8,128)(2,1)S(1)}, u32[]{:S(2)}, u32[]{:S(2)}) collective-permute-start(bf16[96,384]{1,0:T(8,128)(2,1)S(1)} %shard_map.103.refs_0_), channel_id=1, source_target_pairs={{0,1},{1,0},{2,3},{3,2},{4,5},{5,4},{6,7},{7,6},{8,9},{9,8},{10,11... | collective-permute-start | bytes 221192 | tf_op jit(solution)/shard_map/ppermute | solution.py:169
  44.2 1.3 %collective-permute-start.16 = (bf16[96,384]{1,0:T(8,128)(2,1)S(1)}, bf16[96,384]{1,0:T(8,128)(2,1)S(1)}, u32[]{:S(2)}, u32[]{:S(2)}) collective-permute-start(bf16[96,384]{1,0:T(8,128)(2,1)S(1)} %collective-permute-done.15.refs_2_), channel_id=1, source_target_pairs={{0,1},{1,0},{2,3},{3,2},{4,5},{5,4},{6,7},{7,6},{8,9},{9,8},{10,11... | collective-permute-start | bytes 221192 | tf_op jit(solution)/shard_map/ppermute | solution.py:169

commit v9 on v8

--- a/solution.py
+++ b/solution.py
@@ -169,10 +169,9 @@
         return lax.ppermute(array, ("store", "trainer"), pairs)
 
     def store_order(self):
-        up = [(z, x) for z in reversed(range(self.nz)) for x in reversed(range(self.gx))]
-        down = [(z, x) for z in range(self.nz) for x in range(self.gx)]
-        turns = [at for pair in zip(up, down) for at in pair]
-        return [z * self.gx + x for z, x in turns[:self.ns]][::-1]
+        middle = self.ns // 2
+        turns = [s for pair in zip(range(middle, self.ns), range(middle - 1, -1, -1)) for s in pair]
+        return turns
 
 
 def write_rows(plan, trans_ref, *outs):

time: 46.6 us -> 46.9 us (level)
  transfers between devices with their start and end apart: 18 -> 18, of which waited for: 8 -> 9; matrix products, arithmetic and copies ran while one was open for 4% -> 4% of each run, Pallas kernels for 4% -> 4%
where the time goes in v9:
time: 46.9 us; the launch traced here: 46.7 us
  starting transfers between devices  23.6 us (50%)
  waiting for transfers between devices  15.2 us (32%)
  Pallas kernels  5.12 us (11%)
  matrix products  1.25 us (3%)
  between operations  0.78 us (2%)
  other arithmetic  0.7 us (1%)
    ppermute x17, starting transfers between devices, send(): return lax.ppermute(array, ('store', 'trainer'), pairs)  15.6 us
    ppermute x17, waiting for transfers between devices, send(): return lax.ppermute(array, ('store', 'trainer'), pairs)  14.8 us
    all_to_all x1, starting transfers between devices, per_device(): lax.all_to_all(sums.reshape(ns, packed, 128), 'store', split_axis=0, conc...  7.95 us
    pallas_call x11, Pallas kernels, call(): pl.pallas_call(body, out_shape=list(outs), in_specs=[VMEM] * len(args) +...  5.12 us
    dot_general x1, matrix products, dot(): return jnp.dot(a, b, preferred_element_type=F32)  1.25 us
  transfers between devices with their start and end apart: 18, of which 9 were waited for; matrix products, arithmetic and copies ran while one was open for 4% of the time, Pallas kernels for 4%

profile of v9, /device:TPU:0, one launch (start us, length us, event | category | flops | bytes accessed | tf_op | source)
XLA Modules:
  0.0 46.7 jit_solution(4508386856812396859)
XLA Ops:
  0.6 0.0 copy-start
  0.6 2.2 %shard_map.94 = (bf16[640,128]{1,0:T(8,128)(2,1)}, bf16[128,768]{1,0:T(8,128)(2,1)}, bf16[384,128]{1,0:T(8,128)(2,1)}, bf16[384,128]{1,0:T(8,128)(2,1)}) custom-call(f32[128,768]{1,0:T(8,128)} %feat_hbm.1, s32[8,2,12]{2,1,0:T(2,128)} %bitcast.11, f32[128,768]{1,0:T(8,128)} %rest_0_.1), custom_call_target="tpu_custom_call" | custom-call | flops 50331648 | bytes 557056 | tf_op jit(solution)/shard_map/pallas_call | solution.py:23
  2.9 0.0 copy-start.1
  2.9 0.0 copy-start.2
  2.9 0.0 copy-start.4
  2.9 8.0 %all-to-all-start = ((bf16[8,80,128]{2,1,0:T(8,128)(2,1)}), bf16[8,80,128]{2,1,0:T(8,128)(2,1)S(1)}, u32[]{:S(2)}, u32[]{:S(2)}) async-start(bf16[8,80,128]{2,1,0:T(8,128)(2,1)} %bitcast.10), calls=%async_computation | async-start | bytes 327680 | tf_op jit(solution)/shard_map/all_to_all | solution.py:280
  10.9 2.4 %collective-permute-start = (bf16[384,128]{1,0:T(8,128)(2,1)}, bf16[384,128]{1,0:T(8,128)(2,1)S(1)}, u32[]{:S(2)}, u32[]{:S(2)}) collective-permute-start(bf16[384,128]{1,0:T(8,128)(2,1)} %get-tuple-element.27), channel_id=1, source_target_pairs={{0,6},{1,7},{2,4},{3,5},{4,2},{5,3},{6,0},{7,1},{8,14},{9,15},{10,... | collective-permute-start | bytes 294920 | tf_op jit(solution)/shard_map/ppermute | solution.py:169
  13.3 0.6 %collective-permute-start.1 = (bf16[384,128]{1,0:T(8,128)(2,1)}, bf16[384,128]{1,0:T(8,128)(2,1)S(1)}, u32[]{:S(2)}, u32[]{:S(2)}) collective-permute-start(bf16[384,128]{1,0:T(8,128)(2,1)} %get-tuple-element.27), channel_id=1, source_target_pairs={{0,4},{1,5},{2,6},{3,7},{4,0},{5,1},{6,2},{7,3},{8,12},{9,13},{10,... | collective-permute-start | bytes 294920 | tf_op jit(solution)/shard_map/ppermute | solution.py:169
  13.9 0.5 %collective-permute-start.2 = (bf16[384,128]{1,0:T(8,128)(2,1)}, bf16[384,128]{1,0:T(8,128)(2,1)S(1)}, u32[]{:S(2)}, u32[]{:S(2)}) collective-permute-start(bf16[384,128]{1,0:T(8,128)(2,1)} %get-tuple-element.28.refs_3_), channel_id=1, source_target_pairs={{0,2},{1,3},{2,0},{3,1},{4,6},{5,7},{6,4},{7,5},{8,10},{9,11},{10,... | collective-permute-start | bytes 294920 | tf_op jit(solution)/shard_map/ppermute | solution.py:169
  14.4 0.0 copy-done
  14.4 1.2 %fusion.self_ref = f32[128,768]{1,0:T(8,128)S(1)} fusion(bf16[128,768]{1,0:T(8,128)(2,1)} %get-tuple-element.25, bf16[768,768]{1,0:T(8,128)(2,1)S(1)} %copy-done), kind=kOutput, calls=%fused_computation | convolution fusion | flops 150994944 | bytes 1769472 | tf_op jit(solution)/shard_map/dot_general | solution.py:18
  15.6 0.0 copy-start.3
  15.6 0.4 all-to-all-done
  16.1 0.0 copy-done.1
  16.1 0.0 copy-done.2
  16.1 0.0 copy-done.4
  16.1 0.7 %shard_map.95 = (f32[128,768]{1,0:T(8,128)S(1)}, bf16[384,128]{1,0:T(8,128)(2,1)S(1)}, bf16[384,128]{1,0:T(8,128)(2,1)S(1)}, bf16[384,128]{1,0:T(8,128)(2,1)S(1)}, bf16[384,128]{1,0:T(8,128)(2,1)S(1)}) custom-call(bf16[640,128]{1,0:T(8,128)(2,1)S(1)} %bitcast.8, s32[8,12]{1,0:T(8,128)S(1)} %bitcast.9, f32[128,768]{1,0:T(8,128)S(1)} %fusion.self_ref, ...), custom_call_target="tpu_custom_call" | custom-call | flops 176160768 | bytes 2720128 | tf_op jit(solution)/shard_map/pallas_call | solution.py:23
  16.8 1.1 %collective-permute-start.4 = (bf16[384,128]{1,0:T(8,128)(2,1)S(1)}, bf16[384,128]{1,0:T(8,128)(2,1)S(1)}, u32[]{:S(2)}, u32[]{:S(2)}) collective-permute-start(bf16[384,128]{1,0:T(8,128)(2,1)S(1)} %get-tuple-element.30), channel_id=1, source_target_pairs={{0,4},{1,5},{2,6},{3,7},{4,0},{5,1},{6,2},{7,3},{8,12},{9,13},{10,... | collective-permute-start | bytes 294920 | tf_op jit(solution)/shard_map/ppermute | solution.py:169
  17.9 1.5 %collective-permute-start.6 = (bf16[384,128]{1,0:T(8,128)(2,1)S(1)}, bf16[384,128]{1,0:T(8,128)(2,1)S(1)}, u32[]{:S(2)}, u32[]{:S(2)}) collective-permute-start(bf16[384,128]{1,0:T(8,128)(2,1)S(1)} %get-tuple-element.34), channel_id=1, source_target_pairs={{0,2},{1,3},{2,0},{3,1},{4,6},{5,7},{6,4},{7,5},{8,10},{9,11},{10,... | collective-permute-start | bytes 294920 | tf_op jit(solution)/shard_map/ppermute | solution.py:169
  19.5 0.0 collective-permute-done.refs_0_
  19.5 0.5 %collective-permute-start.3 = (bf16[384,128]{1,0:T(8,128)(2,1)S(1)}, bf16[384,128]{1,0:T(8,128)(2,1)S(1)}, u32[]{:S(2)}, u32[]{:S(2)}) collective-permute-start(bf16[384,128]{1,0:T(8,128)(2,1)S(1)} %get-tuple-element.29.refs_4_), channel_id=1, source_target_pairs={{0,2},{1,3},{2,0},{3,1},{4,6},{5,7},{6,4},{7,5},{8,10},{9,11},{10,... | collective-permute-start | bytes 294920 | tf_op jit(solution)/shard_map/ppermute | solution.py:169
  20.0 0.1 collective-permute-done.1.refs_1_
  20.1 0.9 %collective-permute-start.7 = (bf16[384,128]{1,0:T(8,128)(2,1)S(1)}, bf16[384,128]{1,0:T(8,128)(2,1)S(1)}, u32[]{:S(2)}, u32[]{:S(2)}) collective-permute-start(bf16[384,128]{1,0:T(8,128)(2,1)S(1)} %get-tuple-element.33.refs_0_), channel_id=1, source_target_pairs={{0,4},{1,5},{2,6},{3,7},{4,0},{5,1},{6,2},{7,3},{8,12},{9,13},{10,... | collective-permute-start | bytes 294920 | tf_op jit(solution)/shard_map/ppermute | solution.py:169
  21.0 0.0 collective-permute-done.2.refs_2_
  21.0 1.1 %collective-permute-done.4.refs_6_ = bf16[384,128]{1,0:T(8,128)(2,1)S(1)} collective-permute-done((bf16[384,128]{1,0:T(8,128)(2,1)S(1)}, bf16[384,128]{1,0:T(8,128)(2,1)S(1)}, u32[]{:S(2)}, u32[]{:S(2)}) %collective-permute-start.4) | collective-permute-done | bytes 98336 | tf_op jit(solution)/shard_map/ppermute | solution.py:169
  22.1 1.9 %collective-permute-start.5 = (bf16[384,128]{1,0:T(8,128)(2,1)S(1)}, bf16[384,128]{1,0:T(8,128)(2,1)S(1)}, u32[]{:S(2)}, u32[]{:S(2)}) collective-permute-start(bf16[384,128]{1,0:T(8,128)(2,1)S(1)} %collective-permute-done.4.refs_6_), channel_id=1, source_target_pairs={{0,2},{1,3},{2,0},{3,1},{4,6},{5,7},{6,4},{7,5},{8,10},{9,11},{10,... | collective-permute-start | bytes 294920 | tf_op jit(solution)/shard_map/ppermute | solution.py:169
  23.9 0.0 collective-permute-done.6.refs_1_
  23.9 1.2 %collective-permute-start.8 = (bf16[384,128]{1,0:T(8,128)(2,1)S(1)}, bf16[384,128]{1,0:T(8,128)(2,1)S(1)}, u32[]{:S(2)}, u32[]{:S(2)}) collective-permute-start(bf16[384,128]{1,0:T(8,128)(2,1)S(1)} %collective-permute-done.6.refs_1_), channel_id=1, source_target_pairs={{0,4},{1,5},{2,6},{3,7},{4,0},{5,1},{6,2},{7,3},{8,12},{9,13},{10,... | collective-permute-start | bytes 294920 | tf_op jit(solution)/shard_map/ppermute | solution.py:169
  25.1 0.0 collective-permute-done.3.refs_5_
  25.1 1.6 %collective-permute-done.5.refs_7_ = bf16[384,128]{1,0:T(8,128)(2,1)S(1)} collective-permute-done((bf16[384,128]{1,0:T(8,128)(2,1)S(1)}, bf16[384,128]{1,0:T(8,128)(2,1)S(1)}, u32[]{:S(2)}, u32[]{:S(2)}) %collective-permute-start.5) | collective-permute-done | bytes 98336 | tf_op jit(solution)/shard_map/ppermute | solution.py:169
  26.7 0.0 copy-done.3
  26.7 0.1 shard_map.96
  26.8 0.0 collective-permute-done.7.refs_2_
  26.8 1.7 %collective-permute-done.8.refs_3_ = bf16[384,128]{1,0:T(8,128)(2,1)S(1)} collective-permute-done((bf16[384,128]{1,0:T(8,128)(2,1)S(1)}, bf16[384,128]{1,0:T(8,128)(2,1)S(1)}, u32[]{:S(2)}, u32[]{:S(2)}) %collective-permute-start.8) | collective-permute-done | bytes 98336 | tf_op jit(solution)/shard_map/ppermute | solution.py:169
  28.6 0.3 shard_map.101
  28.8 0.1 collective-permute-start.10
  28.9 0.3 shard_map.98
  29.2 0.6 %collective-permute-start.9 = (bf16[192,384]{1,0:T(8,128)(2,1)S(1)}, bf16[192,384]{1,0:T(8,128)(2,1)S(1)}, u32[]{:S(2)}, u32[]{:S(2)}) collective-permute-start(bf16[192,384]{1,0:T(8,128)(2,1)S(1)} %shard_map.98), channel_id=1, source_target_pairs={{0,1},{1,0},{2,3},{3,2},{4,5},{5,4},{6,7},{7,6},{8,9},{9,8},{10,11... | collective-permute-start | bytes 442376 | tf_op jit(solution)/shard_map/ppermute | solution.py:169
  29.7 0.3 shard_map.97.keep_ref
  30.0 0.3 shard_map.100.keep_ref
  30.2 0.0 collective-permute-done.10.got_ref
  30.3 0.8 %collective-permute-start.11 = (bf16[96,384]{1,0:T(8,128)(2,1)S(1)}, bf16[96,384]{1,0:T(8,128)(2,1)S(1)}, u32[]{:S(2)}, u32[]{:S(2)}) collective-permute-start(bf16[96,384]{1,0:T(8,128)(2,1)S(1)} %get-tuple-element.40), channel_id=1, source_target_pairs={{0,16},{1,17},{2,18},{3,19},{4,20},{5,21},{6,22},{7,23},{8,24},{9,... | collective-permute-start | bytes 221192 | tf_op jit(solution)/shard_map/ppermute | solution.py:169
  31.1 2.1 %collective-permute-start.12 = (bf16[96,384]{1,0:T(8,128)(2,1)S(1)}, bf16[96,384]{1,0:T(8,128)(2,1)S(1)}, u32[]{:S(2)}, u32[]{:S(2)}) collective-permute-start(bf16[96,384]{1,0:T(8,128)(2,1)S(1)} %get-tuple-element.41), channel_id=1, source_target_pairs={{0,24},{1,25},{2,26},{3,27},{4,28},{5,29},{6,30},{7,31},{8,16},{9,... | collective-permute-start | bytes 221192 | tf_op jit(solution)/shard_map/ppermute | solution.py:169
  33.2 0.0 collective-permute-done.9.got_ref
  33.2 0.7 %collective-permute-start.13 = (bf16[96,384]{1,0:T(8,128)(2,1)S(1)}, bf16[96,384]{1,0:T(8,128)(2,1)S(1)}, u32[]{:S(2)}, u32[]{:S(2)}) collective-permute-start(bf16[96,384]{1,0:T(8,128)(2,1)S(1)} %get-tuple-element.42), channel_id=1, source_target_pairs={{0,8},{1,9},{2,10},{3,11},{4,12},{5,13},{6,14},{7,15},{8,0},{9,1},... | collective-permute-start | bytes 221192 | tf_op jit(solution)/shard_map/ppermute | solution.py:169
  34.0 4.8 %collective-permute-done.11.refs_1_ = bf16[96,384]{1,0:T(8,128)(2,1)S(1)} collective-permute-done((bf16[96,384]{1,0:T(8,128)(2,1)S(1)}, bf16[96,384]{1,0:T(8,128)(2,1)S(1)}, u32[]{:S(2)}, u32[]{:S(2)}) %collective-permute-start.11) | collective-permute-done | bytes 73760 | tf_op jit(solution)/shard_map/ppermute | solution.py:169
  38.7 0.0 collective-permute-done.12.refs_2_
  38.7 1.3 %collective-permute-done.13.refs_3_ = bf16[96,384]{1,0:T(8,128)(2,1)S(1)} collective-permute-done((bf16[96,384]{1,0:T(8,128)(2,1)S(1)}, bf16[96,384]{1,0:T(8,128)(2,1)S(1)}, u32[]{:S(2)}, u32[]{:S(2)}) %collective-permute-start.13) | collective-permute-done | bytes 73760 | tf_op jit(solution)/shard_map/ppermute | solution.py:169
  40.1 0.8 %collective-permute-start.15 = (bf16[96,384]{1,0:T(8,128)(2,1)S(1)}, bf16[96,384]{1,0:T(8,128)(2,1)S(1)}, u32[]{:S(2)}, u32[]{:S(2)}) collective-permute-start(bf16[96,384]{1,0:T(8,128)(2,1)S(1)} %shard_map.103.refs_0_), channel_id=1, source_target_pairs={{0,2},{1,3},{2,0},{3,1},{4,6},{5,7},{6,4},{7,5},{8,10},{9,11},{10,... | collective-permute-start | bytes 221192 | tf_op jit(solution)/shard_map/ppermute | solution.py:169
  40.9 0.0 collective-permute-start.14
  40.9 3.6 %collective-permute-done.15.refs_2_ = bf16[96,384]{1,0:T(8,128)(2,1)S(1)} collective-permute-done((bf16[96,384]{1,0:T(8,128)(2,1)S(1)}, bf16[96,384]{1,0:T(8,128)(2,1)S(1)}, u32[]{:S(2)}, u32[]{:S(2)}) %collective-permute-start.15) | collective-permute-done | bytes 73760 | tf_op jit(solution)/shard_map/ppermute | solution.py:169
  44.5 0.0 collective-permute-start.16
  44.5 0.7 %convert_element_type.3 = bf16[128,768]{1,0:T(8,128)(2,1)} convert(f32[128,768]{1,0:T(8,128)S(1)} %get-tuple-element.26) | non-fusion elementwise | flops 98304 | bytes 589824 | tf_op jit(solution)/shard_map/convert_element_type | solution.py:354
  45.2 0.0 collective-permute-done.14.refs_1_
  45.2 0.6 %collective-permute-done.16.refs_3_ = bf16[96,384]{1,0:T(8,128)(2,1)S(1)} collective-permute-done((bf16[96,384]{1,0:T(8,128)(2,1)S(1)}, bf16[96,384]{1,0:T(8,128)(2,1)S(1)}, u32[]{:S(2)}, u32[]{:S(2)}) %collective-permute-start.16) | collective-permute-done | bytes 73760 | tf_op jit(solution)/shard_map/ppermute | solution.py:169
  45.8 0.9 %shard_map.104 = (f32[96,768]{1,0:T(8,128)}, f32[96,768]{1,0:T(8,128)}) custom-call(bf16[96,384]{1,0:T(8,128)(2,1)S(1)} %shard_map.103.refs_0_, bf16[96,384]{1,0:T(8,128)(2,1)S(1)} %collective-permute-done.14.refs_1_, bf16[96,384]{1,0:T(8,128)(2,1)S(1)} %collective-permute-done.15.refs_2_, bf16[96,384]{1,0:T(8,128)(2,1)S(1)} %collective-permute-done.16.refs_3_), custom_call_target="tpu_custom_call" | custom-call | bytes 884736 | tf_op jit(solution)/shard_map/pallas_call | solution.py:23
  (3 shorter events, 0.1 us)
Async XLA Ops:
  0.6 13.7 %copy-start = (bf16[768,768]{1,0:T(8,128)(2,1)S(1)}, bf16[768,768]{1,0:T(8,128)(2,1)}, u32[]{:S(2)}) copy-start(bf16[768,768]{1,0:T(8,128)(2,1)} %param.12) | copy-start | bytes 3538948
  2.9 13.2 %copy-start.1 = (bf16[768,768]{1,0:T(8,128)(2,1)S(1)}, bf16[768,768]{1,0:T(8,128)(2,1)}, u32[]{:S(2)}) copy-start(bf16[768,768]{1,0:T(8,128)(2,1)} %w_ref.1) | copy-start | bytes 3538948
  2.9 13.2 %copy-start.2 = (bf16[128,768]{1,0:T(8,128)(2,1)S(1)}, bf16[128,768]{1,0:T(8,128)(2,1)}, u32[]{:S(2)}) copy-start(bf16[128,768]{1,0:T(8,128)(2,1)} %cot_ref.1) | copy-start | bytes 589828
  2.9 13.2 %copy-start.4 = (s32[1,1,8,12]{3,2,1,0:T(8,128)S(1)}, s32[1,1,8,12]{3,2,1,0:T(8,128)}, u32[]{:S(2)}) copy-start(s32[1,1,8,12]{3,2,1,0:T(8,128)} %param.10) | copy-start | bytes 1156
  2.9 13.2 %all-to-all-start = ((bf16[8,80,128]{2,1,0:T(8,128)(2,1)}), bf16[8,80,128]{2,1,0:T(8,128)(2,1)S(1)}, u32[]{:S(2)}, u32[]{:S(2)}) async-start(bf16[8,80,128]{2,1,0:T(8,128)(2,1)} %bitcast.10), calls=%async_computation | async-start | bytes 327680 | tf_op jit(solution)/shard_map/all_to_all | solution.py:280
  10.9 8.6 %collective-permute-start = (bf16[384,128]{1,0:T(8,128)(2,1)}, bf16[384,128]{1,0:T(8,128)(2,1)S(1)}, u32[]{:S(2)}, u32[]{:S(2)}) collective-permute-start(bf16[384,128]{1,0:T(8,128)(2,1)} %get-tuple-element.27), channel_id=1, source_target_pairs={{0,6},{1,7},{2,4},{3,5},{4,2},{5,3},{6,0},{7,1},{8,14},{9,15},{10,... | collective-permute-start | bytes 294920 | tf_op jit(solution)/shard_map/ppermute | solution.py:169
  13.3 6.8 %collective-permute-start.1 = (bf16[384,128]{1,0:T(8,128)(2,1)}, bf16[384,128]{1,0:T(8,128)(2,1)S(1)}, u32[]{:S(2)}, u32[]{:S(2)}) collective-permute-start(bf16[384,128]{1,0:T(8,128)(2,1)} %get-tuple-element.27), channel_id=1, source_target_pairs={{0,4},{1,5},{2,6},{3,7},{4,0},{5,1},{6,2},{7,3},{8,12},{9,13},{10,... | collective-permute-start | bytes 294920 | tf_op jit(solution)/shard_map/ppermute | solution.py:169
  13.9 7.1 %collective-permute-start.2 = (bf16[384,128]{1,0:T(8,128)(2,1)}, bf16[384,128]{1,0:T(8,128)(2,1)S(1)}, u32[]{:S(2)}, u32[]{:S(2)}) collective-permute-start(bf16[384,128]{1,0:T(8,128)(2,1)} %get-tuple-element.28.refs_3_), channel_id=1, source_target_pairs={{0,2},{1,3},{2,0},{3,1},{4,6},{5,7},{6,4},{7,5},{8,10},{9,11},{10,... | collective-permute-start | bytes 294920 | tf_op jit(solution)/shard_map/ppermute | solution.py:169
  15.6 11.1 %copy-start.3 = (bf16[384,128]{1,0:T(8,128)(2,1)S(1)}, bf16[384,128]{1,0:T(8,128)(2,1)}, u32[]{:S(2)}) copy-start(bf16[384,128]{1,0:T(8,128)(2,1)} %get-tuple-element.28.refs_3_) | copy-start | bytes 294916
  16.8 5.2 %collective-permute-start.4 = (bf16[384,128]{1,0:T(8,128)(2,1)S(1)}, bf16[384,128]{1,0:T(8,128)(2,1)S(1)}, u32[]{:S(2)}, u32[]{:S(2)}) collective-permute-start(bf16[384,128]{1,0:T(8,128)(2,1)S(1)} %get-tuple-element.30), channel_id=1, source_target_pairs={{0,4},{1,5},{2,6},{3,7},{4,0},{5,1},{6,2},{7,3},{8,12},{9,13},{10,... | collective-permute-start | bytes 294920 | tf_op jit(solution)/shard_map/ppermute | solution.py:169
  17.9 6.0 %collective-permute-start.6 = (bf16[384,128]{1,0:T(8,128)(2,1)S(1)}, bf16[384,128]{1,0:T(8,128)(2,1)S(1)}, u32[]{:S(2)}, u32[]{:S(2)}) collective-permute-start(bf16[384,128]{1,0:T(8,128)(2,1)S(1)} %get-tuple-element.34), channel_id=1, source_target_pairs={{0,2},{1,3},{2,0},{3,1},{4,6},{5,7},{6,4},{7,5},{8,10},{9,11},{10,... | collective-permute-start | bytes 294920 | tf_op jit(solution)/shard_map/ppermute | solution.py:169
  19.5 5.6 %collective-permute-start.3 = (bf16[384,128]{1,0:T(8,128)(2,1)S(1)}, bf16[384,128]{1,0:T(8,128)(2,1)S(1)}, u32[]{:S(2)}, u32[]{:S(2)}) collective-permute-start(bf16[384,128]{1,0:T(8,128)(2,1)S(1)} %get-tuple-element.29.refs_4_), channel_id=1, source_target_pairs={{0,2},{1,3},{2,0},{3,1},{4,6},{5,7},{6,4},{7,5},{8,10},{9,11},{10,... | collective-permute-start | bytes 294920 | tf_op jit(solution)/shard_map/ppermute | solution.py:169
  20.1 6.7 %collective-permute-start.7 = (bf16[384,128]{1,0:T(8,128)(2,1)S(1)}, bf16[384,128]{1,0:T(8,128)(2,1)S(1)}, u32[]{:S(2)}, u32[]{:S(2)}) collective-permute-start(bf16[384,128]{1,0:T(8,128)(2,1)S(1)} %get-tuple-element.33.refs_0_), channel_id=1, source_target_pairs={{0,4},{1,5},{2,6},{3,7},{4,0},{5,1},{6,2},{7,3},{8,12},{9,13},{10,... | collective-permute-start | bytes 294920 | tf_op jit(solution)/shard_map/ppermute | solution.py:169
  22.1 4.6 %collective-permute-start.5 = (bf16[384,128]{1,0:T(8,128)(2,1)S(1)}, bf16[384,128]{1,0:T(8,128)(2,1)S(1)}, u32[]{:S(2)}, u32[]{:S(2)}) collective-permute-start(bf16[384,128]{1,0:T(8,128)(2,1)S(1)} %collective-permute-done.4.refs_6_), channel_id=1, source_target_pairs={{0,2},{1,3},{2,0},{3,1},{4,6},{5,7},{6,4},{7,5},{8,10},{9,11},{10,... | collective-permute-start | bytes 294920 | tf_op jit(solution)/shard_map/ppermute | solution.py:169
  23.9 4.6 %collective-permute-start.8 = (bf16[384,128]{1,0:T(8,128)(2,1)S(1)}, bf16[384,128]{1,0:T(8,128)(2,1)S(1)}, u32[]{:S(2)}, u32[]{:S(2)}) collective-permute-start(bf16[384,128]{1,0:T(8,128)(2,1)S(1)} %collective-permute-done.6.refs_1_), channel_id=1, source_target_pairs={{0,4},{1,5},{2,6},{3,7},{4,0},{5,1},{6,2},{7,3},{8,12},{9,13},{10,... | collective-permute-start | bytes 294920 | tf_op jit(solution)/shard_map/ppermute | solution.py:169
  28.8 1.4 %collective-permute-start.10 = (bf16[192,384]{1,0:T(8,128)(2,1)S(1)}, bf16[192,384]{1,0:T(8,128)(2,1)S(1)}, u32[]{:S(2)}, u32[]{:S(2)}) collective-permute-start(bf16[192,384]{1,0:T(8,128)(2,1)S(1)} %shard_map.101), channel_id=1, source_target_pairs={{0,1},{1,0},{2,3},{3,2},{4,5},{5,4},{6,7},{7,6},{8,9},{9,8},{10,11... | collective-permute-start | bytes 442376 | tf_op jit(solution)/shard_map/ppermute | solution.py:169
  29.2 4.0 %collective-permute-start.9 = (bf16[192,384]{1,0:T(8,128)(2,1)S(1)}, bf16[192,384]{1,0:T(8,128)(2,1)S(1)}, u32[]{:S(2)}, u32[]{:S(2)}) collective-permute-start(bf16[192,384]{1,0:T(8,128)(2,1)S(1)} %shard_map.98), channel_id=1, source_target_pairs={{0,1},{1,0},{2,3},{3,2},{4,5},{5,4},{6,7},{7,6},{8,9},{9,8},{10,11... | collective-permute-start | bytes 442376 | tf_op jit(solution)/shard_map/ppermute | solution.py:169
  30.3 8.4 %collective-permute-start.11 = (bf16[96,384]{1,0:T(8,128)(2,1)S(1)}, bf16[96,384]{1,0:T(8,128)(2,1)S(1)}, u32[]{:S(2)}, u32[]{:S(2)}) collective-permute-start(bf16[96,384]{1,0:T(8,128)(2,1)S(1)} %get-tuple-element.40), channel_id=1, source_target_pairs={{0,16},{1,17},{2,18},{3,19},{4,20},{5,21},{6,22},{7,23},{8,24},{9,... | collective-permute-start | bytes 221192 | tf_op jit(solution)/shard_map/ppermute | solution.py:169
  31.1 7.6 %collective-permute-start.12 = (bf16[96,384]{1,0:T(8,128)(2,1)S(1)}, bf16[96,384]{1,0:T(8,128)(2,1)S(1)}, u32[]{:S(2)}, u32[]{:S(2)}) collective-permute-start(bf16[96,384]{1,0:T(8,128)(2,1)S(1)} %get-tuple-element.41), channel_id=1, source_target_pairs={{0,24},{1,25},{2,26},{3,27},{4,28},{5,29},{6,30},{7,31},{8,16},{9,... | collective-permute-start | bytes 221192 | tf_op jit(solution)/shard_map/ppermute | solution.py:169
  33.2 6.8 %collective-permute-start.13 = (bf16[96,384]{1,0:T(8,128)(2,1)S(1)}, bf16[96,384]{1,0:T(8,128)(2,1)S(1)}, u32[]{:S(2)}, u32[]{:S(2)}) collective-permute-start(bf16[96,384]{1,0:T(8,128)(2,1)S(1)} %get-tuple-element.42), channel_id=1, source_target_pairs={{0,8},{1,9},{2,10},{3,11},{4,12},{5,13},{6,14},{7,15},{8,0},{9,1},... | collective-permute-start | bytes 221192 | tf_op jit(solution)/shard_map/ppermute | solution.py:169
  40.1 4.4 %collective-permute-start.15 = (bf16[96,384]{1,0:T(8,128)(2,1)S(1)}, bf16[96,384]{1,0:T(8,128)(2,1)S(1)}, u32[]{:S(2)}, u32[]{:S(2)}) collective-permute-start(bf16[96,384]{1,0:T(8,128)(2,1)S(1)} %shard_map.103.refs_0_), channel_id=1, source_target_pairs={{0,2},{1,3},{2,0},{3,1},{4,6},{5,7},{6,4},{7,5},{8,10},{9,11},{10,... | collective-permute-start | bytes 221192 | tf_op jit(solution)/shard_map/ppermute | solution.py:169
  40.9 4.3 %collective-permute-start.14 = (bf16[96,384]{1,0:T(8,128)(2,1)S(1)}, bf16[96,384]{1,0:T(8,128)(2,1)S(1)}, u32[]{:S(2)}, u32[]{:S(2)}) collective-permute-start(bf16[96,384]{1,0:T(8,128)(2,1)S(1)} %shard_map.103.refs_0_), channel_id=1, source_target_pairs={{0,1},{1,0},{2,3},{3,2},{4,5},{5,4},{6,7},{7,6},{8,9},{9,8},{10,11... | collective-permute-start | bytes 221192 | tf_op jit(solution)/shard_map/ppermute | solution.py:169
  44.5 1.3 %collective-permute-start.16 = (bf16[96,384]{1,0:T(8,128)(2,1)S(1)}, bf16[96,384]{1,0:T(8,128)(2,1)S(1)}, u32[]{:S(2)}, u32[]{:S(2)}) collective-permute-start(bf16[96,384]{1,0:T(8,128)(2,1)S(1)} %collective-permute-done.15.refs_2_), channel_id=1, source_target_pairs={{0,1},{1,0},{2,3},{3,2},{4,5},{5,4},{6,7},{7,6},{8,9},{9,8},{10,11... | collective-permute-start | bytes 221192 | tf_op jit(solution)/shard_map/ppermute | solution.py:169

commit v10 on v9

--- a/solution.py
+++ b/solution.py
@@ -188,7 +188,7 @@
     write_rows(plan, trans_ref, here_ref, there_ref)
 
 
-def layer_kernel(plan, cap, order, rows_ref, recv_ref, self_ref, cot_ref, w_ref, hidden_ref, mean_here, mean_there,
+def layer_kernel(plan, cap, order, rows_ref, recv_ref, self_ref, cot_ref, w_ref, _, hidden_ref, mean_here, mean_there,
                  grad_here, grad_there, trans_ref, grad_ref):
     targets = self_ref.shape[0]
     rows = unpack(rows_ref[...], order, cap, hidden_ref.shape[1] // 128)
@@ -304,14 +304,16 @@
         return lax.optimization_barrier((array,) + until)[0]
 
     own, own_here, own_there = owns
-    own_all = [own_here, to_y(own_here), to_x(own_there), to_diagonal(own_there)]
+    own_x = to_x(own_there)
+    own_y = to_y(held(own_here, own_x))
+    own_all = [own_here, own_y, own_x, to_diagonal(held(own_there, own_x))]
     self_term = dot(own, w_self)
 
     hidden, mean_here, mean_there, grad_here, grad_there = call(
         functools.partial(layer_kernel, plan, cap, order),
         [shape((targets, out_width), F32)] + [shape((rows, targets), BF16)] * 2
         + [shape((cols // 128 * targets, 128), BF16)] * 2,
-        [arrived, recv_target[0, 0], self_term, cotangent, w_neigh],
+        [arrived, recv_target[0, 0], self_term, cotangent, w_neigh], unread=[own_y],
         scratch=[pltpu.VMEM((width, targets), BF16), pltpu.VMEM((out_width // 128, targets, 128), BF16)],
         flops=2 * targets * width * (out_width + slots))
     mean_x, grad_y = to_x(mean_there), to_y(grad_there)

time: 46.9 us -> 48 us (1.023)
  starting transfers between devices: 23.6 us -> 24.4 us
    ppermute x17, starting transfers between devices: 15.6 us -> 18.5 us  [send(): return lax.ppermute(array, ('store', 'trainer'), pairs)]
    all_to_all x1, starting transfers between devices: 7.95 us -> 5.91 us  [per_device(): lax.all_to_all(sums.reshape(ns, packed, 128), 'store', split_axis=0, conc...]
  transfers between devices with their start and end apart: 18 -> 18, of which waited for: 9 -> 11; matrix products, arithmetic and copies ran while one was open for 4% -> 4% of each run, Pallas kernels for 4% -> 4%
where the time goes in v10:
time: 48 us; the launch traced here: 47.7 us
  starting transfers between devices  24.4 us (51%)
  waiting for transfers between devices  15.4 us (32%)
  Pallas kernels  5.11 us (11%)
  matrix products  1.25 us (3%)
  between operations  0.77 us (2%)
  other arithmetic  0.7 us (1%)
    ppermute x17, starting transfers between devices, send(): return lax.ppermute(array, ('store', 'trainer'), pairs)  18.5 us
    ppermute x17, waiting for transfers between devices, send(): return lax.ppermute(array, ('store', 'trainer'), pairs)  15 us
    all_to_all x1, starting transfers between devices, per_device(): lax.all_to_all(sums.reshape(ns, packed, 128), 'store', split_axis=0, conc...  5.91 us
    pallas_call x11, Pallas kernels, call(): pl.pallas_call(body, out_shape=list(outs), in_specs=[VMEM] * len(args) +...  5.11 us
    dot_general x1, matrix products, dot(): return jnp.dot(a, b, preferred_element_type=F32)  1.25 us
  transfers between devices with their start and end apart: 18, of which 11 were waited for; matrix products, arithmetic and copies ran while one was open for 4% of the time, Pallas kernels for 4%

profile of v10, /device:TPU:0, one launch (start us, length us, event | category | flops | bytes accessed | tf_op | source)
XLA Modules:
  0.0 47.7 jit_solution(2422260882390410859)
XLA Ops:
  0.6 0.0 copy-start
  0.6 2.2 %shard_map.94 = (bf16[640,128]{1,0:T(8,128)(2,1)}, bf16[128,768]{1,0:T(8,128)(2,1)}, bf16[384,128]{1,0:T(8,128)(2,1)}, bf16[384,128]{1,0:T(8,128)(2,1)}) custom-call(f32[128,768]{1,0:T(8,128)} %feat_hbm.1, s32[8,2,12]{2,1,0:T(2,128)} %bitcast.11, f32[128,768]{1,0:T(8,128)} %rest_0_.1), custom_call_target="tpu_custom_call" | custom-call | flops 50331648 | bytes 557056 | tf_op jit(solution)/shard_map/pallas_call | solution.py:23
  2.9 0.0 copy-start.1
  2.9 0.0 copy-start.2
  2.9 0.0 copy-start.4
  2.9 3.0 %collective-permute-start = (bf16[384,128]{1,0:T(8,128)(2,1)}, bf16[384,128]{1,0:T(8,128)(2,1)S(1)}, u32[]{:S(2)}, u32[]{:S(2)}) collective-permute-start(bf16[384,128]{1,0:T(8,128)(2,1)} %get-tuple-element.32), channel_id=1, source_target_pairs={{0,4},{1,5},{2,6},{3,7},{4,0},{5,1},{6,2},{7,3},{8,12},{9,13},{10,... | collective-permute-start | bytes 294920 | tf_op jit(solution)/shard_map/ppermute | solution.py:169
  5.9 5.9 %all-to-all-start = ((bf16[8,80,128]{2,1,0:T(8,128)(2,1)}), bf16[8,80,128]{2,1,0:T(8,128)(2,1)S(1)}, u32[]{:S(2)}, u32[]{:S(2)}) async-start(bf16[8,80,128]{2,1,0:T(8,128)(2,1)} %bitcast.10), calls=%async_computation | async-start | bytes 327680 | tf_op jit(solution)/shard_map/all_to_all | solution.py:280
  11.8 0.0 collective-permute-done.refs_1_
  11.8 1.5 %collective-permute-start.1 = (bf16[384,128]{1,0:T(8,128)(2,1)}, bf16[384,128]{1,0:T(8,128)(2,1)S(1)}, u32[]{:S(2)}, u32[]{:S(2)}) collective-permute-start(bf16[384,128]{1,0:T(8,128)(2,1)} %get-tuple-element.30.refs_3_), channel_id=1, source_target_pairs={{0,2},{1,3},{2,0},{3,1},{4,6},{5,7},{6,4},{7,5},{8,10},{9,11},{10,... | collective-permute-start | bytes 294920 | tf_op jit(solution)/shard_map/ppermute | solution.py:169
  13.4 0.0 copy-done
  13.4 1.2 %fusion.self_ref = f32[128,768]{1,0:T(8,128)S(1)} fusion(bf16[128,768]{1,0:T(8,128)(2,1)} %get-tuple-element.27, bf16[768,768]{1,0:T(8,128)(2,1)S(1)} %copy-done), kind=kOutput, calls=%fused_computation | convolution fusion | flops 150994944 | bytes 1769472 | tf_op jit(solution)/shard_map/dot_general | solution.py:18
  14.6 0.0 copy-start.3
  14.6 1.5 %collective-permute-start.2 = (bf16[384,128]{1,0:T(8,128)(2,1)}, bf16[384,128]{1,0:T(8,128)(2,1)S(1)}, u32[]{:S(2)}, u32[]{:S(2)}) collective-permute-start(bf16[384,128]{1,0:T(8,128)(2,1)} %get-tuple-element.32), channel_id=1, source_target_pairs={{0,6},{1,7},{2,4},{3,5},{4,2},{5,3},{6,0},{7,1},{8,14},{9,15},{10,... | collective-permute-start | bytes 294920 | tf_op jit(solution)/shard_map/ppermute | solution.py:169
  16.1 0.6 %collective-permute-done.1._.refs_2_ = bf16[384,128]{1,0:T(8,128)(2,1)S(1)} collective-permute-done((bf16[384,128]{1,0:T(8,128)(2,1)}, bf16[384,128]{1,0:T(8,128)(2,1)S(1)}, u32[]{:S(2)}, u32[]{:S(2)}) %collective-permute-start.1) | collective-permute-done | bytes 98336 | tf_op jit(solution)/shard_map/ppermute | solution.py:169
  16.7 0.4 all-to-all-done
  17.0 0.0 copy-done.1
  17.0 0.0 copy-done.2
  17.0 0.0 copy-done.4
  17.0 0.7 %shard_map.95 = (f32[128,768]{1,0:T(8,128)S(1)}, bf16[384,128]{1,0:T(8,128)(2,1)S(1)}, bf16[384,128]{1,0:T(8,128)(2,1)S(1)}, bf16[384,128]{1,0:T(8,128)(2,1)S(1)}, bf16[384,128]{1,0:T(8,128)(2,1)S(1)}) custom-call(bf16[640,128]{1,0:T(8,128)(2,1)S(1)} %bitcast.8, s32[8,12]{1,0:T(8,128)S(1)} %bitcast.9, f32[128,768]{1,0:T(8,128)S(1)} %fusion.self_ref, ...), custom_call_target="tpu_custom_call" | custom-call | flops 176160768 | bytes 2720128 | tf_op jit(solution)/shard_map/pallas_call | solution.py:23
  17.8 1.4 %collective-permute-start.4 = (bf16[384,128]{1,0:T(8,128)(2,1)S(1)}, bf16[384,128]{1,0:T(8,128)(2,1)S(1)}, u32[]{:S(2)}, u32[]{:S(2)}) collective-permute-start(bf16[384,128]{1,0:T(8,128)(2,1)S(1)} %get-tuple-element.34), channel_id=1, source_target_pairs={{0,4},{1,5},{2,6},{3,7},{4,0},{5,1},{6,2},{7,3},{8,12},{9,13},{10,... | collective-permute-start | bytes 294920 | tf_op jit(solution)/shard_map/ppermute | solution.py:169
  19.2 2.4 %collective-permute-start.6 = (bf16[384,128]{1,0:T(8,128)(2,1)S(1)}, bf16[384,128]{1,0:T(8,128)(2,1)S(1)}, u32[]{:S(2)}, u32[]{:S(2)}) collective-permute-start(bf16[384,128]{1,0:T(8,128)(2,1)S(1)} %get-tuple-element.38), channel_id=1, source_target_pairs={{0,2},{1,3},{2,0},{3,1},{4,6},{5,7},{6,4},{7,5},{8,10},{9,11},{10,... | collective-permute-start | bytes 294920 | tf_op jit(solution)/shard_map/ppermute | solution.py:169
  21.5 0.0 collective-permute-start.3
  21.6 0.3 collective-permute-start.7
  21.9 0.0 collective-permute-done.2.refs_0_
  21.9 1.3 %collective-permute-done.4.refs_6_ = bf16[384,128]{1,0:T(8,128)(2,1)S(1)} collective-permute-done((bf16[384,128]{1,0:T(8,128)(2,1)S(1)}, bf16[384,128]{1,0:T(8,128)(2,1)S(1)}, u32[]{:S(2)}, u32[]{:S(2)}) %collective-permute-start.4) | collective-permute-done | bytes 98336 | tf_op jit(solution)/shard_map/ppermute | solution.py:169
  23.2 1.5 %collective-permute-start.5 = (bf16[384,128]{1,0:T(8,128)(2,1)S(1)}, bf16[384,128]{1,0:T(8,128)(2,1)S(1)}, u32[]{:S(2)}, u32[]{:S(2)}) collective-permute-start(bf16[384,128]{1,0:T(8,128)(2,1)S(1)} %collective-permute-done.4.refs_6_), channel_id=1, source_target_pairs={{0,2},{1,3},{2,0},{3,1},{4,6},{5,7},{6,4},{7,5},{8,10},{9,11},{10,... | collective-permute-start | bytes 294920 | tf_op jit(solution)/shard_map/ppermute | solution.py:169
  24.8 0.2 collective-permute-done.6.refs_1_
  25.0 1.1 %collective-permute-start.8 = (bf16[384,128]{1,0:T(8,128)(2,1)S(1)}, bf16[384,128]{1,0:T(8,128)(2,1)S(1)}, u32[]{:S(2)}, u32[]{:S(2)}) collective-permute-start(bf16[384,128]{1,0:T(8,128)(2,1)S(1)} %collective-permute-done.6.refs_1_), channel_id=1, source_target_pairs={{0,4},{1,5},{2,6},{3,7},{4,0},{5,1},{6,2},{7,3},{8,12},{9,13},{10,... | collective-permute-start | bytes 294920 | tf_op jit(solution)/shard_map/ppermute | solution.py:169
  26.1 0.1 collective-permute-done.3.refs_5_
  26.2 1.6 %collective-permute-done.5.refs_7_ = bf16[384,128]{1,0:T(8,128)(2,1)S(1)} collective-permute-done((bf16[384,128]{1,0:T(8,128)(2,1)S(1)}, bf16[384,128]{1,0:T(8,128)(2,1)S(1)}, u32[]{:S(2)}, u32[]{:S(2)}) %collective-permute-start.5) | collective-permute-done | bytes 98336 | tf_op jit(solution)/shard_map/ppermute | solution.py:169
  27.9 0.0 copy-done.3
  27.9 0.1 shard_map.96
  28.0 0.0 collective-permute-done.7.refs_2_
  28.0 1.6 %collective-permute-done.8.refs_3_ = bf16[384,128]{1,0:T(8,128)(2,1)S(1)} collective-permute-done((bf16[384,128]{1,0:T(8,128)(2,1)S(1)}, bf16[384,128]{1,0:T(8,128)(2,1)S(1)}, u32[]{:S(2)}, u32[]{:S(2)}) %collective-permute-start.8) | collective-permute-done | bytes 98336 | tf_op jit(solution)/shard_map/ppermute | solution.py:169
  29.6 0.3 shard_map.101
  29.9 0.1 collective-permute-start.10
  30.0 0.3 shard_map.98
  30.2 0.6 %collective-permute-start.9 = (bf16[192,384]{1,0:T(8,128)(2,1)S(1)}, bf16[192,384]{1,0:T(8,128)(2,1)S(1)}, u32[]{:S(2)}, u32[]{:S(2)}) collective-permute-start(bf16[192,384]{1,0:T(8,128)(2,1)S(1)} %shard_map.98), channel_id=1, source_target_pairs={{0,1},{1,0},{2,3},{3,2},{4,5},{5,4},{6,7},{7,6},{8,9},{9,8},{10,11... | collective-permute-start | bytes 442376 | tf_op jit(solution)/shard_map/ppermute | solution.py:169
  30.8 0.3 shard_map.97.keep_ref
  31.1 0.3 shard_map.100.keep_ref
  31.3 0.0 collective-permute-done.10.got_ref
  31.4 0.7 %collective-permute-start.11 = (bf16[96,384]{1,0:T(8,128)(2,1)S(1)}, bf16[96,384]{1,0:T(8,128)(2,1)S(1)}, u32[]{:S(2)}, u32[]{:S(2)}) collective-permute-start(bf16[96,384]{1,0:T(8,128)(2,1)S(1)} %get-tuple-element.44), channel_id=1, source_target_pairs={{0,16},{1,17},{2,18},{3,19},{4,20},{5,21},{6,22},{7,23},{8,24},{9,... | collective-permute-start | bytes 221192 | tf_op jit(solution)/shard_map/ppermute | solution.py:169
  32.1 2.3 %collective-permute-start.12 = (bf16[96,384]{1,0:T(8,128)(2,1)S(1)}, bf16[96,384]{1,0:T(8,128)(2,1)S(1)}, u32[]{:S(2)}, u32[]{:S(2)}) collective-permute-start(bf16[96,384]{1,0:T(8,128)(2,1)S(1)} %get-tuple-element.45), channel_id=1, source_target_pairs={{0,24},{1,25},{2,26},{3,27},{4,28},{5,29},{6,30},{7,31},{8,16},{9,... | collective-permute-start | bytes 221192 | tf_op jit(solution)/shard_map/ppermute | solution.py:169
  34.3 0.0 collective-permute-done.9.got_ref
  34.4 0.7 %collective-permute-start.13 = (bf16[96,384]{1,0:T(8,128)(2,1)S(1)}, bf16[96,384]{1,0:T(8,128)(2,1)S(1)}, u32[]{:S(2)}, u32[]{:S(2)}) collective-permute-start(bf16[96,384]{1,0:T(8,128)(2,1)S(1)} %get-tuple-element.46), channel_id=1, source_target_pairs={{0,8},{1,9},{2,10},{3,11},{4,12},{5,13},{6,14},{7,15},{8,0},{9,1},... | collective-permute-start | bytes 221192 | tf_op jit(solution)/shard_map/ppermute | solution.py:169
  35.0 4.9 %collective-permute-done.11.refs_1_ = bf16[96,384]{1,0:T(8,128)(2,1)S(1)} collective-permute-done((bf16[96,384]{1,0:T(8,128)(2,1)S(1)}, bf16[96,384]{1,0:T(8,128)(2,1)S(1)}, u32[]{:S(2)}, u32[]{:S(2)}) %collective-permute-start.11) | collective-permute-done | bytes 73760 | tf_op jit(solution)/shard_map/ppermute | solution.py:169
  39.9 0.0 collective-permute-done.12.refs_2_
  39.9 1.2 %collective-permute-done.13.refs_3_ = bf16[96,384]{1,0:T(8,128)(2,1)S(1)} collective-permute-done((bf16[96,384]{1,0:T(8,128)(2,1)S(1)}, bf16[96,384]{1,0:T(8,128)(2,1)S(1)}, u32[]{:S(2)}, u32[]{:S(2)}) %collective-permute-start.13) | collective-permute-done | bytes 73760 | tf_op jit(solution)/shard_map/ppermute | solution.py:169
  41.1 1.5 %collective-permute-start.15 = (bf16[96,384]{1,0:T(8,128)(2,1)S(1)}, bf16[96,384]{1,0:T(8,128)(2,1)S(1)}, u32[]{:S(2)}, u32[]{:S(2)}) collective-permute-start(bf16[96,384]{1,0:T(8,128)(2,1)S(1)} %shard_map.103.refs_0_), channel_id=1, source_target_pairs={{0,2},{1,3},{2,0},{3,1},{4,6},{5,7},{6,4},{7,5},{8,10},{9,11},{10,... | collective-permute-start | bytes 221192 | tf_op jit(solution)/shard_map/ppermute | solution.py:169
  42.6 0.0 collective-permute-start.14
  42.7 2.9 %collective-permute-done.15.refs_2_ = bf16[96,384]{1,0:T(8,128)(2,1)S(1)} collective-permute-done((bf16[96,384]{1,0:T(8,128)(2,1)S(1)}, bf16[96,384]{1,0:T(8,128)(2,1)S(1)}, u32[]{:S(2)}, u32[]{:S(2)}) %collective-permute-start.15) | collective-permute-done | bytes 73760 | tf_op jit(solution)/shard_map/ppermute | solution.py:169
  45.6 0.0 collective-permute-start.16
  45.6 0.7 %convert_element_type.3 = bf16[128,768]{1,0:T(8,128)(2,1)} convert(f32[128,768]{1,0:T(8,128)S(1)} %get-tuple-element.31) | non-fusion elementwise | flops 98304 | bytes 589824 | tf_op jit(solution)/shard_map/convert_element_type | solution.py:356
  46.3 0.0 collective-permute-done.14.refs_1_
  46.3 0.6 %collective-permute-done.16.refs_3_ = bf16[96,384]{1,0:T(8,128)(2,1)S(1)} collective-permute-done((bf16[96,384]{1,0:T(8,128)(2,1)S(1)}, bf16[96,384]{1,0:T(8,128)(2,1)S(1)}, u32[]{:S(2)}, u32[]{:S(2)}) %collective-permute-start.16) | collective-permute-done | bytes 73760 | tf_op jit(solution)/shard_map/ppermute | solution.py:169
  46.8 0.9 %shard_map.104 = (f32[96,768]{1,0:T(8,128)}, f32[96,768]{1,0:T(8,128)}) custom-call(bf16[96,384]{1,0:T(8,128)(2,1)S(1)} %shard_map.103.refs_0_, bf16[96,384]{1,0:T(8,128)(2,1)S(1)} %collective-permute-done.14.refs_1_, bf16[96,384]{1,0:T(8,128)(2,1)S(1)} %collective-permute-done.15.refs_2_, bf16[96,384]{1,0:T(8,128)(2,1)S(1)} %collective-permute-done.16.refs_3_), custom_call_target="tpu_custom_call" | custom-call | bytes 884736 | tf_op jit(solution)/shard_map/pallas_call | solution.py:23
  (3 shorter events, 0.1 us)
Async XLA Ops:
  0.6 12.7 %copy-start = (bf16[768,768]{1,0:T(8,128)(2,1)S(1)}, bf16[768,768]{1,0:T(8,128)(2,1)}, u32[]{:S(2)}) copy-start(bf16[768,768]{1,0:T(8,128)(2,1)} %param.12) | copy-start | bytes 3538948
  2.9 14.1 %copy-start.1 = (bf16[768,768]{1,0:T(8,128)(2,1)S(1)}, bf16[768,768]{1,0:T(8,128)(2,1)}, u32[]{:S(2)}) copy-start(bf16[768,768]{1,0:T(8,128)(2,1)} %w_ref.1) | copy-start | bytes 3538948
  2.9 14.1 %copy-start.2 = (bf16[128,768]{1,0:T(8,128)(2,1)S(1)}, bf16[128,768]{1,0:T(8,128)(2,1)}, u32[]{:S(2)}) copy-start(bf16[128,768]{1,0:T(8,128)(2,1)} %cot_ref.1) | copy-start | bytes 589828
  2.9 14.1 %copy-start.4 = (s32[1,1,8,12]{3,2,1,0:T(8,128)S(1)}, s32[1,1,8,12]{3,2,1,0:T(8,128)}, u32[]{:S(2)}) copy-start(s32[1,1,8,12]{3,2,1,0:T(8,128)} %param.10) | copy-start | bytes 1156
  2.9 8.9 %collective-permute-start = (bf16[384,128]{1,0:T(8,128)(2,1)}, bf16[384,128]{1,0:T(8,128)(2,1)S(1)}, u32[]{:S(2)}, u32[]{:S(2)}) collective-permute-start(bf16[384,128]{1,0:T(8,128)(2,1)} %get-tuple-element.32), channel_id=1, source_target_pairs={{0,4},{1,5},{2,6},{3,7},{4,0},{5,1},{6,2},{7,3},{8,12},{9,13},{10,... | collective-permute-start | bytes 294920 | tf_op jit(solution)/shard_map/ppermute | solution.py:169
  5.9 11.1 %all-to-all-start = ((bf16[8,80,128]{2,1,0:T(8,128)(2,1)}), bf16[8,80,128]{2,1,0:T(8,128)(2,1)S(1)}, u32[]{:S(2)}, u32[]{:S(2)}) async-start(bf16[8,80,128]{2,1,0:T(8,128)(2,1)} %bitcast.10), calls=%async_computation | async-start | bytes 327680 | tf_op jit(solution)/shard_map/all_to_all | solution.py:280
  11.8 4.8 %collective-permute-start.1 = (bf16[384,128]{1,0:T(8,128)(2,1)}, bf16[384,128]{1,0:T(8,128)(2,1)S(1)}, u32[]{:S(2)}, u32[]{:S(2)}) collective-permute-start(bf16[384,128]{1,0:T(8,128)(2,1)} %get-tuple-element.30.refs_3_), channel_id=1, source_target_pairs={{0,2},{1,3},{2,0},{3,1},{4,6},{5,7},{6,4},{7,5},{8,10},{9,11},{10,... | collective-permute-start | bytes 294920 | tf_op jit(solution)/shard_map/ppermute | solution.py:169
  14.6 13.3 %copy-start.3 = (bf16[384,128]{1,0:T(8,128)(2,1)S(1)}, bf16[384,128]{1,0:T(8,128)(2,1)}, u32[]{:S(2)}) copy-start(bf16[384,128]{1,0:T(8,128)(2,1)} %get-tuple-element.30.refs_3_) | copy-start | bytes 294916
  14.6 7.3 %collective-permute-start.2 = (bf16[384,128]{1,0:T(8,128)(2,1)}, bf16[384,128]{1,0:T(8,128)(2,1)S(1)}, u32[]{:S(2)}, u32[]{:S(2)}) collective-permute-start(bf16[384,128]{1,0:T(8,128)(2,1)} %get-tuple-element.32), channel_id=1, source_target_pairs={{0,6},{1,7},{2,4},{3,5},{4,2},{5,3},{6,0},{7,1},{8,14},{9,15},{10,... | collective-permute-start | bytes 294920 | tf_op jit(solution)/shard_map/ppermute | solution.py:169
  17.8 5.5 %collective-permute-start.4 = (bf16[384,128]{1,0:T(8,128)(2,1)S(1)}, bf16[384,128]{1,0:T(8,128)(2,1)S(1)}, u32[]{:S(2)}, u32[]{:S(2)}) collective-permute-start(bf16[384,128]{1,0:T(8,128)(2,1)S(1)} %get-tuple-element.34), channel_id=1, source_target_pairs={{0,4},{1,5},{2,6},{3,7},{4,0},{5,1},{6,2},{7,3},{8,12},{9,13},{10,... | collective-permute-start | bytes 294920 | tf_op jit(solution)/shard_map/ppermute | solution.py:169
  19.2 5.8 %collective-permute-start.6 = (bf16[384,128]{1,0:T(8,128)(2,1)S(1)}, bf16[384,128]{1,0:T(8,128)(2,1)S(1)}, u32[]{:S(2)}, u32[]{:S(2)}) collective-permute-start(bf16[384,128]{1,0:T(8,128)(2,1)S(1)} %get-tuple-element.38), channel_id=1, source_target_pairs={{0,2},{1,3},{2,0},{3,1},{4,6},{5,7},{6,4},{7,5},{8,10},{9,11},{10,... | collective-permute-start | bytes 294920 | tf_op jit(solution)/shard_map/ppermute | solution.py:169
  21.5 4.7 %collective-permute-start.3 = (bf16[384,128]{1,0:T(8,128)(2,1)S(1)}, bf16[384,128]{1,0:T(8,128)(2,1)S(1)}, u32[]{:S(2)}, u32[]{:S(2)}) collective-permute-start(bf16[384,128]{1,0:T(8,128)(2,1)S(1)} %get-tuple-element.33.refs_4_), channel_id=1, source_target_pairs={{0,2},{1,3},{2,0},{3,1},{4,6},{5,7},{6,4},{7,5},{8,10},{9,11},{10,... | collective-permute-start | bytes 294920 | tf_op jit(solution)/shard_map/ppermute | solution.py:169
  21.6 6.5 %collective-permute-start.7 = (bf16[384,128]{1,0:T(8,128)(2,1)S(1)}, bf16[384,128]{1,0:T(8,128)(2,1)S(1)}, u32[]{:S(2)}, u32[]{:S(2)}) collective-permute-start(bf16[384,128]{1,0:T(8,128)(2,1)S(1)} %get-tuple-element.37.refs_0_), channel_id=1, source_target_pairs={{0,4},{1,5},{2,6},{3,7},{4,0},{5,1},{6,2},{7,3},{8,12},{9,13},{10,... | collective-permute-start | bytes 294920 | tf_op jit(solution)/shard_map/ppermute | solution.py:169
  23.2 4.6 %collective-permute-start.5 = (bf16[384,128]{1,0:T(8,128)(2,1)S(1)}, bf16[384,128]{1,0:T(8,128)(2,1)S(1)}, u32[]{:S(2)}, u32[]{:S(2)}) collective-permute-start(bf16[384,128]{1,0:T(8,128)(2,1)S(1)} %collective-permute-done.4.refs_6_), channel_id=1, source_target_pairs={{0,2},{1,3},{2,0},{3,1},{4,6},{5,7},{6,4},{7,5},{8,10},{9,11},{10,... | collective-permute-start | bytes 294920 | tf_op jit(solution)/shard_map/ppermute | solution.py:169
  25.0 4.6 %collective-permute-start.8 = (bf16[384,128]{1,0:T(8,128)(2,1)S(1)}, bf16[384,128]{1,0:T(8,128)(2,1)S(1)}, u32[]{:S(2)}, u32[]{:S(2)}) collective-permute-start(bf16[384,128]{1,0:T(8,128)(2,1)S(1)} %collective-permute-done.6.refs_1_), channel_id=1, source_target_pairs={{0,4},{1,5},{2,6},{3,7},{4,0},{5,1},{6,2},{7,3},{8,12},{9,13},{10,... | collective-permute-start | bytes 294920 | tf_op jit(solution)/shard_map/ppermute | solution.py:169
  29.9 1.4 %collective-permute-start.10 = (bf16[192,384]{1,0:T(8,128)(2,1)S(1)}, bf16[192,384]{1,0:T(8,128)(2,1)S(1)}, u32[]{:S(2)}, u32[]{:S(2)}) collective-permute-start(bf16[192,384]{1,0:T(8,128)(2,1)S(1)} %shard_map.101), channel_id=1, source_target_pairs={{0,1},{1,0},{2,3},{3,2},{4,5},{5,4},{6,7},{7,6},{8,9},{9,8},{10,11... | collective-permute-start | bytes 442376 | tf_op jit(solution)/shard_map/ppermute | solution.py:169
  30.2 4.1 %collective-permute-start.9 = (bf16[192,384]{1,0:T(8,128)(2,1)S(1)}, bf16[192,384]{1,0:T(8,128)(2,1)S(1)}, u32[]{:S(2)}, u32[]{:S(2)}) collective-permute-start(bf16[192,384]{1,0:T(8,128)(2,1)S(1)} %shard_map.98), channel_id=1, source_target_pairs={{0,1},{1,0},{2,3},{3,2},{4,5},{5,4},{6,7},{7,6},{8,9},{9,8},{10,11... | collective-permute-start | bytes 442376 | tf_op jit(solution)/shard_map/ppermute | solution.py:169
  31.4 8.5 %collective-permute-start.11 = (bf16[96,384]{1,0:T(8,128)(2,1)S(1)}, bf16[96,384]{1,0:T(8,128)(2,1)S(1)}, u32[]{:S(2)}, u32[]{:S(2)}) collective-permute-start(bf16[96,384]{1,0:T(8,128)(2,1)S(1)} %get-tuple-element.44), channel_id=1, source_target_pairs={{0,16},{1,17},{2,18},{3,19},{4,20},{5,21},{6,22},{7,23},{8,24},{9,... | collective-permute-start | bytes 221192 | tf_op jit(solution)/shard_map/ppermute | solution.py:169
  32.1 7.8 %collective-permute-start.12 = (bf16[96,384]{1,0:T(8,128)(2,1)S(1)}, bf16[96,384]{1,0:T(8,128)(2,1)S(1)}, u32[]{:S(2)}, u32[]{:S(2)}) collective-permute-start(bf16[96,384]{1,0:T(8,128)(2,1)S(1)} %get-tuple-element.45), channel_id=1, source_target_pairs={{0,24},{1,25},{2,26},{3,27},{4,28},{5,29},{6,30},{7,31},{8,16},{9,... | collective-permute-start | bytes 221192 | tf_op jit(solution)/shard_map/ppermute | solution.py:169
  34.4 6.7 %collective-permute-start.13 = (bf16[96,384]{1,0:T(8,128)(2,1)S(1)}, bf16[96,384]{1,0:T(8,128)(2,1)S(1)}, u32[]{:S(2)}, u32[]{:S(2)}) collective-permute-start(bf16[96,384]{1,0:T(8,128)(2,1)S(1)} %get-tuple-element.46), channel_id=1, source_target_pairs={{0,8},{1,9},{2,10},{3,11},{4,12},{5,13},{6,14},{7,15},{8,0},{9,1},... | collective-permute-start | bytes 221192 | tf_op jit(solution)/shard_map/ppermute | solution.py:169
  41.1 4.4 %collective-permute-start.15 = (bf16[96,384]{1,0:T(8,128)(2,1)S(1)}, bf16[96,384]{1,0:T(8,128)(2,1)S(1)}, u32[]{:S(2)}, u32[]{:S(2)}) collective-permute-start(bf16[96,384]{1,0:T(8,128)(2,1)S(1)} %shard_map.103.refs_0_), channel_id=1, source_target_pairs={{0,2},{1,3},{2,0},{3,1},{4,6},{5,7},{6,4},{7,5},{8,10},{9,11},{10,... | collective-permute-start | bytes 221192 | tf_op jit(solution)/shard_map/ppermute | solution.py:169
  42.6 3.6 %collective-permute-start.14 = (bf16[96,384]{1,0:T(8,128)(2,1)S(1)}, bf16[96,384]{1,0:T(8,128)(2,1)S(1)}, u32[]{:S(2)}, u32[]{:S(2)}) collective-permute-start(bf16[96,384]{1,0:T(8,128)(2,1)S(1)} %shard_map.103.refs_0_), channel_id=1, source_target_pairs={{0,1},{1,0},{2,3},{3,2},{4,5},{5,4},{6,7},{7,6},{8,9},{9,8},{10,11... | collective-permute-start | bytes 221192 | tf_op jit(solution)/shard_map/ppermute | solution.py:169
  45.6 1.3 %collective-permute-start.16 = (bf16[96,384]{1,0:T(8,128)(2,1)S(1)}, bf16[96,384]{1,0:T(8,128)(2,1)S(1)}, u32[]{:S(2)}, u32[]{:S(2)}) collective-permute-start(bf16[96,384]{1,0:T(8,128)(2,1)S(1)} %collective-permute-done.15.refs_2_), channel_id=1, source_target_pairs={{0,1},{1,0},{2,3},{3,2},{4,5},{5,4},{6,7},{7,6},{8,9},{9,8},{10,11... | collective-permute-start | bytes 221192 | tf_op jit(solution)/shard_map/ppermute | solution.py:169

commit v11 on v6

--- a/solution.py
+++ b/solution.py
@@ -169,10 +169,9 @@
         return lax.ppermute(array, ("store", "trainer"), pairs)
 
     def store_order(self):
-        up = [(z, x) for z in reversed(range(self.nz)) for x in reversed(range(self.gx))]
-        down = [(z, x) for z in range(self.nz) for x in range(self.gx)]
-        turns = [at for pair in zip(up, down) for at in pair]
-        return [z * self.gx + x for z, x in turns[:self.ns]]
+        middle = self.ns // 2
+        turns = [s for pair in zip(range(middle, self.ns), range(middle - 1, -1, -1)) for s in pair]
+        return turns
 
 
 def write_rows(plan, trans_ref, *outs):

time: 47.5 us -> 46.5 us (0.979)
  starting transfers between devices: 25.6 us -> 24.1 us
  waiting for transfers between devices: 13.6 us -> 14.1 us
    all_to_all x1, starting transfers between devices: 9.27 us -> 7.82 us  [per_device(): lax.all_to_all(sums.reshape(ns, packed, 128), 'store', split_axis=0, conc...]
where the time goes in v11:
time: 46.5 us; the launch traced here: 46.2 us
  starting transfers between devices  24.1 us (52%)
  waiting for transfers between devices  14.1 us (30%)
  Pallas kernels  5.3 us (11%)
  matrix products  1.25 us (3%)
  between operations  0.75 us (2%)
  other arithmetic  0.7 us (2%)
    ppermute x17, starting transfers between devices, send(): return lax.ppermute(array, ('store', 'trainer'), pairs)  16.3 us
    ppermute x17, waiting for transfers between devices, send(): return lax.ppermute(array, ('store', 'trainer'), pairs)  13.7 us
    all_to_all x1, starting transfers between devices, per_device(): lax.all_to_all(sums.reshape(ns, packed, 128), 'store', split_axis=0, conc...  7.82 us
    pallas_call x12, Pallas kernels, call(): pl.pallas_call(body, out_shape=list(outs), in_specs=[VMEM] * len(args) +...  5.3 us
    dot_general x1, matrix products, dot(): return jnp.dot(a, b, preferred_element_type=F32)  1.25 us
  transfers between devices with their start and end apart: 18, of which 9 were waited for; matrix products, arithmetic and copies ran while one was open for 4% of the time, Pallas kernels for 4%

profile of v11, /device:TPU:0, one launch (start us, length us, event | category | flops | bytes accessed | tf_op | source)
XLA Modules:
  0.0 46.2 jit_solution(1566448232885913883)
XLA Ops:
  0.6 0.0 copy-start
  0.6 2.2 %shard_map.94 = (bf16[640,128]{1,0:T(8,128)(2,1)}, bf16[128,768]{1,0:T(8,128)(2,1)}, bf16[384,128]{1,0:T(8,128)(2,1)}, bf16[384,128]{1,0:T(8,128)(2,1)}) custom-call(f32[128,768]{1,0:T(8,128)} %feat_hbm.1, s32[8,2,12]{2,1,0:T(2,128)} %bitcast.11, f32[128,768]{1,0:T(8,128)} %rest_0_.1), custom_call_target="tpu_custom_call" | custom-call | flops 50331648 | bytes 557056 | tf_op jit(solution)/shard_map/pallas_call | solution.py:23
  2.9 0.0 copy-start.4
  2.9 7.8 %all-to-all-start = ((bf16[8,80,128]{2,1,0:T(8,128)(2,1)}), bf16[8,80,128]{2,1,0:T(8,128)(2,1)S(1)}, u32[]{:S(2)}, u32[]{:S(2)}) async-start(bf16[8,80,128]{2,1,0:T(8,128)(2,1)} %bitcast.10), calls=%async_computation | async-start | bytes 327680 | tf_op jit(solution)/shard_map/all_to_all | solution.py:284
  10.7 0.0 copy-start.1
  10.7 0.0 copy-start.2
  10.7 2.4 %collective-permute-start = (bf16[384,128]{1,0:T(8,128)(2,1)}, bf16[384,128]{1,0:T(8,128)(2,1)S(1)}, u32[]{:S(2)}, u32[]{:S(2)}) collective-permute-start(bf16[384,128]{1,0:T(8,128)(2,1)} %get-tuple-element.29), channel_id=1, source_target_pairs={{0,6},{1,7},{2,4},{3,5},{4,2},{5,3},{6,0},{7,1},{8,14},{9,15},{10,... | collective-permute-start | bytes 294920 | tf_op jit(solution)/shard_map/ppermute | solution.py:169
  13.2 0.6 %collective-permute-start.1 = (bf16[384,128]{1,0:T(8,128)(2,1)}, bf16[384,128]{1,0:T(8,128)(2,1)S(1)}, u32[]{:S(2)}, u32[]{:S(2)}) collective-permute-start(bf16[384,128]{1,0:T(8,128)(2,1)} %get-tuple-element.29), channel_id=1, source_target_pairs={{0,4},{1,5},{2,6},{3,7},{4,0},{5,1},{6,2},{7,3},{8,12},{9,13},{10,... | collective-permute-start | bytes 294920 | tf_op jit(solution)/shard_map/ppermute | solution.py:169
  13.7 0.5 %collective-permute-start.2 = (bf16[384,128]{1,0:T(8,128)(2,1)}, bf16[384,128]{1,0:T(8,128)(2,1)S(1)}, u32[]{:S(2)}, u32[]{:S(2)}) collective-permute-start(bf16[384,128]{1,0:T(8,128)(2,1)} %get-tuple-element.30.refs_3_), channel_id=1, source_target_pairs={{0,2},{1,3},{2,0},{3,1},{4,6},{5,7},{6,4},{7,5},{8,10},{9,11},{10,... | collective-permute-start | bytes 294920 | tf_op jit(solution)/shard_map/ppermute | solution.py:169
  14.2 0.0 copy-done
  14.2 1.2 %fusion._.self_ref = f32[128,768]{1,0:T(8,128)S(1)} fusion(bf16[128,768]{1,0:T(8,128)(2,1)} %get-tuple-element.26, bf16[768,768]{1,0:T(8,128)(2,1)S(1)} %copy-done), kind=kOutput, calls=%fused_computation | convolution fusion | flops 150994944 | bytes 1769472 | tf_op jit(solution)/shard_map/dot_general | solution.py:18
  15.5 0.5 all-to-all-done
  15.9 0.0 copy-done.4
  15.9 0.0 copy-start.3
  15.9 0.5 %shard_map.95 = (bf16[128,768]{1,0:T(8,128)(2,1)S(1)}, bf16[384,128]{1,0:T(8,128)(2,1)S(1)}, bf16[384,128]{1,0:T(8,128)(2,1)S(1)}) custom-call(bf16[640,128]{1,0:T(8,128)(2,1)S(1)} %bitcast.8, s32[8,12]{1,0:T(8,128)S(1)} %bitcast.9, f32[128,768]{1,0:T(8,128)S(1)} %fusion._.self_ref), custom_call_target="tpu_custom_call" | custom-call | flops 25165824 | bytes 950656 | tf_op jit(solution)/shard_map/pallas_call | solution.py:23
  16.5 1.1 %collective-permute-start.4 = (bf16[384,128]{1,0:T(8,128)(2,1)S(1)}, bf16[384,128]{1,0:T(8,128)(2,1)S(1)}, u32[]{:S(2)}, u32[]{:S(2)}) collective-permute-start(bf16[384,128]{1,0:T(8,128)(2,1)S(1)} %get-tuple-element.32), channel_id=1, source_target_pairs={{0,4},{1,5},{2,6},{3,7},{4,0},{5,1},{6,2},{7,3},{8,12},{9,13},{10,... | collective-permute-start | bytes 294920 | tf_op jit(solution)/shard_map/ppermute | solution.py:169
  17.6 0.0 copy-done.1
  17.6 0.0 copy-done.2
  17.6 0.4 shard_map.96
  18.0 1.6 %collective-permute-start.6 = (bf16[384,128]{1,0:T(8,128)(2,1)S(1)}, bf16[384,128]{1,0:T(8,128)(2,1)S(1)}, u32[]{:S(2)}, u32[]{:S(2)}) collective-permute-start(bf16[384,128]{1,0:T(8,128)(2,1)S(1)} %get-tuple-element.36), channel_id=1, source_target_pairs={{0,2},{1,3},{2,0},{3,1},{4,6},{5,7},{6,4},{7,5},{8,10},{9,11},{10,... | collective-permute-start | bytes 294920 | tf_op jit(solution)/shard_map/ppermute | solution.py:169
  19.6 0.0 collective-permute-done.refs_0_
  19.6 0.5 %collective-permute-start.3 = (bf16[384,128]{1,0:T(8,128)(2,1)S(1)}, bf16[384,128]{1,0:T(8,128)(2,1)S(1)}, u32[]{:S(2)}, u32[]{:S(2)}) collective-permute-start(bf16[384,128]{1,0:T(8,128)(2,1)S(1)} %get-tuple-element.31.refs_4_), channel_id=1, source_target_pairs={{0,2},{1,3},{2,0},{3,1},{4,6},{5,7},{6,4},{7,5},{8,10},{9,11},{10,... | collective-permute-start | bytes 294920 | tf_op jit(solution)/shard_map/ppermute | solution.py:169
  20.1 0.0 collective-permute-done.1.refs_1_
  20.1 1.0 %collective-permute-start.7 = (bf16[384,128]{1,0:T(8,128)(2,1)S(1)}, bf16[384,128]{1,0:T(8,128)(2,1)S(1)}, u32[]{:S(2)}, u32[]{:S(2)}) collective-permute-start(bf16[384,128]{1,0:T(8,128)(2,1)S(1)} %get-tuple-element.35.refs_0_), channel_id=1, source_target_pairs={{0,4},{1,5},{2,6},{3,7},{4,0},{5,1},{6,2},{7,3},{8,12},{9,13},{10,... | collective-permute-start | bytes 294920 | tf_op jit(solution)/shard_map/ppermute | solution.py:169
  21.1 0.0 collective-permute-done.2.refs_2_
  21.1 0.4 collective-permute-done.4.refs_6_
  21.5 2.0 %collective-permute-start.5 = (bf16[384,128]{1,0:T(8,128)(2,1)S(1)}, bf16[384,128]{1,0:T(8,128)(2,1)S(1)}, u32[]{:S(2)}, u32[]{:S(2)}) collective-permute-start(bf16[384,128]{1,0:T(8,128)(2,1)S(1)} %collective-permute-done.4.refs_6_), channel_id=1, source_target_pairs={{0,2},{1,3},{2,0},{3,1},{4,6},{5,7},{6,4},{7,5},{8,10},{9,11},{10,... | collective-permute-start | bytes 294920 | tf_op jit(solution)/shard_map/ppermute | solution.py:169
  23.5 0.0 collective-permute-done.6.refs_1_
  23.5 1.0 %collective-permute-start.8 = (bf16[384,128]{1,0:T(8,128)(2,1)S(1)}, bf16[384,128]{1,0:T(8,128)(2,1)S(1)}, u32[]{:S(2)}, u32[]{:S(2)}) collective-permute-start(bf16[384,128]{1,0:T(8,128)(2,1)S(1)} %collective-permute-done.6.refs_1_), channel_id=1, source_target_pairs={{0,4},{1,5},{2,6},{3,7},{4,0},{5,1},{6,2},{7,3},{8,12},{9,13},{10,... | collective-permute-start | bytes 294920 | tf_op jit(solution)/shard_map/ppermute | solution.py:169
  24.5 0.3 collective-permute-done.3.refs_5_
  24.8 1.3 %collective-permute-done.5.refs_7_ = bf16[384,128]{1,0:T(8,128)(2,1)S(1)} collective-permute-done((bf16[384,128]{1,0:T(8,128)(2,1)S(1)}, bf16[384,128]{1,0:T(8,128)(2,1)S(1)}, u32[]{:S(2)}, u32[]{:S(2)}) %collective-permute-start.5) | collective-permute-done | bytes 98336 | tf_op jit(solution)/shard_map/ppermute | solution.py:169
  26.1 0.0 copy-done.3
  26.1 0.1 shard_map.97
  26.3 0.0 collective-permute-done.7.refs_2_
  26.3 1.9 %collective-permute-done.8.refs_3_ = bf16[384,128]{1,0:T(8,128)(2,1)S(1)} collective-permute-done((bf16[384,128]{1,0:T(8,128)(2,1)S(1)}, bf16[384,128]{1,0:T(8,128)(2,1)S(1)}, u32[]{:S(2)}, u32[]{:S(2)}) %collective-permute-start.8) | collective-permute-done | bytes 98336 | tf_op jit(solution)/shard_map/ppermute | solution.py:169
  28.2 0.3 shard_map.102
  28.4 0.1 collective-permute-start.10
  28.5 0.3 shard_map.99
  28.8 0.6 %collective-permute-start.9 = (bf16[192,384]{1,0:T(8,128)(2,1)S(1)}, bf16[192,384]{1,0:T(8,128)(2,1)S(1)}, u32[]{:S(2)}, u32[]{:S(2)}) collective-permute-start(bf16[192,384]{1,0:T(8,128)(2,1)S(1)} %shard_map.99), channel_id=1, source_target_pairs={{0,1},{1,0},{2,3},{3,2},{4,5},{5,4},{6,7},{7,6},{8,9},{9,8},{10,11... | collective-permute-start | bytes 442376 | tf_op jit(solution)/shard_map/ppermute | solution.py:169
  29.3 0.3 shard_map.98.keep_ref
  29.6 0.3 shard_map.101.keep_ref
  29.8 0.0 collective-permute-done.10.got_ref
  29.9 1.1 %collective-permute-start.11 = (bf16[96,384]{1,0:T(8,128)(2,1)S(1)}, bf16[96,384]{1,0:T(8,128)(2,1)S(1)}, u32[]{:S(2)}, u32[]{:S(2)}) collective-permute-start(bf16[96,384]{1,0:T(8,128)(2,1)S(1)} %get-tuple-element.42), channel_id=1, source_target_pairs={{0,16},{1,17},{2,18},{3,19},{4,20},{5,21},{6,22},{7,23},{8,24},{9,... | collective-permute-start | bytes 221192 | tf_op jit(solution)/shard_map/ppermute | solution.py:169
  31.0 2.3 %collective-permute-start.12 = (bf16[96,384]{1,0:T(8,128)(2,1)S(1)}, bf16[96,384]{1,0:T(8,128)(2,1)S(1)}, u32[]{:S(2)}, u32[]{:S(2)}) collective-permute-start(bf16[96,384]{1,0:T(8,128)(2,1)S(1)} %get-tuple-element.43), channel_id=1, source_target_pairs={{0,24},{1,25},{2,26},{3,27},{4,28},{5,29},{6,30},{7,31},{8,16},{9,... | collective-permute-start | bytes 221192 | tf_op jit(solution)/shard_map/ppermute | solution.py:169
  33.2 0.0 collective-permute-done.9.got_ref
  33.3 0.3 collective-permute-start.13
  33.5 5.3 %collective-permute-done.11.refs_1_ = bf16[96,384]{1,0:T(8,128)(2,1)S(1)} collective-permute-done((bf16[96,384]{1,0:T(8,128)(2,1)S(1)}, bf16[96,384]{1,0:T(8,128)(2,1)S(1)}, u32[]{:S(2)}, u32[]{:S(2)}) %collective-permute-start.11) | collective-permute-done | bytes 73760 | tf_op jit(solution)/shard_map/ppermute | solution.py:169
  38.8 0.0 collective-permute-done.12.refs_2_
  38.8 0.8 %collective-permute-done.13.refs_3_ = bf16[96,384]{1,0:T(8,128)(2,1)S(1)} collective-permute-done((bf16[96,384]{1,0:T(8,128)(2,1)S(1)}, bf16[96,384]{1,0:T(8,128)(2,1)S(1)}, u32[]{:S(2)}, u32[]{:S(2)}) %collective-permute-start.13) | collective-permute-done | bytes 73760 | tf_op jit(solution)/shard_map/ppermute | solution.py:169
  39.7 1.3 %collective-permute-start.15 = (bf16[96,384]{1,0:T(8,128)(2,1)S(1)}, bf16[96,384]{1,0:T(8,128)(2,1)S(1)}, u32[]{:S(2)}, u32[]{:S(2)}) collective-permute-start(bf16[96,384]{1,0:T(8,128)(2,1)S(1)} %shard_map.104.refs_0_), channel_id=1, source_target_pairs={{0,2},{1,3},{2,0},{3,1},{4,6},{5,7},{6,4},{7,5},{8,10},{9,11},{10,... | collective-permute-start | bytes 221192 | tf_op jit(solution)/shard_map/ppermute | solution.py:169
  41.0 0.0 collective-permute-start.14
  41.0 3.1 %collective-permute-done.15.refs_2_ = bf16[96,384]{1,0:T(8,128)(2,1)S(1)} collective-permute-done((bf16[96,384]{1,0:T(8,128)(2,1)S(1)}, bf16[96,384]{1,0:T(8,128)(2,1)S(1)}, u32[]{:S(2)}, u32[]{:S(2)}) %collective-permute-start.15) | collective-permute-done | bytes 73760 | tf_op jit(solution)/shard_map/ppermute | solution.py:169
  44.1 0.0 collective-permute-start.16
  44.1 0.7 %convert_element_type.3 = bf16[128,768]{1,0:T(8,128)(2,1)} convert(f32[128,768]{1,0:T(8,128)S(1)} %get-tuple-element.28) | non-fusion elementwise | flops 98304 | bytes 589824 | tf_op jit(solution)/shard_map/convert_element_type | solution.py:361
  44.8 0.0 collective-permute-done.14.refs_1_
  44.8 0.6 %collective-permute-done.16.refs_3_ = bf16[96,384]{1,0:T(8,128)(2,1)S(1)} collective-permute-done((bf16[96,384]{1,0:T(8,128)(2,1)S(1)}, bf16[96,384]{1,0:T(8,128)(2,1)S(1)}, u32[]{:S(2)}, u32[]{:S(2)}) %collective-permute-start.16) | collective-permute-done | bytes 73760 | tf_op jit(solution)/shard_map/ppermute | solution.py:169
  45.4 0.9 %shard_map.105 = (f32[96,768]{1,0:T(8,128)}, f32[96,768]{1,0:T(8,128)}) custom-call(bf16[96,384]{1,0:T(8,128)(2,1)S(1)} %shard_map.104.refs_0_, bf16[96,384]{1,0:T(8,128)(2,1)S(1)} %collective-permute-done.14.refs_1_, bf16[96,384]{1,0:T(8,128)(2,1)S(1)} %collective-permute-done.15.refs_2_, bf16[96,384]{1,0:T(8,128)(2,1)S(1)} %collective-permute-done.16.refs_3_), custom_call_target="tpu_custom_call" | custom-call | bytes 884736 | tf_op jit(solution)/shard_map/pallas_call | solution.py:23
  (3 shorter events, 0.1 us)
Async XLA Ops:
  0.6 13.6 %copy-start = (bf16[768,768]{1,0:T(8,128)(2,1)S(1)}, bf16[768,768]{1,0:T(8,128)(2,1)}, u32[]{:S(2)}) copy-start(bf16[768,768]{1,0:T(8,128)(2,1)} %param.12) | copy-start | bytes 3538948
  2.9 13.0 %copy-start.4 = (s32[1,1,8,12]{3,2,1,0:T(8,128)S(1)}, s32[1,1,8,12]{3,2,1,0:T(8,128)}, u32[]{:S(2)}) copy-start(s32[1,1,8,12]{3,2,1,0:T(8,128)} %param.10) | copy-start | bytes 1156
  2.9 13.0 %all-to-all-start = ((bf16[8,80,128]{2,1,0:T(8,128)(2,1)}), bf16[8,80,128]{2,1,0:T(8,128)(2,1)S(1)}, u32[]{:S(2)}, u32[]{:S(2)}) async-start(bf16[8,80,128]{2,1,0:T(8,128)(2,1)} %bitcast.10), calls=%async_computation | async-start | bytes 327680 | tf_op jit(solution)/shard_map/all_to_all | solution.py:284
  10.7 6.8 %copy-start.1 = (bf16[768,768]{1,0:T(8,128)(2,1)S(1)}, bf16[768,768]{1,0:T(8,128)(2,1)}, u32[]{:S(2)}) copy-start(bf16[768,768]{1,0:T(8,128)(2,1)} %w_ref.1) | copy-start | bytes 3538948
  10.7 6.8 %copy-start.2 = (bf16[128,768]{1,0:T(8,128)(2,1)S(1)}, bf16[128,768]{1,0:T(8,128)(2,1)}, u32[]{:S(2)}) copy-start(bf16[128,768]{1,0:T(8,128)(2,1)} %cot_ref.1) | copy-start | bytes 589828
  10.7 8.8 %collective-permute-start = (bf16[384,128]{1,0:T(8,128)(2,1)}, bf16[384,128]{1,0:T(8,128)(2,1)S(1)}, u32[]{:S(2)}, u32[]{:S(2)}) collective-permute-start(bf16[384,128]{1,0:T(8,128)(2,1)} %get-tuple-element.29), channel_id=1, source_target_pairs={{0,6},{1,7},{2,4},{3,5},{4,2},{5,3},{6,0},{7,1},{8,14},{9,15},{10,... | collective-permute-start | bytes 294920 | tf_op jit(solution)/shard_map/ppermute | solution.py:169
  13.2 6.9 %collective-permute-start.1 = (bf16[384,128]{1,0:T(8,128)(2,1)}, bf16[384,128]{1,0:T(8,128)(2,1)S(1)}, u32[]{:S(2)}, u32[]{:S(2)}) collective-permute-start(bf16[384,128]{1,0:T(8,128)(2,1)} %get-tuple-element.29), channel_id=1, source_target_pairs={{0,4},{1,5},{2,6},{3,7},{4,0},{5,1},{6,2},{7,3},{8,12},{9,13},{10,... | collective-permute-start | bytes 294920 | tf_op jit(solution)/shard_map/ppermute | solution.py:169
  13.7 7.4 %collective-permute-start.2 = (bf16[384,128]{1,0:T(8,128)(2,1)}, bf16[384,128]{1,0:T(8,128)(2,1)S(1)}, u32[]{:S(2)}, u32[]{:S(2)}) collective-permute-start(bf16[384,128]{1,0:T(8,128)(2,1)} %get-tuple-element.30.refs_3_), channel_id=1, source_target_pairs={{0,2},{1,3},{2,0},{3,1},{4,6},{5,7},{6,4},{7,5},{8,10},{9,11},{10,... | collective-permute-start | bytes 294920 | tf_op jit(solution)/shard_map/ppermute | solution.py:169
  15.9 10.2 %copy-start.3 = (bf16[384,128]{1,0:T(8,128)(2,1)S(1)}, bf16[384,128]{1,0:T(8,128)(2,1)}, u32[]{:S(2)}) copy-start(bf16[384,128]{1,0:T(8,128)(2,1)} %get-tuple-element.30.refs_3_) | copy-start | bytes 294916
  16.5 5.0 %collective-permute-start.4 = (bf16[384,128]{1,0:T(8,128)(2,1)S(1)}, bf16[384,128]{1,0:T(8,128)(2,1)S(1)}, u32[]{:S(2)}, u32[]{:S(2)}) collective-permute-start(bf16[384,128]{1,0:T(8,128)(2,1)S(1)} %get-tuple-element.32), channel_id=1, source_target_pairs={{0,4},{1,5},{2,6},{3,7},{4,0},{5,1},{6,2},{7,3},{8,12},{9,13},{10,... | collective-permute-start | bytes 294920 | tf_op jit(solution)/shard_map/ppermute | solution.py:169
  18.0 5.6 %collective-permute-start.6 = (bf16[384,128]{1,0:T(8,128)(2,1)S(1)}, bf16[384,128]{1,0:T(8,128)(2,1)S(1)}, u32[]{:S(2)}, u32[]{:S(2)}) collective-permute-start(bf16[384,128]{1,0:T(8,128)(2,1)S(1)} %get-tuple-element.36), channel_id=1, source_target_pairs={{0,2},{1,3},{2,0},{3,1},{4,6},{5,7},{6,4},{7,5},{8,10},{9,11},{10,... | collective-permute-start | bytes 294920 | tf_op jit(solution)/shard_map/ppermute | solution.py:169
  19.6 5.2 %collective-permute-start.3 = (bf16[384,128]{1,0:T(8,128)(2,1)S(1)}, bf16[384,128]{1,0:T(8,128)(2,1)S(1)}, u32[]{:S(2)}, u32[]{:S(2)}) collective-permute-start(bf16[384,128]{1,0:T(8,128)(2,1)S(1)} %get-tuple-element.31.refs_4_), channel_id=1, source_target_pairs={{0,2},{1,3},{2,0},{3,1},{4,6},{5,7},{6,4},{7,5},{8,10},{9,11},{10,... | collective-permute-start | bytes 294920 | tf_op jit(solution)/shard_map/ppermute | solution.py:169
  20.1 6.2 %collective-permute-start.7 = (bf16[384,128]{1,0:T(8,128)(2,1)S(1)}, bf16[384,128]{1,0:T(8,128)(2,1)S(1)}, u32[]{:S(2)}, u32[]{:S(2)}) collective-permute-start(bf16[384,128]{1,0:T(8,128)(2,1)S(1)} %get-tuple-element.35.refs_0_), channel_id=1, source_target_pairs={{0,4},{1,5},{2,6},{3,7},{4,0},{5,1},{6,2},{7,3},{8,12},{9,13},{10,... | collective-permute-start | bytes 294920 | tf_op jit(solution)/shard_map/ppermute | solution.py:169
  21.5 4.6 %collective-permute-start.5 = (bf16[384,128]{1,0:T(8,128)(2,1)S(1)}, bf16[384,128]{1,0:T(8,128)(2,1)S(1)}, u32[]{:S(2)}, u32[]{:S(2)}) collective-permute-start(bf16[384,128]{1,0:T(8,128)(2,1)S(1)} %collective-permute-done.4.refs_6_), channel_id=1, source_target_pairs={{0,2},{1,3},{2,0},{3,1},{4,6},{5,7},{6,4},{7,5},{8,10},{9,11},{10,... | collective-permute-start | bytes 294920 | tf_op jit(solution)/shard_map/ppermute | solution.py:169
  23.5 4.6 %collective-permute-start.8 = (bf16[384,128]{1,0:T(8,128)(2,1)S(1)}, bf16[384,128]{1,0:T(8,128)(2,1)S(1)}, u32[]{:S(2)}, u32[]{:S(2)}) collective-permute-start(bf16[384,128]{1,0:T(8,128)(2,1)S(1)} %collective-permute-done.6.refs_1_), channel_id=1, source_target_pairs={{0,4},{1,5},{2,6},{3,7},{4,0},{5,1},{6,2},{7,3},{8,12},{9,13},{10,... | collective-permute-start | bytes 294920 | tf_op jit(solution)/shard_map/ppermute | solution.py:169
  28.4 1.4 %collective-permute-start.10 = (bf16[192,384]{1,0:T(8,128)(2,1)S(1)}, bf16[192,384]{1,0:T(8,128)(2,1)S(1)}, u32[]{:S(2)}, u32[]{:S(2)}) collective-permute-start(bf16[192,384]{1,0:T(8,128)(2,1)S(1)} %shard_map.102), channel_id=1, source_target_pairs={{0,1},{1,0},{2,3},{3,2},{4,5},{5,4},{6,7},{7,6},{8,9},{9,8},{10,11... | collective-permute-start | bytes 442376 | tf_op jit(solution)/shard_map/ppermute | solution.py:169
  28.8 4.5 %collective-permute-start.9 = (bf16[192,384]{1,0:T(8,128)(2,1)S(1)}, bf16[192,384]{1,0:T(8,128)(2,1)S(1)}, u32[]{:S(2)}, u32[]{:S(2)}) collective-permute-start(bf16[192,384]{1,0:T(8,128)(2,1)S(1)} %shard_map.99), channel_id=1, source_target_pairs={{0,1},{1,0},{2,3},{3,2},{4,5},{5,4},{6,7},{7,6},{8,9},{9,8},{10,11... | collective-permute-start | bytes 442376 | tf_op jit(solution)/shard_map/ppermute | solution.py:169
  29.9 8.9 %collective-permute-start.11 = (bf16[96,384]{1,0:T(8,128)(2,1)S(1)}, bf16[96,384]{1,0:T(8,128)(2,1)S(1)}, u32[]{:S(2)}, u32[]{:S(2)}) collective-permute-start(bf16[96,384]{1,0:T(8,128)(2,1)S(1)} %get-tuple-element.42), channel_id=1, source_target_pairs={{0,16},{1,17},{2,18},{3,19},{4,20},{5,21},{6,22},{7,23},{8,24},{9,... | collective-permute-start | bytes 221192 | tf_op jit(solution)/shard_map/ppermute | solution.py:169
  31.0 7.8 %collective-permute-start.12 = (bf16[96,384]{1,0:T(8,128)(2,1)S(1)}, bf16[96,384]{1,0:T(8,128)(2,1)S(1)}, u32[]{:S(2)}, u32[]{:S(2)}) collective-permute-start(bf16[96,384]{1,0:T(8,128)(2,1)S(1)} %get-tuple-element.43), channel_id=1, source_target_pairs={{0,24},{1,25},{2,26},{3,27},{4,28},{5,29},{6,30},{7,31},{8,16},{9,... | collective-permute-start | bytes 221192 | tf_op jit(solution)/shard_map/ppermute | solution.py:169
  33.3 6.4 %collective-permute-start.13 = (bf16[96,384]{1,0:T(8,128)(2,1)S(1)}, bf16[96,384]{1,0:T(8,128)(2,1)S(1)}, u32[]{:S(2)}, u32[]{:S(2)}) collective-permute-start(bf16[96,384]{1,0:T(8,128)(2,1)S(1)} %get-tuple-element.44), channel_id=1, source_target_pairs={{0,8},{1,9},{2,10},{3,11},{4,12},{5,13},{6,14},{7,15},{8,0},{9,1},... | collective-permute-start | bytes 221192 | tf_op jit(solution)/shard_map/ppermute | solution.py:169
  39.7 4.4 %collective-permute-start.15 = (bf16[96,384]{1,0:T(8,128)(2,1)S(1)}, bf16[96,384]{1,0:T(8,128)(2,1)S(1)}, u32[]{:S(2)}, u32[]{:S(2)}) collective-permute-start(bf16[96,384]{1,0:T(8,128)(2,1)S(1)} %shard_map.104.refs_0_), channel_id=1, source_target_pairs={{0,2},{1,3},{2,0},{3,1},{4,6},{5,7},{6,4},{7,5},{8,10},{9,11},{10,... | collective-permute-start | bytes 221192 | tf_op jit(solution)/shard_map/ppermute | solution.py:169
  41.0 3.8 %collective-permute-start.14 = (bf16[96,384]{1,0:T(8,128)(2,1)S(1)}, bf16[96,384]{1,0:T(8,128)(2,1)S(1)}, u32[]{:S(2)}, u32[]{:S(2)}) collective-permute-start(bf16[96,384]{1,0:T(8,128)(2,1)S(1)} %shard_map.104.refs_0_), channel_id=1, source_target_pairs={{0,1},{1,0},{2,3},{3,2},{4,5},{5,4},{6,7},{7,6},{8,9},{9,8},{10,11... | collective-permute-start | bytes 221192 | tf_op jit(solution)/shard_map/ppermute | solution.py:169
  44.1 1.3 %collective-permute-start.16 = (bf16[96,384]{1,0:T(8,128)(2,1)S(1)}, bf16[96,384]{1,0:T(8,128)(2,1)S(1)}, u32[]{:S(2)}, u32[]{:S(2)}) collective-permute-start(bf16[96,384]{1,0:T(8,128)(2,1)S(1)} %collective-permute-done.15.refs_2_), channel_id=1, source_target_pairs={{0,1},{1,0},{2,3},{3,2},{4,5},{5,4},{6,7},{7,6},{8,9},{9,8},{10,11... | collective-permute-start | bytes 221192 | tf_op jit(solution)/shard_map/ppermute | solution.py:169

commit v12 on v11

--- a/solution.py
+++ b/solution.py
@@ -170,8 +170,8 @@
 
     def store_order(self):
         middle = self.ns // 2
-        turns = [s for pair in zip(range(middle, self.ns), range(middle - 1, -1, -1)) for s in pair]
-        return turns
+        pairs = list(zip(range(middle, self.ns), range(middle - 1, -1, -1)))
+        return [s for pair in pairs[:-2] + pairs[:-3:-1] for s in pair]
 
 
 def write_rows(plan, trans_ref, *outs):

time: 46.5 us -> 46.9 us (level)
  waiting for transfers between devices: 14.1 us -> 14.7 us
where the time goes in v12:
time: 46.9 us; the launch traced here: 46.6 us
  starting transfers between devices  23.9 us (51%)
  waiting for transfers between devices  14.7 us (31%)
  Pallas kernels  5.3 us (11%)
  matrix products  1.25 us (3%)
  between operations  0.76 us (2%)
  other arithmetic  0.7 us (1%)
    ppermute x17, starting transfers between devices, send(): return lax.ppermute(array, ('store', 'trainer'), pairs)  16 us
    ppermute x17, waiting for transfers between devices, send(): return lax.ppermute(array, ('store', 'trainer'), pairs)  14.2 us
    all_to_all x1, starting transfers between devices, per_device(): lax.all_to_all(sums.reshape(ns, packed, 128), 'store', split_axis=0, conc...  7.82 us
    pallas_call x12, Pallas kernels, call(): pl.pallas_call(body, out_shape=list(outs), in_specs=[VMEM] * len(args) +...  5.3 us
    dot_general x1, matrix products, dot(): return jnp.dot(a, b, preferred_element_type=F32)  1.25 us
  transfers between devices with their start and end apart: 18, of which 9 were waited for; matrix products, arithmetic and copies ran while one was open for 4% of the time, Pallas kernels for 4%

profile of v12, /device:TPU:0, one launch (start us, length us, event | category | flops | bytes accessed | tf_op | source)
XLA Modules:
  0.0 46.6 jit_solution(17645566551915022298)
XLA Ops:
  0.6 0.0 copy-start
  0.6 2.2 %shard_map.94 = (bf16[640,128]{1,0:T(8,128)(2,1)}, bf16[128,768]{1,0:T(8,128)(2,1)}, bf16[384,128]{1,0:T(8,128)(2,1)}, bf16[384,128]{1,0:T(8,128)(2,1)}) custom-call(f32[128,768]{1,0:T(8,128)} %feat_hbm.1, s32[8,2,12]{2,1,0:T(2,128)} %bitcast.11, f32[128,768]{1,0:T(8,128)} %rest_0_.1), custom_call_target="tpu_custom_call" | custom-call | flops 50331648 | bytes 557056 | tf_op jit(solution)/shard_map/pallas_call | solution.py:23
  2.9 0.0 copy-start.4
  2.9 7.8 %all-to-all-start = ((bf16[8,80,128]{2,1,0:T(8,128)(2,1)}), bf16[8,80,128]{2,1,0:T(8,128)(2,1)S(1)}, u32[]{:S(2)}, u32[]{:S(2)}) async-start(bf16[8,80,128]{2,1,0:T(8,128)(2,1)} %bitcast.10), calls=%async_computation | async-start | bytes 327680 | tf_op jit(solution)/shard_map/all_to_all | solution.py:284
  10.7 0.0 copy-start.1
  10.7 0.0 copy-start.2
  10.7 2.4 %collective-permute-start = (bf16[384,128]{1,0:T(8,128)(2,1)}, bf16[384,128]{1,0:T(8,128)(2,1)S(1)}, u32[]{:S(2)}, u32[]{:S(2)}) collective-permute-start(bf16[384,128]{1,0:T(8,128)(2,1)} %get-tuple-element.29), channel_id=1, source_target_pairs={{0,6},{1,7},{2,4},{3,5},{4,2},{5,3},{6,0},{7,1},{8,14},{9,15},{10,... | collective-permute-start | bytes 294920 | tf_op jit(solution)/shard_map/ppermute | solution.py:169
  13.2 0.6 %collective-permute-start.1 = (bf16[384,128]{1,0:T(8,128)(2,1)}, bf16[384,128]{1,0:T(8,128)(2,1)S(1)}, u32[]{:S(2)}, u32[]{:S(2)}) collective-permute-start(bf16[384,128]{1,0:T(8,128)(2,1)} %get-tuple-element.29), channel_id=1, source_target_pairs={{0,4},{1,5},{2,6},{3,7},{4,0},{5,1},{6,2},{7,3},{8,12},{9,13},{10,... | collective-permute-start | bytes 294920 | tf_op jit(solution)/shard_map/ppermute | solution.py:169
  13.7 0.5 %collective-permute-start.2 = (bf16[384,128]{1,0:T(8,128)(2,1)}, bf16[384,128]{1,0:T(8,128)(2,1)S(1)}, u32[]{:S(2)}, u32[]{:S(2)}) collective-permute-start(bf16[384,128]{1,0:T(8,128)(2,1)} %get-tuple-element.30.refs_3_), channel_id=1, source_target_pairs={{0,2},{1,3},{2,0},{3,1},{4,6},{5,7},{6,4},{7,5},{8,10},{9,11},{10,... | collective-permute-start | bytes 294920 | tf_op jit(solution)/shard_map/ppermute | solution.py:169
  14.2 0.0 copy-done
  14.2 1.2 %fusion._.self_ref = f32[128,768]{1,0:T(8,128)S(1)} fusion(bf16[128,768]{1,0:T(8,128)(2,1)} %get-tuple-element.26, bf16[768,768]{1,0:T(8,128)(2,1)S(1)} %copy-done), kind=kOutput, calls=%fused_computation | convolution fusion | flops 150994944 | bytes 1769472 | tf_op jit(solution)/shard_map/dot_general | solution.py:18
  15.5 0.6 %all-to-all-done = bf16[8,80,128]{2,1,0:T(8,128)(2,1)S(1)} async-done(((bf16[8,80,128]{2,1,0:T(8,128)(2,1)}), bf16[8,80,128]{2,1,0:T(8,128)(2,1)S(1)}, u32[]{:S(2)}, u32[]{:S(2)}) %all-to-all-start) | async-done | bytes 163872 | tf_op jit(solution)/shard_map/all_to_all | solution.py:284
  16.0 0.0 copy-done.4
  16.0 0.0 copy-start.3
  16.0 0.5 %shard_map.95 = (bf16[128,768]{1,0:T(8,128)(2,1)S(1)}, bf16[384,128]{1,0:T(8,128)(2,1)S(1)}, bf16[384,128]{1,0:T(8,128)(2,1)S(1)}) custom-call(bf16[640,128]{1,0:T(8,128)(2,1)S(1)} %bitcast.8, s32[8,12]{1,0:T(8,128)S(1)} %bitcast.9, f32[128,768]{1,0:T(8,128)S(1)} %fusion._.self_ref), custom_call_target="tpu_custom_call" | custom-call | flops 25165824 | bytes 950656 | tf_op jit(solution)/shard_map/pallas_call | solution.py:23
  16.6 1.0 %collective-permute-start.4 = (bf16[384,128]{1,0:T(8,128)(2,1)S(1)}, bf16[384,128]{1,0:T(8,128)(2,1)S(1)}, u32[]{:S(2)}, u32[]{:S(2)}) collective-permute-start(bf16[384,128]{1,0:T(8,128)(2,1)S(1)} %get-tuple-element.32), channel_id=1, source_target_pairs={{0,4},{1,5},{2,6},{3,7},{4,0},{5,1},{6,2},{7,3},{8,12},{9,13},{10,... | collective-permute-start | bytes 294920 | tf_op jit(solution)/shard_map/ppermute | solution.py:169
  17.6 0.0 copy-done.1
  17.6 0.0 copy-done.2
  17.6 0.4 shard_map.96
  18.0 1.6 %collective-permute-start.6 = (bf16[384,128]{1,0:T(8,128)(2,1)S(1)}, bf16[384,128]{1,0:T(8,128)(2,1)S(1)}, u32[]{:S(2)}, u32[]{:S(2)}) collective-permute-start(bf16[384,128]{1,0:T(8,128)(2,1)S(1)} %get-tuple-element.36), channel_id=1, source_target_pairs={{0,2},{1,3},{2,0},{3,1},{4,6},{5,7},{6,4},{7,5},{8,10},{9,11},{10,... | collective-permute-start | bytes 294920 | tf_op jit(solution)/shard_map/ppermute | solution.py:169
  19.6 0.0 collective-permute-done.refs_0_
  19.6 0.5 %collective-permute-start.3 = (bf16[384,128]{1,0:T(8,128)(2,1)S(1)}, bf16[384,128]{1,0:T(8,128)(2,1)S(1)}, u32[]{:S(2)}, u32[]{:S(2)}) collective-permute-start(bf16[384,128]{1,0:T(8,128)(2,1)S(1)} %get-tuple-element.31.refs_4_), channel_id=1, source_target_pairs={{0,2},{1,3},{2,0},{3,1},{4,6},{5,7},{6,4},{7,5},{8,10},{9,11},{10,... | collective-permute-start | bytes 294920 | tf_op jit(solution)/shard_map/ppermute | solution.py:169
  20.1 0.0 collective-permute-done.1.refs_1_
  20.1 1.1 %collective-permute-start.7 = (bf16[384,128]{1,0:T(8,128)(2,1)S(1)}, bf16[384,128]{1,0:T(8,128)(2,1)S(1)}, u32[]{:S(2)}, u32[]{:S(2)}) collective-permute-start(bf16[384,128]{1,0:T(8,128)(2,1)S(1)} %get-tuple-element.35.refs_0_), channel_id=1, source_target_pairs={{0,4},{1,5},{2,6},{3,7},{4,0},{5,1},{6,2},{7,3},{8,12},{9,13},{10,... | collective-permute-start | bytes 294920 | tf_op jit(solution)/shard_map/ppermute | solution.py:169
  21.2 0.0 collective-permute-done.2.refs_2_
  21.2 0.5 collective-permute-done.4.refs_6_
  21.6 2.1 %collective-permute-start.5 = (bf16[384,128]{1,0:T(8,128)(2,1)S(1)}, bf16[384,128]{1,0:T(8,128)(2,1)S(1)}, u32[]{:S(2)}, u32[]{:S(2)}) collective-permute-start(bf16[384,128]{1,0:T(8,128)(2,1)S(1)} %collective-permute-done.4.refs_6_), channel_id=1, source_target_pairs={{0,2},{1,3},{2,0},{3,1},{4,6},{5,7},{6,4},{7,5},{8,10},{9,11},{10,... | collective-permute-start | bytes 294920 | tf_op jit(solution)/shard_map/ppermute | solution.py:169
  23.7 0.0 collective-permute-done.6.refs_1_
  23.7 0.7 %collective-permute-start.8 = (bf16[384,128]{1,0:T(8,128)(2,1)S(1)}, bf16[384,128]{1,0:T(8,128)(2,1)S(1)}, u32[]{:S(2)}, u32[]{:S(2)}) collective-permute-start(bf16[384,128]{1,0:T(8,128)(2,1)S(1)} %collective-permute-done.6.refs_1_), channel_id=1, source_target_pairs={{0,4},{1,5},{2,6},{3,7},{4,0},{5,1},{6,2},{7,3},{8,12},{9,13},{10,... | collective-permute-start | bytes 294920 | tf_op jit(solution)/shard_map/ppermute | solution.py:169
  24.5 0.3 collective-permute-done.3.refs_5_
  24.8 1.6 %collective-permute-done.5.refs_7_ = bf16[384,128]{1,0:T(8,128)(2,1)S(1)} collective-permute-done((bf16[384,128]{1,0:T(8,128)(2,1)S(1)}, bf16[384,128]{1,0:T(8,128)(2,1)S(1)}, u32[]{:S(2)}, u32[]{:S(2)}) %collective-permute-start.5) | collective-permute-done | bytes 98336 | tf_op jit(solution)/shard_map/ppermute | solution.py:169
  26.3 0.0 copy-done.3
  26.3 0.1 shard_map.97
  26.5 0.0 collective-permute-done.7.refs_2_
  26.5 1.9 %collective-permute-done.8.refs_3_ = bf16[384,128]{1,0:T(8,128)(2,1)S(1)} collective-permute-done((bf16[384,128]{1,0:T(8,128)(2,1)S(1)}, bf16[384,128]{1,0:T(8,128)(2,1)S(1)}, u32[]{:S(2)}, u32[]{:S(2)}) %collective-permute-start.8) | collective-permute-done | bytes 98336 | tf_op jit(solution)/shard_map/ppermute | solution.py:169
  28.4 0.3 shard_map.102
  28.6 0.1 collective-permute-start.10
  28.7 0.3 shard_map.99
  29.0 0.6 %collective-permute-start.9 = (bf16[192,384]{1,0:T(8,128)(2,1)S(1)}, bf16[192,384]{1,0:T(8,128)(2,1)S(1)}, u32[]{:S(2)}, u32[]{:S(2)}) collective-permute-start(bf16[192,384]{1,0:T(8,128)(2,1)S(1)} %shard_map.99), channel_id=1, source_target_pairs={{0,1},{1,0},{2,3},{3,2},{4,5},{5,4},{6,7},{7,6},{8,9},{9,8},{10,11... | collective-permute-start | bytes 442376 | tf_op jit(solution)/shard_map/ppermute | solution.py:169
  29.5 0.3 shard_map.98.keep_ref
  29.8 0.3 shard_map.101.keep_ref
  30.0 0.0 collective-permute-done.10.got_ref
  30.1 1.1 %collective-permute-start.11 = (bf16[96,384]{1,0:T(8,128)(2,1)S(1)}, bf16[96,384]{1,0:T(8,128)(2,1)S(1)}, u32[]{:S(2)}, u32[]{:S(2)}) collective-permute-start(bf16[96,384]{1,0:T(8,128)(2,1)S(1)} %get-tuple-element.42), channel_id=1, source_target_pairs={{0,16},{1,17},{2,18},{3,19},{4,20},{5,21},{6,22},{7,23},{8,24},{9,... | collective-permute-start | bytes 221192 | tf_op jit(solution)/shard_map/ppermute | solution.py:169
  31.2 2.1 %collective-permute-start.12 = (bf16[96,384]{1,0:T(8,128)(2,1)S(1)}, bf16[96,384]{1,0:T(8,128)(2,1)S(1)}, u32[]{:S(2)}, u32[]{:S(2)}) collective-permute-start(bf16[96,384]{1,0:T(8,128)(2,1)S(1)} %get-tuple-element.43), channel_id=1, source_target_pairs={{0,24},{1,25},{2,26},{3,27},{4,28},{5,29},{6,30},{7,31},{8,16},{9,... | collective-permute-start | bytes 221192 | tf_op jit(solution)/shard_map/ppermute | solution.py:169
  33.2 0.0 collective-permute-done.9.got_ref
  33.3 0.5 %collective-permute-start.13 = (bf16[96,384]{1,0:T(8,128)(2,1)S(1)}, bf16[96,384]{1,0:T(8,128)(2,1)S(1)}, u32[]{:S(2)}, u32[]{:S(2)}) collective-permute-start(bf16[96,384]{1,0:T(8,128)(2,1)S(1)} %get-tuple-element.44), channel_id=1, source_target_pairs={{0,8},{1,9},{2,10},{3,11},{4,12},{5,13},{6,14},{7,15},{8,0},{9,1},... | collective-permute-start | bytes 221192 | tf_op jit(solution)/shard_map/ppermute | solution.py:169
  33.7 5.0 %collective-permute-done.11.refs_1_ = bf16[96,384]{1,0:T(8,128)(2,1)S(1)} collective-permute-done((bf16[96,384]{1,0:T(8,128)(2,1)S(1)}, bf16[96,384]{1,0:T(8,128)(2,1)S(1)}, u32[]{:S(2)}, u32[]{:S(2)}) %collective-permute-start.11) | collective-permute-done | bytes 73760 | tf_op jit(solution)/shard_map/ppermute | solution.py:169
  38.8 0.0 collective-permute-done.12.refs_2_
  38.8 1.2 %collective-permute-done.13.refs_3_ = bf16[96,384]{1,0:T(8,128)(2,1)S(1)} collective-permute-done((bf16[96,384]{1,0:T(8,128)(2,1)S(1)}, bf16[96,384]{1,0:T(8,128)(2,1)S(1)}, u32[]{:S(2)}, u32[]{:S(2)}) %collective-permute-start.13) | collective-permute-done | bytes 73760 | tf_op jit(solution)/shard_map/ppermute | solution.py:169
  40.0 1.3 %collective-permute-start.15 = (bf16[96,384]{1,0:T(8,128)(2,1)S(1)}, bf16[96,384]{1,0:T(8,128)(2,1)S(1)}, u32[]{:S(2)}, u32[]{:S(2)}) collective-permute-start(bf16[96,384]{1,0:T(8,128)(2,1)S(1)} %shard_map.104.refs_0_), channel_id=1, source_target_pairs={{0,2},{1,3},{2,0},{3,1},{4,6},{5,7},{6,4},{7,5},{8,10},{9,11},{10,... | collective-permute-start | bytes 221192 | tf_op jit(solution)/shard_map/ppermute | solution.py:169
  41.3 0.0 collective-permute-start.14
  41.3 3.1 %collective-permute-done.15.refs_2_ = bf16[96,384]{1,0:T(8,128)(2,1)S(1)} collective-permute-done((bf16[96,384]{1,0:T(8,128)(2,1)S(1)}, bf16[96,384]{1,0:T(8,128)(2,1)S(1)}, u32[]{:S(2)}, u32[]{:S(2)}) %collective-permute-start.15) | collective-permute-done | bytes 73760 | tf_op jit(solution)/shard_map/ppermute | solution.py:169
  44.4 0.0 collective-permute-start.16
  44.4 0.7 %convert_element_type.3 = bf16[128,768]{1,0:T(8,128)(2,1)} convert(f32[128,768]{1,0:T(8,128)S(1)} %get-tuple-element.28) | non-fusion elementwise | flops 98304 | bytes 589824 | tf_op jit(solution)/shard_map/convert_element_type | solution.py:361
  45.1 0.0 collective-permute-done.14.refs_1_
  45.1 0.6 %collective-permute-done.16.refs_3_ = bf16[96,384]{1,0:T(8,128)(2,1)S(1)} collective-permute-done((bf16[96,384]{1,0:T(8,128)(2,1)S(1)}, bf16[96,384]{1,0:T(8,128)(2,1)S(1)}, u32[]{:S(2)}, u32[]{:S(2)}) %collective-permute-start.16) | collective-permute-done | bytes 73760 | tf_op jit(solution)/shard_map/ppermute | solution.py:169
  45.7 0.9 %shard_map.105 = (f32[96,768]{1,0:T(8,128)}, f32[96,768]{1,0:T(8,128)}) custom-call(bf16[96,384]{1,0:T(8,128)(2,1)S(1)} %shard_map.104.refs_0_, bf16[96,384]{1,0:T(8,128)(2,1)S(1)} %collective-permute-done.14.refs_1_, bf16[96,384]{1,0:T(8,128)(2,1)S(1)} %collective-permute-done.15.refs_2_, bf16[96,384]{1,0:T(8,128)(2,1)S(1)} %collective-permute-done.16.refs_3_), custom_call_target="tpu_custom_call" | custom-call | bytes 884736 | tf_op jit(solution)/shard_map/pallas_call | solution.py:23
  (3 shorter events, 0.1 us)
Async XLA Ops:
  0.6 13.6 %copy-start = (bf16[768,768]{1,0:T(8,128)(2,1)S(1)}, bf16[768,768]{1,0:T(8,128)(2,1)}, u32[]{:S(2)}) copy-start(bf16[768,768]{1,0:T(8,128)(2,1)} %param.12) | copy-start | bytes 3538948
  2.9 13.1 %copy-start.4 = (s32[1,1,8,12]{3,2,1,0:T(8,128)S(1)}, s32[1,1,8,12]{3,2,1,0:T(8,128)}, u32[]{:S(2)}) copy-start(s32[1,1,8,12]{3,2,1,0:T(8,128)} %param.10) | copy-start | bytes 1156
  2.9 13.1 %all-to-all-start = ((bf16[8,80,128]{2,1,0:T(8,128)(2,1)}), bf16[8,80,128]{2,1,0:T(8,128)(2,1)S(1)}, u32[]{:S(2)}, u32[]{:S(2)}) async-start(bf16[8,80,128]{2,1,0:T(8,128)(2,1)} %bitcast.10), calls=%async_computation | async-start | bytes 327680 | tf_op jit(solution)/shard_map/all_to_all | solution.py:284
  10.7 6.8 %copy-start.1 = (bf16[768,768]{1,0:T(8,128)(2,1)S(1)}, bf16[768,768]{1,0:T(8,128)(2,1)}, u32[]{:S(2)}) copy-start(bf16[768,768]{1,0:T(8,128)(2,1)} %w_ref.1) | copy-start | bytes 3538948
  10.7 6.8 %copy-start.2 = (bf16[128,768]{1,0:T(8,128)(2,1)S(1)}, bf16[128,768]{1,0:T(8,128)(2,1)}, u32[]{:S(2)}) copy-start(bf16[128,768]{1,0:T(8,128)(2,1)} %cot_ref.1) | copy-start | bytes 589828
  10.7 8.8 %collective-permute-start = (bf16[384,128]{1,0:T(8,128)(2,1)}, bf16[384,128]{1,0:T(8,128)(2,1)S(1)}, u32[]{:S(2)}, u32[]{:S(2)}) collective-permute-start(bf16[384,128]{1,0:T(8,128)(2,1)} %get-tuple-element.29), channel_id=1, source_target_pairs={{0,6},{1,7},{2,4},{3,5},{4,2},{5,3},{6,0},{7,1},{8,14},{9,15},{10,... | collective-permute-start | bytes 294920 | tf_op jit(solution)/shard_map/ppermute | solution.py:169
  13.2 6.9 %collective-permute-start.1 = (bf16[384,128]{1,0:T(8,128)(2,1)}, bf16[384,128]{1,0:T(8,128)(2,1)S(1)}, u32[]{:S(2)}, u32[]{:S(2)}) collective-permute-start(bf16[384,128]{1,0:T(8,128)(2,1)} %get-tuple-element.29), channel_id=1, source_target_pairs={{0,4},{1,5},{2,6},{3,7},{4,0},{5,1},{6,2},{7,3},{8,12},{9,13},{10,... | collective-permute-start | bytes 294920 | tf_op jit(solution)/shard_map/ppermute | solution.py:169
  13.7 7.5 %collective-permute-start.2 = (bf16[384,128]{1,0:T(8,128)(2,1)}, bf16[384,128]{1,0:T(8,128)(2,1)S(1)}, u32[]{:S(2)}, u32[]{:S(2)}) collective-permute-start(bf16[384,128]{1,0:T(8,128)(2,1)} %get-tuple-element.30.refs_3_), channel_id=1, source_target_pairs={{0,2},{1,3},{2,0},{3,1},{4,6},{5,7},{6,4},{7,5},{8,10},{9,11},{10,... | collective-permute-start | bytes 294920 | tf_op jit(solution)/shard_map/ppermute | solution.py:169
  16.0 10.3 %copy-start.3 = (bf16[384,128]{1,0:T(8,128)(2,1)S(1)}, bf16[384,128]{1,0:T(8,128)(2,1)}, u32[]{:S(2)}) copy-start(bf16[384,128]{1,0:T(8,128)(2,1)} %get-tuple-element.30.refs_3_) | copy-start | bytes 294916
  16.6 5.1 %collective-permute-start.4 = (bf16[384,128]{1,0:T(8,128)(2,1)S(1)}, bf16[384,128]{1,0:T(8,128)(2,1)S(1)}, u32[]{:S(2)}, u32[]{:S(2)}) collective-permute-start(bf16[384,128]{1,0:T(8,128)(2,1)S(1)} %get-tuple-element.32), channel_id=1, source_target_pairs={{0,4},{1,5},{2,6},{3,7},{4,0},{5,1},{6,2},{7,3},{8,12},{9,13},{10,... | collective-permute-start | bytes 294920 | tf_op jit(solution)/shard_map/ppermute | solution.py:169
  18.0 5.8 %collective-permute-start.6 = (bf16[384,128]{1,0:T(8,128)(2,1)S(1)}, bf16[384,128]{1,0:T(8,128)(2,1)S(1)}, u32[]{:S(2)}, u32[]{:S(2)}) collective-permute-start(bf16[384,128]{1,0:T(8,128)(2,1)S(1)} %get-tuple-element.36), channel_id=1, source_target_pairs={{0,2},{1,3},{2,0},{3,1},{4,6},{5,7},{6,4},{7,5},{8,10},{9,11},{10,... | collective-permute-start | bytes 294920 | tf_op jit(solution)/shard_map/ppermute | solution.py:169
  19.6 5.2 %collective-permute-start.3 = (bf16[384,128]{1,0:T(8,128)(2,1)S(1)}, bf16[384,128]{1,0:T(8,128)(2,1)S(1)}, u32[]{:S(2)}, u32[]{:S(2)}) collective-permute-start(bf16[384,128]{1,0:T(8,128)(2,1)S(1)} %get-tuple-element.31.refs_4_), channel_id=1, source_target_pairs={{0,2},{1,3},{2,0},{3,1},{4,6},{5,7},{6,4},{7,5},{8,10},{9,11},{10,... | collective-permute-start | bytes 294920 | tf_op jit(solution)/shard_map/ppermute | solution.py:169
  20.1 6.4 %collective-permute-start.7 = (bf16[384,128]{1,0:T(8,128)(2,1)S(1)}, bf16[384,128]{1,0:T(8,128)(2,1)S(1)}, u32[]{:S(2)}, u32[]{:S(2)}) collective-permute-start(bf16[384,128]{1,0:T(8,128)(2,1)S(1)} %get-tuple-element.35.refs_0_), channel_id=1, source_target_pairs={{0,4},{1,5},{2,6},{3,7},{4,0},{5,1},{6,2},{7,3},{8,12},{9,13},{10,... | collective-permute-start | bytes 294920 | tf_op jit(solution)/shard_map/ppermute | solution.py:169
  21.6 4.7 %collective-permute-start.5 = (bf16[384,128]{1,0:T(8,128)(2,1)S(1)}, bf16[384,128]{1,0:T(8,128)(2,1)S(1)}, u32[]{:S(2)}, u32[]{:S(2)}) collective-permute-start(bf16[384,128]{1,0:T(8,128)(2,1)S(1)} %collective-permute-done.4.refs_6_), channel_id=1, source_target_pairs={{0,2},{1,3},{2,0},{3,1},{4,6},{5,7},{6,4},{7,5},{8,10},{9,11},{10,... | collective-permute-start | bytes 294920 | tf_op jit(solution)/shard_map/ppermute | solution.py:169
  23.7 4.6 %collective-permute-start.8 = (bf16[384,128]{1,0:T(8,128)(2,1)S(1)}, bf16[384,128]{1,0:T(8,128)(2,1)S(1)}, u32[]{:S(2)}, u32[]{:S(2)}) collective-permute-start(bf16[384,128]{1,0:T(8,128)(2,1)S(1)} %collective-permute-done.6.refs_1_), channel_id=1, source_target_pairs={{0,4},{1,5},{2,6},{3,7},{4,0},{5,1},{6,2},{7,3},{8,12},{9,13},{10,... | collective-permute-start | bytes 294920 | tf_op jit(solution)/shard_map/ppermute | solution.py:169
  28.6 1.4 %collective-permute-start.10 = (bf16[192,384]{1,0:T(8,128)(2,1)S(1)}, bf16[192,384]{1,0:T(8,128)(2,1)S(1)}, u32[]{:S(2)}, u32[]{:S(2)}) collective-permute-start(bf16[192,384]{1,0:T(8,128)(2,1)S(1)} %shard_map.102), channel_id=1, source_target_pairs={{0,1},{1,0},{2,3},{3,2},{4,5},{5,4},{6,7},{7,6},{8,9},{9,8},{10,11... | collective-permute-start | bytes 442376 | tf_op jit(solution)/shard_map/ppermute | solution.py:169
  29.0 4.3 %collective-permute-start.9 = (bf16[192,384]{1,0:T(8,128)(2,1)S(1)}, bf16[192,384]{1,0:T(8,128)(2,1)S(1)}, u32[]{:S(2)}, u32[]{:S(2)}) collective-permute-start(bf16[192,384]{1,0:T(8,128)(2,1)S(1)} %shard_map.99), channel_id=1, source_target_pairs={{0,1},{1,0},{2,3},{3,2},{4,5},{5,4},{6,7},{7,6},{8,9},{9,8},{10,11... | collective-permute-start | bytes 442376 | tf_op jit(solution)/shard_map/ppermute | solution.py:169
  30.1 8.7 %collective-permute-start.11 = (bf16[96,384]{1,0:T(8,128)(2,1)S(1)}, bf16[96,384]{1,0:T(8,128)(2,1)S(1)}, u32[]{:S(2)}, u32[]{:S(2)}) collective-permute-start(bf16[96,384]{1,0:T(8,128)(2,1)S(1)} %get-tuple-element.42), channel_id=1, source_target_pairs={{0,16},{1,17},{2,18},{3,19},{4,20},{5,21},{6,22},{7,23},{8,24},{9,... | collective-permute-start | bytes 221192 | tf_op jit(solution)/shard_map/ppermute | solution.py:169
  31.2 7.6 %collective-permute-start.12 = (bf16[96,384]{1,0:T(8,128)(2,1)S(1)}, bf16[96,384]{1,0:T(8,128)(2,1)S(1)}, u32[]{:S(2)}, u32[]{:S(2)}) collective-permute-start(bf16[96,384]{1,0:T(8,128)(2,1)S(1)} %get-tuple-element.43), channel_id=1, source_target_pairs={{0,24},{1,25},{2,26},{3,27},{4,28},{5,29},{6,30},{7,31},{8,16},{9,... | collective-permute-start | bytes 221192 | tf_op jit(solution)/shard_map/ppermute | solution.py:169
  33.3 6.7 %collective-permute-start.13 = (bf16[96,384]{1,0:T(8,128)(2,1)S(1)}, bf16[96,384]{1,0:T(8,128)(2,1)S(1)}, u32[]{:S(2)}, u32[]{:S(2)}) collective-permute-start(bf16[96,384]{1,0:T(8,128)(2,1)S(1)} %get-tuple-element.44), channel_id=1, source_target_pairs={{0,8},{1,9},{2,10},{3,11},{4,12},{5,13},{6,14},{7,15},{8,0},{9,1},... | collective-permute-start | bytes 221192 | tf_op jit(solution)/shard_map/ppermute | solution.py:169
  40.0 4.4 %collective-permute-start.15 = (bf16[96,384]{1,0:T(8,128)(2,1)S(1)}, bf16[96,384]{1,0:T(8,128)(2,1)S(1)}, u32[]{:S(2)}, u32[]{:S(2)}) collective-permute-start(bf16[96,384]{1,0:T(8,128)(2,1)S(1)} %shard_map.104.refs_0_), channel_id=1, source_target_pairs={{0,2},{1,3},{2,0},{3,1},{4,6},{5,7},{6,4},{7,5},{8,10},{9,11},{10,... | collective-permute-start | bytes 221192 | tf_op jit(solution)/shard_map/ppermute | solution.py:169
  41.3 3.8 %collective-permute-start.14 = (bf16[96,384]{1,0:T(8,128)(2,1)S(1)}, bf16[96,384]{1,0:T(8,128)(2,1)S(1)}, u32[]{:S(2)}, u32[]{:S(2)}) collective-permute-start(bf16[96,384]{1,0:T(8,128)(2,1)S(1)} %shard_map.104.refs_0_), channel_id=1, source_target_pairs={{0,1},{1,0},{2,3},{3,2},{4,5},{5,4},{6,7},{7,6},{8,9},{9,8},{10,11... | collective-permute-start | bytes 221192 | tf_op jit(solution)/shard_map/ppermute | solution.py:169
  44.4 1.3 %collective-permute-start.16 = (bf16[96,384]{1,0:T(8,128)(2,1)S(1)}, bf16[96,384]{1,0:T(8,128)(2,1)S(1)}, u32[]{:S(2)}, u32[]{:S(2)}) collective-permute-start(bf16[96,384]{1,0:T(8,128)(2,1)S(1)} %collective-permute-done.15.refs_2_), channel_id=1, source_target_pairs={{0,1},{1,0},{2,3},{3,2},{4,5},{5,4},{6,7},{7,6},{8,9},{9,8},{10,11... | collective-permute-start | bytes 221192 | tf_op jit(solution)/shard_map/ppermute | solution.py:169

commit v13 on v11

--- a/solution.py
+++ b/solution.py
@@ -155,7 +155,7 @@
         return s // self.gx, s % self.gx, t // self.gc, t % self.gc
 
     def far(self):
-        return list(range(2, self.nz))
+        return list(range(2, self.nz))[::-1]
 
     def near(self):
         return list(range(min(2, self.nz)))[::-1]
@@ -340,9 +340,12 @@
     lefts = call(functools.partial(left_kernel, plan),
                  [shape((len(half) * plan.shard, n * targets), BF16) for half in halves * 2],
                  own_all[::-1] + mean_all)
-    got, mine = [], None
+    got, mine, earlier = [], None, None
     for half, give_left, keep_left in zip(halves, lefts[:2], lefts[2:]):
         came = to_core(terms(give_left, BF16))
+        if earlier is not None:
+            keep_left = held(keep_left, earlier)
+        earlier = came
         sums = call(functools.partial(core_sum_kernel, plan),
                     [shape(block, BF16 if k else F32) for k in half], [terms(keep_left, F32), came])
         for k, part in zip(half, sums):

time: 46.5 us -> 46.3 us (level)
  waiting for transfers between devices: 14.1 us -> 13.1 us
  starting transfers between devices: 24.1 us -> 24.9 us
    ppermute x17, waiting for transfers between devices: 13.7 us -> 12.6 us  [send(): return lax.ppermute(array, ('store', 'trainer'), pairs)]
    ppermute x17, starting transfers between devices: 16.3 us -> 17.1 us  [send(): return lax.ppermute(array, ('store', 'trainer'), pairs)]
  transfers between devices with their start and end apart: 18 -> 18, of which waited for: 9 -> 10; matrix products, arithmetic and copies ran while one was open for 4% -> 4% of each run, Pallas kernels for 4% -> 4%
where the time goes in v13:
time: 46.3 us; the launch traced here: 46 us
  starting transfers between devices  24.9 us (54%)
  waiting for transfers between devices  13.1 us (28%)
  Pallas kernels  5.3 us (11%)
  matrix products  1.25 us (3%)
  between operations  0.76 us (2%)
  other arithmetic  0.7 us (2%)
    ppermute x17, starting transfers between devices, send(): return lax.ppermute(array, ('store', 'trainer'), pairs)  17.1 us
    ppermute x17, waiting for transfers between devices, send(): return lax.ppermute(array, ('store', 'trainer'), pairs)  12.6 us
    all_to_all x1, starting transfers between devices, per_device(): lax.all_to_all(sums.reshape(ns, packed, 128), 'store', split_axis=0, conc...  7.82 us
    pallas_call x12, Pallas kernels, call(): pl.pallas_call(body, out_shape=list(outs), in_specs=[VMEM] * len(args) +...  5.3 us
    dot_general x1, matrix products, dot(): return jnp.dot(a, b, preferred_element_type=F32)  1.25 us
  transfers between devices with their start and end apart: 18, of which 10 were waited for; matrix products, arithmetic and copies ran while one was open for 4% of the time, Pallas kernels for 4%

profile of v13, /device:TPU:0, one launch (start us, length us, event | category | flops | bytes accessed | tf_op | source)
XLA Modules:
  0.0 46.0 jit_solution(13112316448529291204)
XLA Ops:
  0.6 0.0 copy-start
  0.6 2.2 %shard_map.94 = (bf16[640,128]{1,0:T(8,128)(2,1)}, bf16[128,768]{1,0:T(8,128)(2,1)}, bf16[384,128]{1,0:T(8,128)(2,1)}, bf16[384,128]{1,0:T(8,128)(2,1)}) custom-call(f32[128,768]{1,0:T(8,128)} %feat_hbm.1, s32[8,2,12]{2,1,0:T(2,128)} %bitcast.11, f32[128,768]{1,0:T(8,128)} %rest_0_.1), custom_call_target="tpu_custom_call" | custom-call | flops 50331648 | bytes 557056 | tf_op jit(solution)/shard_map/pallas_call | solution.py:23
  2.9 0.0 copy-start.4
  2.9 7.8 %all-to-all-start = ((bf16[8,80,128]{2,1,0:T(8,128)(2,1)}), bf16[8,80,128]{2,1,0:T(8,128)(2,1)S(1)}, u32[]{:S(2)}, u32[]{:S(2)}) async-start(bf16[8,80,128]{2,1,0:T(8,128)(2,1)} %bitcast.10), calls=%async_computation | async-start | bytes 327680 | tf_op jit(solution)/shard_map/all_to_all | solution.py:284
  10.7 0.0 copy-start.1
  10.7 0.0 copy-start.2
  10.7 2.4 %collective-permute-start = (bf16[384,128]{1,0:T(8,128)(2,1)}, bf16[384,128]{1,0:T(8,128)(2,1)S(1)}, u32[]{:S(2)}, u32[]{:S(2)}) collective-permute-start(bf16[384,128]{1,0:T(8,128)(2,1)} %get-tuple-element.30), channel_id=1, source_target_pairs={{0,6},{1,7},{2,4},{3,5},{4,2},{5,3},{6,0},{7,1},{8,14},{9,15},{10,... | collective-permute-start | bytes 294920 | tf_op jit(solution)/shard_map/ppermute | solution.py:169
  13.2 0.6 %collective-permute-start.1 = (bf16[384,128]{1,0:T(8,128)(2,1)}, bf16[384,128]{1,0:T(8,128)(2,1)S(1)}, u32[]{:S(2)}, u32[]{:S(2)}) collective-permute-start(bf16[384,128]{1,0:T(8,128)(2,1)} %get-tuple-element.30), channel_id=1, source_target_pairs={{0,4},{1,5},{2,6},{3,7},{4,0},{5,1},{6,2},{7,3},{8,12},{9,13},{10,... | collective-permute-start | bytes 294920 | tf_op jit(solution)/shard_map/ppermute | solution.py:169
  13.7 0.5 %collective-permute-start.2 = (bf16[384,128]{1,0:T(8,128)(2,1)}, bf16[384,128]{1,0:T(8,128)(2,1)S(1)}, u32[]{:S(2)}, u32[]{:S(2)}) collective-permute-start(bf16[384,128]{1,0:T(8,128)(2,1)} %get-tuple-element.31.refs_3_), channel_id=1, source_target_pairs={{0,2},{1,3},{2,0},{3,1},{4,6},{5,7},{6,4},{7,5},{8,10},{9,11},{10,... | collective-permute-start | bytes 294920 | tf_op jit(solution)/shard_map/ppermute | solution.py:169
  14.2 0.0 copy-done
  14.2 1.2 %fusion._.self_ref = f32[128,768]{1,0:T(8,128)S(1)} fusion(bf16[128,768]{1,0:T(8,128)(2,1)} %get-tuple-element.27, bf16[768,768]{1,0:T(8,128)(2,1)S(1)} %copy-done), kind=kOutput, calls=%fused_computation | convolution fusion | flops 150994944 | bytes 1769472 | tf_op jit(solution)/shard_map/dot_general | solution.py:18
  15.5 0.5 all-to-all-done
  15.9 0.0 copy-done.4
  15.9 0.0 copy-start.3
  15.9 0.5 %shard_map.95 = (bf16[128,768]{1,0:T(8,128)(2,1)S(1)}, bf16[384,128]{1,0:T(8,128)(2,1)S(1)}, bf16[384,128]{1,0:T(8,128)(2,1)S(1)}) custom-call(bf16[640,128]{1,0:T(8,128)(2,1)S(1)} %bitcast.8, s32[8,12]{1,0:T(8,128)S(1)} %bitcast.9, f32[128,768]{1,0:T(8,128)S(1)} %fusion._.self_ref), custom_call_target="tpu_custom_call" | custom-call | flops 25165824 | bytes 950656 | tf_op jit(solution)/shard_map/pallas_call | solution.py:23
  16.5 1.1 %collective-permute-start.4 = (bf16[384,128]{1,0:T(8,128)(2,1)S(1)}, bf16[384,128]{1,0:T(8,128)(2,1)S(1)}, u32[]{:S(2)}, u32[]{:S(2)}) collective-permute-start(bf16[384,128]{1,0:T(8,128)(2,1)S(1)} %get-tuple-element.33), channel_id=1, source_target_pairs={{0,4},{1,5},{2,6},{3,7},{4,0},{5,1},{6,2},{7,3},{8,12},{9,13},{10,... | collective-permute-start | bytes 294920 | tf_op jit(solution)/shard_map/ppermute | solution.py:169
  17.6 0.0 copy-done.1
  17.6 0.0 copy-done.2
  17.6 0.4 shard_map.96
  18.0 1.6 %collective-permute-start.6 = (bf16[384,128]{1,0:T(8,128)(2,1)S(1)}, bf16[384,128]{1,0:T(8,128)(2,1)S(1)}, u32[]{:S(2)}, u32[]{:S(2)}) collective-permute-start(bf16[384,128]{1,0:T(8,128)(2,1)S(1)} %get-tuple-element.38), channel_id=1, source_target_pairs={{0,2},{1,3},{2,0},{3,1},{4,6},{5,7},{6,4},{7,5},{8,10},{9,11},{10,... | collective-permute-start | bytes 294920 | tf_op jit(solution)/shard_map/ppermute | solution.py:169
  19.6 0.0 collective-permute-done.refs_0_
  19.6 0.5 %collective-permute-start.3 = (bf16[384,128]{1,0:T(8,128)(2,1)S(1)}, bf16[384,128]{1,0:T(8,128)(2,1)S(1)}, u32[]{:S(2)}, u32[]{:S(2)}) collective-permute-start(bf16[384,128]{1,0:T(8,128)(2,1)S(1)} %get-tuple-element.32.refs_4_), channel_id=1, source_target_pairs={{0,2},{1,3},{2,0},{3,1},{4,6},{5,7},{6,4},{7,5},{8,10},{9,11},{10,... | collective-permute-start | bytes 294920 | tf_op jit(solution)/shard_map/ppermute | solution.py:169
  20.1 0.0 collective-permute-done.1.refs_1_
  20.1 1.0 %collective-permute-start.7 = (bf16[384,128]{1,0:T(8,128)(2,1)S(1)}, bf16[384,128]{1,0:T(8,128)(2,1)S(1)}, u32[]{:S(2)}, u32[]{:S(2)}) collective-permute-start(bf16[384,128]{1,0:T(8,128)(2,1)S(1)} %get-tuple-element.37.refs_0_), channel_id=1, source_target_pairs={{0,4},{1,5},{2,6},{3,7},{4,0},{5,1},{6,2},{7,3},{8,12},{9,13},{10,... | collective-permute-start | bytes 294920 | tf_op jit(solution)/shard_map/ppermute | solution.py:169
  21.1 0.0 collective-permute-done.2.refs_2_
  21.1 0.4 collective-permute-done.4.refs_6_
  21.5 2.0 %collective-permute-start.5 = (bf16[384,128]{1,0:T(8,128)(2,1)S(1)}, bf16[384,128]{1,0:T(8,128)(2,1)S(1)}, u32[]{:S(2)}, u32[]{:S(2)}) collective-permute-start(bf16[384,128]{1,0:T(8,128)(2,1)S(1)} %collective-permute-done.4.refs_6_), channel_id=1, source_target_pairs={{0,2},{1,3},{2,0},{3,1},{4,6},{5,7},{6,4},{7,5},{8,10},{9,11},{10,... | collective-permute-start | bytes 294920 | tf_op jit(solution)/shard_map/ppermute | solution.py:169
  23.5 0.0 collective-permute-done.6.refs_1_
  23.5 1.0 %collective-permute-start.8 = (bf16[384,128]{1,0:T(8,128)(2,1)S(1)}, bf16[384,128]{1,0:T(8,128)(2,1)S(1)}, u32[]{:S(2)}, u32[]{:S(2)}) collective-permute-start(bf16[384,128]{1,0:T(8,128)(2,1)S(1)} %collective-permute-done.6.refs_1_), channel_id=1, source_target_pairs={{0,4},{1,5},{2,6},{3,7},{4,0},{5,1},{6,2},{7,3},{8,12},{9,13},{10,... | collective-permute-start | bytes 294920 | tf_op jit(solution)/shard_map/ppermute | solution.py:169
  24.5 0.3 collective-permute-done.3.refs_5_
  24.8 1.3 %collective-permute-done.5.refs_7_ = bf16[384,128]{1,0:T(8,128)(2,1)S(1)} collective-permute-done((bf16[384,128]{1,0:T(8,128)(2,1)S(1)}, bf16[384,128]{1,0:T(8,128)(2,1)S(1)}, u32[]{:S(2)}, u32[]{:S(2)}) %collective-permute-start.5) | collective-permute-done | bytes 98336 | tf_op jit(solution)/shard_map/ppermute | solution.py:169
  26.1 0.0 copy-done.3
  26.1 0.1 shard_map.97
  26.3 0.0 collective-permute-done.7.refs_2_
  26.3 1.9 %collective-permute-done.8.refs_3_ = bf16[384,128]{1,0:T(8,128)(2,1)S(1)} collective-permute-done((bf16[384,128]{1,0:T(8,128)(2,1)S(1)}, bf16[384,128]{1,0:T(8,128)(2,1)S(1)}, u32[]{:S(2)}, u32[]{:S(2)}) %collective-permute-start.8) | collective-permute-done | bytes 98336 | tf_op jit(solution)/shard_map/ppermute | solution.py:169
  28.2 0.3 shard_map.98
  28.4 0.1 collective-permute-start.9
  28.5 0.3 shard_map.100
  28.8 0.6 %collective-permute-start.10 = (bf16[192,384]{1,0:T(8,128)(2,1)S(1)}, bf16[192,384]{1,0:T(8,128)(2,1)S(1)}, u32[]{:S(2)}, u32[]{:S(2)}) collective-permute-start(bf16[192,384]{1,0:T(8,128)(2,1)S(1)} %shard_map.100), channel_id=1, source_target_pairs={{0,1},{1,0},{2,3},{3,2},{4,5},{5,4},{6,7},{7,6},{8,9},{9,8},{10,11... | collective-permute-start | bytes 442376 | tf_op jit(solution)/shard_map/ppermute | solution.py:169
  29.3 0.3 shard_map.102.keep_ref
  29.6 0.3 collective-permute-done.9.got_ref
  29.9 1.4 %collective-permute-start.11 = (bf16[96,384]{1,0:T(8,128)(2,1)S(1)}, bf16[96,384]{1,0:T(8,128)(2,1)S(1)}, u32[]{:S(2)}, u32[]{:S(2)}) collective-permute-start(bf16[96,384]{1,0:T(8,128)(2,1)S(1)} %get-tuple-element.44), channel_id=1, source_target_pairs={{0,24},{1,25},{2,26},{3,27},{4,28},{5,29},{6,30},{7,31},{8,16},{9,... | collective-permute-start | bytes 221192 | tf_op jit(solution)/shard_map/ppermute | solution.py:169
  31.3 1.0 %collective-permute-start.12 = (bf16[96,384]{1,0:T(8,128)(2,1)S(1)}, bf16[96,384]{1,0:T(8,128)(2,1)S(1)}, u32[]{:S(2)}, u32[]{:S(2)}) collective-permute-start(bf16[96,384]{1,0:T(8,128)(2,1)S(1)} %get-tuple-element.45), channel_id=1, source_target_pairs={{0,16},{1,17},{2,18},{3,19},{4,20},{5,21},{6,22},{7,23},{8,24},{9,... | collective-permute-start | bytes 221192 | tf_op jit(solution)/shard_map/ppermute | solution.py:169
  32.3 0.3 shard_map.99.keep_ref
  32.6 0.0 collective-permute-done.10.got_ref
  32.6 2.1 %collective-permute-start.13 = (bf16[96,384]{1,0:T(8,128)(2,1)S(1)}, bf16[96,384]{1,0:T(8,128)(2,1)S(1)}, u32[]{:S(2)}, u32[]{:S(2)}) collective-permute-start(bf16[96,384]{1,0:T(8,128)(2,1)S(1)} %get-tuple-element.46), channel_id=1, source_target_pairs={{0,8},{1,9},{2,10},{3,11},{4,12},{5,13},{6,14},{7,15},{8,0},{9,1},... | collective-permute-start | bytes 221192 | tf_op jit(solution)/shard_map/ppermute | solution.py:169
  34.7 2.2 %collective-permute-done.11.refs_1_ = bf16[96,384]{1,0:T(8,128)(2,1)S(1)} collective-permute-done((bf16[96,384]{1,0:T(8,128)(2,1)S(1)}, bf16[96,384]{1,0:T(8,128)(2,1)S(1)}, u32[]{:S(2)}, u32[]{:S(2)}) %collective-permute-start.11) | collective-permute-done | bytes 73760 | tf_op jit(solution)/shard_map/ppermute | solution.py:169
  37.0 2.5 %collective-permute-done.12.refs_2_ = bf16[96,384]{1,0:T(8,128)(2,1)S(1)} collective-permute-done((bf16[96,384]{1,0:T(8,128)(2,1)S(1)}, bf16[96,384]{1,0:T(8,128)(2,1)S(1)}, u32[]{:S(2)}, u32[]{:S(2)}) %collective-permute-start.12) | collective-permute-done | bytes 73760 | tf_op jit(solution)/shard_map/ppermute | solution.py:169
  39.4 0.0 collective-permute-done.13.refs_3_
  39.5 1.3 %collective-permute-start.15 = (bf16[96,384]{1,0:T(8,128)(2,1)S(1)}, bf16[96,384]{1,0:T(8,128)(2,1)S(1)}, u32[]{:S(2)}, u32[]{:S(2)}) collective-permute-start(bf16[96,384]{1,0:T(8,128)(2,1)S(1)} %shard_map.104.refs_0_), channel_id=1, source_target_pairs={{0,2},{1,3},{2,0},{3,1},{4,6},{5,7},{6,4},{7,5},{8,10},{9,11},{10,... | collective-permute-start | bytes 221192 | tf_op jit(solution)/shard_map/ppermute | solution.py:169
  40.7 0.0 collective-permute-start.14
  40.7 3.1 %collective-permute-done.15.refs_2_ = bf16[96,384]{1,0:T(8,128)(2,1)S(1)} collective-permute-done((bf16[96,384]{1,0:T(8,128)(2,1)S(1)}, bf16[96,384]{1,0:T(8,128)(2,1)S(1)}, u32[]{:S(2)}, u32[]{:S(2)}) %collective-permute-start.15) | collective-permute-done | bytes 73760 | tf_op jit(solution)/shard_map/ppermute | solution.py:169
  43.9 0.0 collective-permute-start.16
  43.9 0.7 %convert_element_type.3 = bf16[128,768]{1,0:T(8,128)(2,1)} convert(f32[128,768]{1,0:T(8,128)S(1)} %get-tuple-element.29) | non-fusion elementwise | flops 98304 | bytes 589824 | tf_op jit(solution)/shard_map/convert_element_type | solution.py:364
  44.6 0.0 collective-permute-done.14.refs_1_
  44.6 0.6 %collective-permute-done.16.refs_3_ = bf16[96,384]{1,0:T(8,128)(2,1)S(1)} collective-permute-done((bf16[96,384]{1,0:T(8,128)(2,1)S(1)}, bf16[96,384]{1,0:T(8,128)(2,1)S(1)}, u32[]{:S(2)}, u32[]{:S(2)}) %collective-permute-start.16) | collective-permute-done | bytes 73760 | tf_op jit(solution)/shard_map/ppermute | solution.py:169
  45.1 0.9 %shard_map.105 = (f32[96,768]{1,0:T(8,128)}, f32[96,768]{1,0:T(8,128)}) custom-call(bf16[96,384]{1,0:T(8,128)(2,1)S(1)} %shard_map.104.refs_0_, bf16[96,384]{1,0:T(8,128)(2,1)S(1)} %collective-permute-done.14.refs_1_, bf16[96,384]{1,0:T(8,128)(2,1)S(1)} %collective-permute-done.15.refs_2_, bf16[96,384]{1,0:T(8,128)(2,1)S(1)} %collective-permute-done.16.refs_3_), custom_call_target="tpu_custom_call" | custom-call | bytes 884736 | tf_op jit(solution)/shard_map/pallas_call | solution.py:23
  (3 shorter events, 0.1 us)
Async XLA Ops:
  0.6 13.6 %copy-start = (bf16[768,768]{1,0:T(8,128)(2,1)S(1)}, bf16[768,768]{1,0:T(8,128)(2,1)}, u32[]{:S(2)}) copy-start(bf16[768,768]{1,0:T(8,128)(2,1)} %param.12) | copy-start | bytes 3538948
  2.9 13.0 %copy-start.4 = (s32[1,1,8,12]{3,2,1,0:T(8,128)S(1)}, s32[1,1,8,12]{3,2,1,0:T(8,128)}, u32[]{:S(2)}) copy-start(s32[1,1,8,12]{3,2,1,0:T(8,128)} %param.10) | copy-start | bytes 1156
  2.9 13.0 %all-to-all-start = ((bf16[8,80,128]{2,1,0:T(8,128)(2,1)}), bf16[8,80,128]{2,1,0:T(8,128)(2,1)S(1)}, u32[]{:S(2)}, u32[]{:S(2)}) async-start(bf16[8,80,128]{2,1,0:T(8,128)(2,1)} %bitcast.10), calls=%async_computation | async-start | bytes 327680 | tf_op jit(solution)/shard_map/all_to_all | solution.py:284
  10.7 6.8 %copy-start.1 = (bf16[768,768]{1,0:T(8,128)(2,1)S(1)}, bf16[768,768]{1,0:T(8,128)(2,1)}, u32[]{:S(2)}) copy-start(bf16[768,768]{1,0:T(8,128)(2,1)} %w_ref.1) | copy-start | bytes 3538948
  10.7 6.8 %copy-start.2 = (bf16[128,768]{1,0:T(8,128)(2,1)S(1)}, bf16[128,768]{1,0:T(8,128)(2,1)}, u32[]{:S(2)}) copy-start(bf16[128,768]{1,0:T(8,128)(2,1)} %cot_ref.1) | copy-start | bytes 589828
  10.7 8.8 %collective-permute-start = (bf16[384,128]{1,0:T(8,128)(2,1)}, bf16[384,128]{1,0:T(8,128)(2,1)S(1)}, u32[]{:S(2)}, u32[]{:S(2)}) collective-permute-start(bf16[384,128]{1,0:T(8,128)(2,1)} %get-tuple-element.30), channel_id=1, source_target_pairs={{0,6},{1,7},{2,4},{3,5},{4,2},{5,3},{6,0},{7,1},{8,14},{9,15},{10,... | collective-permute-start | bytes 294920 | tf_op jit(solution)/shard_map/ppermute | solution.py:169
  13.2 6.9 %collective-permute-start.1 = (bf16[384,128]{1,0:T(8,128)(2,1)}, bf16[384,128]{1,0:T(8,128)(2,1)S(1)}, u32[]{:S(2)}, u32[]{:S(2)}) collective-permute-start(bf16[384,128]{1,0:T(8,128)(2,1)} %get-tuple-element.30), channel_id=1, source_target_pairs={{0,4},{1,5},{2,6},{3,7},{4,0},{5,1},{6,2},{7,3},{8,12},{9,13},{10,... | collective-permute-start | bytes 294920 | tf_op jit(solution)/shard_map/ppermute | solution.py:169
  13.7 7.4 %collective-permute-start.2 = (bf16[384,128]{1,0:T(8,128)(2,1)}, bf16[384,128]{1,0:T(8,128)(2,1)S(1)}, u32[]{:S(2)}, u32[]{:S(2)}) collective-permute-start(bf16[384,128]{1,0:T(8,128)(2,1)} %get-tuple-element.31.refs_3_), channel_id=1, source_target_pairs={{0,2},{1,3},{2,0},{3,1},{4,6},{5,7},{6,4},{7,5},{8,10},{9,11},{10,... | collective-permute-start | bytes 294920 | tf_op jit(solution)/shard_map/ppermute | solution.py:169
  15.9 10.2 %copy-start.3 = (bf16[384,128]{1,0:T(8,128)(2,1)S(1)}, bf16[384,128]{1,0:T(8,128)(2,1)}, u32[]{:S(2)}) copy-start(bf16[384,128]{1,0:T(8,128)(2,1)} %get-tuple-element.31.refs_3_) | copy-start | bytes 294916
  16.5 5.0 %collective-permute-start.4 = (bf16[384,128]{1,0:T(8,128)(2,1)S(1)}, bf16[384,128]{1,0:T(8,128)(2,1)S(1)}, u32[]{:S(2)}, u32[]{:S(2)}) collective-permute-start(bf16[384,128]{1,0:T(8,128)(2,1)S(1)} %get-tuple-element.33), channel_id=1, source_target_pairs={{0,4},{1,5},{2,6},{3,7},{4,0},{5,1},{6,2},{7,3},{8,12},{9,13},{10,... | collective-permute-start | bytes 294920 | tf_op jit(solution)/shard_map/ppermute | solution.py:169
  18.0 5.6 %collective-permute-start.6 = (bf16[384,128]{1,0:T(8,128)(2,1)S(1)}, bf16[384,128]{1,0:T(8,128)(2,1)S(1)}, u32[]{:S(2)}, u32[]{:S(2)}) collective-permute-start(bf16[384,128]{1,0:T(8,128)(2,1)S(1)} %get-tuple-element.38), channel_id=1, source_target_pairs={{0,2},{1,3},{2,0},{3,1},{4,6},{5,7},{6,4},{7,5},{8,10},{9,11},{10,... | collective-permute-start | bytes 294920 | tf_op jit(solution)/shard_map/ppermute | solution.py:169
  19.6 5.2 %collective-permute-start.3 = (bf16[384,128]{1,0:T(8,128)(2,1)S(1)}, bf16[384,128]{1,0:T(8,128)(2,1)S(1)}, u32[]{:S(2)}, u32[]{:S(2)}) collective-permute-start(bf16[384,128]{1,0:T(8,128)(2,1)S(1)} %get-tuple-element.32.refs_4_), channel_id=1, source_target_pairs={{0,2},{1,3},{2,0},{3,1},{4,6},{5,7},{6,4},{7,5},{8,10},{9,11},{10,... | collective-permute-start | bytes 294920 | tf_op jit(solution)/shard_map/ppermute | solution.py:169
  20.1 6.2 %collective-permute-start.7 = (bf16[384,128]{1,0:T(8,128)(2,1)S(1)}, bf16[384,128]{1,0:T(8,128)(2,1)S(1)}, u32[]{:S(2)}, u32[]{:S(2)}) collective-permute-start(bf16[384,128]{1,0:T(8,128)(2,1)S(1)} %get-tuple-element.37.refs_0_), channel_id=1, source_target_pairs={{0,4},{1,5},{2,6},{3,7},{4,0},{5,1},{6,2},{7,3},{8,12},{9,13},{10,... | collective-permute-start | bytes 294920 | tf_op jit(solution)/shard_map/ppermute | solution.py:169
  21.5 4.6 %collective-permute-start.5 = (bf16[384,128]{1,0:T(8,128)(2,1)S(1)}, bf16[384,128]{1,0:T(8,128)(2,1)S(1)}, u32[]{:S(2)}, u32[]{:S(2)}) collective-permute-start(bf16[384,128]{1,0:T(8,128)(2,1)S(1)} %collective-permute-done.4.refs_6_), channel_id=1, source_target_pairs={{0,2},{1,3},{2,0},{3,1},{4,6},{5,7},{6,4},{7,5},{8,10},{9,11},{10,... | collective-permute-start | bytes 294920 | tf_op jit(solution)/shard_map/ppermute | solution.py:169
  23.5 4.6 %collective-permute-start.8 = (bf16[384,128]{1,0:T(8,128)(2,1)S(1)}, bf16[384,128]{1,0:T(8,128)(2,1)S(1)}, u32[]{:S(2)}, u32[]{:S(2)}) collective-permute-start(bf16[384,128]{1,0:T(8,128)(2,1)S(1)} %collective-permute-done.6.refs_1_), channel_id=1, source_target_pairs={{0,4},{1,5},{2,6},{3,7},{4,0},{5,1},{6,2},{7,3},{8,12},{9,13},{10,... | collective-permute-start | bytes 294920 | tf_op jit(solution)/shard_map/ppermute | solution.py:169
  28.4 1.4 %collective-permute-start.9 = (bf16[192,384]{1,0:T(8,128)(2,1)S(1)}, bf16[192,384]{1,0:T(8,128)(2,1)S(1)}, u32[]{:S(2)}, u32[]{:S(2)}) collective-permute-start(bf16[192,384]{1,0:T(8,128)(2,1)S(1)} %shard_map.98), channel_id=1, source_target_pairs={{0,1},{1,0},{2,3},{3,2},{4,5},{5,4},{6,7},{7,6},{8,9},{9,8},{10,11... | collective-permute-start | bytes 442376 | tf_op jit(solution)/shard_map/ppermute | solution.py:169
  28.8 3.8 %collective-permute-start.10 = (bf16[192,384]{1,0:T(8,128)(2,1)S(1)}, bf16[192,384]{1,0:T(8,128)(2,1)S(1)}, u32[]{:S(2)}, u32[]{:S(2)}) collective-permute-start(bf16[192,384]{1,0:T(8,128)(2,1)S(1)} %shard_map.100), channel_id=1, source_target_pairs={{0,1},{1,0},{2,3},{3,2},{4,5},{5,4},{6,7},{7,6},{8,9},{9,8},{10,11... | collective-permute-start | bytes 442376 | tf_op jit(solution)/shard_map/ppermute | solution.py:169
  29.9 7.1 %collective-permute-start.11 = (bf16[96,384]{1,0:T(8,128)(2,1)S(1)}, bf16[96,384]{1,0:T(8,128)(2,1)S(1)}, u32[]{:S(2)}, u32[]{:S(2)}) collective-permute-start(bf16[96,384]{1,0:T(8,128)(2,1)S(1)} %get-tuple-element.44), channel_id=1, source_target_pairs={{0,24},{1,25},{2,26},{3,27},{4,28},{5,29},{6,30},{7,31},{8,16},{9,... | collective-permute-start | bytes 221192 | tf_op jit(solution)/shard_map/ppermute | solution.py:169
  31.3 8.1 %collective-permute-start.12 = (bf16[96,384]{1,0:T(8,128)(2,1)S(1)}, bf16[96,384]{1,0:T(8,128)(2,1)S(1)}, u32[]{:S(2)}, u32[]{:S(2)}) collective-permute-start(bf16[96,384]{1,0:T(8,128)(2,1)S(1)} %get-tuple-element.45), channel_id=1, source_target_pairs={{0,16},{1,17},{2,18},{3,19},{4,20},{5,21},{6,22},{7,23},{8,24},{9,... | collective-permute-start | bytes 221192 | tf_op jit(solution)/shard_map/ppermute | solution.py:169
  32.6 6.8 %collective-permute-start.13 = (bf16[96,384]{1,0:T(8,128)(2,1)S(1)}, bf16[96,384]{1,0:T(8,128)(2,1)S(1)}, u32[]{:S(2)}, u32[]{:S(2)}) collective-permute-start(bf16[96,384]{1,0:T(8,128)(2,1)S(1)} %get-tuple-element.46), channel_id=1, source_target_pairs={{0,8},{1,9},{2,10},{3,11},{4,12},{5,13},{6,14},{7,15},{8,0},{9,1},... | collective-permute-start | bytes 221192 | tf_op jit(solution)/shard_map/ppermute | solution.py:169
  39.5 4.4 %collective-permute-start.15 = (bf16[96,384]{1,0:T(8,128)(2,1)S(1)}, bf16[96,384]{1,0:T(8,128)(2,1)S(1)}, u32[]{:S(2)}, u32[]{:S(2)}) collective-permute-start(bf16[96,384]{1,0:T(8,128)(2,1)S(1)} %shard_map.104.refs_0_), channel_id=1, source_target_pairs={{0,2},{1,3},{2,0},{3,1},{4,6},{5,7},{6,4},{7,5},{8,10},{9,11},{10,... | collective-permute-start | bytes 221192 | tf_op jit(solution)/shard_map/ppermute | solution.py:169
  40.7 3.9 %collective-permute-start.14 = (bf16[96,384]{1,0:T(8,128)(2,1)S(1)}, bf16[96,384]{1,0:T(8,128)(2,1)S(1)}, u32[]{:S(2)}, u32[]{:S(2)}) collective-permute-start(bf16[96,384]{1,0:T(8,128)(2,1)S(1)} %shard_map.104.refs_0_), channel_id=1, source_target_pairs={{0,1},{1,0},{2,3},{3,2},{4,5},{5,4},{6,7},{7,6},{8,9},{9,8},{10,11... | collective-permute-start | bytes 221192 | tf_op jit(solution)/shard_map/ppermute | solution.py:169
  43.9 1.3 %collective-permute-start.16 = (bf16[96,384]{1,0:T(8,128)(2,1)S(1)}, bf16[96,384]{1,0:T(8,128)(2,1)S(1)}, u32[]{:S(2)}, u32[]{:S(2)}) collective-permute-start(bf16[96,384]{1,0:T(8,128)(2,1)S(1)} %collective-permute-done.15.refs_2_), channel_id=1, source_target_pairs={{0,1},{1,0},{2,3},{3,2},{4,5},{5,4},{6,7},{7,6},{8,9},{9,8},{10,11... | collective-permute-start | bytes 221192 | tf_op jit(solution)/shard_map/ppermute | solution.py:169

commit v14 on v13

--- a/solution.py
+++ b/solution.py
@@ -228,13 +228,20 @@
                 outs[2 + j][to, at] = jnp.where(keep_own, o[rows, :], m[rows, :])
 
 
-def terms_kernel(left_ref, *refs):
+def right_factor(grad, targets):
+    return jnp.concatenate(
+        [jnp.concatenate([g[b * targets:(b + 1) * targets, :] for b in range(g.shape[0] // targets)], axis=1)
+         for g in grad], axis=0)
+
+
+def first_terms_kernel(targets, left_ref, *refs):
     grad, out_ref = refs[:-1], refs[-1]
-    targets = left_ref.shape[1] // len(grad)
-    right = jnp.concatenate(
-        [jnp.concatenate([g[b * targets:(b + 1) * targets, :] for b in range(grad[0].shape[0] // targets)], axis=1)
-         for g in grad], axis=0)
-    out_ref[...] = dot(left_ref[...], right).astype(out_ref.dtype)
+    out_ref[...] = dot(left_ref[:, :len(grad) * targets], right_factor(grad, targets))
+
+
+def last_terms_kernel(targets, left_ref, first_ref, grad_ref, out_ref):
+    last = dot(left_ref[:, left_ref.shape[1] - targets:], right_factor([grad_ref], targets))
+    out_ref[...] = (first_ref[...] + last).astype(out_ref.dtype)
 
 
 def core_sum_kernel(plan, keep_ref, got_ref, *outs):
@@ -332,8 +339,10 @@
         return plan.send(array, lambda z, x, y, c: (z ^ k, x, y, c))
 
     def terms(left, kind):
-        return call(terms_kernel, [shape((left.shape[0], cols), kind)], [left] + grad_all,
-                    flops=2 * left.shape[0] * cols * targets * n)[0]
+        first = call(functools.partial(first_terms_kernel, targets), [shape((left.shape[0], cols), F32)],
+                     [left] + grad_all[:-1], flops=2 * left.shape[0] * cols * targets * (n - 1))
+        return call(functools.partial(last_terms_kernel, targets), [shape((left.shape[0], cols), kind)],
+                    [left] + list(first) + grad_all[-1:], flops=2 * left.shape[0] * cols * targets)[0]
 
     block = (plan.shard, cols)
     halves = [plan.far(), plan.near()]

time: 46.3 us -> 46.3 us (level)
  Pallas kernels: 5.3 us -> 5.98 us
  starting transfers between devices: 24.9 us -> 24.4 us
    pallas_call x12 -> x16, Pallas kernels: 5.3 us -> 5.98 us  [call(): pl.pallas_call(body, out_shape=list(outs), in_specs=[VMEM] * len(args) +...]
    ppermute x17, starting transfers between devices: 17.1 us -> 16.6 us  [send(): return lax.ppermute(array, ('store', 'trainer'), pairs)]
  transfers between devices with their start and end apart: 18 -> 18, of which waited for: 10 -> 10; matrix products, arithmetic and copies ran while one was open for 4% -> 4% of each run, Pallas kernels for 4% -> 6%
where the time goes in v14:
time: 46.3 us; the launch traced here: 46.1 us
  starting transfers between devices  24.4 us (53%)
  waiting for transfers between devices  12.9 us (28%)
  Pallas kernels  5.98 us (13%)
  matrix products  1.25 us (3%)
  between operations  0.8 us (2%)
  other arithmetic  0.7 us (2%)
    ppermute x17, starting transfers between devices, send(): return lax.ppermute(array, ('store', 'trainer'), pairs)  16.6 us
    ppermute x17, waiting for transfers between devices, send(): return lax.ppermute(array, ('store', 'trainer'), pairs)  12.5 us
    all_to_all x1, starting transfers between devices, per_device(): lax.all_to_all(sums.reshape(ns, packed, 128), 'store', split_axis=0, conc...  7.82 us
    pallas_call x16, Pallas kernels, call(): pl.pallas_call(body, out_shape=list(outs), in_specs=[VMEM] * len(args) +...  5.98 us
    dot_general x1, matrix products, dot(): return jnp.dot(a, b, preferred_element_type=F32)  1.25 us
  transfers between devices with their start and end apart: 18, of which 10 were waited for; matrix products, arithmetic and copies ran while one was open for 4% of the time, Pallas kernels for 6%

profile of v14, /device:TPU:0, one launch (start us, length us, event | category | flops | bytes accessed | tf_op | source)
XLA Modules:
  0.0 46.1 jit_solution(15143103011877592601)
XLA Ops:
  0.6 0.0 copy-start
  0.6 2.2 %shard_map.94 = (bf16[640,128]{1,0:T(8,128)(2,1)}, bf16[128,768]{1,0:T(8,128)(2,1)}, bf16[384,128]{1,0:T(8,128)(2,1)}, bf16[384,128]{1,0:T(8,128)(2,1)}) custom-call(f32[128,768]{1,0:T(8,128)} %feat_hbm.1, s32[8,2,12]{2,1,0:T(2,128)} %bitcast.11, f32[128,768]{1,0:T(8,128)} %rest_0_.1), custom_call_target="tpu_custom_call" | custom-call | flops 50331648 | bytes 557056 | tf_op jit(solution)/shard_map/pallas_call | solution.py:23
  2.9 0.0 copy-start.4
  2.9 7.8 %all-to-all-start = ((bf16[8,80,128]{2,1,0:T(8,128)(2,1)}), bf16[8,80,128]{2,1,0:T(8,128)(2,1)S(1)}, u32[]{:S(2)}, u32[]{:S(2)}) async-start(bf16[8,80,128]{2,1,0:T(8,128)(2,1)} %bitcast.10), calls=%async_computation | async-start | bytes 327680 | tf_op jit(solution)/shard_map/all_to_all | solution.py:291
  10.7 0.0 copy-start.1
  10.7 0.0 copy-start.2
  10.7 2.4 %collective-permute-start = (bf16[384,128]{1,0:T(8,128)(2,1)}, bf16[384,128]{1,0:T(8,128)(2,1)S(1)}, u32[]{:S(2)}, u32[]{:S(2)}) collective-permute-start(bf16[384,128]{1,0:T(8,128)(2,1)} %get-tuple-element.30), channel_id=1, source_target_pairs={{0,6},{1,7},{2,4},{3,5},{4,2},{5,3},{6,0},{7,1},{8,14},{9,15},{10,... | collective-permute-start | bytes 294920 | tf_op jit(solution)/shard_map/ppermute | solution.py:169
  13.2 0.6 %collective-permute-start.1 = (bf16[384,128]{1,0:T(8,128)(2,1)}, bf16[384,128]{1,0:T(8,128)(2,1)S(1)}, u32[]{:S(2)}, u32[]{:S(2)}) collective-permute-start(bf16[384,128]{1,0:T(8,128)(2,1)} %get-tuple-element.30), channel_id=1, source_target_pairs={{0,4},{1,5},{2,6},{3,7},{4,0},{5,1},{6,2},{7,3},{8,12},{9,13},{10,... | collective-permute-start | bytes 294920 | tf_op jit(solution)/shard_map/ppermute | solution.py:169
  13.7 0.5 %collective-permute-start.2 = (bf16[384,128]{1,0:T(8,128)(2,1)}, bf16[384,128]{1,0:T(8,128)(2,1)S(1)}, u32[]{:S(2)}, u32[]{:S(2)}) collective-permute-start(bf16[384,128]{1,0:T(8,128)(2,1)} %get-tuple-element.31.refs_3_), channel_id=1, source_target_pairs={{0,2},{1,3},{2,0},{3,1},{4,6},{5,7},{6,4},{7,5},{8,10},{9,11},{10,... | collective-permute-start | bytes 294920 | tf_op jit(solution)/shard_map/ppermute | solution.py:169
  14.2 0.0 copy-done
  14.2 1.2 %fusion._.self_ref = f32[128,768]{1,0:T(8,128)S(1)} fusion(bf16[128,768]{1,0:T(8,128)(2,1)} %get-tuple-element.27, bf16[768,768]{1,0:T(8,128)(2,1)S(1)} %copy-done), kind=kOutput, calls=%fused_computation | convolution fusion | flops 150994944 | bytes 1769472 | tf_op jit(solution)/shard_map/dot_general | solution.py:18
  15.5 0.5 all-to-all-done
  15.9 0.0 copy-done.4
  15.9 0.0 copy-start.3
  15.9 0.5 %shard_map.95 = (bf16[128,768]{1,0:T(8,128)(2,1)S(1)}, bf16[384,128]{1,0:T(8,128)(2,1)S(1)}, bf16[384,128]{1,0:T(8,128)(2,1)S(1)}) custom-call(bf16[640,128]{1,0:T(8,128)(2,1)S(1)} %bitcast.8, s32[8,12]{1,0:T(8,128)S(1)} %bitcast.9, f32[128,768]{1,0:T(8,128)S(1)} %fusion._.self_ref), custom_call_target="tpu_custom_call" | custom-call | flops 25165824 | bytes 950656 | tf_op jit(solution)/shard_map/pallas_call | solution.py:23
  16.5 1.1 %collective-permute-start.4 = (bf16[384,128]{1,0:T(8,128)(2,1)S(1)}, bf16[384,128]{1,0:T(8,128)(2,1)S(1)}, u32[]{:S(2)}, u32[]{:S(2)}) collective-permute-start(bf16[384,128]{1,0:T(8,128)(2,1)S(1)} %get-tuple-element.33), channel_id=1, source_target_pairs={{0,4},{1,5},{2,6},{3,7},{4,0},{5,1},{6,2},{7,3},{8,12},{9,13},{10,... | collective-permute-start | bytes 294920 | tf_op jit(solution)/shard_map/ppermute | solution.py:169
  17.6 0.0 copy-done.1
  17.6 0.0 copy-done.2
  17.6 0.4 shard_map.96
  18.0 1.6 %collective-permute-start.6 = (bf16[384,128]{1,0:T(8,128)(2,1)S(1)}, bf16[384,128]{1,0:T(8,128)(2,1)S(1)}, u32[]{:S(2)}, u32[]{:S(2)}) collective-permute-start(bf16[384,128]{1,0:T(8,128)(2,1)S(1)} %get-tuple-element.38), channel_id=1, source_target_pairs={{0,2},{1,3},{2,0},{3,1},{4,6},{5,7},{6,4},{7,5},{8,10},{9,11},{10,... | collective-permute-start | bytes 294920 | tf_op jit(solution)/shard_map/ppermute | solution.py:169
  19.6 0.0 collective-permute-done.refs_0_
  19.6 0.5 %collective-permute-start.3 = (bf16[384,128]{1,0:T(8,128)(2,1)S(1)}, bf16[384,128]{1,0:T(8,128)(2,1)S(1)}, u32[]{:S(2)}, u32[]{:S(2)}) collective-permute-start(bf16[384,128]{1,0:T(8,128)(2,1)S(1)} %get-tuple-element.32.refs_4_), channel_id=1, source_target_pairs={{0,2},{1,3},{2,0},{3,1},{4,6},{5,7},{6,4},{7,5},{8,10},{9,11},{10,... | collective-permute-start | bytes 294920 | tf_op jit(solution)/shard_map/ppermute | solution.py:169
  20.1 0.0 collective-permute-done.1.refs_1_
  20.1 0.0 collective-permute-done.2.refs_2_
  20.1 1.1 %collective-permute-done.4.refs_6_ = bf16[384,128]{1,0:T(8,128)(2,1)S(1)} collective-permute-done((bf16[384,128]{1,0:T(8,128)(2,1)S(1)}, bf16[384,128]{1,0:T(8,128)(2,1)S(1)}, u32[]{:S(2)}, u32[]{:S(2)}) %collective-permute-start.4) | collective-permute-done | bytes 98336 | tf_op jit(solution)/shard_map/ppermute | solution.py:169
  21.2 1.5 %collective-permute-start.5 = (bf16[384,128]{1,0:T(8,128)(2,1)S(1)}, bf16[384,128]{1,0:T(8,128)(2,1)S(1)}, u32[]{:S(2)}, u32[]{:S(2)}) collective-permute-start(bf16[384,128]{1,0:T(8,128)(2,1)S(1)} %collective-permute-done.4.refs_6_), channel_id=1, source_target_pairs={{0,2},{1,3},{2,0},{3,1},{4,6},{5,7},{6,4},{7,5},{8,10},{9,11},{10,... | collective-permute-start | bytes 294920 | tf_op jit(solution)/shard_map/ppermute | solution.py:169
  22.7 1.0 %collective-permute-start.7 = (bf16[384,128]{1,0:T(8,128)(2,1)S(1)}, bf16[384,128]{1,0:T(8,128)(2,1)S(1)}, u32[]{:S(2)}, u32[]{:S(2)}) collective-permute-start(bf16[384,128]{1,0:T(8,128)(2,1)S(1)} %get-tuple-element.37.refs_0_), channel_id=1, source_target_pairs={{0,4},{1,5},{2,6},{3,7},{4,0},{5,1},{6,2},{7,3},{8,12},{9,13},{10,... | collective-permute-start | bytes 294920 | tf_op jit(solution)/shard_map/ppermute | solution.py:169
  23.7 0.0 collective-permute-done.6.refs_1_
  23.7 1.0 %collective-permute-start.8 = (bf16[384,128]{1,0:T(8,128)(2,1)S(1)}, bf16[384,128]{1,0:T(8,128)(2,1)S(1)}, u32[]{:S(2)}, u32[]{:S(2)}) collective-permute-start(bf16[384,128]{1,0:T(8,128)(2,1)S(1)} %collective-permute-done.6.refs_1_), channel_id=1, source_target_pairs={{0,4},{1,5},{2,6},{3,7},{4,0},{5,1},{6,2},{7,3},{8,12},{9,13},{10,... | collective-permute-start | bytes 294920 | tf_op jit(solution)/shard_map/ppermute | solution.py:169
  24.7 0.1 collective-permute-done.3.refs_5_
  24.8 1.1 %collective-permute-done.5.refs_7_ = bf16[384,128]{1,0:T(8,128)(2,1)S(1)} collective-permute-done((bf16[384,128]{1,0:T(8,128)(2,1)S(1)}, bf16[384,128]{1,0:T(8,128)(2,1)S(1)}, u32[]{:S(2)}, u32[]{:S(2)}) %collective-permute-start.5) | collective-permute-done | bytes 98336 | tf_op jit(solution)/shard_map/ppermute | solution.py:169
  25.8 0.0 copy-done.3
  25.8 0.1 shard_map.97
  26.0 1.3 %collective-permute-done.7.refs_2_ = bf16[384,128]{1,0:T(8,128)(2,1)S(1)} collective-permute-done((bf16[384,128]{1,0:T(8,128)(2,1)S(1)}, bf16[384,128]{1,0:T(8,128)(2,1)S(1)}, u32[]{:S(2)}, u32[]{:S(2)}) %collective-permute-start.7) | collective-permute-done | bytes 98336 | tf_op jit(solution)/shard_map/ppermute | solution.py:169
  27.3 0.2 shard_map.98.first_ref
  27.5 0.8 %collective-permute-done.8.grad_ref = bf16[384,128]{1,0:T(8,128)(2,1)S(1)} collective-permute-done((bf16[384,128]{1,0:T(8,128)(2,1)S(1)}, bf16[384,128]{1,0:T(8,128)(2,1)S(1)}, u32[]{:S(2)}, u32[]{:S(2)}) %collective-permute-start.8) | collective-permute-done | bytes 98336 | tf_op jit(solution)/shard_map/ppermute | solution.py:169
  28.3 0.2 shard_map.99
  28.5 0.1 collective-permute-start.9
  28.6 0.2 shard_map.102.first_ref
  28.8 0.2 shard_map.103
  29.0 0.6 %collective-permute-start.10 = (bf16[192,384]{1,0:T(8,128)(2,1)S(1)}, bf16[192,384]{1,0:T(8,128)(2,1)S(1)}, u32[]{:S(2)}, u32[]{:S(2)}) collective-permute-start(bf16[192,384]{1,0:T(8,128)(2,1)S(1)} %shard_map.103), channel_id=1, source_target_pairs={{0,1},{1,0},{2,3},{3,2},{4,5},{5,4},{6,7},{7,6},{8,9},{9,8},{10,11... | collective-permute-start | bytes 442376 | tf_op jit(solution)/shard_map/ppermute | solution.py:169
  29.6 0.2 shard_map.105.first_ref
  29.8 0.2 shard_map.106.keep_ref
  30.0 0.0 collective-permute-done.9.got_ref
  30.1 2.0 %collective-permute-start.11 = (bf16[96,384]{1,0:T(8,128)(2,1)S(1)}, bf16[96,384]{1,0:T(8,128)(2,1)S(1)}, u32[]{:S(2)}, u32[]{:S(2)}) collective-permute-start(bf16[96,384]{1,0:T(8,128)(2,1)S(1)} %get-tuple-element.44), channel_id=1, source_target_pairs={{0,24},{1,25},{2,26},{3,27},{4,28},{5,29},{6,30},{7,31},{8,16},{9,... | collective-permute-start | bytes 221192 | tf_op jit(solution)/shard_map/ppermute | solution.py:169
  32.1 0.3 collective-permute-start.12
  32.4 0.2 shard_map.100.first_ref
  32.6 0.2 shard_map.101.keep_ref
  32.8 0.0 collective-permute-done.10.got_ref
  32.9 2.2 %collective-permute-start.13 = (bf16[96,384]{1,0:T(8,128)(2,1)S(1)}, bf16[96,384]{1,0:T(8,128)(2,1)S(1)}, u32[]{:S(2)}, u32[]{:S(2)}) collective-permute-start(bf16[96,384]{1,0:T(8,128)(2,1)S(1)} %get-tuple-element.46), channel_id=1, source_target_pairs={{0,8},{1,9},{2,10},{3,11},{4,12},{5,13},{6,14},{7,15},{8,0},{9,1},... | collective-permute-start | bytes 221192 | tf_op jit(solution)/shard_map/ppermute | solution.py:169
  35.1 2.0 %collective-permute-done.11.refs_1_ = bf16[96,384]{1,0:T(8,128)(2,1)S(1)} collective-permute-done((bf16[96,384]{1,0:T(8,128)(2,1)S(1)}, bf16[96,384]{1,0:T(8,128)(2,1)S(1)}, u32[]{:S(2)}, u32[]{:S(2)}) %collective-permute-start.11) | collective-permute-done | bytes 73760 | tf_op jit(solution)/shard_map/ppermute | solution.py:169
  37.1 2.4 %collective-permute-done.12.refs_2_ = bf16[96,384]{1,0:T(8,128)(2,1)S(1)} collective-permute-done((bf16[96,384]{1,0:T(8,128)(2,1)S(1)}, bf16[96,384]{1,0:T(8,128)(2,1)S(1)}, u32[]{:S(2)}, u32[]{:S(2)}) %collective-permute-start.12) | collective-permute-done | bytes 73760 | tf_op jit(solution)/shard_map/ppermute | solution.py:169
  39.4 0.0 collective-permute-done.13.refs_3_
  39.5 1.2 %collective-permute-start.15 = (bf16[96,384]{1,0:T(8,128)(2,1)S(1)}, bf16[96,384]{1,0:T(8,128)(2,1)S(1)}, u32[]{:S(2)}, u32[]{:S(2)}) collective-permute-start(bf16[96,384]{1,0:T(8,128)(2,1)S(1)} %shard_map.108.refs_0_), channel_id=1, source_target_pairs={{0,2},{1,3},{2,0},{3,1},{4,6},{5,7},{6,4},{7,5},{8,10},{9,11},{10,... | collective-permute-start | bytes 221192 | tf_op jit(solution)/shard_map/ppermute | solution.py:169
  40.7 0.0 collective-permute-start.14
  40.7 3.2 %collective-permute-done.15.refs_2_ = bf16[96,384]{1,0:T(8,128)(2,1)S(1)} collective-permute-done((bf16[96,384]{1,0:T(8,128)(2,1)S(1)}, bf16[96,384]{1,0:T(8,128)(2,1)S(1)}, u32[]{:S(2)}, u32[]{:S(2)}) %collective-permute-start.15) | collective-permute-done | bytes 73760 | tf_op jit(solution)/shard_map/ppermute | solution.py:169
  43.9 0.0 collective-permute-start.16
  43.9 0.7 %convert_element_type.3 = bf16[128,768]{1,0:T(8,128)(2,1)} convert(f32[128,768]{1,0:T(8,128)S(1)} %get-tuple-element.29) | non-fusion elementwise | flops 98304 | bytes 589824 | tf_op jit(solution)/shard_map/convert_element_type | solution.py:373
  44.6 0.0 collective-permute-done.14.refs_1_
  44.6 0.6 %collective-permute-done.16.refs_3_ = bf16[96,384]{1,0:T(8,128)(2,1)S(1)} collective-permute-done((bf16[96,384]{1,0:T(8,128)(2,1)S(1)}, bf16[96,384]{1,0:T(8,128)(2,1)S(1)}, u32[]{:S(2)}, u32[]{:S(2)}) %collective-permute-start.16) | collective-permute-done | bytes 73760 | tf_op jit(solution)/shard_map/ppermute | solution.py:169
  45.2 0.9 %shard_map.109 = (f32[96,768]{1,0:T(8,128)}, f32[96,768]{1,0:T(8,128)}) custom-call(bf16[96,384]{1,0:T(8,128)(2,1)S(1)} %shard_map.108.refs_0_, bf16[96,384]{1,0:T(8,128)(2,1)S(1)} %collective-permute-done.14.refs_1_, bf16[96,384]{1,0:T(8,128)(2,1)S(1)} %collective-permute-done.15.refs_2_, bf16[96,384]{1,0:T(8,128)(2,1)S(1)} %collective-permute-done.16.refs_3_), custom_call_target="tpu_custom_call" | custom-call | bytes 884736 | tf_op jit(solution)/shard_map/pallas_call | solution.py:23
  (3 shorter events, 0.1 us)
Async XLA Ops:
  0.6 13.6 %copy-start = (bf16[768,768]{1,0:T(8,128)(2,1)S(1)}, bf16[768,768]{1,0:T(8,128)(2,1)}, u32[]{:S(2)}) copy-start(bf16[768,768]{1,0:T(8,128)(2,1)} %param.12) | copy-start | bytes 3538948
  2.9 13.0 %copy-start.4 = (s32[1,1,8,12]{3,2,1,0:T(8,128)S(1)}, s32[1,1,8,12]{3,2,1,0:T(8,128)}, u32[]{:S(2)}) copy-start(s32[1,1,8,12]{3,2,1,0:T(8,128)} %param.10) | copy-start | bytes 1156
  2.9 13.0 %all-to-all-start = ((bf16[8,80,128]{2,1,0:T(8,128)(2,1)}), bf16[8,80,128]{2,1,0:T(8,128)(2,1)S(1)}, u32[]{:S(2)}, u32[]{:S(2)}) async-start(bf16[8,80,128]{2,1,0:T(8,128)(2,1)} %bitcast.10), calls=%async_computation | async-start | bytes 327680 | tf_op jit(solution)/shard_map/all_to_all | solution.py:291
  10.7 6.8 %copy-start.1 = (bf16[768,768]{1,0:T(8,128)(2,1)S(1)}, bf16[768,768]{1,0:T(8,128)(2,1)}, u32[]{:S(2)}) copy-start(bf16[768,768]{1,0:T(8,128)(2,1)} %w_ref.1) | copy-start | bytes 3538948
  10.7 6.8 %copy-start.2 = (bf16[128,768]{1,0:T(8,128)(2,1)S(1)}, bf16[128,768]{1,0:T(8,128)(2,1)}, u32[]{:S(2)}) copy-start(bf16[128,768]{1,0:T(8,128)(2,1)} %cot_ref.1) | copy-start | bytes 589828
  10.7 8.8 %collective-permute-start = (bf16[384,128]{1,0:T(8,128)(2,1)}, bf16[384,128]{1,0:T(8,128)(2,1)S(1)}, u32[]{:S(2)}, u32[]{:S(2)}) collective-permute-start(bf16[384,128]{1,0:T(8,128)(2,1)} %get-tuple-element.30), channel_id=1, source_target_pairs={{0,6},{1,7},{2,4},{3,5},{4,2},{5,3},{6,0},{7,1},{8,14},{9,15},{10,... | collective-permute-start | bytes 294920 | tf_op jit(solution)/shard_map/ppermute | solution.py:169
  13.2 6.9 %collective-permute-start.1 = (bf16[384,128]{1,0:T(8,128)(2,1)}, bf16[384,128]{1,0:T(8,128)(2,1)S(1)}, u32[]{:S(2)}, u32[]{:S(2)}) collective-permute-start(bf16[384,128]{1,0:T(8,128)(2,1)} %get-tuple-element.30), channel_id=1, source_target_pairs={{0,4},{1,5},{2,6},{3,7},{4,0},{5,1},{6,2},{7,3},{8,12},{9,13},{10,... | collective-permute-start | bytes 294920 | tf_op jit(solution)/shard_map/ppermute | solution.py:169
  13.7 6.4 %collective-permute-start.2 = (bf16[384,128]{1,0:T(8,128)(2,1)}, bf16[384,128]{1,0:T(8,128)(2,1)S(1)}, u32[]{:S(2)}, u32[]{:S(2)}) collective-permute-start(bf16[384,128]{1,0:T(8,128)(2,1)} %get-tuple-element.31.refs_3_), channel_id=1, source_target_pairs={{0,2},{1,3},{2,0},{3,1},{4,6},{5,7},{6,4},{7,5},{8,10},{9,11},{10,... | collective-permute-start | bytes 294920 | tf_op jit(solution)/shard_map/ppermute | solution.py:169
  15.9 9.9 %copy-start.3 = (bf16[384,128]{1,0:T(8,128)(2,1)S(1)}, bf16[384,128]{1,0:T(8,128)(2,1)}, u32[]{:S(2)}) copy-start(bf16[384,128]{1,0:T(8,128)(2,1)} %get-tuple-element.31.refs_3_) | copy-start | bytes 294916
  16.5 4.7 %collective-permute-start.4 = (bf16[384,128]{1,0:T(8,128)(2,1)S(1)}, bf16[384,128]{1,0:T(8,128)(2,1)S(1)}, u32[]{:S(2)}, u32[]{:S(2)}) collective-permute-start(bf16[384,128]{1,0:T(8,128)(2,1)S(1)} %get-tuple-element.33), channel_id=1, source_target_pairs={{0,4},{1,5},{2,6},{3,7},{4,0},{5,1},{6,2},{7,3},{8,12},{9,13},{10,... | collective-permute-start | bytes 294920 | tf_op jit(solution)/shard_map/ppermute | solution.py:169
  18.0 5.7 %collective-permute-start.6 = (bf16[384,128]{1,0:T(8,128)(2,1)S(1)}, bf16[384,128]{1,0:T(8,128)(2,1)S(1)}, u32[]{:S(2)}, u32[]{:S(2)}) collective-permute-start(bf16[384,128]{1,0:T(8,128)(2,1)S(1)} %get-tuple-element.38), channel_id=1, source_target_pairs={{0,2},{1,3},{2,0},{3,1},{4,6},{5,7},{6,4},{7,5},{8,10},{9,11},{10,... | collective-permute-start | bytes 294920 | tf_op jit(solution)/shard_map/ppermute | solution.py:169
  19.6 5.2 %collective-permute-start.3 = (bf16[384,128]{1,0:T(8,128)(2,1)S(1)}, bf16[384,128]{1,0:T(8,128)(2,1)S(1)}, u32[]{:S(2)}, u32[]{:S(2)}) collective-permute-start(bf16[384,128]{1,0:T(8,128)(2,1)S(1)} %get-tuple-element.32.refs_4_), channel_id=1, source_target_pairs={{0,2},{1,3},{2,0},{3,1},{4,6},{5,7},{6,4},{7,5},{8,10},{9,11},{10,... | collective-permute-start | bytes 294920 | tf_op jit(solution)/shard_map/ppermute | solution.py:169
  21.2 4.7 %collective-permute-start.5 = (bf16[384,128]{1,0:T(8,128)(2,1)S(1)}, bf16[384,128]{1,0:T(8,128)(2,1)S(1)}, u32[]{:S(2)}, u32[]{:S(2)}) collective-permute-start(bf16[384,128]{1,0:T(8,128)(2,1)S(1)} %collective-permute-done.4.refs_6_), channel_id=1, source_target_pairs={{0,2},{1,3},{2,0},{3,1},{4,6},{5,7},{6,4},{7,5},{8,10},{9,11},{10,... | collective-permute-start | bytes 294920 | tf_op jit(solution)/shard_map/ppermute | solution.py:169
  22.7 4.6 %collective-permute-start.7 = (bf16[384,128]{1,0:T(8,128)(2,1)S(1)}, bf16[384,128]{1,0:T(8,128)(2,1)S(1)}, u32[]{:S(2)}, u32[]{:S(2)}) collective-permute-start(bf16[384,128]{1,0:T(8,128)(2,1)S(1)} %get-tuple-element.37.refs_0_), channel_id=1, source_target_pairs={{0,4},{1,5},{2,6},{3,7},{4,0},{5,1},{6,2},{7,3},{8,12},{9,13},{10,... | collective-permute-start | bytes 294920 | tf_op jit(solution)/shard_map/ppermute | solution.py:169
  23.7 4.6 %collective-permute-start.8 = (bf16[384,128]{1,0:T(8,128)(2,1)S(1)}, bf16[384,128]{1,0:T(8,128)(2,1)S(1)}, u32[]{:S(2)}, u32[]{:S(2)}) collective-permute-start(bf16[384,128]{1,0:T(8,128)(2,1)S(1)} %collective-permute-done.6.refs_1_), channel_id=1, source_target_pairs={{0,4},{1,5},{2,6},{3,7},{4,0},{5,1},{6,2},{7,3},{8,12},{9,13},{10,... | collective-permute-start | bytes 294920 | tf_op jit(solution)/shard_map/ppermute | solution.py:169
  28.5 1.5 %collective-permute-start.9 = (bf16[192,384]{1,0:T(8,128)(2,1)S(1)}, bf16[192,384]{1,0:T(8,128)(2,1)S(1)}, u32[]{:S(2)}, u32[]{:S(2)}) collective-permute-start(bf16[192,384]{1,0:T(8,128)(2,1)S(1)} %shard_map.99), channel_id=1, source_target_pairs={{0,1},{1,0},{2,3},{3,2},{4,5},{5,4},{6,7},{7,6},{8,9},{9,8},{10,11... | collective-permute-start | bytes 442376 | tf_op jit(solution)/shard_map/ppermute | solution.py:169
  29.0 3.8 %collective-permute-start.10 = (bf16[192,384]{1,0:T(8,128)(2,1)S(1)}, bf16[192,384]{1,0:T(8,128)(2,1)S(1)}, u32[]{:S(2)}, u32[]{:S(2)}) collective-permute-start(bf16[192,384]{1,0:T(8,128)(2,1)S(1)} %shard_map.103), channel_id=1, source_target_pairs={{0,1},{1,0},{2,3},{3,2},{4,5},{5,4},{6,7},{7,6},{8,9},{9,8},{10,11... | collective-permute-start | bytes 442376 | tf_op jit(solution)/shard_map/ppermute | solution.py:169
  30.1 7.0 %collective-permute-start.11 = (bf16[96,384]{1,0:T(8,128)(2,1)S(1)}, bf16[96,384]{1,0:T(8,128)(2,1)S(1)}, u32[]{:S(2)}, u32[]{:S(2)}) collective-permute-start(bf16[96,384]{1,0:T(8,128)(2,1)S(1)} %get-tuple-element.44), channel_id=1, source_target_pairs={{0,24},{1,25},{2,26},{3,27},{4,28},{5,29},{6,30},{7,31},{8,16},{9,... | collective-permute-start | bytes 221192 | tf_op jit(solution)/shard_map/ppermute | solution.py:169
  32.1 7.4 %collective-permute-start.12 = (bf16[96,384]{1,0:T(8,128)(2,1)S(1)}, bf16[96,384]{1,0:T(8,128)(2,1)S(1)}, u32[]{:S(2)}, u32[]{:S(2)}) collective-permute-start(bf16[96,384]{1,0:T(8,128)(2,1)S(1)} %get-tuple-element.45), channel_id=1, source_target_pairs={{0,16},{1,17},{2,18},{3,19},{4,20},{5,21},{6,22},{7,23},{8,24},{9,... | collective-permute-start | bytes 221192 | tf_op jit(solution)/shard_map/ppermute | solution.py:169
  32.9 6.6 %collective-permute-start.13 = (bf16[96,384]{1,0:T(8,128)(2,1)S(1)}, bf16[96,384]{1,0:T(8,128)(2,1)S(1)}, u32[]{:S(2)}, u32[]{:S(2)}) collective-permute-start(bf16[96,384]{1,0:T(8,128)(2,1)S(1)} %get-tuple-element.46), channel_id=1, source_target_pairs={{0,8},{1,9},{2,10},{3,11},{4,12},{5,13},{6,14},{7,15},{8,0},{9,1},... | collective-permute-start | bytes 221192 | tf_op jit(solution)/shard_map/ppermute | solution.py:169
  39.5 4.4 %collective-permute-start.15 = (bf16[96,384]{1,0:T(8,128)(2,1)S(1)}, bf16[96,384]{1,0:T(8,128)(2,1)S(1)}, u32[]{:S(2)}, u32[]{:S(2)}) collective-permute-start(bf16[96,384]{1,0:T(8,128)(2,1)S(1)} %shard_map.108.refs_0_), channel_id=1, source_target_pairs={{0,2},{1,3},{2,0},{3,1},{4,6},{5,7},{6,4},{7,5},{8,10},{9,11},{10,... | collective-permute-start | bytes 221192 | tf_op jit(solution)/shard_map/ppermute | solution.py:169
  40.7 3.9 %collective-permute-start.14 = (bf16[96,384]{1,0:T(8,128)(2,1)S(1)}, bf16[96,384]{1,0:T(8,128)(2,1)S(1)}, u32[]{:S(2)}, u32[]{:S(2)}) collective-permute-start(bf16[96,384]{1,0:T(8,128)(2,1)S(1)} %shard_map.108.refs_0_), channel_id=1, source_target_pairs={{0,1},{1,0},{2,3},{3,2},{4,5},{5,4},{6,7},{7,6},{8,9},{9,8},{10,11... | collective-permute-start | bytes 221192 | tf_op jit(solution)/shard_map/ppermute | solution.py:169
  43.9 1.3 %collective-permute-start.16 = (bf16[96,384]{1,0:T(8,128)(2,1)S(1)}, bf16[96,384]{1,0:T(8,128)(2,1)S(1)}, u32[]{:S(2)}, u32[]{:S(2)}) collective-permute-start(bf16[96,384]{1,0:T(8,128)(2,1)S(1)} %collective-permute-done.15.refs_2_), channel_id=1, source_target_pairs={{0,1},{1,0},{2,3},{3,2},{4,5},{5,4},{6,7},{7,6},{8,9},{9,8},{10,11... | collective-permute-start | bytes 221192 | tf_op jit(solution)/shard_map/ppermute | solution.py:169
